TPU v7x, 32 devices: a whole 2x2x4 slice. The times are simulated.
32 devices in a mesh: gx: 2 (over y), gy: 4 (over z), gz: 4 (over x, core).
Axes of the slice: x: 2, y: 2, z: 4, core: 2. Of those that a mesh axis runs over, the one named last changes fastest.
Arguments:
- right_side: float32 [32, 64, 1024], P('gx', 'gy', 'gz'), may hold values from -8 to 8
- conductance: float32 [3, 32, 64, 1024], P(None, 'gx', 'gy', 'gz'), may hold values from 0.2 to 5
- storage: float32 [32, 64, 1024], P('gx', 'gy', 'gz'), may hold values from 0.05 to 0.8
- dirichlet: int32 [32, 64, 1024], P('gx', 'gy', 'gz'), may hold values 0 or 1
- basis: float32 [16, 32, 64, 1024], P(None, 'gx', 'gy', 'gz'), may hold values from -2 to 2
- coarse_inverse: float32 [512, 512], P(('gx', 'gy', 'gz')), may hold values from 0 to 2, as said below
Outputs:
- solution_field: float32 [32, 64, 1024], P('gx', 'gy', 'gz')
- residual: float32 [32, 64, 1024], P('gx', 'gy', 'gz')
Inputs may be any that keep to these rules, and one draw needn't show every extreme that they name: `coarse_inverse`: symmetric positive definite.
All inputs are finite; a program needn't handle non-finite values. No bound on the sum of `dirichlet` on one device may be relied on, other than what follows from the above.
Results may differ from a plain program's by a relative error of at most 0.0003.
Values sent between devices are 32-bit elements; how exact they have to be, the bound alone decides.
No kernel may reach another device: no remote copies, remote signals or barrier semaphores. Data moves between devices by JAX's collectives and lax.ppermute only.
A program may use at most 128 MiB of HBM per device.

v0:
```python
import jax
import jax.numpy as jnp
from jax import lax
from jax.sharding import PartitionSpec as P

SWEEPS = 4
ITERS = 2


RELAX = 2.0 / 3.0


def padded(value, sides, width):
    for axis, dim in sides:
        count, length = (lax.axis_size(axis), value.shape[dim])
        up = [(i, (i + 1) % count) for i in range(count - 1)]
        down = [(j, i) for i, j in up]
        last = lax.slice_in_dim(value, length - width, length, axis=dim)
        leading = lax.slice_in_dim(value, 0, width, axis=dim)
        before = lax.ppermute(last, axis, up)
        after = lax.ppermute(leading, axis, down)
        value = jnp.concatenate([before, value, after], axis=dim)
    return value


def pad_cond(cond):
    return jnp.pad(cond, ((0, 0), (1, 1), (1, 1), (1, 1)))


def stencil(padded_free, padded_cond, field, storage, free):
    middle = padded_free[1:-1, 1:-1, 1:-1]
    total = storage * middle
    total = (
        total
        + padded_cond[0, 1:-1, 1:-1, 1:-1] * (middle - padded_free[2:, 1:-1, 1:-1])
        + padded_cond[0, :-2, 1:-1, 1:-1] * (middle - padded_free[:-2, 1:-1, 1:-1])
    )
    total = (
        total
        + padded_cond[1, 1:-1, 1:-1, 1:-1] * (middle - padded_free[1:-1, 2:, 1:-1])
        + padded_cond[1, 1:-1, :-2, 1:-1] * (middle - padded_free[1:-1, :-2, 1:-1])
    )
    total = (
        total
        + padded_cond[2, 1:-1, 1:-1, 1:-1] * (middle - padded_free[1:-1, 1:-1, 2:])
        + padded_cond[2, 1:-1, 1:-1, :-2] * (middle - padded_free[1:-1, 1:-1, :-2])
    )
    return free * total + (1.0 - free) * field


def diagonal_of(padded_cond, storage, free):
    total = storage + padded_cond[0, 1:-1, 1:-1, 1:-1] + padded_cond[0, :-2, 1:-1, 1:-1]
    total = total + padded_cond[1, 1:-1, 1:-1, 1:-1] + padded_cond[1, 1:-1, :-2, 1:-1]
    total = total + padded_cond[2, 1:-1, 1:-1, 1:-1] + padded_cond[2, 1:-1, 1:-1, :-2]
    return free * total + (1.0 - free)


def jacobi(rhs_box, padded_cond, diagonal, storage_box, free_box):
    guess = jnp.zeros_like(rhs_box)
    for sweep in range(SWEEPS):
        image = stencil(jnp.pad(free_box * guess, 1), padded_cond, guess, storage_box, free_box)
        guess = guess + RELAX * (rhs_box - image) / diagonal
    return guess


def project(basis, field):
    return jnp.dot(
        basis.reshape(basis.shape[0], -1), field.reshape(-1), precision=lax.Precision.HIGHEST
    )


def expand(basis, weights, field):
    return jnp.dot(
        weights, basis.reshape(basis.shape[0], -1), precision=lax.Precision.HIGHEST
    ).reshape(field.shape)


def gather_coarse(values):
    return lax.all_gather(values, ("gx", "gy", "gz"), axis=0, tiled=True)


def residual_rim(field):
    return padded(field, (("gx", 0), ("gy", 1), ("gz", 2)), 2)


def norm_sum(value):
    return lax.psum(value, ("gx", "gy", "gz"))


def shards(right_side, conductance, storage, dirichlet, basis, coarse_inverse):
    free = 1.0 - dirichlet.astype(jnp.float32)
    stacked = jnp.concatenate([conductance, storage[None], free[None]], axis=0)
    wide = padded(stacked, (("gx", 1), ("gy", 2), ("gz", 3)), 3)
    cond_face = wide[:3, 2:-2, 2:-2, 2:-2]
    free_face = wide[4, 2:-2, 2:-2, 2:-2]
    cond_box = wide[:3, 1:-1, 1:-1, 1:-1]
    storage_box = wide[3, 1:-1, 1:-1, 1:-1]
    free_box = wide[4, 1:-1, 1:-1, 1:-1]
    box_cond = pad_cond(cond_box)
    box_diag = diagonal_of(box_cond, storage_box, free_box)

    def schwarz(rhs_box):
        return jacobi(rhs_box, box_cond, box_diag, storage_box, free_box)[2:-2, 2:-2, 2:-2]

    solution = jnp.zeros_like(right_side)
    residual = right_side
    rhs_box = residual_rim(residual)
    coarse_now = project(basis, residual)
    weights = jnp.dot(coarse_inverse, gather_coarse(coarse_now), precision=lax.Precision.HIGHEST)
    precond = schwarz(rhs_box) + expand(basis, weights, residual)
    norm_now = norm_sum(jnp.sum(residual * precond))
    direction = precond
    for step in range(ITERS):
        near_dir = padded(direction, (("gx", 0), ("gy", 1), ("gz", 2)), 1)
        image = stencil(free_face * near_dir, cond_face, direction, storage, free)
        local_curve = jnp.sum(direction * image)
        curvature = lax.psum(local_curve, ("gx", "gy", "gz"))
        alpha = norm_now / curvature
        solution = solution + alpha * direction
        residual = residual - alpha * image
        if step + 1 < ITERS:
            rhs_box = residual_rim(residual)
            coarse_now = project(basis, residual)
            gathered = gather_coarse(coarse_now)
            weights = jnp.dot(coarse_inverse, gathered, precision=lax.Precision.HIGHEST)
            precond = schwarz(rhs_box) + expand(basis, weights, residual)
            norm_next = norm_sum(jnp.sum(residual * precond))
            direction = precond + norm_next / norm_now * direction
            norm_now = norm_next
    return (solution, residual)


def solution(mesh):
    placed = (
        P("gx", "gy", "gz"),
        P(None, "gx", "gy", "gz"),
        P("gx", "gy", "gz"),
        P("gx", "gy", "gz"),
        P(None, "gx", "gy", "gz"),
        P(("gx", "gy", "gz"), None),
    )
    return jax.shard_map(
        shards,
        mesh=mesh,
        in_specs=placed,
        out_specs=(P("gx", "gy", "gz"), P("gx", "gy", "gz")),
        check_vma=False,
    )
```

profile of v0, /device:TPU:0, one launch (start us, length us, event | category | flops | bytes accessed | tf_op | source)
XLA Modules:
  0.0 457.3 jit_solution(1106240369725356794)
XLA Ops:
  2.9 4.9 %collective-permute-start.6 = (f32[5,3,16,256]{3,2,1,0:T(8,128)S(1)}, f32[5,3,16,256]{3,2,1,0:T(8,128)S(1)}, u32[]{:S(2)}, u32[]{:S(2)}) collective-permute-start(f32[5,3,16,256]{3,2,1,0:T(8,128)S(1)} %get-tuple-element.36), channel_id=1, source_target_pairs={{0,16},{1,17},{2,18},{3,19},{4,20},{5,21},{6,22},{7,23},{8,24},{9,... | collective-permute-start | bytes 737288 | tf_op jit(solution)/shard_map/ppermute | solution.py:20
  9.9 5.2 %collective-permute-start = (f32[2,16,256]{2,1,0:T(8,128)S(1)}, f32[2,16,256]{2,1,0:T(8,128)S(1)}, u32[]{:S(2)}, u32[]{:S(2)}) collective-permute-start(f32[2,16,256]{2,1,0:T(8,128)S(1)} %get-tuple-element.61), channel_id=1, source_target_pairs={{0,16},{1,17},{2,18},{3,19},{4,20},{5,21},{6,22},{7,23},{8,24},{9,... | collective-permute-start | bytes 98312 | tf_op jit(solution)/shard_map/ppermute | solution.py:20
  16.4 8.8 %fusion.8 = f32[16]{0:T(128)S(1)} fusion(f32[16,16,16,256]{3,2,1,0:T(8,128)} %param.10, f32[16,16,256,1]{2,1,0,3:T(8,128)} %bitcast.289), kind=kOutput, calls=%fused_computation.16 | convolution fusion | flops 12582912 | bytes 4456512 | tf_op jit(solution)/shard_map/dot_general | solution.py:67
  25.4 41.7 %all-reduce.8 = f32[512]{0:T(512)S(1)} all-reduce(f32[512]{0:T(512)S(1)} %dynamic-update-slice), channel_id=1, replica_groups=mesh['gx'=2,'gy'=4,'gz'=4] {'gx','gy','gz'}, use_global_device_ids=true, to_apply=%add.8 | all-reduce | flops 512 | bytes 4096
  67.3 3.7 collective-permute-start.2
  74.6 5.3 %collective-permute-start.8 = (f32[5,22,3,256]{3,1,2,0:T(8,128)}, f32[5,22,3,256]{3,1,2,0:T(8,128)}, u32[]{:S(2)}, u32[]{:S(2)}) collective-permute-start(f32[5,22,3,256]{3,1,2,0:T(8,128)} %copy.55), channel_id=1, source_target_pairs={{0,4},{4,8},{8,12},{1,5},{5,9},{9,13},{2,6},{6,10},{10,14},{3,7},{... | collective-permute-start | bytes 1013768 | tf_op jit(solution)/shard_map/ppermute | solution.py:20
  80.7 1.7 collective-permute-start.9
  82.4 5.1 %fusion.2 = f32[1,16,16,256]{3,0,2,1:T(1,128)} fusion(f32[16,1,1,1]{0,1,3,2:T(1,128)S(1)} %convolution_bitcast_fusion.1, f32[16,16,256,16]{2,1,0,3:T(8,128)S(1)} %bitcast.284), kind=kOutput, calls=%fused_computation.4 | convolution fusion | flops 12582912 | bytes 4456512 | tf_op jit(solution)/shard_map/dot_general | solution.py:73
  87.6 8.1 %copy.37 = f32[5,22,16,256]{2,1,3,0:T(8,128)} copy(f32[5,22,16,256]{3,2,1,0:T(8,128)S(1)} %pad_maximum_fusion.2) | data formatting | bytes 3604480 | tf_op jit(solution)/shard_map/concatenate | solution.py:22
  95.8 8.9 %copy.36 = f32[5,22,3,256]{2,1,3,0:T(8,128)} copy(f32[5,22,3,256]{3,1,2,0:T(8,128)} %collective-permute-done.8) | data formatting | bytes 675840 | tf_op jit(solution)/shard_map/ppermute | solution.py:20
  104.7 9.0 %copy.38 = f32[5,22,3,256]{2,1,3,0:T(8,128)} copy(f32[5,22,3,256]{3,1,2,0:T(8,128)} %collective-permute-done.9) | data formatting | bytes 675840 | tf_op jit(solution)/shard_map/ppermute | solution.py:21
  113.6 16.9 %pad_maximum_fusion = f32[5,22,22,256]{2,1,3,0:T(8,128)S(1)} fusion(f32[5,22,3,256]{2,1,3,0:T(8,128)} %copy.38, f32[5,22,16,256]{2,1,3,0:T(8,128)} %copy.37, f32[5,22,3,256]{2,1,3,0:T(8,128)} %copy.36), kind=kLoop, calls=%fused_computation | loop fusion | flops 1239040 | bytes 4956160 | tf_op jit(solution)/shard_map/concatenate | solution.py:22
  130.5 5.4 %copy-done.4 = f32[5,22,22,256]{2,1,3,0:T(8,128)} copy-done((f32[5,22,22,256]{2,1,3,0:T(8,128)}, f32[5,22,22,256]{2,1,3,0:T(8,128)S(1)}, u32[]{:S(2)}) %copy-start.4) | copy-done | bytes 2478104
  136.7 2.0 collective-permute-start.10
  140.8 4.9 %collective-permute-start.4 = (f32[20,20,2]{2,1,0:T(8,128)}, f32[20,20,2]{2,1,0:T(8,128)S(1)}, u32[]{:S(2)}, u32[]{:S(2)}) collective-permute-start(f32[20,20,2]{2,1,0:T(8,128)} %get-tuple-element.40), channel_id=1, source_target_pairs={{0,1},{1,2},{2,3},{4,5},{5,6},{6,7},{8,9},{9,10},{10,11},{12,13},{... | collective-permute-start | bytes 9608 | tf_op jit(solution)/shard_map/ppermute | solution.py:20
  147.1 9.2 %copy.40 = f32[5,22,22,256]{3,2,1,0:T(8,128)S(1)} copy(f32[5,22,22,256]{2,1,3,0:T(8,128)} %copy-done.4) | data formatting | bytes 4956160 | tf_op jit(solution)/shard_map/concatenate | solution.py:22
  156.4 3.1 copy.39
  159.5 2.8 copy.41
  162.2 3.2 pad_maximum_fusion.1
  166.9 3.8 fusion.213
  170.7 1.9 fusion.218
  172.6 2.7 fusion.217
  175.4 1.8 broadcast_subtract_fusion
  177.3 2.0 fusion.208
  179.2 2.6 collective-permute-start.12
  183.2 4.2 collective-permute-done.13
  187.5 4.7 %collective-permute-start.14 = (f32[18,1,256]{2,1,0:T(1,128)S(1)}, f32[18,1,256]{2,1,0:T(1,128)S(1)}, u32[]{:S(2)}, u32[]{:S(2)}) collective-permute-start(f32[18,1,256]{2,1,0:T(1,128)S(1)} %get-tuple-element.52), channel_id=1, source_target_pairs={{0,4},{4,8},{8,12},{1,5},{5,9},{9,13},{2,6},{6,10},{10,14},{3,7},{... | collective-permute-start | bytes 55304 | tf_op jit(solution)/shard_map/ppermute | solution.py:20
  193.7 4.2 collective-permute-done.15
  202.0 5.0 %collective-permute-done.17 = f32[18,18,1]{2,1,0:T(8,128)S(1)} collective-permute-done((f32[18,18,1]{2,1,0:T(8,128)S(1)}, f32[18,18,1]{2,1,0:T(8,128)S(1)}, u32[]{:S(2)}, u32[]{:S(2)}) %collective-permute-start.17) | collective-permute-done | bytes 1328 | tf_op jit(solution)/shard_map/ppermute | solution.py:21
  207.7 2.2 multiply_reduce_fusion.2
  209.9 41.0 %all-reduce.10 = (f32[]{:T(128)}, f32[]{:T(128)}) all-reduce(f32[]{:T(128)} %get-tuple-element.5, f32[]{:T(128)} %get-tuple-element.4), channel_id=1, replica_groups=mesh['gx'=2,'gy'=4,'gz'=4] {'gx','gy','gz'}, use_global_device_ids=true, to_apply=%region_1.2 | all-reduce | flops 2 | bytes 16 | tf_op jit(solution)/shard_map/psum | solution.py:87
  254.0 4.4 collective-permute-start.18
  259.7 8.6 %fusion.11 = f32[16]{0:T(128)S(1)} fusion(f32[16,16,16,256]{3,2,1,0:T(8,128)} %param.10, f32[16,16,256,1]{2,1,0,3:T(8,128)S(1)} %bitcast.285), kind=kOutput, calls=%fused_computation.17 | convolution fusion | flops 12582912 | bytes 4456512 | tf_op jit(solution)/shard_map/dot_general | solution.py:67
  268.6 42.2 %all-reduce.9 = f32[512]{0:T(512)S(1)} all-reduce(f32[512]{0:T(512)S(1)} %dynamic-update-slice.1), channel_id=1, replica_groups=mesh['gx'=2,'gy'=4,'gz'=4] {'gx','gy','gz'}, use_global_device_ids=true, to_apply=%add.9 | all-reduce | flops 512 | bytes 4096
  311.7 2.7 collective-permute-start.20
  316.1 4.2 collective-permute-done.21
  324.2 6.4 %fusion = f32[1,16,16,256]{3,0,2,1:T(1,128)S(1)} fusion(f32[16,1,1,1]{0,1,3,2:T(1,128)S(1)} %convolution_bitcast_fusion, f32[16,16,256,16]{2,1,0,3:T(8,128)} %bitcast.283), kind=kOutput, calls=%fused_computation.2 | convolution fusion | flops 12582912 | bytes 4456512 | tf_op jit(solution)/shard_map/dot_general | solution.py:73
  332.1 2.0 fusion.216
  334.1 1.9 fusion.215
  337.7 2.5 multiply_reduce_fusion.1
  340.3 42.4 %psum.30 = f32[]{:T(128)} all-reduce(f32[]{:T(128)} %get-tuple-element.10), channel_id=1, replica_groups=mesh['gx'=2,'gy'=4,'gz'=4] {'gx','gy','gz'}, use_global_device_ids=true, to_apply=%region_5.6 | all-reduce | flops 1 | bytes 8 | tf_op jit(solution)/shard_map/psum | solution.py:87
  384.1 4.4 collective-permute-start.24
  389.9 4.2 collective-permute-done.25
  394.1 2.8 collective-permute-start.26
  398.4 4.2 collective-permute-done.27
  405.4 4.2 collective-permute-done.29
  411.3 2.3 multiply_reduce_fusion
  413.7 41.0 %psum.31 = f32[]{:T(128)} all-reduce(f32[]{:T(128)} %get-tuple-element.8), channel_id=1, replica_groups=mesh['gx'=2,'gy'=4,'gz'=4] {'gx','gy','gz'}, use_global_device_ids=true, to_apply=%region_7.8 | all-reduce | flops 1 | bytes 8 | tf_op jit(solution)/shard_map/psum | solution.py:117
  (140 shorter events, 44.9 us)
Async XLA Ops:
  0.6 66.4 %copy-start = (f32[16,512]{1,0:T(8,128)S(1)}, f32[16,512]{1,0:T(8,128)}, u32[]{:S(2)}) copy-start(f32[16,512]{1,0:T(8,128)} %param.11) | copy-start | bytes 98308
  0.6 71.7 %copy-start.13 = (f32[16,16,256]{2,1,0:T(8,128)S(1)}, f32[16,16,256]{2,1,0:T(8,128)}, u32[]{:S(2)}) copy-start(f32[16,16,256]{2,1,0:T(8,128)} %param.8) | copy-start | bytes 786436
  0.7 71.7 %copy-start.7 = (f32[3,16,16,256]{3,2,1,0:T(8,128)S(1)}, f32[3,16,16,256]{3,2,1,0:T(8,128)}, u32[]{:S(2)}) copy-start(f32[3,16,16,256]{3,2,1,0:T(8,128)} %param.7) | copy-start | bytes 2359300
  0.7 66.6 %copy-start.15 = (f32[16,16,256]{2,1,0:T(8,128)S(1)}, f32[16,16,256]{2,1,0:T(8,128)}, u32[]{:S(2)}) copy-start(f32[16,16,256]{2,1,0:T(8,128)} %param.6) | copy-start | bytes 786436
  1.8 71.8 %copy-start.17 = (f32[1,16,16,256]{3,2,1,0:T(8,128)}, f32[1,16,16,256]{3,2,1,0:T(8,128)S(1)}, u32[]{:S(2)}) copy-start(f32[1,16,16,256]{3,2,1,0:T(8,128)S(1)} %fusion.212) | copy-start | bytes 786436
  2.9 69.4 %collective-permute-start.6 = (f32[5,3,16,256]{3,2,1,0:T(8,128)S(1)}, f32[5,3,16,256]{3,2,1,0:T(8,128)S(1)}, u32[]{:S(2)}, u32[]{:S(2)}) collective-permute-start(f32[5,3,16,256]{3,2,1,0:T(8,128)S(1)} %get-tuple-element.36), channel_id=1, source_target_pairs={{0,16},{1,17},{2,18},{3,19},{4,20},{5,21},{6,22},{7,23},{8,24},{9,... | collective-permute-start | bytes 737288 | tf_op jit(solution)/shard_map/ppermute | solution.py:20
  7.8 64.5 %collective-permute-start.7 = (f32[5,3,16,256]{3,2,1,0:T(8,128)S(1)}, f32[5,3,16,256]{3,2,1,0:T(8,128)}, u32[]{:S(2)}, u32[]{:S(2)}) collective-permute-start(f32[5,3,16,256]{3,2,1,0:T(8,128)S(1)} %get-tuple-element.37), channel_id=1, source_target_pairs={{16,0},{17,1},{18,2},{19,3},{20,4},{21,5},{22,6},{23,7},{24,8},{25... | collective-permute-start | bytes 737288 | tf_op jit(solution)/shard_map/ppermute | solution.py:21
  9.9 57.3 %collective-permute-start = (f32[2,16,256]{2,1,0:T(8,128)S(1)}, f32[2,16,256]{2,1,0:T(8,128)S(1)}, u32[]{:S(2)}, u32[]{:S(2)}) collective-permute-start(f32[2,16,256]{2,1,0:T(8,128)S(1)} %get-tuple-element.61), channel_id=1, source_target_pairs={{0,16},{1,17},{2,18},{3,19},{4,20},{5,21},{6,22},{7,23},{8,24},{9,... | collective-permute-start | bytes 98312 | tf_op jit(solution)/shard_map/ppermute | solution.py:20
  15.1 52.1 %collective-permute-start.1 = (f32[2,16,256]{2,1,0:T(8,128)S(1)}, f32[2,16,256]{2,1,0:T(8,128)S(1)}, u32[]{:S(2)}, u32[]{:S(2)}) collective-permute-start(f32[2,16,256]{2,1,0:T(8,128)S(1)} %get-tuple-element.60), channel_id=1, source_target_pairs={{16,0},{17,1},{18,2},{19,3},{20,4},{21,5},{22,6},{23,7},{24,8},{25... | collective-permute-start | bytes 98312 | tf_op jit(solution)/shard_map/ppermute | solution.py:21
  67.3 20.2 %copy-start.22 = (f32[20,16,256]{2,1,0:T(8,128)}, f32[20,16,256]{2,1,0:T(8,128)S(1)}, u32[]{:S(2)}) copy-start(f32[20,16,256]{2,1,0:T(8,128)S(1)} %constant_dynamic-update-slice_fusion) | copy-start | bytes 983044
  67.3 20.2 %collective-permute-start.2 = (f32[20,2,256]{2,1,0:T(2,128)S(1)}, f32[20,2,256]{2,1,0:T(2,128)S(1)}, u32[]{:S(2)}, u32[]{:S(2)}) collective-permute-start(f32[20,2,256]{2,1,0:T(2,128)S(1)} %get-tuple-element.48), channel_id=1, source_target_pairs={{0,4},{4,8},{8,12},{1,5},{5,9},{9,13},{2,6},{6,10},{10,14},{3,7},{... | collective-permute-start | bytes 122888 | tf_op jit(solution)/shard_map/ppermute | solution.py:20
  71.0 16.5 %collective-permute-start.3 = (f32[20,2,256]{2,1,0:T(2,128)S(1)}, f32[20,2,256]{2,1,0:T(2,128)S(1)}, u32[]{:S(2)}, u32[]{:S(2)}) collective-permute-start(f32[20,2,256]{2,1,0:T(2,128)S(1)} %get-tuple-element.49), channel_id=1, source_target_pairs={{4,0},{8,4},{12,8},{5,1},{9,5},{13,9},{6,2},{10,6},{14,10},{7,3},{... | collective-permute-start | bytes 122888 | tf_op jit(solution)/shard_map/ppermute | solution.py:21
  74.6 21.2 %collective-permute-start.8 = (f32[5,22,3,256]{3,1,2,0:T(8,128)}, f32[5,22,3,256]{3,1,2,0:T(8,128)}, u32[]{:S(2)}, u32[]{:S(2)}) collective-permute-start(f32[5,22,3,256]{3,1,2,0:T(8,128)} %copy.55), channel_id=1, source_target_pairs={{0,4},{4,8},{8,12},{1,5},{5,9},{9,13},{2,6},{6,10},{10,14},{3,7},{... | collective-permute-start | bytes 1013768 | tf_op jit(solution)/shard_map/ppermute | solution.py:20
  80.7 24.0 %collective-permute-start.9 = (f32[5,22,3,256]{3,1,2,0:T(8,128)}, f32[5,22,3,256]{3,1,2,0:T(8,128)}, u32[]{:S(2)}, u32[]{:S(2)}) collective-permute-start(f32[5,22,3,256]{3,1,2,0:T(8,128)} %copy.56), channel_id=1, source_target_pairs={{4,0},{8,4},{12,8},{5,1},{9,5},{13,9},{6,2},{10,6},{14,10},{7,3},{... | collective-permute-start | bytes 1013768 | tf_op jit(solution)/shard_map/ppermute | solution.py:21
  136.7 19.7 %collective-permute-start.10 = (f32[5,22,22,3]{2,1,3,0:T(8,128)}, f32[5,22,22,3]{2,1,3,0:T(8,128)}, u32[]{:S(2)}, u32[]{:S(2)}) collective-permute-start(f32[5,22,22,3]{2,1,3,0:T(8,128)} %get-tuple-element.30), channel_id=1, source_target_pairs={{0,1},{1,2},{2,3},{4,5},{5,6},{6,7},{8,9},{9,10},{10,11},{12,13},{... | collective-permute-start | bytes 87128 | tf_op jit(solution)/shard_map/ppermute | solution.py:20
  138.6 20.8 %collective-permute-start.11 = (f32[5,22,22,3]{2,1,3,0:T(8,128)}, f32[5,22,22,3]{2,1,3,0:T(8,128)}, u32[]{:S(2)}, u32[]{:S(2)}) collective-permute-start(f32[5,22,22,3]{2,1,3,0:T(8,128)} %get-tuple-element.31), channel_id=1, source_target_pairs={{1,0},{2,1},{3,2},{5,4},{6,5},{7,6},{9,8},{10,9},{11,10},{13,12},{... | collective-permute-start | bytes 87128 | tf_op jit(solution)/shard_map/ppermute | solution.py:21
  140.8 26.1 %collective-permute-start.4 = (f32[20,20,2]{2,1,0:T(8,128)}, f32[20,20,2]{2,1,0:T(8,128)S(1)}, u32[]{:S(2)}, u32[]{:S(2)}) collective-permute-start(f32[20,20,2]{2,1,0:T(8,128)} %get-tuple-element.40), channel_id=1, source_target_pairs={{0,1},{1,2},{2,3},{4,5},{5,6},{6,7},{8,9},{9,10},{10,11},{12,13},{... | collective-permute-start | bytes 9608 | tf_op jit(solution)/shard_map/ppermute | solution.py:20
  145.6 21.2 %collective-permute-start.5 = (f32[20,20,2]{2,1,0:T(8,128)S(1)}, f32[20,20,2]{2,1,0:T(8,128)}, u32[]{:S(2)}, u32[]{:S(2)}) collective-permute-start(f32[20,20,2]{2,1,0:T(8,128)S(1)} %get-tuple-element.41), channel_id=1, source_target_pairs={{1,0},{2,1},{3,2},{5,4},{6,5},{7,6},{9,8},{10,9},{11,10},{13,12},{... | collective-permute-start | bytes 9608 | tf_op jit(solution)/shard_map/ppermute | solution.py:21
  165.5 41.5 %copy-start.1 = (f32[5,22,22,262]{3,2,1,0:T(8,128)}, f32[5,22,22,262]{3,2,1,0:T(8,128)S(1)}, u32[]{:S(2)}) copy-start(f32[5,22,22,262]{3,2,1,0:T(8,128)S(1)} %pad_maximum_fusion.1) | copy-start | bytes 7608484
  177.2 32.7 %copy-start.21 = (f32[20,20,260]{2,1,0:T(8,128)}, f32[20,20,260]{2,1,0:T(8,128)S(1)}, u32[]{:S(2)}) copy-start(f32[20,20,260]{2,1,0:T(8,128)S(1)} %get-tuple-element.32) | copy-start | bytes 1248004
  177.2 30.5 %copy-start.6 = (f32[5,22,22,256]{3,2,1,0:T(8,128)S(1)}, f32[5,22,22,256]{3,2,1,0:T(8,128)}, u32[]{:S(2)}) copy-start(f32[5,22,22,256]{3,2,1,0:T(8,128)} %copy-done.5) | copy-start | bytes 7434244
  177.2 30.5 %copy-start.8 = (f32[3,16,16,256]{3,2,1,0:T(8,128)S(1)}, f32[3,16,16,256]{3,2,1,0:T(8,128)}, u32[]{:S(2)}) copy-start(f32[3,16,16,256]{3,2,1,0:T(8,128)} %param.7) | copy-start | bytes 2359300
  177.2 30.5 %copy-start.10 = (f32[5,22,22,3]{3,2,1,0:T(8,128)S(1)}, f32[5,22,22,3]{3,2,1,0:T(8,128)}, u32[]{:S(2)}) copy-start(f32[5,22,22,3]{3,2,1,0:T(8,128)} %copy.39) | copy-start | bytes 87124
  177.2 30.5 %copy-start.16 = (f32[16,16,256]{2,1,0:T(8,128)S(1)}, f32[16,16,256]{2,1,0:T(8,128)}, u32[]{:S(2)}) copy-start(f32[16,16,256]{2,1,0:T(8,128)} %param.6) | copy-start | bytes 786436
  177.2 30.5 %copy-start.18 = (f32[1,16,16,256]{3,2,1,0:T(8,128)S(1)}, f32[1,16,16,256]{3,2,1,0:T(8,128)}, u32[]{:S(2)}) copy-start(f32[1,16,16,256]{3,2,1,0:T(8,128)} %copy-done.17) | copy-start | bytes 786436
  177.2 30.5 %copy-start.19 = (s32[16,16,256]{2,1,0:T(8,128)S(1)}, s32[16,16,256]{2,1,0:T(8,128)}, u32[]{:S(2)}) copy-start(s32[16,16,256]{2,1,0:T(8,128)} %param.9) | copy-start | bytes 786436
  177.2 30.4 %copy-start.26 = (f32[5,3,16,256]{3,2,1,0:T(8,128)S(1)}, f32[5,3,16,256]{3,2,1,0:T(8,128)}, u32[]{:S(2)}) copy-start(f32[5,3,16,256]{3,2,1,0:T(8,128)} %copy-done.25) | copy-start | bytes 737284
  179.2 4.0 collective-permute-start.12
  181.8 5.6 %collective-permute-start.13 = (f32[1,16,256]{2,1,0:T(8,128)S(1)}, f32[1,16,256]{2,1,0:T(8,128)S(1)}, u32[]{:S(2)}, u32[]{:S(2)}) collective-permute-start(f32[1,16,256]{2,1,0:T(8,128)S(1)} %get-tuple-element.59), channel_id=1, source_target_pairs={{16,0},{17,1},{18,2},{19,3},{20,4},{21,5},{22,6},{23,7},{24,8},{25... | collective-permute-start | bytes 49160 | tf_op jit(solution)/shard_map/ppermute | solution.py:21
  187.5 6.2 %collective-permute-start.14 = (f32[18,1,256]{2,1,0:T(1,128)S(1)}, f32[18,1,256]{2,1,0:T(1,128)S(1)}, u32[]{:S(2)}, u32[]{:S(2)}) collective-permute-start(f32[18,1,256]{2,1,0:T(1,128)S(1)} %get-tuple-element.52), channel_id=1, source_target_pairs={{0,4},{4,8},{8,12},{1,5},{5,9},{9,13},{2,6},{6,10},{10,14},{3,7},{... | collective-permute-start | bytes 55304 | tf_op jit(solution)/shard_map/ppermute | solution.py:20
  192.2 5.7 %collective-permute-start.15 = (f32[18,1,256]{2,1,0:T(1,128)S(1)}, f32[18,1,256]{2,1,0:T(1,128)S(1)}, u32[]{:S(2)}, u32[]{:S(2)}) collective-permute-start(f32[18,1,256]{2,1,0:T(1,128)S(1)} %get-tuple-element.53), channel_id=1, source_target_pairs={{4,0},{8,4},{12,8},{5,1},{9,5},{13,9},{6,2},{10,6},{14,10},{7,3},{... | collective-permute-start | bytes 55304 | tf_op jit(solution)/shard_map/ppermute | solution.py:21
  198.1 3.9 collective-permute-start.16
  199.5 7.5 %collective-permute-start.17 = (f32[18,18,1]{2,1,0:T(8,128)S(1)}, f32[18,18,1]{2,1,0:T(8,128)S(1)}, u32[]{:S(2)}, u32[]{:S(2)}) collective-permute-start(f32[18,18,1]{2,1,0:T(8,128)S(1)} %get-tuple-element.45), channel_id=1, source_target_pairs={{1,0},{2,1},{3,2},{5,4},{6,5},{7,6},{9,8},{10,9},{11,10},{13,12},{... | collective-permute-start | bytes 3896 | tf_op jit(solution)/shard_map/ppermute | solution.py:21
  254.0 56.8 %collective-permute-start.18 = (f32[2,16,256]{2,1,0:T(8,128)}, f32[2,16,256]{2,1,0:T(8,128)S(1)}, u32[]{:S(2)}, u32[]{:S(2)}) collective-permute-start(f32[2,16,256]{2,1,0:T(8,128)} %get-tuple-element.56), channel_id=1, source_target_pairs={{0,16},{1,17},{2,18},{3,19},{4,20},{5,21},{6,22},{7,23},{8,24},{9,... | collective-permute-start | bytes 98312 | tf_op jit(solution)/shard_map/ppermute | solution.py:20
  258.4 52.4 %collective-permute-start.19 = (f32[2,16,256]{2,1,0:T(8,128)}, f32[2,16,256]{2,1,0:T(8,128)}, u32[]{:S(2)}, u32[]{:S(2)}) collective-permute-start(f32[2,16,256]{2,1,0:T(8,128)} %get-tuple-element.57), channel_id=1, source_target_pairs={{16,0},{17,1},{18,2},{19,3},{20,4},{21,5},{22,6},{23,7},{24,8},{25... | collective-permute-start | bytes 98312 | tf_op jit(solution)/shard_map/ppermute | solution.py:21
  310.8 19.8 %copy-start.12 = (f32[20,20,260]{2,1,0:T(8,128)S(1)}, f32[20,20,260]{2,1,0:T(8,128)}, u32[]{:S(2)}) copy-start(f32[20,20,260]{2,1,0:T(8,128)} %copy-done.11) | copy-start | bytes 1248004
  311.7 4.4 collective-permute-start.20
  314.4 5.9 %collective-permute-start.21 = (f32[20,2,256]{2,1,0:T(2,128)S(1)}, f32[20,2,256]{2,1,0:T(2,128)S(1)}, u32[]{:S(2)}, u32[]{:S(2)}) collective-permute-start(f32[20,2,256]{2,1,0:T(2,128)S(1)} %get-tuple-element.47), channel_id=1, source_target_pairs={{4,0},{8,4},{12,8},{5,1},{9,5},{13,9},{6,2},{10,6},{14,10},{7,3},{... | collective-permute-start | bytes 122888 | tf_op jit(solution)/shard_map/ppermute | solution.py:21
  321.3 9.3 %collective-permute-start.22 = (f32[20,20,2]{2,1,0:T(8,128)S(1)}, f32[20,20,2]{2,1,0:T(8,128)S(1)}, u32[]{:S(2)}, u32[]{:S(2)}) collective-permute-start(f32[20,20,2]{2,1,0:T(8,128)S(1)} %get-tuple-element.38), channel_id=1, source_target_pairs={{0,1},{1,2},{2,3},{4,5},{5,6},{6,7},{8,9},{9,10},{10,11},{12,13},{... | collective-permute-start | bytes 9608 | tf_op jit(solution)/shard_map/ppermute | solution.py:20
  322.6 8.0 %collective-permute-start.23 = (f32[20,20,2]{2,1,0:T(8,128)S(1)}, f32[20,20,2]{2,1,0:T(8,128)S(1)}, u32[]{:S(2)}, u32[]{:S(2)}) collective-permute-start(f32[20,20,2]{2,1,0:T(8,128)S(1)} %get-tuple-element.39), channel_id=1, source_target_pairs={{1,0},{2,1},{3,2},{5,4},{6,5},{7,6},{9,8},{10,9},{11,10},{13,12},{... | collective-permute-start | bytes 9608 | tf_op jit(solution)/shard_map/ppermute | solution.py:21
  337.7 73.6 %copy-start.9 = (f32[3,16,16,256]{3,2,1,0:T(8,128)S(1)}, f32[3,16,16,256]{3,2,1,0:T(8,128)}, u32[]{:S(2)}) copy-start(f32[3,16,16,256]{3,2,1,0:T(8,128)} %param.7) | copy-start | bytes 2359300
  337.7 73.6 %copy-start.14 = (f32[16,16,256]{2,1,0:T(8,128)S(1)}, f32[16,16,256]{2,1,0:T(8,128)}, u32[]{:S(2)}) copy-start(f32[16,16,256]{2,1,0:T(8,128)} %param.8) | copy-start | bytes 786436
  384.1 5.8 %collective-permute-start.24 = (f32[1,16,256]{2,1,0:T(8,128)S(1)}, f32[1,16,256]{2,1,0:T(8,128)S(1)}, u32[]{:S(2)}, u32[]{:S(2)}) collective-permute-start(f32[1,16,256]{2,1,0:T(8,128)S(1)} %get-tuple-element.54), channel_id=1, source_target_pairs={{0,16},{1,17},{2,18},{3,19},{4,20},{5,21},{6,22},{7,23},{8,24},{9,... | collective-permute-start | bytes 49160 | tf_op jit(solution)/shard_map/ppermute | solution.py:20
  388.5 5.6 %collective-permute-start.25 = (f32[1,16,256]{2,1,0:T(8,128)S(1)}, f32[1,16,256]{2,1,0:T(8,128)S(1)}, u32[]{:S(2)}, u32[]{:S(2)}) collective-permute-start(f32[1,16,256]{2,1,0:T(8,128)S(1)} %get-tuple-element.55), channel_id=1, source_target_pairs={{16,0},{17,1},{18,2},{19,3},{20,4},{21,5},{22,6},{23,7},{24,8},{25... | collective-permute-start | bytes 49160 | tf_op jit(solution)/shard_map/ppermute | solution.py:21
  394.1 4.2 collective-permute-start.26
  396.9 5.7 %collective-permute-start.27 = (f32[18,1,256]{2,1,0:T(1,128)S(1)}, f32[18,1,256]{2,1,0:T(1,128)S(1)}, u32[]{:S(2)}, u32[]{:S(2)}) collective-permute-start(f32[18,1,256]{2,1,0:T(1,128)S(1)} %get-tuple-element.51), channel_id=1, source_target_pairs={{4,0},{8,4},{12,8},{5,1},{9,5},{13,9},{6,2},{10,6},{14,10},{7,3},{... | collective-permute-start | bytes 55304 | tf_op jit(solution)/shard_map/ppermute | solution.py:21
  402.8 2.6 collective-permute-start.28
  404.1 5.5 %collective-permute-start.29 = (f32[18,18,1]{2,1,0:T(8,128)S(1)}, f32[18,18,1]{2,1,0:T(8,128)S(1)}, u32[]{:S(2)}, u32[]{:S(2)}) collective-permute-start(f32[18,18,1]{2,1,0:T(8,128)S(1)} %get-tuple-element.43), channel_id=1, source_target_pairs={{1,0},{2,1},{3,2},{5,4},{6,5},{7,6},{9,8},{10,9},{11,10},{13,12},{... | collective-permute-start | bytes 3896 | tf_op jit(solution)/shard_map/ppermute | solution.py:21
  (11 other events, 91.0 us)
where the time goes:
time: 465 us; the launch traced here: 457 us
  blocking collectives  208 us (45%)
  starting transfers between devices  71.8 us (15%)
  other arithmetic  56.4 us (12%)
  local copies, waits for them, and re-layouts  54.6 us (12%)
  waiting for transfers between devices  31.1 us (7%)
  matrix products  29.1 us (6%)
  between operations  6.08 us (1%)
    unnamed x2, blocking collectives  83.9 us
    psum x2, blocking collectives, norm_sum(): return lax.psum(value, ('gx', 'gy', 'gz'))  83.4 us
    ppermute x15, starting transfers between devices, padded(): before = lax.ppermute(last, axis, up)  51.5 us
    psum x1, blocking collectives, shards(): curvature = lax.psum(local_curve, ('gx', 'gy', 'gz'))  41 us
    ppermute x15, waiting for transfers between devices, padded(): after = lax.ppermute(leading, axis, down)  30.3 us
    concatenate x7, other arithmetic, padded(): value = jnp.concatenate([before, value, after], axis=dim)  22.3 us
    ppermute x15, starting transfers between devices, padded(): after = lax.ppermute(leading, axis, down)  20.2 us
    dot_general x2, matrix products, project(): jnp.dot(basis.reshape(basis.shape[0], -1), field.reshape(-1), precision=l...  17.4 us
  transfers between devices with their start and end apart: 30, of which 12 were waited for; matrix products, arithmetic and copies ran while one was open for 16% of the time, Pallas kernels for 0%

commit v1 on v0

v1 whole, which is shorter than its diff:
```python
import functools

import jax
import jax.numpy as jnp
from jax import lax
from jax.experimental import pallas as pl
from jax.experimental.pallas import tpu as pltpu
from jax.sharding import PartitionSpec as P

SWEEPS = 4
RELAX = 2.0 / 3.0
AXES = ("gx", "gy", "gz")
LANES = 128
COARSE_LANE = 96
VMEM_LIMIT = 40 * 1024 * 1024
F32 = jnp.float32


def rounds_of(count):
    return (0, 1)[: 1 if count <= 2 else 2]


def mate(index, odd, count):
    other = index + 1 if index % 2 == odd else index - 1
    return other if 0 <= other < count else None


def swap(value, sizes, along):
    pairs = []
    nx, ny, nz = sizes
    for ix in range(nx):
        for iy in range(ny):
            for iz in range(nz):
                here = [ix, iy, iz]
                there = [
                    mate(here[a], along[a], sizes[a]) if a in along else here[a] for a in range(3)
                ]
                if None in there:
                    if 2 in along:
                        spare = nz - 1 - iz if iz in (0, nz - 1) else None
                    else:
                        spare = iz ^ 1 if nz % 2 == 0 else None
                    if spare is None:
                        continue
                    there = [ix, iy, spare]
                pairs.append(
                    ((ix * ny + iy) * nz + iz, (there[0] * ny + there[1]) * nz + there[2])
                )
    return lax.ppermute(value, AXES, pairs)


def upward(index, odd):
    return lax.rem(index, 2) == odd


def where_am_i():
    return [lax.axis_index(a) for a in AXES]


def lane_iota(shape):
    return lax.broadcasted_iota(jnp.int32, shape, len(shape) - 1)


def pack_x(out, fields, odd, index, width):
    nx = fields[0].shape[0]
    high = upward(index, odd)
    for cond, first in ((high, nx - width), (jnp.logical_not(high), 0)):

        @pl.when(cond)
        def _(first=first):
            for k, field in enumerate(fields):
                out[k * width : (k + 1) * width] = field[first : first + width]


def pack_y(out, fields, odd, index, width):
    ny = fields[0].shape[1]
    high = upward(index, odd)
    for cond, first in ((high, ny - width), (jnp.logical_not(high), 0)):

        @pl.when(cond)
        def _(first=first):
            for k, field in enumerate(fields):
                for j in range(width):
                    out[k * width + j] = field[:, first + j, :]


def pack_xy(out, fields, rx, ry, ix, iy):
    nx, ny, _ = fields[0].shape
    for xhigh in (False, True):
        for yhigh in (False, True):

            @pl.when((upward(ix, rx) == xhigh) & (upward(iy, ry) == yhigh))
            def _(x0=(nx - 2 if xhigh else 0), y0=(ny - 2 if yhigh else 0)):
                for k, field in enumerate(fields):
                    for i in range(2):
                        out[4 * k + 2 * i : 4 * k + 2 * i + 2, :] = field[x0 + i, y0 : y0 + 2, :]


def pack_z(fields):
    nx, ny, nz = fields[0].shape
    lane = lane_iota((nx, ny, LANES))
    total = jnp.zeros((nx, ny, LANES), F32)
    for k, field in enumerate(fields):
        ends = jnp.where(lane < 64, field[:, :, 0:LANES], field[:, :, nz - LANES : nz])
        turned = pltpu.roll(ends, 4 * k + 2, 2)
        total = jnp.where((lane >= 4 * k) & (lane < 4 * k + 4), turned, total)
    return total


def edge_tiles(ends, count):
    nx, ny, _ = ends.shape
    rows = jnp.concatenate(
        [
            ends[0:2].reshape(2 * ny, LANES),
            ends[nx - 2 : nx].reshape(2 * ny, LANES),
            ends[:, 0, :],
            ends[:, 1, :],
            ends[:, ny - 2, :],
            ends[:, ny - 1, :],
        ],
        axis=0,
    )
    turned = rows.T
    lane = lane_iota((8, LANES))
    tiles = []
    for t in range(4):
        tile = jnp.zeros((8, LANES), F32)
        for q in range((4 * count + 7) // 8):
            part = pltpu.roll(turned[8 * q : 8 * q + 8, :], (32 * q - 32 * t) % LANES, 1)
            tile = jnp.where((lane >= 32 * q) & (lane < 32 * q + 32), part, tile)
        tiles.append(tile)
    return tiles


def project(basis_ref, field):
    vecs, nx, ny, nz = basis_ref.shape
    row = lax.broadcasted_iota(jnp.int32, (8, LANES), 0)
    lane = lane_iota((8, LANES))
    tile = jnp.zeros((8, LANES), F32)
    for k in range(vecs):
        prod = jnp.sum(basis_ref[k] * field, axis=0)
        part = jnp.zeros((8, LANES), F32)
        for y in range(ny // 8):
            for z in range(nz // LANES):
                part = part + prod[8 * y : 8 * y + 8, LANES * z : LANES * (z + 1)]
        value = jnp.sum(part)
        tile = jnp.where((row == 0) & (lane == COARSE_LANE + k), value, tile)
    return tile


def put_scalars(tile, values):
    row = lax.broadcasted_iota(jnp.int32, (8, LANES), 0)
    lane = lane_iota((8, LANES))
    for i, value in enumerate(values):
        tile = jnp.where((row == 1) & (lane == COARSE_LANE + i), value, tile)
    return tile


def fill_rows(out, sizes, tiles, common):
    ix, iy, _ = where_am_i()
    nx, ny, nz = sizes
    low_x, high_x, low_y, high_y = [t + common for t in tiles]
    for jx in range(nx):
        for jy in range(ny):
            tile = jnp.where(
                jx > ix, high_x, jnp.where(jx < ix, low_x, jnp.where(jy > iy, high_y, low_y))
            )
            for jz in range(nz):
                out[(jx * ny + jy) * nz + jz] = tile


def box_shape(shape):
    nx, ny, nz = shape
    return (nx + 6, ny + 8, nz + LANES)


def clear(box):
    def body(x, carry):
        box[x] = jnp.zeros(box.shape[1:], F32)
        return carry

    lax.fori_loop(0, box.shape[0], body, 0)


def each_round(sizes, a, index, act):
    for r in rounds_of(sizes[a]):
        high = upward(index, r)

        @pl.when(high & (index + 1 < sizes[a]))
        def _(r=r):
            act(r, True)

        @pl.when(jnp.logical_not(high) & (index > 0))
        def _(r=r):
            act(r, False)


def unpack_faces(boxes, owns, xs, ys, sizes, width):
    nx, ny, nz = owns[0].shape
    ix, iy, _ = where_am_i()
    for k, (box, own) in enumerate(zip(boxes, owns)):
        box[3 : 3 + nx, 0:ny, 0:nz] = own[...]

    def put_x(r, above):
        first = 3 + nx if above else 3 - width
        for k, box in enumerate(boxes):
            box[first : first + width, 0:ny, 0:nz] = xs[r][k * width : (k + 1) * width]

    each_round(sizes, 0, ix, put_x)

    def put_y(r, above):
        first = ny if above else ny + 8 - width
        for k, box in enumerate(boxes):
            for j in range(width):
                box[3 : 3 + nx, first + j, 0:nz] = ys[r][k * width + j]

    each_round(sizes, 1, iy, put_y)


def unpack_xy(boxes, shape, xys, sizes):
    nx, ny, nz = shape
    ix, iy, _ = where_am_i()

    def put(rx, xabove):
        x0 = 3 + nx if xabove else 1

        def inner(ry, yabove):
            y0 = ny if yabove else ny + 6
            for k, box in enumerate(boxes):
                for i in range(2):
                    box[x0 + i, y0 : y0 + 2, 0:nz] = xys[(rx, ry)][
                        4 * k + 2 * i : 4 * k + 2 * i + 2, :
                    ]

        each_round(sizes, 1, iy, inner)

    each_round(sizes, 0, ix, put)


def pick_z(zs, sizes, iz, shape):
    count = sizes[2]
    lane = lane_iota(shape)
    first = lax.rem(lane, 4) < 2
    total = jnp.zeros(shape, F32)
    for r in rounds_of(count):
        high = upward(iz, r)
        below = jnp.logical_not(high) & (iz > 0)
        above = high & (iz + 1 < count)
        total = jnp.where((first & below) | (jnp.logical_not(first) & above), zs[r][...], total)
    return total


def halo_lanes(tile, k):
    lane = lane_iota(tile.shape)
    axis = len(tile.shape) - 1
    turned = pltpu.roll(tile, (-(4 * k + 2)) % LANES, axis)
    return jnp.where((lane < 2) | (lane >= LANES - 2), turned, 0.0)


def unpack_z(boxes, shape, zs, sizes):
    nx, ny, nz = shape
    iz = lax.axis_index("gz")
    tile = pick_z(zs, sizes, iz, (nx, ny, LANES))
    for k, box in enumerate(boxes):
        box[3 : 3 + nx, 0:ny, nz : nz + LANES] = halo_lanes(tile, k)


def unpack_edges(boxes, shape, rows_ref, sizes):
    nx, ny, nz = shape
    here = where_am_i()
    combos = [(dx, dy) for dx in (-1, 0, 1) for dy in (-1, 0, 1) if dx or dy]
    row = lax.broadcasted_iota(jnp.int32, (8, LANES), 0)
    first = lax.rem(row, 4) < 2
    merged = []
    for dx, dy in combos:
        parts = []
        for dz in (-1, 1):
            spot = [h + d for h, d in zip(here, (dx, dy, dz))]
            valid = True
            for s, n in zip(spot, sizes):
                valid = valid & (s >= 0) & (s < n)
            spot = [jnp.clip(s, 0, n - 1) for s, n in zip(spot, sizes)]
            j = (spot[0] * sizes[1] + spot[1]) * sizes[2] + spot[2]
            parts.append(jnp.where(valid, rows_ref[j], 0.0))
        merged.append(jnp.where(first, parts[0], parts[1]))
    merged += [jnp.zeros((8, LANES), F32)] * (LANES // 8 - len(merged))
    turned = jnp.concatenate(merged, axis=0).T
    lane = lane_iota((32, LANES))
    for c, (dx, dy) in enumerate(combos):
        tile = jnp.zeros((32, LANES), F32)
        for q in range((4 * len(boxes) + 7) // 8):
            part = pltpu.roll(turned[32 * q : 32 * q + 32, :], (8 * q - 8 * c) % LANES, 1)
            tile = jnp.where((lane >= 8 * q) & (lane < 8 * q + 8), part, tile)
        for k, box in enumerate(boxes):
            piece = halo_lanes(tile, k)
            x0 = 1 if dx < 0 else 3 + nx
            y0 = ny + 6 if dy < 0 else ny
            if dx and dy:
                inside = ny - 2 if dy < 0 else 0
                for i in range(2):
                    box[x0 + i, y0 : y0 + 2, nz : nz + LANES] = piece[
                        i * ny + inside : i * ny + inside + 2
                    ]
            elif dx:
                box[x0 : x0 + 2, 0:ny, nz : nz + LANES] = piece.reshape(2, ny, LANES)
            else:
                for j in range(2):
                    box[3 : 3 + nx, y0 + j, nz : nz + LANES] = piece[j * nx : (j + 1) * nx]


def ahead(plane, axis):
    return pltpu.roll(plane, plane.shape[axis] - 1, axis)


def behind(plane, axis):
    return pltpu.roll(plane, 1, axis)


def neighbours(g, links, x):
    lx, ly, lz = links
    mid = g[x]
    y = ly[x]
    z = lz[x]
    total = lx[x] * g[x + 1] + lx[x - 1] * g[x - 1]
    total = total + y * ahead(mid, 0) + behind(y * mid, 0)
    return total + z * ahead(mid, 1) + behind(z * mid, 1)


def coefficients(fields, links, diag, step):
    tx, ty, tz, store, free, _ = fields
    lx, ly, lz = links
    last = tx.shape[0] - 1
    for ref in (lx, ly, lz, diag, step):
        ref[0] = jnp.zeros(ref.shape[1:], F32)
        ref[last] = jnp.zeros(ref.shape[1:], F32)

    def body(x, carry):
        f = free[x]
        a, b, c = tx[x], ty[x], tz[x]
        total = store[x] + a + tx[x - 1] + b + behind(b, 0) + c + behind(c, 1)
        d = f * total + (1.0 - f)
        diag[x] = d
        step[x] = RELAX / d
        lx[x] = a * f * free[x + 1]
        ly[x] = b * f * ahead(f, 0)
        lz[x] = c * f * ahead(f, 1)
        return carry

    lax.fori_loop(1, last, body, 0)


def jacobi(rhs, step, links, ga, gb, source):
    planes = rhs.shape[0]
    for g in (ga, gb):
        g[0] = jnp.zeros(g.shape[1:], F32)
        g[planes - 1] = jnp.zeros(g.shape[1:], F32)

    def first(x, carry):
        value = step[x] * rhs[x]
        source[x] = value
        ga[x] = value
        return carry

    lax.fori_loop(1, planes - 1, first, 0)
    now, then = ga, gb
    for sweep in range(1, SWEEPS):
        low, high = (3, planes - 3) if sweep == SWEEPS - 1 else (1, planes - 1)

        def body(x, carry, now=now, then=then):
            then[x] = (1.0 - RELAX) * now[x] + source[x] + step[x] * neighbours(now, links, x)
            return carry

        lax.fori_loop(low, high, body, 0)
        now, then = then, now
    return now


def coarse_sum(rows_ref):
    count = rows_ref.shape[0]
    each = 16
    per = LANES // each
    lane = lane_iota((count, LANES))
    row = lax.broadcasted_iota(jnp.int32, (count, LANES), 0)
    all_rows = rows_ref[:, 0, :]
    total = jnp.zeros((count, LANES), F32)
    for m in range(per):
        turned = pltpu.roll(all_rows, (each * m - COARSE_LANE) % LANES, 1)
        keep = (lax.rem(row, per) == m) & (lane >= each * m) & (lane < each * (m + 1))
        total = jnp.where(keep, turned, total)
    return jnp.sum(total.reshape(count // per, per, LANES), axis=1)


def scalar_sums(rows_ref, count):
    total = jnp.sum(rows_ref[:, 1, :], axis=0, keepdims=True)
    return [total[0:1, COARSE_LANE + i : COARSE_LANE + i + 1] for i in range(count)]


def coarse_weights(inverse_ref, sums):
    total = jnp.zeros((inverse_ref.shape[0], LANES), F32)
    for g in range(sums.shape[0]):
        total = total + inverse_ref[:, LANES * g : LANES * (g + 1)] * sums[g : g + 1, :]
    return jnp.sum(total, axis=1, keepdims=True)


def add_coarse(out, smooth, basis_ref, weights):
    vecs, nx, ny, nz = basis_ref.shape
    scale = [jnp.broadcast_to(weights[k : k + 1, 0:1], (8, LANES)) for k in range(vecs)]
    scale = [jnp.tile(s, (ny // 8, nz // LANES)) for s in scale]

    def body(x, carry):
        total = smooth[x + 3, 0:ny, 0:nz]
        for k in range(vecs):
            total = total + scale[k] * basis_ref[k, x]
        out[x] = total
        return carry

    lax.fori_loop(0, nx, body, 0)


def full_sum(value):
    return jnp.sum(value)


def call(kernel, outs, args, scratch=(), flops=0):
    whole = pl.BlockSpec(memory_space=pltpu.VMEM)
    size = sum(a.size * 4 for a in jax.tree.leaves(args)) + sum(
        o.size * 4 for o in jax.tree.leaves(outs)
    )
    return pl.pallas_call(
        kernel,
        out_shape=outs,
        in_specs=jax.tree.map(lambda _: whole, list(args)),
        out_specs=jax.tree.map(lambda _: whole, outs),
        scratch_shapes=list(scratch),
        compiler_params=pltpu.CompilerParams(vmem_limit_bytes=VMEM_LIMIT),
        cost_estimate=pl.CostEstimate(flops=flops, bytes_accessed=size, transcendentals=0),
    )(*args)


def shaped(*shape):
    return jax.ShapeDtypeStruct(shape, F32)


def face_shapes(shape, sizes, count, width):
    nx, ny, nz = shape
    outs = {
        "x": {r: shaped(count * width, ny, nz) for r in rounds_of(sizes[0])},
        "y": {r: shaped(count * width, nx, nz) for r in rounds_of(sizes[1])},
        "z": shaped(nx, ny, LANES),
    }
    if width == 2:
        outs["xy"] = {
            (rx, ry): shaped(max(8, 4 * count), nz)
            for rx in rounds_of(sizes[0])
            for ry in rounds_of(sizes[1])
        }
    return outs


def pack_faces(out, fields, sizes, width):
    ix, iy, _ = where_am_i()
    out["z"][...] = pack_z(fields)
    for r, ref in out["x"].items():
        pack_x(ref, fields, r, ix, width)
    for r, ref in out["y"].items():
        pack_y(ref, fields, r, iy, width)
    for (rx, ry), ref in out.get("xy", {}).items():
        pack_xy(ref, fields, rx, ry, ix, iy)


def send_faces(faces, sizes):
    got = {
        "x": {r: swap(v, sizes, {0: r}) for r, v in faces["x"].items()},
        "y": {r: swap(v, sizes, {1: r}) for r, v in faces["y"].items()},
        "z": {r: swap(faces["z"], sizes, {2: r}) for r in rounds_of(sizes[2])},
    }
    if "xy" in faces:
        got["xy"] = {(rx, ry): swap(v, sizes, {0: rx, 1: ry}) for (rx, ry), v in faces["xy"].items()}
    return got


def spread(rows):
    return lax.all_to_all(rows, AXES, 0, 0, tiled=True)


def shards(sizes, right_side, conductance, storage, dirichlet, basis, coarse_inverse):
    shape = right_side.shape
    nx, ny, nz = shape
    boxed = box_shape(shape)
    devices = sizes[0] * sizes[1] * sizes[2]
    row_shape = shaped(devices, 8, LANES)
    box = shaped(*boxed)
    vbox = pltpu.VMEM(boxed, F32)

    def pack_all(cond, store, fixed, rhs, out, free):
        free[...] = 1.0 - fixed[...].astype(F32)
        pack_faces(out, [cond.at[0], cond.at[1], cond.at[2], store, free, rhs], sizes, 2)

    faces = call(
        pack_all,
        face_shapes(shape, sizes, 6, 2),
        (conductance, storage, dirichlet, right_side),
        [pltpu.VMEM(shape, F32)],
    )

    def first_rows(ends, base, rhs, out):
        fill_rows(out, sizes, edge_tiles(ends, 6), project(base, rhs[...]))

    rows = call(first_rows, row_shape, (faces["z"], basis, right_side))
    got = send_faces(faces, sizes)
    rows_a = spread(rows)

    def first_solve(cond, store, fixed, rhs, base, inverse, got, rows, outs, scr, *work):
        (ga, gb, source), boxes = work[:3], list(work[3:]) + [outs["rhs"]]
        free = scr
        free[...] = 1.0 - fixed[...].astype(F32)
        owns = [cond.at[0], cond.at[1], cond.at[2], store, free, rhs]
        for b in boxes:
            clear(b)
        unpack_faces(boxes, owns, got["x"], got["y"], sizes, 2)
        unpack_xy(boxes, shape, got["xy"], sizes)
        unpack_z(boxes, shape, got["z"], sizes)
        unpack_edges(boxes, shape, rows, sizes)
        links = outs["links"]
        coefficients(boxes, links, outs["diag"], outs["step"])
        smooth = jacobi(outs["rhs"], outs["step"], links, ga, gb, source)
        weights = coarse_weights(inverse, coarse_sum(rows))
        add_coarse(outs["z"], smooth, base, weights)
        pack_faces(outs["faces"], [outs["z"]], sizes, 1)

    solved = call(
        first_solve,
        {
            "z": shaped(*shape),
            "links": [box, box, box],
            "diag": box,
            "step": box,
            "rhs": box,
            "faces": face_shapes(shape, sizes, 1, 1),
        },
        (conductance, storage, dirichlet, right_side, basis, coarse_inverse, got, rows_a),
        [pltpu.VMEM(shape, F32)] + [vbox] * 8,
    )
    links, diag, step = solved["links"], solved["diag"], solved["step"]
    direction = solved["z"]
    got = send_faces(solved["faces"], sizes)

    def apply(field, got, links, diag, out, vb):
        clear(vb)
        unpack_faces([vb], [field], got["x"], got["y"], sizes, 1)
        unpack_z([vb], shape, got["z"], sizes)

        def body(x, carry):
            whole = diag[x + 3] * vb[x + 3] - neighbours(vb, links, x + 3)
            out[x] = whole[0:ny, 0:nz]
            return carry

        lax.fori_loop(0, nx, body, 0)

    def first_image(field, got, links, diag, rhs, outs, vb):
        apply(field, got, links, diag, outs["image"], vb)
        pack_faces(outs["faces"], [outs["image"]], sizes, 2)
        tile = jnp.zeros((8, LANES), F32)
        values = [full_sum(rhs[...] * field[...]), full_sum(field[...] * outs["image"][...])]
        outs["sums"][...] = put_scalars(tile, values)

    imaged = call(
        first_image,
        {
            "image": shaped(*shape),
            "faces": face_shapes(shape, sizes, 1, 2),
            "sums": shaped(8, LANES),
        },
        (direction, got, links, diag, right_side),
        [vbox],
    )
    image = imaged["image"]

    def second_rows(ends, base, field, sums, out):
        fill_rows(out, sizes, edge_tiles(ends, 1), project(base, field[...]) + sums[...])

    rows = call(second_rows, row_shape, (imaged["faces"]["z"], basis, image, imaged["sums"]))
    got = send_faces(imaged["faces"], sizes)
    rows_c = spread(rows)

    def second_solve(
        field, rhs, rhs_box, base, inverse, links, step, got, rows_a, rows, outs, *work
    ):
        ga, gb, source, vb = work
        clear(vb)
        unpack_faces([vb], [field], got["x"], got["y"], sizes, 2)
        unpack_xy([vb], shape, got["xy"], sizes)
        unpack_z([vb], shape, got["z"], sizes)
        unpack_edges([vb], shape, rows, sizes)
        norm, curve = scalar_sums(rows, 2)
        alpha = norm / curve

        def body(x, carry):
            vb[x] = rhs_box[x] - alpha * vb[x]
            return carry

        lax.fori_loop(0, boxed[0], body, 0)
        outs["residual"][...] = vb[3 : 3 + nx, 0:ny, 0:nz]
        smooth = jacobi(vb, step, links, ga, gb, source)
        sums = coarse_sum(rows_a) - alpha * coarse_sum(rows)
        add_coarse(outs["z"], smooth, base, coarse_weights(inverse, sums))
        pack_faces(outs["faces"], [outs["z"]], sizes, 1)
        outs["scalars"][...] = jnp.concatenate(
            [jnp.broadcast_to(norm, (8, LANES)), jnp.broadcast_to(curve, (8, LANES))], axis=0
        )

    solved = call(
        second_solve,
        {
            "z": shaped(*shape),
            "residual": shaped(*shape),
            "scalars": shaped(16, LANES),
            "faces": face_shapes(shape, sizes, 1, 1),
        },
        (
            image,
            right_side,
            solved["rhs"],
            basis,
            coarse_inverse,
            links,
            step,
            got,
            rows_a,
            rows_c,
        ),
        [vbox] * 4,
    )
    precond, residual = solved["z"], solved["residual"]
    got = send_faces(solved["faces"], sizes)

    def second_image(field, got, links, diag, image, residual, outs, vb):
        apply(field, got, links, diag, outs["image"], vb)
        values = [
            full_sum(residual[...] * field[...]),
            full_sum(field[...] * outs["image"][...]),
            full_sum(field[...] * image[...]),
        ]
        tile = put_scalars(jnp.zeros((8, LANES), F32), values)
        outs["rows"][...] = jnp.broadcast_to(tile[None], outs["rows"].shape)

    last = call(
        second_image,
        {"image": shaped(*shape), "rows": row_shape},
        (precond, got, links, diag, image, residual),
        [vbox],
    )
    rows_e = spread(last["rows"])

    def finish(rows, scalars, direction, image, precond, precond_image, residual, out_field, out_rest):
        norm = scalars[0:1, 0:1]
        curve = scalars[8:9, 0:1]
        norm_next, curve_z, curve_mixed = scalar_sums(rows, 3)
        alpha = norm / curve
        beta = norm_next / norm
        curve_next = curve_z + 2.0 * beta * curve_mixed + beta * beta * curve
        alpha_next = norm_next / curve_next
        out_field[...] = alpha * direction[...] + alpha_next * (
            precond[...] + beta * direction[...]
        )
        out_rest[...] = residual[...] - alpha_next * (precond_image[...] + beta * image[...])

    return call(
        finish,
        (shaped(*shape), shaped(*shape)),
        (rows_e, solved["scalars"], direction, image, precond, last["image"], residual),
    )


def solution(mesh):
    sizes = tuple(mesh.shape[a] for a in AXES)
    placed = (
        P("gx", "gy", "gz"),
        P(None, "gx", "gy", "gz"),
        P("gx", "gy", "gz"),
        P("gx", "gy", "gz"),
        P(None, "gx", "gy", "gz"),
        P(("gx", "gy", "gz"), None),
    )
    return jax.shard_map(
        functools.partial(shards, sizes),
        mesh=mesh,
        in_specs=placed,
        out_specs=(P("gx", "gy", "gz"), P("gx", "gy", "gz")),
        check_vma=False,
    )
```

time: 465 us -> 128 us (0.28); the launches traced: 457 us -> 127 us
  blocking collectives: 208 us -> 13.7 us
  other arithmetic: 56.4 us -> 0 us
  starting transfers between devices: 71.8 us -> 33.5 us
  matrix products: 29.1 us -> 0 us
  Pallas kernels: 0 us -> 29 us
  local copies, waits for them, and re-layouts: 54.6 us -> 33.3 us
  waiting for transfers between devices: 31.1 us -> 16.4 us
  between operations: 6.08 us -> 0.83 us
    psum x3 -> x0, blocking collectives: 124 us -> none  [the longest x2 83.4 us: norm_sum(): return lax.psum(value, ('gx', 'gy', 'gz'))]
    unnamed x2 -> x0, blocking collectives: 83.9 us -> none
    ppermute x30 -> x24, starting transfers between devices: 71.8 us -> 22 us  [swap(): return lax.ppermute(value, AXES, pairs)]
    dot_general x6 -> x0, matrix products: 29.1 us -> none  [the longest x2 17.4 us: project(): jnp.dot(basis.reshape(basis.shape[0], -1), field.reshape(-1), precision=l...]
    pallas_call x0 -> x8, Pallas kernels: none -> 29 us  [call(): pl.pallas_call(kernel, out_shape=outs, in_specs=jax.tree.map(lambda _: wh...]
    unnamed x66 -> x92, local copies, waits for them, and re-layouts: 7.67 us -> 33.3 us
    ppermute x5 -> x0, local copies, waits for them, and re-layouts: 24.9 us -> none  [the longest x3 13.2 us: padded(): before = lax.ppermute(last, axis, up)]
    concatenate x7 -> x0, other arithmetic: 22.3 us -> none  [padded(): value = jnp.concatenate([before, value, after], axis=dim)]
  transfers between devices with their start and end apart: 30 -> 26, of which waited for: 12 -> 7; matrix products, arithmetic and copies ran while one was open for 16% -> 0% of each run, Pallas kernels for 0% -> 0%
where the time goes in v1:
time: 128 us; the launch traced here: 127 us
  starting transfers between devices  33.5 us (26%)
  local copies, waits for them, and re-layouts  33.3 us (26%)
  Pallas kernels  29 us (23%)
  waiting for transfers between devices  16.4 us (13%)
  blocking collectives  13.7 us (11%)
    unnamed x92, local copies, waits for them, and re-layouts  33.3 us
    pallas_call x8, Pallas kernels, call(): pl.pallas_call(kernel, out_shape=outs, in_specs=jax.tree.map(lambda _: wh...  29 us
    ppermute x24, starting transfers between devices, swap(): return lax.ppermute(value, AXES, pairs)  22 us
    ppermute x24, waiting for transfers between devices, swap(): return lax.ppermute(value, AXES, pairs)  16.4 us
    all_to_all x1, blocking collectives, spread(): return lax.all_to_all(rows, AXES, 0, 0, tiled=True)  13.7 us
    all_to_all x2, starting transfers between devices, spread(): return lax.all_to_all(rows, AXES, 0, 0, tiled=True)  11.5 us
  transfers between devices with their start and end apart: 26, of which 7 were waited for; matrix products, arithmetic and copies ran while one was open for 0% of the time, Pallas kernels for 0%

profile of v1, /device:TPU:0, one launch (start us, length us, event | category | flops | bytes accessed | tf_op | source)
XLA Modules:
  0.0 126.7 jit_solution(9707480953081278367)
XLA Ops:
  0.6 0.9 copy-done.4
  1.6 1.1 copy-done.9
  2.7 0.9 copy-done.16
  3.7 0.9 copy-done.18
  5.1 2.2 %copy-done = f32[16,16,16,256]{3,2,1,0:T(8,128)S(1)} copy-done((f32[16,16,16,256]{3,2,1,0:T(8,128)S(1)}, f32[16,16,16,256]{3,2,1,0:T(8,128)}, u32[]{:S(2)}) %copy-start) | copy-done | bytes 4194328
  7.3 0.9 copy-done.5
  8.2 1.3 %shard_map.78 = f32[32,8,128]{2,1,0:T(8,128)} custom-call(f32[16,16,128]{2,1,0:T(8,128)S(1)} %get-tuple-element.41.ends, f32[16,16,16,256]{3,2,1,0:T(8,128)S(1)} %copy-done, f32[16,16,256]{2,1,0:T(8,128)S(1)} %copy-done.5), custom_call_target="tpu_custom_call" | custom-call | bytes 4718592 | tf_op jit(solution)/shard_map/pallas_call | solution.py:429
  9.5 7.3 %all-to-all-start = ((f32[32,8,128]{2,1,0:T(8,128)}), f32[32,8,128]{2,1,0:T(8,128)S(1)}, u32[]{:S(2)}, u32[]{:S(2)}) async-start(f32[32,8,128]{2,1,0:T(8,128)} %shard_map.78), calls=%async_computation | async-start | bytes 262144 | tf_op jit(solution)/shard_map/all_to_all | solution.py:483
  16.9 1.8 %collective-permute-start = (f32[12,16,256]{2,1,0:T(8,128)S(1)}, f32[12,16,256]{2,1,0:T(8,128)S(1)}, u32[]{:S(2)}, u32[]{:S(2)}) collective-permute-start(f32[12,16,256]{2,1,0:T(8,128)S(1)} %get-tuple-element.36), channel_id=1, source_target_pairs={{0,16},{1,17},{2,18},{3,19},{4,20},{5,21},{6,22},{7,23},{8,24},{9,... | collective-permute-start | bytes 589832 | tf_op jit(solution)/shard_map/ppermute | solution.py:49
  18.7 1.5 %collective-permute-start.3 = (f32[12,16,256]{2,1,0:T(8,128)S(1)}, f32[12,16,256]{2,1,0:T(8,128)S(1)}, u32[]{:S(2)}, u32[]{:S(2)}) collective-permute-start(f32[12,16,256]{2,1,0:T(8,128)S(1)} %get-tuple-element.39), channel_id=1, source_target_pairs={{0,4},{1,5},{2,6},{3,7},{4,0},{5,1},{6,2},{7,3},{8,12},{9,13},{10,... | collective-permute-start | bytes 589832 | tf_op jit(solution)/shard_map/ppermute | solution.py:49
  20.2 3.0 %collective-permute-start.1 = (f32[24,256]{1,0:T(8,128)S(1)}, f32[24,256]{1,0:T(8,128)S(1)}, u32[]{:S(2)}, u32[]{:S(2)}) collective-permute-start(f32[24,256]{1,0:T(8,128)S(1)} %get-tuple-element.37), channel_id=1, source_target_pairs={{0,20},{1,21},{2,22},{3,23},{4,16},{5,17},{6,18},{7,19},{8,28},{9,... | collective-permute-start | bytes 73736 | tf_op jit(solution)/shard_map/ppermute | solution.py:49
  23.1 4.3 %collective-permute-done.1.got__xy____0__0__ = f32[24,256]{1,0:T(8,128)S(1)} collective-permute-done((f32[24,256]{1,0:T(8,128)S(1)}, f32[24,256]{1,0:T(8,128)S(1)}, u32[]{:S(2)}, u32[]{:S(2)}) %collective-permute-start.1) | collective-permute-done | bytes 24608 | tf_op jit(solution)/shard_map/ppermute | solution.py:49
  28.7 1.2 collective-permute-start.5
  29.8 3.2 %collective-permute-done.6.got__z___1_ = f32[16,16,128]{2,1,0:T(8,128)S(1)} collective-permute-done((f32[16,16,128]{2,1,0:T(8,128)S(1)}, f32[16,16,128]{2,1,0:T(8,128)S(1)}, u32[]{:S(2)}, u32[]{:S(2)}) %collective-permute-start.6) | collective-permute-done | bytes 131104 | tf_op jit(solution)/shard_map/ppermute | solution.py:49
  37.1 2.2 %copy-done.1 = f32[16,16,16,256]{3,2,1,0:T(8,128)S(1)} copy-done((f32[16,16,16,256]{3,2,1,0:T(8,128)S(1)}, f32[16,16,16,256]{3,2,1,0:T(8,128)}, u32[]{:S(2)}) %copy-start.1) | copy-done | bytes 4194328
  39.3 0.9 copy-done.12
  40.2 0.9 copy-done.17
  41.1 0.9 copy-done.19
  42.1 0.9 copy-done.25
  43.0 0.9 copy-done.27
  43.9 0.9 copy-done.29
  44.9 0.9 copy-done.31
  45.8 0.9 copy-done.33
  47.4 10.2 %shard_map.79 = (f32[22,24,384]{2,1,0:T(8,128)S(1)}, f32[1,16,256]{2,1,0:T(8,128)S(1)}, f32[1,16,256]{2,1,0:T(8,128)S(1)}, f32[1,16,256]{2,1,0:T(8,128)S(1)}, f3...) custom-call(f32[3,16,16,256]{3,2,1,0:T(8,128)S(1)} %copy-done.10, ...), custom_call_target="tpu_custom_call" | custom-call | bytes 12140544 | tf_op jit(solution)/shard_map/pallas_call | solution.py:429
  58.4 0.8 collective-permute-start.10
  59.2 0.9 collective-permute-start.7
  60.0 2.9 %collective-permute-done.7.got__x___0_ = f32[1,16,256]{2,1,0:T(8,128)S(1)} collective-permute-done((f32[1,16,256]{2,1,0:T(8,128)S(1)}, f32[1,16,256]{2,1,0:T(8,128)S(1)}, u32[]{:S(2)}, u32[]{:S(2)}) %collective-permute-start.7) | collective-permute-done | bytes 16416 | tf_op jit(solution)/shard_map/ppermute | solution.py:49
  62.9 0.9 collective-permute-done.8.got__y___0_
  63.8 2.6 %shard_map.80 = (f32[2,16,256]{2,1,0:T(8,128)S(1)}, f32[8,256]{1,0:T(8,128)}, f32[8,256]{1,0:T(8,128)}, f32[2,16,256]{2,1,0:T(8,128)S(1)}, f32[2,16,256]{2,1,0:T...) custom-call(f32[16,16,256]{2,1,0:T(8,128)S(1)} %get-tuple-element.42.field.direction, ...), custom_call_target="tpu_custom_call" | custom-call | bytes 4591616 | tf_op jit(solution)/shard_map/pallas_call | solution.py:429
  66.4 0.9 copy-done.7
  69.2 2.1 %shard_map.81 = f32[32,8,128]{2,1,0:T(8,128)} custom-call(f32[16,16,128]{2,1,0:T(8,128)} %get-tuple-element.59.ends, f32[16,16,16,256]{3,2,1,0:T(8,128)S(1)} %copy-done.2, f32[16,16,256]{2,1,0:T(8,128)S(1)} %get-tuple-element.51.field.image, f32[8,128]{1,0:T(8,128)S(1)} %get-tuple-element.60.sums), custom_call_target="tpu_custom_call" | custom-call | bytes 4722688 | tf_op jit(solution)/shard_map/pallas_call | solution.py:429
  71.3 4.2 %all-to-all-start.1 = ((f32[32,8,128]{2,1,0:T(8,128)}), f32[32,8,128]{2,1,0:T(8,128)S(1)}, u32[]{:S(2)}, u32[]{:S(2)}) async-start(f32[32,8,128]{2,1,0:T(8,128)} %shard_map.81), calls=%async_computation.1 | async-start | bytes 262144 | tf_op jit(solution)/shard_map/all_to_all | solution.py:483
  75.5 1.6 %collective-permute-start.18 = (f32[16,16,128]{2,1,0:T(8,128)}, f32[16,16,128]{2,1,0:T(8,128)S(1)}, u32[]{:S(2)}, u32[]{:S(2)}) collective-permute-start(f32[16,16,128]{2,1,0:T(8,128)} %get-tuple-element.59.ends), channel_id=1, source_target_pairs={{0,3},{1,2},{2,1},{3,0},{4,7},{5,6},{6,5},{7,4},{8,11},{9,10},{10,... | collective-permute-start | bytes 393224 | tf_op jit(solution)/shard_map/ppermute | solution.py:49
  77.4 2.4 %collective-permute-start.13 = (f32[8,256]{1,0:T(8,128)}, f32[8,256]{1,0:T(8,128)S(1)}, u32[]{:S(2)}, u32[]{:S(2)}) collective-permute-start(f32[8,256]{1,0:T(8,128)} %get-tuple-element.55), channel_id=1, source_target_pairs={{0,20},{1,21},{2,22},{3,23},{4,16},{5,17},{6,18},{7,19},{8,28},{9,... | collective-permute-start | bytes 24584 | tf_op jit(solution)/shard_map/ppermute | solution.py:49
  80.4 1.8 %collective-permute-done.13.got__xy____0__0__ = f32[8,256]{1,0:T(8,128)S(1)} collective-permute-done((f32[8,256]{1,0:T(8,128)}, f32[8,256]{1,0:T(8,128)S(1)}, u32[]{:S(2)}, u32[]{:S(2)}) %collective-permute-start.13) | collective-permute-done | bytes 8224 | tf_op jit(solution)/shard_map/ppermute | solution.py:49
  82.2 2.1 %collective-permute-start.15 = (f32[2,16,256]{2,1,0:T(8,128)}, f32[2,16,256]{2,1,0:T(8,128)S(1)}, u32[]{:S(2)}, u32[]{:S(2)}) collective-permute-start(f32[2,16,256]{2,1,0:T(8,128)} %copy-done.44), channel_id=1, source_target_pairs={{0,4},{1,5},{2,6},{3,7},{4,0},{5,1},{6,2},{7,3},{8,12},{9,13},{10,... | collective-permute-start | bytes 98312 | tf_op jit(solution)/shard_map/ppermute | solution.py:49
  84.9 1.5 %collective-permute-done.15.got__y___0_ = f32[2,16,256]{2,1,0:T(8,128)S(1)} collective-permute-done((f32[2,16,256]{2,1,0:T(8,128)}, f32[2,16,256]{2,1,0:T(8,128)S(1)}, u32[]{:S(2)}, u32[]{:S(2)}) %collective-permute-start.15) | collective-permute-done | bytes 32800 | tf_op jit(solution)/shard_map/ppermute | solution.py:49
  87.7 2.2 %copy-done.3 = f32[16,16,16,256]{3,2,1,0:T(8,128)S(1)} copy-done((f32[16,16,16,256]{3,2,1,0:T(8,128)S(1)}, f32[16,16,16,256]{3,2,1,0:T(8,128)}, u32[]{:S(2)}) %copy-start.3) | copy-done | bytes 4194328
  89.8 1.1 copy-done.21
  91.0 1.1 copy-done.23
  92.1 0.8 copy-done.36
  94.3 9.3 %shard_map.82 = (f32[1,16,256]{2,1,0:T(8,128)S(1)}, f32[1,16,256]{2,1,0:T(8,128)S(1)}, f32[1,16,256]{2,1,0:T(8,128)S(1)}, f32[16,16,128]{2,1,0:T(8,128)S(1)}, f3...) custom-call(f32[16,16,256]{2,1,0:T(8,128)S(1)} %get-tuple-element.51.field.image, ...), custom_call_target="tpu_custom_call" | custom-call | bytes 10158080 | tf_op jit(solution)/shard_map/pallas_call | solution.py:429
  104.3 1.4 %collective-permute-start.19 = (f32[1,16,256]{2,1,0:T(8,128)S(1)}, f32[1,16,256]{2,1,0:T(8,128)S(1)}, u32[]{:S(2)}, u32[]{:S(2)}) collective-permute-start(f32[1,16,256]{2,1,0:T(8,128)S(1)} %get-tuple-element.62), channel_id=1, source_target_pairs={{0,16},{1,17},{2,18},{3,19},{4,20},{5,21},{6,22},{7,23},{8,24},{9,... | collective-permute-start | bytes 49160 | tf_op jit(solution)/shard_map/ppermute | solution.py:49
  105.7 2.4 %collective-permute-start.20 = (f32[1,16,256]{2,1,0:T(8,128)S(1)}, f32[1,16,256]{2,1,0:T(8,128)S(1)}, u32[]{:S(2)}, u32[]{:S(2)}) collective-permute-start(f32[1,16,256]{2,1,0:T(8,128)S(1)} %get-tuple-element.63), channel_id=1, source_target_pairs={{0,4},{1,5},{2,6},{3,7},{4,0},{5,1},{6,2},{7,3},{8,12},{9,13},{10,... | collective-permute-start | bytes 49160 | tf_op jit(solution)/shard_map/ppermute | solution.py:49
  108.2 1.7 %collective-permute-done.20.got__y___0_ = f32[1,16,256]{2,1,0:T(8,128)S(1)} collective-permute-done((f32[1,16,256]{2,1,0:T(8,128)S(1)}, f32[1,16,256]{2,1,0:T(8,128)S(1)}, u32[]{:S(2)}, u32[]{:S(2)}) %collective-permute-start.20) | collective-permute-done | bytes 16416 | tf_op jit(solution)/shard_map/ppermute | solution.py:49
  109.9 1.9 %shard_map.83 = (f32[16,16,256]{2,1,0:T(8,128)S(1)}, f32[32,8,128]{2,1,0:T(8,128)S(1)}) custom-call(f32[16,16,256]{2,1,0:T(8,128)S(1)} %get-tuple-element.61.field.precond, f32[1,16,256]{2,1,0:T(8,128)S(1)} %collective-permute-done.19.got__x___0_, f32[1,16,256]{2,1,0:T(8,128)S(1)} %collective-permute-done.20.got__y___0_, ...), custom_call_target="tpu_custom_call" | custom-call | bytes 4734976 | tf_op jit(solution)/shard_map/pallas_call | solution.py:429
  111.8 13.7 %all_to_all.15.rows = f32[32,8,128]{2,1,0:T(8,128)S(1)} all-to-all(f32[32,8,128]{2,1,0:T(8,128)S(1)} %get-tuple-element.67), channel_id=1, replica_groups=mesh['gx'=2,'gy'=4,'gz'=4] {'gx','gy','gz'}, dimensions={0} | all-to-all | bytes 262144 | tf_op jit(solution)/shard_map/all_to_all | solution.py:483
  125.5 1.2 shard_map.84
  (105 shorter events, 14.0 us)
Async XLA Ops:
  0.6 1.0 copy-start.4
  1.6 1.1 copy-start.9
  2.7 0.9 copy-start.16
  3.7 0.9 copy-start.18
  4.6 32.5 %copy-start.6 = (f32[16,16,256]{2,1,0:T(8,128)S(1)}, f32[16,16,256]{2,1,0:T(8,128)}, u32[]{:S(2)}) copy-start(f32[16,16,256]{2,1,0:T(8,128)} %rhs.9) | copy-start | bytes 786436
  4.6 32.5 %copy-start.10 = (f32[3,16,16,256]{3,2,1,0:T(8,128)S(1)}, f32[3,16,16,256]{3,2,1,0:T(8,128)}, u32[]{:S(2)}) copy-start(f32[3,16,16,256]{3,2,1,0:T(8,128)} %cond.3) | copy-start | bytes 2359300
  4.6 32.5 %copy-start.34 = (f32[16,512]{1,0:T(8,128)S(1)}, f32[16,512]{1,0:T(8,128)}, u32[]{:S(2)}) copy-start(f32[16,512]{1,0:T(8,128)} %inverse.3) | copy-start | bytes 98308
  5.1 2.2 %copy-start = (f32[16,16,16,256]{3,2,1,0:T(8,128)S(1)}, f32[16,16,16,256]{3,2,1,0:T(8,128)}, u32[]{:S(2)}) copy-start(f32[16,16,16,256]{3,2,1,0:T(8,128)} %base.7) | copy-start | bytes 12582916
  7.3 0.9 copy-start.5
  9.5 26.9 %all-to-all-start = ((f32[32,8,128]{2,1,0:T(8,128)}), f32[32,8,128]{2,1,0:T(8,128)S(1)}, u32[]{:S(2)}, u32[]{:S(2)}) async-start(f32[32,8,128]{2,1,0:T(8,128)} %shard_map.78), calls=%async_computation | async-start | bytes 262144 | tf_op jit(solution)/shard_map/all_to_all | solution.py:483
  16.9 17.5 %collective-permute-start = (f32[12,16,256]{2,1,0:T(8,128)S(1)}, f32[12,16,256]{2,1,0:T(8,128)S(1)}, u32[]{:S(2)}, u32[]{:S(2)}) collective-permute-start(f32[12,16,256]{2,1,0:T(8,128)S(1)} %get-tuple-element.36), channel_id=1, source_target_pairs={{0,16},{1,17},{2,18},{3,19},{4,20},{5,21},{6,22},{7,23},{8,24},{9,... | collective-permute-start | bytes 589832 | tf_op jit(solution)/shard_map/ppermute | solution.py:49
  18.7 16.4 %collective-permute-start.3 = (f32[12,16,256]{2,1,0:T(8,128)S(1)}, f32[12,16,256]{2,1,0:T(8,128)S(1)}, u32[]{:S(2)}, u32[]{:S(2)}) collective-permute-start(f32[12,16,256]{2,1,0:T(8,128)S(1)} %get-tuple-element.39), channel_id=1, source_target_pairs={{0,4},{1,5},{2,6},{3,7},{4,0},{5,1},{6,2},{7,3},{8,12},{9,13},{10,... | collective-permute-start | bytes 589832 | tf_op jit(solution)/shard_map/ppermute | solution.py:49
  20.2 15.6 %collective-permute-start.4 = (f32[12,16,256]{2,1,0:T(8,128)S(1)}, f32[12,16,256]{2,1,0:T(8,128)S(1)}, u32[]{:S(2)}, u32[]{:S(2)}) collective-permute-start(f32[12,16,256]{2,1,0:T(8,128)S(1)} %get-tuple-element.40), channel_id=1, source_target_pairs={{0,1},{1,0},{2,3},{3,2},{4,8},{5,9},{6,10},{7,11},{8,4},{9,5},{10,... | collective-permute-start | bytes 589832 | tf_op jit(solution)/shard_map/ppermute | solution.py:49
  20.2 7.3 %collective-permute-start.1 = (f32[24,256]{1,0:T(8,128)S(1)}, f32[24,256]{1,0:T(8,128)S(1)}, u32[]{:S(2)}, u32[]{:S(2)}) collective-permute-start(f32[24,256]{1,0:T(8,128)S(1)} %get-tuple-element.37), channel_id=1, source_target_pairs={{0,20},{1,21},{2,22},{3,23},{4,16},{5,17},{6,18},{7,19},{8,28},{9,... | collective-permute-start | bytes 73736 | tf_op jit(solution)/shard_map/ppermute | solution.py:49
  23.1 4.9 %collective-permute-start.2 = (f32[24,256]{1,0:T(8,128)S(1)}, f32[24,256]{1,0:T(8,128)S(1)}, u32[]{:S(2)}, u32[]{:S(2)}) collective-permute-start(f32[24,256]{1,0:T(8,128)S(1)} %get-tuple-element.38), channel_id=1, source_target_pairs={{0,1},{1,0},{2,3},{3,2},{4,24},{5,25},{6,26},{7,27},{8,20},{9,21},... | collective-permute-start | bytes 73736 | tf_op jit(solution)/shard_map/ppermute | solution.py:49
  27.5 5.6 %collective-permute-start.6 = (f32[16,16,128]{2,1,0:T(8,128)S(1)}, f32[16,16,128]{2,1,0:T(8,128)S(1)}, u32[]{:S(2)}, u32[]{:S(2)}) collective-permute-start(f32[16,16,128]{2,1,0:T(8,128)S(1)} %get-tuple-element.41.ends), channel_id=1, source_target_pairs={{0,3},{1,2},{2,1},{3,0},{4,7},{5,6},{6,5},{7,4},{8,11},{9,10},{10,... | collective-permute-start | bytes 393224 | tf_op jit(solution)/shard_map/ppermute | solution.py:49
  28.7 5.1 %collective-permute-start.5 = (f32[16,16,128]{2,1,0:T(8,128)S(1)}, f32[16,16,128]{2,1,0:T(8,128)S(1)}, u32[]{:S(2)}, u32[]{:S(2)}) collective-permute-start(f32[16,16,128]{2,1,0:T(8,128)S(1)} %get-tuple-element.41.ends), channel_id=1, source_target_pairs={{0,1},{1,0},{2,3},{3,2},{4,5},{5,4},{6,7},{7,6},{8,9},{9,8},{10,11... | collective-permute-start | bytes 393224 | tf_op jit(solution)/shard_map/ppermute | solution.py:49
  37.1 2.2 %copy-start.1 = (f32[16,16,16,256]{3,2,1,0:T(8,128)S(1)}, f32[16,16,16,256]{3,2,1,0:T(8,128)}, u32[]{:S(2)}) copy-start(f32[16,16,16,256]{3,2,1,0:T(8,128)} %base.7) | copy-start | bytes 12582916
  40.2 0.9 copy-start.17
  41.1 0.9 copy-start.19
  47.4 21.8 %copy-start.2 = (f32[16,16,16,256]{3,2,1,0:T(8,128)S(1)}, f32[16,16,16,256]{3,2,1,0:T(8,128)}, u32[]{:S(2)}) copy-start(f32[16,16,16,256]{3,2,1,0:T(8,128)} %base.7) | copy-start | bytes 12582916
  57.6 8.8 %copy-start.14 = (f32[16,16,256]{2,1,0:T(8,128)}, f32[16,16,256]{2,1,0:T(8,128)S(1)}, u32[]{:S(2)}) copy-start(f32[16,16,256]{2,1,0:T(8,128)S(1)} %get-tuple-element.42.field.direction) | copy-start | bytes 786436
  57.6 11.6 %copy-start.20 = (f32[22,24,384]{2,1,0:T(8,128)}, f32[22,24,384]{2,1,0:T(8,128)S(1)}, u32[]{:S(2)}) copy-start(f32[22,24,384]{2,1,0:T(8,128)S(1)} %get-tuple-element.52.rhs_box) | copy-start | bytes 2433028
  57.6 11.6 %copy-start.22 = (f32[22,24,384]{2,1,0:T(8,128)}, f32[22,24,384]{2,1,0:T(8,128)S(1)}, u32[]{:S(2)}) copy-start(f32[22,24,384]{2,1,0:T(8,128)S(1)} %get-tuple-element.53.step) | copy-start | bytes 2433028
  57.6 6.2 %collective-permute-start.11 = (f32[16,16,128]{2,1,0:T(8,128)S(1)}, f32[16,16,128]{2,1,0:T(8,128)S(1)}, u32[]{:S(2)}, u32[]{:S(2)}) collective-permute-start(f32[16,16,128]{2,1,0:T(8,128)S(1)} %get-tuple-element.46), channel_id=1, source_target_pairs={{0,3},{1,2},{2,1},{3,0},{4,7},{5,6},{6,5},{7,4},{8,11},{9,10},{10,... | collective-permute-start | bytes 393224 | tf_op jit(solution)/shard_map/ppermute | solution.py:49
  58.4 5.4 %collective-permute-start.10 = (f32[16,16,128]{2,1,0:T(8,128)S(1)}, f32[16,16,128]{2,1,0:T(8,128)S(1)}, u32[]{:S(2)}, u32[]{:S(2)}) collective-permute-start(f32[16,16,128]{2,1,0:T(8,128)S(1)} %get-tuple-element.46), channel_id=1, source_target_pairs={{0,1},{1,0},{2,3},{3,2},{4,5},{5,4},{6,7},{7,6},{8,9},{9,8},{10,11... | collective-permute-start | bytes 393224 | tf_op jit(solution)/shard_map/ppermute | solution.py:49
  59.2 3.7 %collective-permute-start.7 = (f32[1,16,256]{2,1,0:T(8,128)S(1)}, f32[1,16,256]{2,1,0:T(8,128)S(1)}, u32[]{:S(2)}, u32[]{:S(2)}) collective-permute-start(f32[1,16,256]{2,1,0:T(8,128)S(1)} %get-tuple-element.43), channel_id=1, source_target_pairs={{0,16},{1,17},{2,18},{3,19},{4,20},{5,21},{6,22},{7,23},{8,24},{9,... | collective-permute-start | bytes 49160 | tf_op jit(solution)/shard_map/ppermute | solution.py:49
  60.0 3.7 %collective-permute-start.8 = (f32[1,16,256]{2,1,0:T(8,128)S(1)}, f32[1,16,256]{2,1,0:T(8,128)S(1)}, u32[]{:S(2)}, u32[]{:S(2)}) collective-permute-start(f32[1,16,256]{2,1,0:T(8,128)S(1)} %get-tuple-element.44), channel_id=1, source_target_pairs={{0,4},{1,5},{2,6},{3,7},{4,0},{5,1},{6,2},{7,3},{8,12},{9,13},{10,... | collective-permute-start | bytes 49160 | tf_op jit(solution)/shard_map/ppermute | solution.py:49
  60.0 3.7 %collective-permute-start.9 = (f32[1,16,256]{2,1,0:T(8,128)S(1)}, f32[1,16,256]{2,1,0:T(8,128)S(1)}, u32[]{:S(2)}, u32[]{:S(2)}) collective-permute-start(f32[1,16,256]{2,1,0:T(8,128)S(1)} %get-tuple-element.45), channel_id=1, source_target_pairs={{0,1},{1,0},{2,3},{3,2},{4,8},{5,9},{6,10},{7,11},{8,4},{9,5},{10,... | collective-permute-start | bytes 49160 | tf_op jit(solution)/shard_map/ppermute | solution.py:49
  63.8 23.9 %copy-start.13 = (f32[32,8,128]{2,1,0:T(8,128)S(1)}, f32[32,8,128]{2,1,0:T(8,128)}, u32[]{:S(2)}) copy-start(f32[32,8,128]{2,1,0:T(8,128)} %copy-done.11) | copy-start | bytes 393220
  71.3 16.4 %all-to-all-start.1 = ((f32[32,8,128]{2,1,0:T(8,128)}), f32[32,8,128]{2,1,0:T(8,128)S(1)}, u32[]{:S(2)}, u32[]{:S(2)}) async-start(f32[32,8,128]{2,1,0:T(8,128)} %shard_map.81), calls=%async_computation.1 | async-start | bytes 262144 | tf_op jit(solution)/shard_map/all_to_all | solution.py:483
  75.5 12.1 %collective-permute-start.18 = (f32[16,16,128]{2,1,0:T(8,128)}, f32[16,16,128]{2,1,0:T(8,128)S(1)}, u32[]{:S(2)}, u32[]{:S(2)}) collective-permute-start(f32[16,16,128]{2,1,0:T(8,128)} %get-tuple-element.59.ends), channel_id=1, source_target_pairs={{0,3},{1,2},{2,1},{3,0},{4,7},{5,6},{6,5},{7,4},{8,11},{9,10},{10,... | collective-permute-start | bytes 393224 | tf_op jit(solution)/shard_map/ppermute | solution.py:49
  77.1 10.6 %collective-permute-start.17 = (f32[16,16,128]{2,1,0:T(8,128)}, f32[16,16,128]{2,1,0:T(8,128)S(1)}, u32[]{:S(2)}, u32[]{:S(2)}) collective-permute-start(f32[16,16,128]{2,1,0:T(8,128)} %get-tuple-element.59.ends), channel_id=1, source_target_pairs={{0,1},{1,0},{2,3},{3,2},{4,5},{5,4},{6,7},{7,6},{8,9},{9,8},{10,11... | collective-permute-start | bytes 393224 | tf_op jit(solution)/shard_map/ppermute | solution.py:49
  77.4 4.8 %collective-permute-start.13 = (f32[8,256]{1,0:T(8,128)}, f32[8,256]{1,0:T(8,128)S(1)}, u32[]{:S(2)}, u32[]{:S(2)}) collective-permute-start(f32[8,256]{1,0:T(8,128)} %get-tuple-element.55), channel_id=1, source_target_pairs={{0,20},{1,21},{2,22},{3,23},{4,16},{5,17},{6,18},{7,19},{8,28},{9,... | collective-permute-start | bytes 24584 | tf_op jit(solution)/shard_map/ppermute | solution.py:49
  79.8 4.5 %collective-permute-start.14 = (f32[8,256]{1,0:T(8,128)}, f32[8,256]{1,0:T(8,128)S(1)}, u32[]{:S(2)}, u32[]{:S(2)}) collective-permute-start(f32[8,256]{1,0:T(8,128)} %get-tuple-element.56), channel_id=1, source_target_pairs={{0,1},{1,0},{2,3},{3,2},{4,24},{5,25},{6,26},{7,27},{8,20},{9,21},... | collective-permute-start | bytes 24584 | tf_op jit(solution)/shard_map/ppermute | solution.py:49
  79.8 5.1 %collective-permute-start.12 = (f32[2,16,256]{2,1,0:T(8,128)}, f32[2,16,256]{2,1,0:T(8,128)S(1)}, u32[]{:S(2)}, u32[]{:S(2)}) collective-permute-start(f32[2,16,256]{2,1,0:T(8,128)} %copy-done.45), channel_id=1, source_target_pairs={{0,16},{1,17},{2,18},{3,19},{4,20},{5,21},{6,22},{7,23},{8,24},{9,... | collective-permute-start | bytes 98312 | tf_op jit(solution)/shard_map/ppermute | solution.py:49
  82.2 4.2 %collective-permute-start.15 = (f32[2,16,256]{2,1,0:T(8,128)}, f32[2,16,256]{2,1,0:T(8,128)S(1)}, u32[]{:S(2)}, u32[]{:S(2)}) collective-permute-start(f32[2,16,256]{2,1,0:T(8,128)} %copy-done.44), channel_id=1, source_target_pairs={{0,4},{1,5},{2,6},{3,7},{4,0},{5,1},{6,2},{7,3},{8,12},{9,13},{10,... | collective-permute-start | bytes 98312 | tf_op jit(solution)/shard_map/ppermute | solution.py:49
  84.9 2.1 %collective-permute-start.16 = (f32[2,16,256]{2,1,0:T(8,128)}, f32[2,16,256]{2,1,0:T(8,128)S(1)}, u32[]{:S(2)}, u32[]{:S(2)}) collective-permute-start(f32[2,16,256]{2,1,0:T(8,128)} %copy-done.43), channel_id=1, source_target_pairs={{0,1},{1,0},{2,3},{3,2},{4,8},{5,9},{6,10},{7,11},{8,4},{9,5},{10,... | collective-permute-start | bytes 98312 | tf_op jit(solution)/shard_map/ppermute | solution.py:49
  87.7 2.2 %copy-start.3 = (f32[16,16,16,256]{3,2,1,0:T(8,128)S(1)}, f32[16,16,16,256]{3,2,1,0:T(8,128)}, u32[]{:S(2)}) copy-start(f32[16,16,16,256]{3,2,1,0:T(8,128)} %base.7) | copy-start | bytes 12582916
  89.8 1.1 copy-start.21
  91.0 1.1 copy-start.23
  94.3 15.5 %copy-start.8 = (f32[22,24,384]{2,1,0:T(8,128)S(1)}, f32[22,24,384]{2,1,0:T(8,128)}, u32[]{:S(2)}) copy-start(f32[22,24,384]{2,1,0:T(8,128)} %copy-done.7) | copy-start | bytes 2433028
  103.6 21.9 %copy-start.15 = (f32[16,16,256]{2,1,0:T(8,128)S(1)}, f32[16,16,256]{2,1,0:T(8,128)}, u32[]{:S(2)}) copy-start(f32[16,16,256]{2,1,0:T(8,128)} %copy-done.14) | copy-start | bytes 786436
  103.6 6.3 %collective-permute-start.23 = (f32[16,16,128]{2,1,0:T(8,128)S(1)}, f32[16,16,128]{2,1,0:T(8,128)S(1)}, u32[]{:S(2)}, u32[]{:S(2)}) collective-permute-start(f32[16,16,128]{2,1,0:T(8,128)S(1)} %get-tuple-element.65), channel_id=1, source_target_pairs={{0,3},{1,2},{2,1},{3,0},{4,7},{5,6},{6,5},{7,4},{8,11},{9,10},{10,... | collective-permute-start | bytes 393224 | tf_op jit(solution)/shard_map/ppermute | solution.py:49
  103.6 6.2 %collective-permute-start.22 = (f32[16,16,128]{2,1,0:T(8,128)S(1)}, f32[16,16,128]{2,1,0:T(8,128)S(1)}, u32[]{:S(2)}, u32[]{:S(2)}) collective-permute-start(f32[16,16,128]{2,1,0:T(8,128)S(1)} %get-tuple-element.65), channel_id=1, source_target_pairs={{0,1},{1,0},{2,3},{3,2},{4,5},{5,4},{6,7},{7,6},{8,9},{9,8},{10,11... | collective-permute-start | bytes 393224 | tf_op jit(solution)/shard_map/ppermute | solution.py:49
  104.3 3.9 %collective-permute-start.19 = (f32[1,16,256]{2,1,0:T(8,128)S(1)}, f32[1,16,256]{2,1,0:T(8,128)S(1)}, u32[]{:S(2)}, u32[]{:S(2)}) collective-permute-start(f32[1,16,256]{2,1,0:T(8,128)S(1)} %get-tuple-element.62), channel_id=1, source_target_pairs={{0,16},{1,17},{2,18},{3,19},{4,20},{5,21},{6,22},{7,23},{8,24},{9,... | collective-permute-start | bytes 49160 | tf_op jit(solution)/shard_map/ppermute | solution.py:49
  105.7 4.1 %collective-permute-start.20 = (f32[1,16,256]{2,1,0:T(8,128)S(1)}, f32[1,16,256]{2,1,0:T(8,128)S(1)}, u32[]{:S(2)}, u32[]{:S(2)}) collective-permute-start(f32[1,16,256]{2,1,0:T(8,128)S(1)} %get-tuple-element.63), channel_id=1, source_target_pairs={{0,4},{1,5},{2,6},{3,7},{4,0},{5,1},{6,2},{7,3},{8,12},{9,13},{10,... | collective-permute-start | bytes 49160 | tf_op jit(solution)/shard_map/ppermute | solution.py:49
  108.2 1.7 %collective-permute-start.21 = (f32[1,16,256]{2,1,0:T(8,128)S(1)}, f32[1,16,256]{2,1,0:T(8,128)S(1)}, u32[]{:S(2)}, u32[]{:S(2)}) collective-permute-start(f32[1,16,256]{2,1,0:T(8,128)S(1)} %get-tuple-element.64), channel_id=1, source_target_pairs={{0,1},{1,0},{2,3},{3,2},{4,8},{5,9},{6,10},{7,11},{8,4},{9,5},{10,... | collective-permute-start | bytes 49160 | tf_op jit(solution)/shard_map/ppermute | solution.py:49
  (24 other events, 17.6 us)

commit v2 on v1

v2 whole, which is shorter than its diff:
```python
import functools
import math

import jax
import jax.numpy as jnp
from jax import lax
from jax.experimental import pallas as pl
from jax.experimental.pallas import tpu as pltpu
from jax.sharding import PartitionSpec as P

SWEEPS = 4
RELAX = 2.0 / 3.0
AXES = ("gx", "gy", "gz")
LANES = 128
VMEM_LIMIT = 24 * 1024 * 1024
F32 = jnp.float32
UNROLL = 4
PARTS = 4
SMOOTH_FLOPS = 10**9


def rounds_of(count):
    return (0, 1)[: 1 if count <= 2 else 2]


def mate(index, odd, count):
    other = index + 1 if index % 2 == odd else index - 1
    return other if 0 <= other < count else None


def swap(value, sizes, along):
    pairs = []
    nx, ny, nz = sizes
    for ix in range(nx):
        for iy in range(ny):
            for iz in range(nz):
                here = [ix, iy, iz]
                there = [
                    mate(here[a], along[a], sizes[a]) if a in along else here[a] for a in range(3)
                ]
                if None in there:
                    if 2 in along:
                        spare = nz - 1 - iz if iz in (0, nz - 1) else None
                    else:
                        spare = iz ^ 1 if nz % 2 == 0 else None
                    if spare is None:
                        continue
                    there = [ix, iy, spare]
                pairs.append(
                    ((ix * ny + iy) * nz + iz, (there[0] * ny + there[1]) * nz + there[2])
                )
    return lax.ppermute(value, AXES, pairs)


def upward(index, odd):
    return lax.rem(index, 2) == odd


def where_am_i():
    return [lax.axis_index(a) for a in AXES]


def lane_iota(shape):
    return lax.broadcasted_iota(jnp.int32, shape, len(shape) - 1)


def pack_x(out, fields, odd, index, width, ends=None):
    nx, _, nz = fields[0].shape
    count = len(fields) * width
    high = upward(index, odd)
    for cond, first in ((high, nx - width), (jnp.logical_not(high), 0)):

        @pl.when(cond)
        def _(first=first):
            for k, field in enumerate(fields):
                out[k * width : (k + 1) * width] = field[first : first + width]
            if ends is not None:
                for i in range(width):
                    out[count, :, LANES * i : LANES * (i + 1)] = ends[first + i]


def pack_y(out, fields, odd, index, width, ends=None):
    _, ny, nz = fields[0].shape
    count = len(fields) * width
    high = upward(index, odd)
    for cond, first in ((high, ny - width), (jnp.logical_not(high), 0)):

        @pl.when(cond)
        def _(first=first):
            for j in range(width):
                for k, field in enumerate(fields):
                    out[k * width + j] = field[:, first + j, :]
                if ends is not None:
                    out[count, :, LANES * j : LANES * (j + 1)] = ends[:, first + j, :]


def pack_xy(out, fields, rx, ry, ix, iy, ends):
    nx, ny, _ = fields[0].shape
    count = len(fields)
    for xhigh in (False, True):
        for yhigh in (False, True):

            @pl.when((upward(ix, rx) == xhigh) & (upward(iy, ry) == yhigh))
            def _(x0=(nx - 2 if xhigh else 0), y0=(ny - 2 if yhigh else 0)):
                for i in range(2):
                    for k, field in enumerate(fields):
                        out[4 * k + 2 * i : 4 * k + 2 * i + 2, :] = field[x0 + i, y0 : y0 + 2, :]
                    out[4 * count + 2 * i : 4 * count + 2 * i + 2, 0:LANES] = ends[
                        x0 + i, y0 : y0 + 2, :
                    ]


def z_rows(count):
    return (4 * count + 7) // 8 * 8


def pack_z(fields):
    nx, ny, nz = fields[0].shape
    lane = lane_iota((nx, ny, LANES))
    total = jnp.zeros((nx, ny, LANES), F32)
    for k, field in enumerate(fields):
        ends = jnp.where(lane < 64, field[:, :, 0:LANES], field[:, :, nz - LANES : nz])
        turned = pltpu.roll(ends, 4 * k + 2, 2)
        total = jnp.where((lane >= 4 * k) & (lane < 4 * k + 4), turned, total)
    return total.reshape(nx * ny, LANES).T[0 : z_rows(len(fields))]


def project(basis, field):
    nx, ny, nz = field.shape
    rows = []
    for piece in basis:
        vectors = piece.get()
        for k in range(vectors.shape[0]):
            prod = jnp.sum(vectors[k] * field, axis=0)
            part = jnp.zeros((8, LANES), F32)
            for y in range(ny // 8):
                for z in range(nz // LANES):
                    part = part + prod[8 * y : 8 * y + 8, LANES * z : LANES * (z + 1)]
            rows.append(jnp.sum(part, axis=0, keepdims=True))
    vecs = len(rows)
    totals = jnp.sum(jnp.concatenate(rows, axis=0), axis=1, keepdims=True)
    row = lax.broadcasted_iota(jnp.int32, (vecs, LANES), 0)
    return jnp.sum(jnp.where(lane_iota((vecs, LANES)) == row, totals, 0.0), axis=0, keepdims=True)


def put_scalars(row, first, values):
    lane = lane_iota(row.shape)
    for i, value in enumerate(values):
        row = jnp.where(lane == first + i, value, row)
    return row


def box_shape(shape):
    nx, ny, nz = shape
    return (nx + 6, ny + 8, nz + LANES)


def clear(box):
    def body(x, carry):
        box[x] = jnp.zeros(box.shape[1:], F32)
        return carry

    loop(0, box.shape[0], body)


def each_round(sizes, a, index, act):
    for r in rounds_of(sizes[a]):
        high = upward(index, r)

        @pl.when(high & (index + 1 < sizes[a]))
        def _(r=r):
            act(r, True)

        @pl.when(jnp.logical_not(high) & (index > 0))
        def _(r=r):
            act(r, False)


def unpack_faces(boxes, owns, xs, ys, sizes, width, ends=None):
    nx, ny, nz = owns[0].shape
    count = len(boxes) * width
    ix, iy, _ = where_am_i()
    for k, (box, own) in enumerate(zip(boxes, owns)):
        box[3 : 3 + nx, 0:ny, 0:nz] = own[...]
        if ends is not None:
            box[3 : 3 + nx, 0:ny, nz : nz + LANES] = halo_lanes(ends, k)

    def put_x(r, above):
        first = 3 + nx if above else 3 - width
        for k, box in enumerate(boxes):
            box[first : first + width, 0:ny, 0:nz] = xs[r][k * width : (k + 1) * width]
            if ends is not None:
                for i in range(width):
                    tile = xs[r][count, :, LANES * i : LANES * (i + 1)]
                    box[first + i, 0:ny, nz : nz + LANES] = halo_lanes(tile, k)

    each_round(sizes, 0, ix, put_x)

    def put_y(r, above):
        first = ny if above else ny + 8 - width
        for k, box in enumerate(boxes):
            for j in range(width):
                box[3 : 3 + nx, first + j, 0:nz] = ys[r][k * width + j]
                if ends is not None:
                    tile = ys[r][count, :, LANES * j : LANES * (j + 1)]
                    box[3 : 3 + nx, first + j, nz : nz + LANES] = halo_lanes(tile, k)

    each_round(sizes, 1, iy, put_y)


def unpack_xy(boxes, shape, xys, sizes):
    nx, ny, nz = shape
    count = len(boxes)
    ix, iy, _ = where_am_i()

    def put(rx, xabove):
        x0 = 3 + nx if xabove else 1

        def inner(ry, yabove):
            y0 = ny if yabove else ny + 6
            rows = xys[(rx, ry)]
            tile = rows[4 * count : 4 * count + 4, 0:LANES]
            for k, box in enumerate(boxes):
                turned = halo_lanes(tile, k)
                for i in range(2):
                    box[x0 + i, y0 : y0 + 2, 0:nz] = rows[4 * k + 2 * i : 4 * k + 2 * i + 2, :]
                    box[x0 + i, y0 : y0 + 2, nz : nz + LANES] = turned[2 * i : 2 * i + 2]

        each_round(sizes, 1, iy, inner)

    each_round(sizes, 0, ix, put)


def pick_z(zs, sizes, shape):
    count = sizes[2]
    iz = lax.axis_index("gz")
    rows, cells = zs[0].shape
    first = lax.rem(lax.broadcasted_iota(jnp.int32, (rows, cells), 0), 4) < 2
    total = jnp.zeros((rows, cells), F32)
    for r in rounds_of(count):
        high = upward(iz, r)
        below = jnp.logical_not(high) & (iz > 0)
        above = high & (iz + 1 < count)
        total = jnp.where((first & below) | (jnp.logical_not(first) & above), zs[r][...], total)
    filled = jnp.concatenate([total, jnp.zeros((LANES - rows, cells), F32)], axis=0)
    return filled.T.reshape(shape)


def halo_lanes(tile, k):
    lane = lane_iota(tile.shape)
    axis = len(tile.shape) - 1
    turned = pltpu.roll(tile, (-(4 * k + 2)) % LANES, axis)
    return jnp.where((lane < 2) | (lane >= LANES - 2), turned, 0.0)


def ahead(plane, axis):
    return pltpu.roll(plane, plane.shape[axis] - 1, axis)


def behind(plane, axis):
    return pltpu.roll(plane, 1, axis)


def neighbours(g, links, x):
    lx, ly, lz = links
    mid = g[x]
    y = ly[x]
    z = lz[x]
    total = lx[x] * g[x + 1] + lx[x - 1] * g[x - 1]
    total = total + y * ahead(mid, 0) + behind(y * mid, 0)
    return total + z * ahead(mid, 1) + behind(z * mid, 1)


def coefficients(fields, links, diag, step):
    tx, ty, tz, store, free, _ = fields
    lx, ly, lz = links
    last = tx.shape[0] - 1
    for ref in (lx, ly, lz, diag, step):
        ref[0] = jnp.zeros(ref.shape[1:], F32)
        ref[last] = jnp.zeros(ref.shape[1:], F32)

    def body(x, carry):
        f = free[x]
        a, b, c = tx[x], ty[x], tz[x]
        total = store[x] + a + tx[x - 1] + b + behind(b, 0) + c + behind(c, 1)
        d = f * total + (1.0 - f)
        diag[x] = d
        step[x] = RELAX / d
        lx[x] = a * f * free[x + 1]
        ly[x] = b * f * ahead(f, 0)
        lz[x] = c * f * ahead(f, 1)
        return carry

    loop(1, last, body)


def jacobi(rhs, step, links, ga, gb, source, out):
    planes = rhs.shape[0]
    nx, ny, nz = out.shape
    for g in (ga, gb, source):
        g[0] = jnp.zeros(g.shape[1:], F32)
        g[planes - 1] = jnp.zeros(g.shape[1:], F32)

    def first(x, carry):
        source[x] = step[x] * rhs[x]
        return carry

    loop(1, planes - 1, first)

    def swept(now, x):
        return (1.0 - RELAX) * now[x] + source[x] + step[x] * neighbours(now, links, x)

    now, then, spare = source, ga, gb
    for sweep in range(1, SWEEPS - 1):
        edge = max(1, 3 - (SWEEPS - 1 - sweep))

        def body(x, carry, now=now, then=then):
            then[x] = swept(now, x)
            return carry

        loop(edge, planes - edge, body)
        now, then, spare = then, spare, then

    def final(x, carry):
        out[x] = swept(now, x + 3)[0:ny, 0:nz]
        return carry

    loop(0, nx, final)


def coarse_sum(rows_ref, vecs):
    count = rows_ref.shape[0]
    per = LANES // vecs
    lane = lane_iota((count, LANES))
    row = lax.broadcasted_iota(jnp.int32, (count, LANES), 0)
    all_rows = rows_ref[...]
    total = jnp.zeros((count, LANES), F32)
    for m in range(per):
        turned = pltpu.roll(all_rows, vecs * m, 1) if m else all_rows
        keep = (lax.rem(row, per) == m) & (lane >= vecs * m) & (lane < vecs * (m + 1))
        total = jnp.where(keep, turned, total)
    return jnp.sum(total.reshape(count // per, per, LANES), axis=1)


def scalar_sums(rows_ref, first, count):
    total = jnp.sum(rows_ref[...], axis=0, keepdims=True)
    return [total[0:1, first + i : first + i + 1] for i in range(count)]


def coarse_weights(inverse_ref, sums):
    total = jnp.zeros((inverse_ref.shape[0], LANES), F32)
    for g in range(sums.shape[0]):
        total = total + inverse_ref[:, LANES * g : LANES * (g + 1)] * sums[g : g + 1, :]
    return jnp.sum(total, axis=1, keepdims=True)


def add_coarse(out, smooth, basis_ref, weights):
    vecs, nx, ny, nz = basis_ref.shape
    scale = [jnp.broadcast_to(weights[k : k + 1, 0:1], (8, LANES)) for k in range(vecs)]
    scale = [jnp.tile(s, (ny // 8, nz // LANES)) for s in scale]

    def body(x, carry):
        total = smooth[x]
        for k in range(vecs):
            total = total + scale[k] * basis_ref[k, x]
        out[x] = total
        return carry

    loop(0, nx, body)


def full_sum(value):
    return jnp.sum(value)


class Arriving:
    def __init__(self, buffer, copy=None):
        self.copy = copy
        self.buffer = buffer

    def get(self):
        if self.copy is not None:
            self.copy.wait()
            self.copy = None
        return self.buffer


class Far:
    def __init__(self, value, parts=False):
        self.value, self.parts = value, parts


class Stored:
    def __init__(self, *shape):
        self.shape = shape


class Leaving:
    def __init__(self, target, sem):
        self.target, self.sem, self.copy = target, sem, None

    def put(self, source):
        self.copy = pltpu.make_async_copy(source, self.target, self.sem)
        self.copy.start()


def call(kernel, outs, args, scratch=(), flops=0):
    leaves, tree = jax.tree.flatten(list(args), is_leaf=lambda one: isinstance(one, Far))
    out_leaves, out_tree = jax.tree.flatten(outs, is_leaf=lambda one: isinstance(one, Stored))
    count, n_out = len(leaves), len(out_leaves)
    far = [i for i, a in enumerate(leaves) if isinstance(a, Far)]
    stored = [i for i, a in enumerate(out_leaves) if isinstance(a, Stored)]
    parts = [i for i in far if leaves[i].parts]
    leaves = [
        pltpu.with_memory_space_constraint(a.value, pltpu.HBM) if isinstance(a, Far) else a
        for a in leaves
    ]

    def body(*refs):
        sources, results = refs[:count], list(refs[count : count + n_out])
        rest = refs[count + n_out :]
        sems, rest = rest[0], rest[1:]
        coming = [Arriving(a) for a in sources]
        used = 0
        for n, i in enumerate(far):
            pieces = [(sources[i], rest[n])]
            if i in parts:
                pieces = [(sources[i].at[p], rest[n].at[p]) for p in chunks(leaves[i].shape[0])]
            arrivals = []
            for source, target in pieces:
                copy = pltpu.make_async_copy(source, target, sems.at[used])
                copy.start()
                arrivals.append(Arriving(target, copy))
                used += 1
            coming[i] = arrivals if i in parts else arrivals[0]
        for n, i in enumerate(stored):
            results[i] = Leaving(results[i], sems.at[used])
            used += 1
        kernel(
            *jax.tree.unflatten(tree, coming),
            jax.tree.unflatten(out_tree, results),
            *rest[len(far) :],
        )
        fetch(coming)
        for i in stored:
            results[i].copy.wait()

    n_sems = len(far) - len(parts) + len(stored) + len(parts) * PARTS
    size = sum(4 * math.prod(a.shape) for a in leaves + out_leaves)
    given = pl.pallas_call(
        body,
        out_shape=[pltpu.HBM(a.shape, F32) if isinstance(a, Stored) else a for a in out_leaves],
        in_specs=[
            pl.BlockSpec(
                memory_space=pltpu.HBM if i in far else pltpu.VMEM
            )
            for i in range(count)
        ],
        out_specs=[
            pl.BlockSpec(memory_space=pltpu.HBM if i in stored else pltpu.VMEM)
            for i in range(n_out)
        ],
        scratch_shapes=[pltpu.SemaphoreType.DMA((max(1, n_sems),))]
        + [pltpu.VMEM(leaves[i].shape, leaves[i].dtype) for i in far]
        + list(scratch),
        compiler_params=pltpu.CompilerParams(vmem_limit_bytes=VMEM_LIMIT),
        cost_estimate=pl.CostEstimate(flops=flops, bytes_accessed=size, transcendentals=0),
    )(*leaves)
    return jax.tree.unflatten(out_tree, given)


def chunks(count):
    each = count // PARTS
    return [pl.ds(p * each, each) for p in range(PARTS)]


def far(tree):
    return jax.tree.map(Far, tree)


def fetch(tree):
    return jax.tree.map(lambda one: one.get(), tree, is_leaf=lambda one: isinstance(one, Arriving))


def loop(first, last, body):
    lax.fori_loop(first, last, body, 0, unroll=UNROLL)


def shaped(*shape):
    return jax.ShapeDtypeStruct(shape, F32)


def face_shapes(shape, sizes, count, width):
    nx, ny, nz = shape
    blocks = count * width + (1 if width == 2 else 0)
    outs = {
        "x": {r: shaped(blocks, ny, nz) for r in rounds_of(sizes[0])},
        "y": {r: shaped(blocks, nx, nz) for r in rounds_of(sizes[1])},
    }
    if width == 2:
        outs["xy"] = {
            (rx, ry): shaped(4 * count + 4, nz)
            for rx in rounds_of(sizes[0])
            for ry in rounds_of(sizes[1])
        }
    return outs


def pack_faces(out, fields, sizes, width, ends=None):
    ix, iy, _ = where_am_i()
    for r, ref in out["x"].items():
        pack_x(ref, fields, r, ix, width, ends)
    for r, ref in out["y"].items():
        pack_y(ref, fields, r, iy, width, ends)
    for (rx, ry), ref in out.get("xy", {}).items():
        pack_xy(ref, fields, rx, ry, ix, iy, ends)


def send_z(tile, sizes):
    return {r: swap(tile, sizes, {2: r}) for r in rounds_of(sizes[2])}


def send_faces(faces, sizes):
    got = {
        "x": {r: swap(v, sizes, {0: r}) for r, v in faces["x"].items()},
        "y": {r: swap(v, sizes, {1: r}) for r, v in faces["y"].items()},
    }
    if "xy" in faces:
        got["xy"] = {(rx, ry): swap(v, sizes, {0: rx, 1: ry}) for (rx, ry), v in faces["xy"].items()}
    return got


def spread(rows):
    return lax.all_to_all(rows, AXES, 0, 0, tiled=True)


def shards(sizes, right_side, conductance, storage, dirichlet, basis, coarse_inverse):
    shape = right_side.shape
    nx, ny, nz = shape
    vecs = basis.shape[0]
    boxed = box_shape(shape)
    devices = sizes[0] * sizes[1] * sizes[2]
    row_shape = shaped(devices, LANES)
    sum_shape = (devices * vecs // LANES, LANES)
    ends_shape = (nx, ny, LANES)
    box = shaped(*boxed)
    vbox = pltpu.VMEM(boxed, F32)
    inputs = (Far(conductance), Far(storage), Far(dirichlet), Far(right_side))

    def six(cond, store, fixed, rhs, free):
        cond, store, fixed, rhs = fetch((cond, store, fixed, rhs))
        free[...] = 1.0 - fixed[...].astype(F32)
        return [cond.at[0], cond.at[1], cond.at[2], store, free, rhs]

    def pack_first(cond, store, fixed, rhs, out, free):
        out[...] = pack_z(six(cond, store, fixed, rhs, free))

    tile = call(pack_first, shaped(z_rows(6), nx * ny), inputs, [pltpu.VMEM(shape, F32)])
    got_z = send_z(tile, sizes)

    def first_rows(rhs, base, out):
        row = project(base, rhs.get()[...])
        out[...] = jnp.broadcast_to(row, out.shape)

    rows = call(first_rows, row_shape, (Far(right_side), Far(basis, True)))
    rows_a = spread(rows)

    def pack_all(got_z, cond, store, fixed, rhs, rows, outs, free, ends):
        fields = six(cond, store, fixed, rhs, free)
        ends[...] = pick_z(fetch(got_z), sizes, ends_shape)
        outs["ends"].put(ends)
        pack_faces(outs["faces"], fields, sizes, 2, ends)

    packed = call(
        pack_all,
        {"ends": Stored(*ends_shape), "faces": face_shapes(shape, sizes, 6, 2)},
        (got_z,) + inputs + (rows,),
        [pltpu.VMEM(shape, F32), pltpu.VMEM(ends_shape, F32)],
    )
    got = send_faces(packed["faces"], sizes)

    def first_smooth(got, cond, store, fixed, rhs, ends, outs, free, *work):
        ga, gb, source, step = work[:4]
        boxes = list(work[4:])
        for b in boxes:
            clear(b)
        owns = six(cond, store, fixed, rhs, free)
        got = fetch(got)
        unpack_faces(boxes, owns, got["x"], got["y"], sizes, 2, ends.get()[...])
        unpack_xy(boxes, shape, got["xy"], sizes)
        links = outs["links"]
        coefficients(boxes, links, outs["diag"], step)
        for name, value in (("diag", outs["diag"]), ("step", step)):
            outs["kept"][name].put(value)
        for kept, link in zip(outs["kept"]["links"], links):
            kept.put(link)
        jacobi(boxes[-1], step, links, ga, gb, source, outs["smooth"])

    smoothed = call(
        first_smooth,
        {
            "smooth": shaped(*shape),
            "links": [box, box, box],
            "diag": box,
            "kept": {
                "links": [Stored(*boxed), Stored(*boxed), Stored(*boxed)],
                "diag": Stored(*boxed),
                "step": Stored(*boxed),
            },
        },
        (far(got),) + inputs + (Far(packed["ends"]),),
        [pltpu.VMEM(shape, F32)] + [vbox] * 10,
        flops=SMOOTH_FLOPS,
    )
    kept = smoothed["kept"]
    links, diag = smoothed["links"], smoothed["diag"]

    def first_direction(smooth, rows, inverse, base, outs):
        smooth, rows = fetch((smooth, rows))
        weights = coarse_weights(inverse.get(), coarse_sum(rows, vecs))
        add_coarse(outs["z"], smooth, base.get(), weights)
        outs["kept"].put(outs["z"])
        pack_faces(outs["faces"], [outs["z"]], sizes, 1)
        outs["tile"][...] = pack_z([outs["z"]])

    directed = call(
        first_direction,
        {
            "z": shaped(*shape),
            "kept": Stored(*shape),
            "faces": face_shapes(shape, sizes, 1, 1),
            "tile": shaped(z_rows(1), nx * ny),
        },
        (smoothed["smooth"], rows_a, Far(coarse_inverse), Far(basis)),
    )
    direction, kept_z = directed["z"], directed["kept"]
    got = send_faces(directed["faces"], sizes)
    got_z = send_z(directed["tile"], sizes)

    def apply(field, got, got_z, links, diag, out, vb):
        clear(vb)
        field, got, got_z = fetch((field, got, got_z))
        unpack_faces([vb], [field], got["x"], got["y"], sizes, 1)
        vb[3 : 3 + nx, 0:ny, nz : nz + LANES] = halo_lanes(pick_z(got_z, sizes, ends_shape), 0)
        links, diag = fetch((links, diag))

        def body(x, carry):
            whole = diag[x + 3] * vb[x + 3] - neighbours(vb, links, x + 3)
            out[x] = whole[0:ny, 0:nz]
            return carry

        loop(0, nx, body)

    def first_image(got, got_z, field, links, diag, rhs, outs, vb):
        image = outs["image"]
        apply(field, got, got_z, links, diag, image, vb)
        outs["kept"].put(image)
        outs["tile"][...] = pack_z([image])
        field, rhs = fetch((field, rhs))
        values = [full_sum(rhs[...] * field[...]), full_sum(field[...] * image[...])]
        outs["sums"][...] = put_scalars(jnp.zeros((1, LANES), F32), vecs, values)

    imaged = call(
        first_image,
        {
            "image": shaped(*shape),
            "kept": Stored(*shape),
            "tile": shaped(z_rows(1), nx * ny),
            "sums": shaped(1, LANES),
        },
        (far(got), got_z, direction, links, diag, Far(right_side)),
        [vbox],
    )
    got_z = send_z(imaged["tile"], sizes)

    def second_rows(base, field, sums, out):
        row = project(base, field.get()[...]) + sums.get()[...]
        out[...] = jnp.broadcast_to(row, out.shape)

    rows = call(second_rows, row_shape, (Far(basis, True), imaged["image"], imaged["sums"]))
    rows_c = spread(rows)

    def pack_image(got_z, field, rows, outs, ends):
        ends[...] = pick_z(fetch(got_z), sizes, ends_shape)
        outs["ends"].put(ends)
        pack_faces(outs["faces"], [field.get()], sizes, 2, ends)

    packed = call(
        pack_image,
        {"ends": Stored(*ends_shape), "faces": face_shapes(shape, sizes, 1, 2)},
        (got_z, imaged["image"], rows),
        [pltpu.VMEM(ends_shape, F32)],
    )
    got = send_faces(packed["faces"], sizes)

    def second_smooth(got, field, step, links, ends, out, *work):
        ga, gb, source, vb = work
        clear(vb)
        field, got, ends = fetch((field, got, ends))
        unpack_faces([vb], [field], got["x"], got["y"], sizes, 2, ends[...])
        unpack_xy([vb], shape, got["xy"], sizes)
        step, links = fetch((step, links))
        jacobi(vb, step, links, ga, gb, source, out)

    smooth = call(
        second_smooth,
        shaped(*shape),
        (far(got), Far(imaged["kept"]), Far(kept["step"]), far(kept["links"]), Far(packed["ends"])),
        [vbox] * 4,
        flops=SMOOTH_FLOPS,
    )

    def second_direction(smooth, rows, inverse, field, rhs, before, base, outs):
        smooth, rows = fetch((smooth, rows))
        norm, curve = scalar_sums(rows, vecs, 2)
        alpha = norm / curve
        weights = coarse_weights(inverse.get(), coarse_sum(rows, vecs))
        field, rhs, before = fetch((field, rhs, before))
        outs["residual"][...] = rhs[...] - alpha * field[...]
        add_coarse(outs["z"], smooth, base.get(), weights)
        outs["z"][...] = before[...] - alpha * outs["z"][...]
        pack_faces(outs["faces"], [outs["z"]], sizes, 1)
        outs["tile"][...] = pack_z([outs["z"]])
        outs["scalars"][...] = jnp.concatenate(
            [jnp.broadcast_to(norm, (8, LANES)), jnp.broadcast_to(curve, (8, LANES))], axis=0
        )

    directed = call(
        second_direction,
        {
            "z": shaped(*shape),
            "residual": shaped(*shape),
            "scalars": shaped(16, LANES),
            "faces": face_shapes(shape, sizes, 1, 1),
            "tile": shaped(z_rows(1), nx * ny),
        },
        (
            smooth,
            rows_c,
            Far(coarse_inverse),
            Far(imaged["kept"]),
            Far(right_side),
            Far(kept_z),
            Far(basis),
        ),
    )
    precond, residual = directed["z"], directed["residual"]
    got = send_faces(directed["faces"], sizes)
    got_z = send_z(directed["tile"], sizes)
    image, direction = Far(imaged["kept"]), Far(kept_z)

    def second_image(got, got_z, field, links, diag, image, residual, outs, vb):
        apply(field, got, got_z, links, diag, outs["image"], vb)
        field, image, residual = fetch((field, image, residual))
        values = [
            full_sum(residual[...] * field[...]),
            full_sum(field[...] * outs["image"][...]),
            full_sum(field[...] * image[...]),
        ]
        row = put_scalars(jnp.zeros((1, LANES), F32), 0, values)
        outs["rows"][...] = jnp.broadcast_to(row, outs["rows"].shape)

    last = call(
        second_image,
        {"image": shaped(*shape), "rows": row_shape},
        (
            far(got),
            got_z,
            precond,
            far(kept["links"]),
            Far(kept["diag"]),
            image,
            residual,
        ),
        [vbox],
    )
    rows_e = spread(last["rows"])

    def finish(rows, scalars, direction, image, precond, precond_image, residual, outs):
        rows, scalars = fetch((rows, scalars))
        norm = scalars[0:1, 0:1]
        curve = scalars[8:9, 0:1]
        norm_next, curve_z, curve_mixed = scalar_sums(rows, 0, 3)
        alpha = norm / curve
        beta = norm_next / norm
        curve_next = curve_z + 2.0 * beta * curve_mixed + beta * beta * curve
        alpha_next = norm_next / curve_next
        direction, image, precond = fetch((direction, image, precond))
        precond_image, residual = fetch((precond_image, residual))
        outs[0][...] = alpha * direction[...] + alpha_next * (
            precond[...] + beta * direction[...]
        )
        outs[1][...] = residual[...] - alpha_next * (precond_image[...] + beta * image[...])

    return tuple(
        call(
            finish,
            [shaped(*shape), shaped(*shape)],
            (rows_e, directed["scalars"], direction, image, precond, last["image"], residual),
        )
    )


def solution(mesh):
    sizes = tuple(mesh.shape[a] for a in AXES)
    placed = (
        P("gx", "gy", "gz"),
        P(None, "gx", "gy", "gz"),
        P("gx", "gy", "gz"),
        P("gx", "gy", "gz"),
        P(None, "gx", "gy", "gz"),
        P(("gx", "gy", "gz"), None),
    )
    return jax.shard_map(
        functools.partial(shards, sizes),
        mesh=mesh,
        in_specs=placed,
        out_specs=(P("gx", "gy", "gz"), P("gx", "gy", "gz")),
        check_vma=False,
    )
```

time: 128 us -> 88.3 us (0.69)
  local copies, waits for them, and re-layouts: 33.3 us -> 3.22 us
  waiting for transfers between devices: 16.4 us -> 5.55 us
  Pallas kernels: 29 us -> 36.1 us
  starting transfers between devices: 33.5 us -> 30.7 us
  blocking collectives: 13.7 us -> 11.2 us
    unnamed x92 -> x32, local copies, waits for them, and re-layouts: 33.3 us -> 3.22 us
    ppermute x24, waiting for transfers between devices: 16.4 us -> 4.04 us  [swap(): return lax.ppermute(value, AXES, pairs)]
    pallas_call x8 -> x12, Pallas kernels: 29 us -> 36.1 us  [call(): pl.pallas_call(body, out_shape=[pltpu.HBM(a.shape, F32) if isinstance(a,...]
    all_to_all x2, starting transfers between devices: 11.5 us -> 6.6 us  [spread(): return lax.all_to_all(rows, AXES, 0, 0, tiled=True)]
    all_to_all x1, blocking collectives: 13.7 us -> 11.2 us  [spread(): return lax.all_to_all(rows, AXES, 0, 0, tiled=True)]
    ppermute x24, starting transfers between devices: 22 us -> 24.1 us  [swap(): return lax.ppermute(value, AXES, pairs)]
    all_to_all x2, waiting for transfers between devices: 0.01 us -> 1.51 us  [spread(): return lax.all_to_all(rows, AXES, 0, 0, tiled=True)]
  transfers between devices with their start and end apart: 26 -> 26, of which waited for: 7 -> 4; matrix products, arithmetic and copies ran while one was open for 0% -> 0% of each run, Pallas kernels for 0% -> 19%
where the time goes in v2:
time: 88.3 us; the launch traced here: 87.7 us
  Pallas kernels  36.1 us (41%)
  starting transfers between devices  30.7 us (35%)
  blocking collectives  11.2 us (13%)
  waiting for transfers between devices  5.55 us (6%)
  local copies, waits for them, and re-layouts  3.22 us (4%)
  between operations  0.98 us (1%)
    pallas_call x12, Pallas kernels, call(): pl.pallas_call(body, out_shape=[pltpu.HBM(a.shape, F32) if isinstance(a,...  36.1 us
    ppermute x24, starting transfers between devices, swap(): return lax.ppermute(value, AXES, pairs)  24.1 us
    all_to_all x1, blocking collectives, spread(): return lax.all_to_all(rows, AXES, 0, 0, tiled=True)  11.2 us
    all_to_all x2, starting transfers between devices, spread(): return lax.all_to_all(rows, AXES, 0, 0, tiled=True)  6.6 us
    ppermute x24, waiting for transfers between devices, swap(): return lax.ppermute(value, AXES, pairs)  4.04 us
    unnamed x32, local copies, waits for them, and re-layouts  3.22 us
  transfers between devices with their start and end apart: 26, of which 4 were waited for; matrix products, arithmetic and copies ran while one was open for 0% of the time, Pallas kernels for 19%

profile of v2, /device:TPU:0, one launch (start us, length us, event | category | flops | bytes accessed | tf_op | source)
XLA Modules:
  0.0 87.7 jit_solution(11085303244042514053)
XLA Ops:
  0.6 1.7 %shard_map.77 = f32[24,256]{1,0:T(8,128)S(1)} custom-call(f32[3,16,16,256]{3,2,1,0:T(8,128)} %refs_5_.3, f32[16,16,256]{2,1,0:T(8,128)} %refs_6_.2, s32[16,16,256]{2,1,0:T(8,128)} %refs_7_.1, f32[16,16,256]{2,1,0:T(8,128)} %refs_4_.3), custom_call_target="tpu_custom_call" | custom-call | bytes 1597440 | tf_op jit(solution)/shard_map/pallas_call | solution.py:450
  2.3 2.4 %collective-permute-start.1 = (f32[24,256]{1,0:T(8,128)S(1)}, f32[24,256]{1,0:T(8,128)S(1)}, u32[]{:S(2)}, u32[]{:S(2)}) collective-permute-start(f32[24,256]{1,0:T(8,128)S(1)} %shard_map.77), channel_id=1, source_target_pairs={{0,3},{1,2},{2,1},{3,0},{4,7},{5,6},{6,5},{7,4},{8,11},{9,10},{10,... | collective-permute-start | bytes 73736 | tf_op jit(solution)/shard_map/ppermute | solution.py:52
  4.8 0.7 collective-permute-start
  5.5 3.1 %shard_map.78.refs_6_ = f32[32,128]{1,0:T(8,128)} custom-call(f32[16,16,256]{2,1,0:T(8,128)} %refs_4_.3, f32[16,16,16,256]{3,2,1,0:T(8,128)} %refs_6_.3), custom_call_target="tpu_custom_call" | custom-call | bytes 4472832 | tf_op jit(solution)/shard_map/pallas_call | solution.py:450
  8.6 2.9 %shard_map.79 = (f32[16,16,128]{2,1,0:T(8,128)}, f32[13,16,256]{2,1,0:T(8,128)S(1)}, f32[28,256]{1,0:T(8,128)S(1)}, f32[28,256]{1,0:T(8,128)S(1)}, f32[13,16,256...) custom-call(f32[24,256]{1,0:T(8,128)S(1)} %collective-permute-done.refs_0_, f32[24,256]{1,0:T(8,128)S(1)} %collective-permute-done.1.refs_1_, ...), custom_call_target="tpu_custom_call" | custom-call | bytes 2465792 | tf_op jit(solution)/shard_map/pallas_call | solution.py:450
  11.4 1.6 %collective-permute-start.2 = (f32[13,16,256]{2,1,0:T(8,128)S(1)}, f32[13,16,256]{2,1,0:T(8,128)S(1)}, u32[]{:S(2)}, u32[]{:S(2)}) collective-permute-start(f32[13,16,256]{2,1,0:T(8,128)S(1)} %get-tuple-element.43), channel_id=1, source_target_pairs={{0,16},{1,17},{2,18},{3,19},{4,20},{5,21},{6,22},{7,23},{8,24},{9,... | collective-permute-start | bytes 638984 | tf_op jit(solution)/shard_map/ppermute | solution.py:52
  13.0 1.6 %collective-permute-start.5 = (f32[13,16,256]{2,1,0:T(8,128)S(1)}, f32[13,16,256]{2,1,0:T(8,128)S(1)}, u32[]{:S(2)}, u32[]{:S(2)}) collective-permute-start(f32[13,16,256]{2,1,0:T(8,128)S(1)} %get-tuple-element.46), channel_id=1, source_target_pairs={{0,4},{1,5},{2,6},{3,7},{4,0},{5,1},{6,2},{7,3},{8,12},{9,13},{10,... | collective-permute-start | bytes 638984 | tf_op jit(solution)/shard_map/ppermute | solution.py:52
  14.6 3.1 %collective-permute-start.3 = (f32[28,256]{1,0:T(8,128)S(1)}, f32[28,256]{1,0:T(8,128)S(1)}, u32[]{:S(2)}, u32[]{:S(2)}) collective-permute-start(f32[28,256]{1,0:T(8,128)S(1)} %get-tuple-element.44), channel_id=1, source_target_pairs={{0,20},{1,21},{2,22},{3,23},{4,16},{5,17},{6,18},{7,19},{8,28},{9,... | collective-permute-start | bytes 86024 | tf_op jit(solution)/shard_map/ppermute | solution.py:52
  17.7 2.8 %all-to-all-start = ((f32[32,1,128]{2,1,0:T(1,128)}), f32[32,1,128]{2,1,0:T(1,128)S(1)}, u32[]{:S(2)}, u32[]{:S(2)}) async-start(f32[32,1,128]{2,1,0:T(1,128)} %bitcast.1), calls=%async_computation | async-start | bytes 32768 | tf_op jit(solution)/shard_map/all_to_all | solution.py:534
  20.5 0.1 collective-permute-done.3.refs_1_
  20.6 0.6 copy-done.15
  21.2 0.1 copy-done.11
  21.3 0.1 copy-done.12
  21.3 0.7 copy-done.13
  22.0 5.7 %shard_map.80 = (f32[22,24,384]{2,1,0:T(8,128)S(1)}, f32[22,24,384]{2,1,0:T(8,128)}, f32[22,24,384]{2,1,0:T(8,128)}, f32[22,24,384]{2,1,0:T(8,128)}, f32[22,24,3...) custom-call(f32[13,16,256]{2,1,0:T(8,128)} %copy-done.11, ...), custom_call_target="tpu_custom_call" | custom-call | flops 1000000000 | bytes 9961472 | tf_op jit(solution)/shard_map/pallas_call | solution.py:450
  27.8 3.3 %shard_map.81 = (f32[1,16,256]{2,1,0:T(8,128)S(1)}, f32[1,16,256]{2,1,0:T(8,128)S(1)}, f32[1,16,256]{2,1,0:T(8,128)S(1)}, f32[16,16,256]{2,1,0:T(8,128)}, f32[8,...) custom-call(f32[16,16,256]{2,1,0:T(8,128)S(1)} %get-tuple-element.49.refs_0_, f32[32,128]{1,0:T(8,128)S(1)} %bitcast.12, ...), custom_call_target="tpu_custom_call" | custom-call | bytes 5087232 | tf_op jit(solution)/shard_map/pallas_call | solution.py:450
  31.1 1.8 %collective-permute-start.7 = (f32[1,16,256]{2,1,0:T(8,128)S(1)}, f32[1,16,256]{2,1,0:T(8,128)S(1)}, u32[]{:S(2)}, u32[]{:S(2)}) collective-permute-start(f32[1,16,256]{2,1,0:T(8,128)S(1)} %get-tuple-element.50), channel_id=1, source_target_pairs={{0,16},{1,17},{2,18},{3,19},{4,20},{5,21},{6,22},{7,23},{8,24},{9,... | collective-permute-start | bytes 49160 | tf_op jit(solution)/shard_map/ppermute | solution.py:52
  32.9 2.7 %collective-permute-start.8 = (f32[1,16,256]{2,1,0:T(8,128)S(1)}, f32[1,16,256]{2,1,0:T(8,128)S(1)}, u32[]{:S(2)}, u32[]{:S(2)}) collective-permute-start(f32[1,16,256]{2,1,0:T(8,128)S(1)} %get-tuple-element.51), channel_id=1, source_target_pairs={{0,4},{1,5},{2,6},{3,7},{4,0},{5,1},{6,2},{7,3},{8,12},{9,13},{10,... | collective-permute-start | bytes 49160 | tf_op jit(solution)/shard_map/ppermute | solution.py:52
  35.6 0.6 collective-permute-start.11
  36.2 2.4 %collective-permute-done.11.refs_4_ = f32[8,256]{1,0:T(8,128)S(1)} collective-permute-done((f32[8,256]{1,0:T(8,128)S(1)}, f32[8,256]{1,0:T(8,128)S(1)}, u32[]{:S(2)}, u32[]{:S(2)}) %collective-permute-start.11) | collective-permute-done | bytes 8224 | tf_op jit(solution)/shard_map/ppermute | solution.py:52
  38.7 0.6 copy-done.3
  39.3 0.0 copy-done.5
  39.3 0.0 copy-done.7
  39.3 2.3 %shard_map.82 = (f32[16,16,256]{2,1,0:T(8,128)S(1)}, f32[16,16,256]{2,1,0:T(8,128)}, f32[1,128]{1,0:T(1,128)S(1)}, f32[8,256]{1,0:T(8,128)S(1)}) custom-call(f32[1,16,256]{2,1,0:T(8,128)} %copy-done.3, f32[1,16,256]{2,1,0:T(8,128)} %copy-done.5, f32[1,16,256]{2,1,0:T(8,128)} %copy-done.7, f32[8,256]{1,0:T(8,128)S(1)} %collective-permute-done.10.refs_3_, ...), custom_call_target="tpu_custom_call" | custom-call | bytes 4366848 | tf_op jit(solution)/shard_map/pallas_call | solution.py:450
  41.6 0.7 collective-permute-start.13
  42.3 3.0 %shard_map.83.refs_3_ = f32[32,128]{1,0:T(8,128)} custom-call(f32[16,16,16,256]{3,2,1,0:T(8,128)} %refs_6_.3, f32[16,16,256]{2,1,0:T(8,128)S(1)} %get-tuple-element.60.refs_1_.refs_2_, f32[1,128]{1,0:T(1,128)S(1)} %get-tuple-element.61.refs_2_), custom_call_target="tpu_custom_call" | custom-call | bytes 4473344 | tf_op jit(solution)/shard_map/pallas_call | solution.py:450
  45.4 1.5 %shard_map.84 = (f32[16,16,128]{2,1,0:T(8,128)}, f32[3,16,256]{2,1,0:T(8,128)S(1)}, f32[8,256]{1,0:T(8,128)S(1)}, f32[8,256]{1,0:T(8,128)S(1)}, f32[3,16,256]{2,1,0:T(8,128)S(1)}, /*index=5*/f32[3,16,256]{2,1,0:T(8,128)S(1)}) custom-call(f32[8,256]{1,0:T(8,128)S(1)} %collective-permute-done.12.refs_0_, f32[8,256]{1,0:T(8,128)S(1)} %collective-permute-done.13.refs_1_, ...), custom_call_target="tpu_custom_call" | custom-call | bytes 589824 | tf_op jit(solution)/shard_map/pallas_call | solution.py:450
  46.9 0.5 collective-permute-start.14
  47.4 2.8 %collective-permute-start.17 = (f32[3,16,256]{2,1,0:T(8,128)S(1)}, f32[3,16,256]{2,1,0:T(8,128)S(1)}, u32[]{:S(2)}, u32[]{:S(2)}) collective-permute-start(f32[3,16,256]{2,1,0:T(8,128)S(1)} %get-tuple-element.65), channel_id=1, source_target_pairs={{0,4},{1,5},{2,6},{3,7},{4,0},{5,1},{6,2},{7,3},{8,12},{9,13},{10,... | collective-permute-start | bytes 147464 | tf_op jit(solution)/shard_map/ppermute | solution.py:52
  50.2 2.0 %collective-permute-start.15 = (f32[8,256]{1,0:T(8,128)S(1)}, f32[8,256]{1,0:T(8,128)S(1)}, u32[]{:S(2)}, u32[]{:S(2)}) collective-permute-start(f32[8,256]{1,0:T(8,128)S(1)} %get-tuple-element.63), channel_id=1, source_target_pairs={{0,20},{1,21},{2,22},{3,23},{4,16},{5,17},{6,18},{7,19},{8,28},{9,... | collective-permute-start | bytes 24584 | tf_op jit(solution)/shard_map/ppermute | solution.py:52
  52.2 3.8 %all-to-all-start.1 = ((f32[32,1,128]{2,1,0:T(1,128)}), f32[32,1,128]{2,1,0:T(1,128)S(1)}, u32[]{:S(2)}, u32[]{:S(2)}) async-start(f32[32,1,128]{2,1,0:T(1,128)} %bitcast.4), calls=%async_computation.1 | async-start | bytes 32768 | tf_op jit(solution)/shard_map/all_to_all | solution.py:534
  56.1 0.5 copy-done.9
  56.6 0.0 copy-done.10
  56.6 0.0 copy-done
  56.7 0.0 copy-done.2
  56.7 4.9 %shard_map.85.refs_0_ = f32[16,16,256]{2,1,0:T(8,128)S(1)} custom-call(f32[3,16,256]{2,1,0:T(8,128)} %copy-done, f32[8,256]{1,0:T(8,128)} %copy-done.9, f32[8,256]{1,0:T(8,128)} %copy-done.10, f32[3,16,256]{2,1,0:T(8,128)} %copy-done.1, f32[3,16,256]{2,1,0:T(8,128)} %copy-done.2, f32[16,16,256]{2,1,0:T(8,128)} %get-tuple-element.67.refs_5_.refs_3_.refs_10_, ...), custom_call_target="tpu_custom_call" | custom-call | flops 1000000000 | bytes 4063232 | tf_op jit(solution)/shard_map/pallas_call | solution.py:450
  61.7 1.5 %all-to-all-done.1 = f32[32,1,128]{2,1,0:T(1,128)S(1)} async-done(((f32[32,1,128]{2,1,0:T(1,128)}), f32[32,1,128]{2,1,0:T(1,128)S(1)}, u32[]{:S(2)}, u32[]{:S(2)}) %all-to-all-start.1) | async-done | bytes 16416 | tf_op jit(solution)/shard_map/all_to_all | solution.py:534
  63.2 3.0 %shard_map.86 = (f32[1,16,256]{2,1,0:T(8,128)S(1)}, f32[1,16,256]{2,1,0:T(8,128)S(1)}, f32[1,16,256]{2,1,0:T(8,128)S(1)}, f32[16,16,256]{2,1,0:T(8,128)S(1)}, f3...) custom-call(f32[16,16,256]{2,1,0:T(8,128)S(1)} %shard_map.85.refs_0_, ...), custom_call_target="tpu_custom_call" | custom-call | bytes 5881856 | tf_op jit(solution)/shard_map/pallas_call | solution.py:450
  66.2 0.7 collective-permute-start.19
  66.9 1.3 %collective-permute-start.20 = (f32[1,16,256]{2,1,0:T(8,128)S(1)}, f32[1,16,256]{2,1,0:T(8,128)S(1)}, u32[]{:S(2)}, u32[]{:S(2)}) collective-permute-start(f32[1,16,256]{2,1,0:T(8,128)S(1)} %get-tuple-element.75), channel_id=1, source_target_pairs={{0,4},{1,5},{2,6},{3,7},{4,0},{5,1},{6,2},{7,3},{8,12},{9,13},{10,... | collective-permute-start | bytes 49160 | tf_op jit(solution)/shard_map/ppermute | solution.py:52
  68.2 1.6 %collective-permute-start.23 = (f32[8,256]{1,0:T(8,128)S(1)}, f32[8,256]{1,0:T(8,128)S(1)}, u32[]{:S(2)}, u32[]{:S(2)}) collective-permute-start(f32[8,256]{1,0:T(8,128)S(1)} %get-tuple-element.77), channel_id=1, source_target_pairs={{0,3},{1,2},{2,1},{3,0},{4,7},{5,6},{6,5},{7,4},{8,11},{9,10},{10,... | collective-permute-start | bytes 24584 | tf_op jit(solution)/shard_map/ppermute | solution.py:52
  69.8 1.5 %collective-permute-done.23.refs_4_ = f32[8,256]{1,0:T(8,128)S(1)} collective-permute-done((f32[8,256]{1,0:T(8,128)S(1)}, f32[8,256]{1,0:T(8,128)S(1)}, u32[]{:S(2)}, u32[]{:S(2)}) %collective-permute-start.23) | collective-permute-done | bytes 8224 | tf_op jit(solution)/shard_map/ppermute | solution.py:52
  71.3 0.6 copy-done.4
  71.9 0.0 copy-done.6
  71.9 0.0 copy-done.8
  71.9 2.7 %shard_map.87 = (f32[16,16,256]{2,1,0:T(8,128)S(1)}, f32[32,128]{1,0:T(8,128)S(1)}) custom-call(f32[1,16,256]{2,1,0:T(8,128)} %copy-done.4, f32[1,16,256]{2,1,0:T(8,128)} %copy-done.6, f32[1,16,256]{2,1,0:T(8,128)} %copy-done.8, f32[8,256]{1,0:T(8,128)S(1)} %collective-permute-done.22.refs_3_, f32[8,256]{1,0:T(8,128)S(1)} %collective-permute-done.23.refs_4_, ...), custom_call_target="tpu_custom_call" | custom-call | bytes 4374528 | tf_op jit(solution)/shard_map/pallas_call | solution.py:450
  74.6 11.2 %all_to_all.33 = f32[32,1,128]{2,1,0:T(1,128)S(1)} all-to-all(f32[32,1,128]{2,1,0:T(1,128)S(1)} %bitcast.15), channel_id=1, replica_groups=mesh['gx'=2,'gy'=4,'gz'=4] {'gx','gy','gz'}, dimensions={0} | all-to-all | bytes 32768 | tf_op jit(solution)/shard_map/all_to_all | solution.py:534
  85.8 1.9 %shard_map.88 = (f32[16,16,256]{2,1,0:T(8,128)}, f32[16,16,256]{2,1,0:T(8,128)}) custom-call(f32[32,128]{1,0:T(8,128)S(1)} %bitcast.14, f32[16,128]{1,0:T(8,128)S(1)} %get-tuple-element.82.refs_1_, f32[16,16,256]{2,1,0:T(8,128)} %get-tuple-element.73.refs_5_.refs_2_, f32[16,16,256]{2,1,0:T(8,128)} %get-tuple-element.67.refs_5_.refs_3_.refs_10_, ...), custom_call_target="tpu_custom_call" | custom-call | bytes 1859584 | tf_op jit(solution)/shard_map/pallas_call | solution.py:450
  (49 shorter events, 0.1 us)
Async XLA Ops:
  2.3 6.2 %collective-permute-start.1 = (f32[24,256]{1,0:T(8,128)S(1)}, f32[24,256]{1,0:T(8,128)S(1)}, u32[]{:S(2)}, u32[]{:S(2)}) collective-permute-start(f32[24,256]{1,0:T(8,128)S(1)} %shard_map.77), channel_id=1, source_target_pairs={{0,3},{1,2},{2,1},{3,0},{4,7},{5,6},{6,5},{7,4},{8,11},{9,10},{10,... | collective-permute-start | bytes 73736 | tf_op jit(solution)/shard_map/ppermute | solution.py:52
  4.8 3.8 %collective-permute-start = (f32[24,256]{1,0:T(8,128)S(1)}, f32[24,256]{1,0:T(8,128)S(1)}, u32[]{:S(2)}, u32[]{:S(2)}) collective-permute-start(f32[24,256]{1,0:T(8,128)S(1)} %shard_map.77), channel_id=1, source_target_pairs={{0,1},{1,0},{2,3},{3,2},{4,5},{5,4},{6,7},{7,6},{8,9},{9,8},{10,11... | collective-permute-start | bytes 73736 | tf_op jit(solution)/shard_map/ppermute | solution.py:52
  11.4 9.1 %collective-permute-start.2 = (f32[13,16,256]{2,1,0:T(8,128)S(1)}, f32[13,16,256]{2,1,0:T(8,128)S(1)}, u32[]{:S(2)}, u32[]{:S(2)}) collective-permute-start(f32[13,16,256]{2,1,0:T(8,128)S(1)} %get-tuple-element.43), channel_id=1, source_target_pairs={{0,16},{1,17},{2,18},{3,19},{4,20},{5,21},{6,22},{7,23},{8,24},{9,... | collective-permute-start | bytes 638984 | tf_op jit(solution)/shard_map/ppermute | solution.py:52
  13.0 7.6 %collective-permute-start.5 = (f32[13,16,256]{2,1,0:T(8,128)S(1)}, f32[13,16,256]{2,1,0:T(8,128)S(1)}, u32[]{:S(2)}, u32[]{:S(2)}) collective-permute-start(f32[13,16,256]{2,1,0:T(8,128)S(1)} %get-tuple-element.46), channel_id=1, source_target_pairs={{0,4},{1,5},{2,6},{3,7},{4,0},{5,1},{6,2},{7,3},{8,12},{9,13},{10,... | collective-permute-start | bytes 638984 | tf_op jit(solution)/shard_map/ppermute | solution.py:52
  14.6 6.0 %collective-permute-start.6 = (f32[13,16,256]{2,1,0:T(8,128)S(1)}, f32[13,16,256]{2,1,0:T(8,128)S(1)}, u32[]{:S(2)}, u32[]{:S(2)}) collective-permute-start(f32[13,16,256]{2,1,0:T(8,128)S(1)} %get-tuple-element.47), channel_id=1, source_target_pairs={{0,1},{1,0},{2,3},{3,2},{4,8},{5,9},{6,10},{7,11},{8,4},{9,5},{10,... | collective-permute-start | bytes 638984 | tf_op jit(solution)/shard_map/ppermute | solution.py:52
  14.6 5.9 %collective-permute-start.3 = (f32[28,256]{1,0:T(8,128)S(1)}, f32[28,256]{1,0:T(8,128)S(1)}, u32[]{:S(2)}, u32[]{:S(2)}) collective-permute-start(f32[28,256]{1,0:T(8,128)S(1)} %get-tuple-element.44), channel_id=1, source_target_pairs={{0,20},{1,21},{2,22},{3,23},{4,16},{5,17},{6,18},{7,19},{8,28},{9,... | collective-permute-start | bytes 86024 | tf_op jit(solution)/shard_map/ppermute | solution.py:52
  17.7 2.9 %collective-permute-start.4 = (f32[28,256]{1,0:T(8,128)S(1)}, f32[28,256]{1,0:T(8,128)S(1)}, u32[]{:S(2)}, u32[]{:S(2)}) collective-permute-start(f32[28,256]{1,0:T(8,128)S(1)} %get-tuple-element.45), channel_id=1, source_target_pairs={{0,1},{1,0},{2,3},{3,2},{4,24},{5,25},{6,26},{7,27},{8,20},{9,21},... | collective-permute-start | bytes 86024 | tf_op jit(solution)/shard_map/ppermute | solution.py:52
  17.7 10.1 %all-to-all-start = ((f32[32,1,128]{2,1,0:T(1,128)}), f32[32,1,128]{2,1,0:T(1,128)S(1)}, u32[]{:S(2)}, u32[]{:S(2)}) async-start(f32[32,1,128]{2,1,0:T(1,128)} %bitcast.1), calls=%async_computation | async-start | bytes 32768 | tf_op jit(solution)/shard_map/all_to_all | solution.py:534
  20.6 1.5 %copy-start.14 = (f32[28,256]{1,0:T(8,128)}, f32[28,256]{1,0:T(8,128)S(1)}, u32[]{:S(2)}) copy-start(f32[28,256]{1,0:T(8,128)S(1)} %collective-permute-done.3.refs_1_) | copy-start | bytes 86020
  20.6 0.6 copy-start.15
  20.6 0.7 copy-start.11
  20.6 0.7 copy-start.12
  21.3 0.7 copy-start.13
  31.1 7.6 %collective-permute-start.7 = (f32[1,16,256]{2,1,0:T(8,128)S(1)}, f32[1,16,256]{2,1,0:T(8,128)S(1)}, u32[]{:S(2)}, u32[]{:S(2)}) collective-permute-start(f32[1,16,256]{2,1,0:T(8,128)S(1)} %get-tuple-element.50), channel_id=1, source_target_pairs={{0,16},{1,17},{2,18},{3,19},{4,20},{5,21},{6,22},{7,23},{8,24},{9,... | collective-permute-start | bytes 49160 | tf_op jit(solution)/shard_map/ppermute | solution.py:52
  32.9 5.8 %collective-permute-start.8 = (f32[1,16,256]{2,1,0:T(8,128)S(1)}, f32[1,16,256]{2,1,0:T(8,128)S(1)}, u32[]{:S(2)}, u32[]{:S(2)}) collective-permute-start(f32[1,16,256]{2,1,0:T(8,128)S(1)} %get-tuple-element.51), channel_id=1, source_target_pairs={{0,4},{1,5},{2,6},{3,7},{4,0},{5,1},{6,2},{7,3},{8,12},{9,13},{10,... | collective-permute-start | bytes 49160 | tf_op jit(solution)/shard_map/ppermute | solution.py:52
  35.6 3.1 %collective-permute-start.9 = (f32[1,16,256]{2,1,0:T(8,128)S(1)}, f32[1,16,256]{2,1,0:T(8,128)S(1)}, u32[]{:S(2)}, u32[]{:S(2)}) collective-permute-start(f32[1,16,256]{2,1,0:T(8,128)S(1)} %get-tuple-element.52), channel_id=1, source_target_pairs={{0,1},{1,0},{2,3},{3,2},{4,8},{5,9},{6,10},{7,11},{8,4},{9,5},{10,... | collective-permute-start | bytes 49160 | tf_op jit(solution)/shard_map/ppermute | solution.py:52
  35.6 3.1 %collective-permute-start.11 = (f32[8,256]{1,0:T(8,128)S(1)}, f32[8,256]{1,0:T(8,128)S(1)}, u32[]{:S(2)}, u32[]{:S(2)}) collective-permute-start(f32[8,256]{1,0:T(8,128)S(1)} %get-tuple-element.53), channel_id=1, source_target_pairs={{0,3},{1,2},{2,1},{3,0},{4,7},{5,6},{6,5},{7,4},{8,11},{9,10},{10,... | collective-permute-start | bytes 24584 | tf_op jit(solution)/shard_map/ppermute | solution.py:52
  36.2 2.4 %collective-permute-start.10 = (f32[8,256]{1,0:T(8,128)S(1)}, f32[8,256]{1,0:T(8,128)S(1)}, u32[]{:S(2)}, u32[]{:S(2)}) collective-permute-start(f32[8,256]{1,0:T(8,128)S(1)} %get-tuple-element.53), channel_id=1, source_target_pairs={{0,1},{1,0},{2,3},{3,2},{4,5},{5,4},{6,7},{7,6},{8,9},{9,8},{10,11... | collective-permute-start | bytes 24584 | tf_op jit(solution)/shard_map/ppermute | solution.py:52
  38.7 0.6 copy-start.3
  38.7 0.6 copy-start.5
  38.7 0.6 copy-start.7
  41.6 3.7 %collective-permute-start.13 = (f32[8,256]{1,0:T(8,128)S(1)}, f32[8,256]{1,0:T(8,128)S(1)}, u32[]{:S(2)}, u32[]{:S(2)}) collective-permute-start(f32[8,256]{1,0:T(8,128)S(1)} %get-tuple-element.59), channel_id=1, source_target_pairs={{0,3},{1,2},{2,1},{3,0},{4,7},{5,6},{6,5},{7,4},{8,11},{9,10},{10,... | collective-permute-start | bytes 24584 | tf_op jit(solution)/shard_map/ppermute | solution.py:52
  42.3 3.0 %collective-permute-start.12 = (f32[8,256]{1,0:T(8,128)S(1)}, f32[8,256]{1,0:T(8,128)S(1)}, u32[]{:S(2)}, u32[]{:S(2)}) collective-permute-start(f32[8,256]{1,0:T(8,128)S(1)} %get-tuple-element.59), channel_id=1, source_target_pairs={{0,1},{1,0},{2,3},{3,2},{4,5},{5,4},{6,7},{7,6},{8,9},{9,8},{10,11... | collective-permute-start | bytes 24584 | tf_op jit(solution)/shard_map/ppermute | solution.py:52
  46.9 9.2 %collective-permute-start.14 = (f32[3,16,256]{2,1,0:T(8,128)S(1)}, f32[3,16,256]{2,1,0:T(8,128)S(1)}, u32[]{:S(2)}, u32[]{:S(2)}) collective-permute-start(f32[3,16,256]{2,1,0:T(8,128)S(1)} %get-tuple-element.62), channel_id=1, source_target_pairs={{0,16},{1,17},{2,18},{3,19},{4,20},{5,21},{6,22},{7,23},{8,24},{9,... | collective-permute-start | bytes 147464 | tf_op jit(solution)/shard_map/ppermute | solution.py:52
  47.4 8.7 %collective-permute-start.17 = (f32[3,16,256]{2,1,0:T(8,128)S(1)}, f32[3,16,256]{2,1,0:T(8,128)S(1)}, u32[]{:S(2)}, u32[]{:S(2)}) collective-permute-start(f32[3,16,256]{2,1,0:T(8,128)S(1)} %get-tuple-element.65), channel_id=1, source_target_pairs={{0,4},{1,5},{2,6},{3,7},{4,0},{5,1},{6,2},{7,3},{8,12},{9,13},{10,... | collective-permute-start | bytes 147464 | tf_op jit(solution)/shard_map/ppermute | solution.py:52
  50.2 5.9 %collective-permute-start.18 = (f32[3,16,256]{2,1,0:T(8,128)S(1)}, f32[3,16,256]{2,1,0:T(8,128)S(1)}, u32[]{:S(2)}, u32[]{:S(2)}) collective-permute-start(f32[3,16,256]{2,1,0:T(8,128)S(1)} %get-tuple-element.66), channel_id=1, source_target_pairs={{0,1},{1,0},{2,3},{3,2},{4,8},{5,9},{6,10},{7,11},{8,4},{9,5},{10,... | collective-permute-start | bytes 147464 | tf_op jit(solution)/shard_map/ppermute | solution.py:52
  50.2 5.8 %collective-permute-start.15 = (f32[8,256]{1,0:T(8,128)S(1)}, f32[8,256]{1,0:T(8,128)S(1)}, u32[]{:S(2)}, u32[]{:S(2)}) collective-permute-start(f32[8,256]{1,0:T(8,128)S(1)} %get-tuple-element.63), channel_id=1, source_target_pairs={{0,20},{1,21},{2,22},{3,23},{4,16},{5,17},{6,18},{7,19},{8,28},{9,... | collective-permute-start | bytes 24584 | tf_op jit(solution)/shard_map/ppermute | solution.py:52
  52.2 3.9 %collective-permute-start.16 = (f32[8,256]{1,0:T(8,128)S(1)}, f32[8,256]{1,0:T(8,128)S(1)}, u32[]{:S(2)}, u32[]{:S(2)}) collective-permute-start(f32[8,256]{1,0:T(8,128)S(1)} %get-tuple-element.64), channel_id=1, source_target_pairs={{0,1},{1,0},{2,3},{3,2},{4,24},{5,25},{6,26},{7,27},{8,20},{9,21},... | collective-permute-start | bytes 24584 | tf_op jit(solution)/shard_map/ppermute | solution.py:52
  52.2 11.0 %all-to-all-start.1 = ((f32[32,1,128]{2,1,0:T(1,128)}), f32[32,1,128]{2,1,0:T(1,128)S(1)}, u32[]{:S(2)}, u32[]{:S(2)}) async-start(f32[32,1,128]{2,1,0:T(1,128)} %bitcast.4), calls=%async_computation.1 | async-start | bytes 32768 | tf_op jit(solution)/shard_map/all_to_all | solution.py:534
  56.0 0.6 copy-start.9
  56.0 0.6 copy-start.10
  56.1 0.6 copy-start
  56.1 0.6 copy-start.1
  56.1 0.6 copy-start.2
  66.2 5.1 %collective-permute-start.19 = (f32[1,16,256]{2,1,0:T(8,128)S(1)}, f32[1,16,256]{2,1,0:T(8,128)S(1)}, u32[]{:S(2)}, u32[]{:S(2)}) collective-permute-start(f32[1,16,256]{2,1,0:T(8,128)S(1)} %get-tuple-element.74), channel_id=1, source_target_pairs={{0,16},{1,17},{2,18},{3,19},{4,20},{5,21},{6,22},{7,23},{8,24},{9,... | collective-permute-start | bytes 49160 | tf_op jit(solution)/shard_map/ppermute | solution.py:52
  66.9 4.4 %collective-permute-start.20 = (f32[1,16,256]{2,1,0:T(8,128)S(1)}, f32[1,16,256]{2,1,0:T(8,128)S(1)}, u32[]{:S(2)}, u32[]{:S(2)}) collective-permute-start(f32[1,16,256]{2,1,0:T(8,128)S(1)} %get-tuple-element.75), channel_id=1, source_target_pairs={{0,4},{1,5},{2,6},{3,7},{4,0},{5,1},{6,2},{7,3},{8,12},{9,13},{10,... | collective-permute-start | bytes 49160 | tf_op jit(solution)/shard_map/ppermute | solution.py:52
  68.2 3.1 %collective-permute-start.21 = (f32[1,16,256]{2,1,0:T(8,128)S(1)}, f32[1,16,256]{2,1,0:T(8,128)S(1)}, u32[]{:S(2)}, u32[]{:S(2)}) collective-permute-start(f32[1,16,256]{2,1,0:T(8,128)S(1)} %get-tuple-element.76), channel_id=1, source_target_pairs={{0,1},{1,0},{2,3},{3,2},{4,8},{5,9},{6,10},{7,11},{8,4},{9,5},{10,... | collective-permute-start | bytes 49160 | tf_op jit(solution)/shard_map/ppermute | solution.py:52
  68.2 3.1 %collective-permute-start.23 = (f32[8,256]{1,0:T(8,128)S(1)}, f32[8,256]{1,0:T(8,128)S(1)}, u32[]{:S(2)}, u32[]{:S(2)}) collective-permute-start(f32[8,256]{1,0:T(8,128)S(1)} %get-tuple-element.77), channel_id=1, source_target_pairs={{0,3},{1,2},{2,1},{3,0},{4,7},{5,6},{6,5},{7,4},{8,11},{9,10},{10,... | collective-permute-start | bytes 24584 | tf_op jit(solution)/shard_map/ppermute | solution.py:52
  69.8 1.5 %collective-permute-start.22 = (f32[8,256]{1,0:T(8,128)S(1)}, f32[8,256]{1,0:T(8,128)S(1)}, u32[]{:S(2)}, u32[]{:S(2)}) collective-permute-start(f32[8,256]{1,0:T(8,128)S(1)} %get-tuple-element.77), channel_id=1, source_target_pairs={{0,1},{1,0},{2,3},{3,2},{4,5},{5,4},{6,7},{7,6},{8,9},{9,8},{10,11... | collective-permute-start | bytes 24584 | tf_op jit(solution)/shard_map/ppermute | solution.py:52
  71.3 0.6 copy-start.4
  71.3 0.6 copy-start.6
  71.3 0.6 copy-start.8

commit v3 on v2

--- a/solution.py
+++ b/solution.py
@@ -163,6 +163,25 @@
     loop(0, box.shape[0], body)
 
 
+def clear_round(box, shape):
+    nx, ny, nz = shape
+    planes, rows, lanes = box.shape
+    for x in (0, 1, 2, planes - 3, planes - 2, planes - 1):
+        box[x] = jnp.zeros((rows, lanes), F32)
+
+    def body(x, carry):
+        box[x, ny:rows, :] = jnp.zeros((rows - ny, lanes), F32)
+        box[x, 0:ny, nz:lanes] = jnp.zeros((ny, lanes - nz), F32)
+        return carry
+
+    loop(3, 3 + nx, body)
+
+
+def own_cells(box, shape):
+    nx, ny, nz = shape
+    return box.at[3 : 3 + nx, 0:ny, 0:nz]
+
+
 def each_round(sizes, a, index, act):
     for r in rounds_of(sizes[a]):
         high = upward(index, r)
@@ -177,11 +196,12 @@
 
 
 def unpack_faces(boxes, owns, xs, ys, sizes, width, ends=None):
-    nx, ny, nz = owns[0].shape
+    nx, ny, nz = boxes[0].shape[0] - 6, boxes[0].shape[1] - 8, boxes[0].shape[2] - LANES
     count = len(boxes) * width
     ix, iy, _ = where_am_i()
     for k, (box, own) in enumerate(zip(boxes, owns)):
-        box[3 : 3 + nx, 0:ny, 0:nz] = own[...]
+        if own is not None:
+            box[3 : 3 + nx, 0:ny, 0:nz] = own[...]
         if ends is not None:
             box[3 : 3 + nx, 0:ny, nz : nz + LANES] = halo_lanes(ends, k)
 
@@ -271,33 +291,48 @@
     return total + z * ahead(mid, 1) + behind(z * mid, 1)
 
 
-def coefficients(fields, links, diag, step):
+def coefficients(fields, links, step, own):
     tx, ty, tz, store, free, _ = fields
     lx, ly, lz = links
+    _, nx, ny, nz = own.shape
     last = tx.shape[0] - 1
-    for ref in (lx, ly, lz, diag, step):
+    for ref in (lx, ly, lz, step):
         ref[0] = jnp.zeros(ref.shape[1:], F32)
         ref[last] = jnp.zeros(ref.shape[1:], F32)
 
-    def body(x, carry):
+    def body(x, carry, inside):
         f = free[x]
         a, b, c = tx[x], ty[x], tz[x]
         total = store[x] + a + tx[x - 1] + b + behind(b, 0) + c + behind(c, 1)
         d = f * total + (1.0 - f)
-        diag[x] = d
         step[x] = RELAX / d
-        lx[x] = a * f * free[x + 1]
-        ly[x] = b * f * ahead(f, 0)
-        lz[x] = c * f * ahead(f, 1)
+        links_here = (a * f * free[x + 1], b * f * ahead(f, 0), c * f * ahead(f, 1))
+        for ref, value in zip(links, links_here):
+            ref[x] = value
+        if inside:
+            x_link, y_link, z_link = links_here
+            mine = (
+                d,
+                x_link,
+                lx[x - 1],
+                y_link,
+                behind(y_link, 0),
+                z_link,
+                behind(z_link, 1),
+            )
+            for n, value in enumerate(mine):
+                own[n, x - 3] = value[0:ny, 0:nz]
         return carry
 
-    loop(1, last, body)
+    loop(1, 3, functools.partial(body, inside=False))
+    loop(3, 3 + nx, functools.partial(body, inside=True))
+    loop(3 + nx, last, functools.partial(body, inside=False))
 
 
 def jacobi(rhs, step, links, ga, gb, source, out):
     planes = rhs.shape[0]
     nx, ny, nz = out.shape
-    for g in (ga, gb, source):
+    for g in (ga, gb):
         g[0] = jnp.zeros(g.shape[1:], F32)
         g[planes - 1] = jnp.zeros(g.shape[1:], F32)
 
@@ -354,19 +389,25 @@
     return jnp.sum(total, axis=1, keepdims=True)
 
 
-def add_coarse(out, smooth, basis_ref, weights):
-    vecs, nx, ny, nz = basis_ref.shape
-    scale = [jnp.broadcast_to(weights[k : k + 1, 0:1], (8, LANES)) for k in range(vecs)]
-    scale = [jnp.tile(s, (ny // 8, nz // LANES)) for s in scale]
-
-    def body(x, carry):
-        total = smooth[x]
-        for k in range(vecs):
-            total = total + scale[k] * basis_ref[k, x]
-        out[x] = total
-        return carry
-
-    loop(0, nx, body)
+def add_coarse(out, smooth, basis, weights):
+    nx, ny, nz = out.shape
+    k = 0
+    for piece in basis:
+        vectors = piece.get()
+        count = vectors.shape[0]
+        scale = [jnp.broadcast_to(weights[k + i : k + i + 1, 0:1], (8, LANES)) for i in range(count)]
+        scale = [jnp.tile(s, (ny // 8, nz // LANES)) for s in scale]
+        source = smooth if k == 0 else out
+
+        def body(x, carry, vectors=vectors, scale=scale, source=source):
+            total = source[x]
+            for i, s in enumerate(scale):
+                total = total + s * vectors[i, x]
+            out[x] = total
+            return carry
+
+        loop(0, nx, body)
+        k += count
 
 
 def full_sum(value):
@@ -390,9 +431,13 @@
         self.value, self.parts = value, parts
 
 
+class Raw(Far):
+    pass
+
+
 class Stored:
-    def __init__(self, *shape):
-        self.shape = shape
+    def __init__(self, *shape, near=False):
+        self.shape, self.near = shape, near
 
 
 class Leaving:
@@ -402,13 +447,21 @@
     def put(self, source):
         self.copy = pltpu.make_async_copy(source, self.target, self.sem)
         self.copy.start()
+
+    def done(self):
+        if self.copy is not None:
+            self.copy.wait()
+            self.copy = None
+        return self.target
 
 
 def call(kernel, outs, args, scratch=(), flops=0):
     leaves, tree = jax.tree.flatten(list(args), is_leaf=lambda one: isinstance(one, Far))
     out_leaves, out_tree = jax.tree.flatten(outs, is_leaf=lambda one: isinstance(one, Stored))
     count, n_out = len(leaves), len(out_leaves)
-    far = [i for i, a in enumerate(leaves) if isinstance(a, Far)]
+    raw = [i for i, a in enumerate(leaves) if isinstance(a, Raw)]
+    far = [i for i, a in enumerate(leaves) if isinstance(a, Far) and i not in raw]
+    distant = [i for i, a in enumerate(out_leaves) if isinstance(a, Stored) and not a.near]
     stored = [i for i, a in enumerate(out_leaves) if isinstance(a, Stored)]
     parts = [i for i in far if leaves[i].parts]
     leaves = [
@@ -443,21 +496,24 @@
         )
         fetch(coming)
         for i in stored:
-            results[i].copy.wait()
+            results[i].done()
 
     n_sems = len(far) - len(parts) + len(stored) + len(parts) * PARTS
     size = sum(4 * math.prod(a.shape) for a in leaves + out_leaves)
     given = pl.pallas_call(
         body,
-        out_shape=[pltpu.HBM(a.shape, F32) if isinstance(a, Stored) else a for a in out_leaves],
+        out_shape=[
+            pltpu.HBM(a.shape, F32) if i in distant else shaped(*a.shape)
+            for i, a in enumerate(out_leaves)
+        ],
         in_specs=[
             pl.BlockSpec(
-                memory_space=pltpu.HBM if i in far else pltpu.VMEM
+                memory_space=pltpu.HBM if i in far + raw else pltpu.VMEM
             )
             for i in range(count)
         ],
         out_specs=[
-            pl.BlockSpec(memory_space=pltpu.HBM if i in stored else pltpu.VMEM)
+            pl.BlockSpec(memory_space=pltpu.HBM if i in distant else pltpu.VMEM)
             for i in range(n_out)
         ],
         scratch_shapes=[pltpu.SemaphoreType.DMA((max(1, n_sems),))]
@@ -543,20 +599,26 @@
     row_shape = shaped(devices, LANES)
     sum_shape = (devices * vecs // LANES, LANES)
     ends_shape = (nx, ny, LANES)
-    box = shaped(*boxed)
     vbox = pltpu.VMEM(boxed, F32)
-    inputs = (Far(conductance), Far(storage), Far(dirichlet), Far(right_side))
-
-    def six(cond, store, fixed, rhs, free):
-        cond, store, fixed, rhs = fetch((cond, store, fixed, rhs))
+    def pack_first(cond, store, fixed, rhs, outs):
+        near, free = outs["near"], outs["free"]
+        for target, source in zip(near, (cond, store, rhs)):
+            target.put(source.get())
+        fixed = fixed.get()
         free[...] = 1.0 - fixed[...].astype(F32)
-        return [cond.at[0], cond.at[1], cond.at[2], store, free, rhs]
-
-    def pack_first(cond, store, fixed, rhs, out, free):
-        out[...] = pack_z(six(cond, store, fixed, rhs, free))
-
-    tile = call(pack_first, shaped(z_rows(6), nx * ny), inputs, [pltpu.VMEM(shape, F32)])
-    got_z = send_z(tile, sizes)
+        cond, store, rhs = [one.done() for one in near]
+        outs["tile"][...] = pack_z([cond.at[0], cond.at[1], cond.at[2], store, free, rhs])
+
+    first = call(
+        pack_first,
+        {
+            "near": [Stored(*a.shape, near=True) for a in (conductance, storage, right_side)],
+            "free": shaped(*shape),
+            "tile": shaped(z_rows(6), nx * ny),
+        },
+        (Raw(conductance), Raw(storage), Far(dirichlet), Raw(right_side)),
+    )
+    got_z = send_z(first["tile"], sizes)
 
     def first_rows(rhs, base, out):
         row = project(base, rhs.get()[...])
@@ -565,8 +627,9 @@
     rows = call(first_rows, row_shape, (Far(right_side), Far(basis, True)))
     rows_a = spread(rows)
 
-    def pack_all(got_z, cond, store, fixed, rhs, rows, outs, free, ends):
-        fields = six(cond, store, fixed, rhs, free)
+    def pack_all(got_z, near, free, rows, outs, ends):
+        cond, store, rhs = fetch(near)
+        fields = [cond.at[0], cond.at[1], cond.at[2], store, free.get(), rhs]
         ends[...] = pick_z(fetch(got_z), sizes, ends_shape)
         outs["ends"].put(ends)
         pack_faces(outs["faces"], fields, sizes, 2, ends)
@@ -574,51 +637,67 @@
     packed = call(
         pack_all,
         {"ends": Stored(*ends_shape), "faces": face_shapes(shape, sizes, 6, 2)},
-        (got_z,) + inputs + (rows,),
-        [pltpu.VMEM(shape, F32), pltpu.VMEM(ends_shape, F32)],
+        (got_z, first["near"], first["free"], rows),
+        [pltpu.VMEM(ends_shape, F32)],
     )
     got = send_faces(packed["faces"], sizes)
 
-    def first_smooth(got, cond, store, fixed, rhs, ends, outs, free, *work):
-        ga, gb, source, step = work[:4]
-        boxes = list(work[4:])
-        for b in boxes:
-            clear(b)
-        owns = six(cond, store, fixed, rhs, free)
-        got = fetch(got)
-        unpack_faces(boxes, owns, got["x"], got["y"], sizes, 2, ends.get()[...])
-        unpack_xy(boxes, shape, got["xy"], sizes)
-        links = outs["links"]
-        coefficients(boxes, links, outs["diag"], step)
-        for name, value in (("diag", outs["diag"]), ("step", step)):
+    def first_smooth(got, cond, store, fixed, rhs, ends, outs, sems, step, *boxes):
+        boxes = list(boxes)
+        cond, store, rhs = fetch((cond, store, rhs))
+        owns = [cond.at[0], cond.at[1], cond.at[2], store, None, rhs]
+        copies = []
+        for k, own in enumerate(owns):
+            if own is not None:
+                copies.append(
+                    pltpu.make_async_copy(own, own_cells(boxes[k], shape), sems.at[k])
+                )
+                copies[-1].start()
+        for b in boxes[:6]:
+            clear_round(b, shape)
+        got, fixed = fetch((got, fixed))
+        boxes[4][3 : 3 + nx, 0:ny, 0:nz] = 1.0 - fixed[...].astype(F32)
+        unpack_faces(boxes[:6], [None] * 6, got["x"], got["y"], sizes, 2, ends.get()[...])
+        unpack_xy(boxes[:6], shape, got["xy"], sizes)
+        for copy in copies:
+            copy.wait()
+        links, boxes = boxes[6:], boxes[:6]
+        coefficients(boxes, links, step, outs["own"])
+        for name, value in (("step", step), ("own", outs["own"])):
             outs["kept"][name].put(value)
         for kept, link in zip(outs["kept"]["links"], links):
             kept.put(link)
-        jacobi(boxes[-1], step, links, ga, gb, source, outs["smooth"])
+        jacobi(boxes[5], step, links, boxes[0], boxes[1], boxes[5], outs["smooth"])
 
     smoothed = call(
         first_smooth,
         {
             "smooth": shaped(*shape),
-            "links": [box, box, box],
-            "diag": box,
+            "own": shaped(7, *shape),
             "kept": {
                 "links": [Stored(*boxed), Stored(*boxed), Stored(*boxed)],
-                "diag": Stored(*boxed),
                 "step": Stored(*boxed),
+                "own": Stored(7, *shape),
             },
         },
-        (far(got),) + inputs + (Far(packed["ends"]),),
-        [pltpu.VMEM(shape, F32)] + [vbox] * 10,
+        (
+            far(got),
+            Raw(conductance),
+            Raw(storage),
+            Far(dirichlet),
+            Raw(right_side),
+            Far(packed["ends"]),
+        ),
+        [pltpu.SemaphoreType.DMA((6,))] + [vbox] * 10,
         flops=SMOOTH_FLOPS,
     )
     kept = smoothed["kept"]
-    links, diag = smoothed["links"], smoothed["diag"]
+    own = smoothed["own"]
 
     def first_direction(smooth, rows, inverse, base, outs):
         smooth, rows = fetch((smooth, rows))
         weights = coarse_weights(inverse.get(), coarse_sum(rows, vecs))
-        add_coarse(outs["z"], smooth, base.get(), weights)
+        add_coarse(outs["z"], smooth, base, weights)
         outs["kept"].put(outs["z"])
         pack_faces(outs["faces"], [outs["z"]], sizes, 1)
         outs["tile"][...] = pack_z([outs["z"]])
@@ -631,29 +710,34 @@
             "faces": face_shapes(shape, sizes, 1, 1),
             "tile": shaped(z_rows(1), nx * ny),
         },
-        (smoothed["smooth"], rows_a, Far(coarse_inverse), Far(basis)),
+        (smoothed["smooth"], rows_a, Far(coarse_inverse), Far(basis, True)),
     )
     direction, kept_z = directed["z"], directed["kept"]
     got = send_faces(directed["faces"], sizes)
     got_z = send_z(directed["tile"], sizes)
 
-    def apply(field, got, got_z, links, diag, out, vb):
-        clear(vb)
+    def apply(field, got, got_z, own, out, vb):
+        clear_round(vb, shape)
         field, got, got_z = fetch((field, got, got_z))
         unpack_faces([vb], [field], got["x"], got["y"], sizes, 1)
         vb[3 : 3 + nx, 0:ny, nz : nz + LANES] = halo_lanes(pick_z(got_z, sizes, ends_shape), 0)
-        links, diag = fetch((links, diag))
+        own = own.get()
 
         def body(x, carry):
-            whole = diag[x + 3] * vb[x + 3] - neighbours(vb, links, x + 3)
-            out[x] = whole[0:ny, 0:nz]
+            mid = vb[x + 3]
+            around = (mid, vb[x + 4], vb[x + 2])
+            around += (ahead(mid, 0), behind(mid, 0), ahead(mid, 1), behind(mid, 1))
+            total = own[0, x] * mid[0:ny, 0:nz]
+            for n in range(1, 7):
+                total = total - own[n, x] * around[n][0:ny, 0:nz]
+            out[x] = total
             return carry
 
         loop(0, nx, body)
 
-    def first_image(got, got_z, field, links, diag, rhs, outs, vb):
+    def first_image(got, got_z, field, own, rhs, outs, vb):
         image = outs["image"]
-        apply(field, got, got_z, links, diag, image, vb)
+        apply(field, got, got_z, own, image, vb)
         outs["kept"].put(image)
         outs["tile"][...] = pack_z([image])
         field, rhs = fetch((field, rhs))
@@ -668,7 +752,7 @@
             "tile": shaped(z_rows(1), nx * ny),
             "sums": shaped(1, LANES),
         },
-        (far(got), got_z, direction, links, diag, Far(right_side)),
+        (got, got_z, direction, own, Far(right_side)),
         [vbox],
     )
     got_z = send_z(imaged["tile"], sizes)
@@ -693,20 +777,28 @@
     )
     got = send_faces(packed["faces"], sizes)
 
-    def second_smooth(got, field, step, links, ends, out, *work):
-        ga, gb, source, vb = work
-        clear(vb)
-        field, got, ends = fetch((field, got, ends))
-        unpack_faces([vb], [field], got["x"], got["y"], sizes, 2, ends[...])
+    def second_smooth(got, field, ends, step, links, outs, sem, ga, gb, vb):
+        copy = pltpu.make_async_copy(field.get(), own_cells(vb, shape), sem)
+        copy.start()
+        clear_round(vb, shape)
+        got, ends = fetch((got, ends))
+        unpack_faces([vb], [None], got["x"], got["y"], sizes, 2, ends[...])
         unpack_xy([vb], shape, got["xy"], sizes)
+        copy.wait()
         step, links = fetch((step, links))
-        jacobi(vb, step, links, ga, gb, source, out)
-
-    smooth = call(
+        jacobi(vb, step, links, ga, gb, vb, outs["smooth"])
+
+    smoothed = call(
         second_smooth,
-        shaped(*shape),
-        (far(got), Far(imaged["kept"]), Far(kept["step"]), far(kept["links"]), Far(packed["ends"])),
-        [vbox] * 4,
+        {"smooth": shaped(*shape)},
+        (
+            got,
+            Raw(imaged["kept"]),
+            Far(packed["ends"]),
+            Far(kept["step"]),
+            far(kept["links"]),
+        ),
+        [pltpu.SemaphoreType.DMA] + [vbox] * 3,
         flops=SMOOTH_FLOPS,
     )
 
@@ -717,7 +809,7 @@
         weights = coarse_weights(inverse.get(), coarse_sum(rows, vecs))
         field, rhs, before = fetch((field, rhs, before))
         outs["residual"][...] = rhs[...] - alpha * field[...]
-        add_coarse(outs["z"], smooth, base.get(), weights)
+        add_coarse(outs["z"], smooth, base, weights)
         outs["z"][...] = before[...] - alpha * outs["z"][...]
         pack_faces(outs["faces"], [outs["z"]], sizes, 1)
         outs["tile"][...] = pack_z([outs["z"]])
@@ -735,22 +827,22 @@
             "tile": shaped(z_rows(1), nx * ny),
         },
         (
-            smooth,
+            smoothed["smooth"],
             rows_c,
             Far(coarse_inverse),
             Far(imaged["kept"]),
             Far(right_side),
             Far(kept_z),
-            Far(basis),
+            Far(basis, True),
         ),
     )
     precond, residual = directed["z"], directed["residual"]
     got = send_faces(directed["faces"], sizes)
     got_z = send_z(directed["tile"], sizes)
-    image, direction = Far(imaged["kept"]), Far(kept_z)
-
-    def second_image(got, got_z, field, links, diag, image, residual, outs, vb):
-        apply(field, got, got_z, links, diag, outs["image"], vb)
+    image, direction = imaged["kept"], kept_z
+
+    def second_image(got, got_z, field, own, image, residual, outs, vb):
+        apply(field, got, got_z, own, outs["image"], vb)
         field, image, residual = fetch((field, image, residual))
         values = [
             full_sum(residual[...] * field[...]),
@@ -764,11 +856,10 @@
         second_image,
         {"image": shaped(*shape), "rows": row_shape},
         (
-            far(got),
+            got,
             got_z,
             precond,
-            far(kept["links"]),
-            Far(kept["diag"]),
+            Far(kept["own"]),
             image,
             residual,
         ),

time: 88.3 us -> 81.7 us (0.925)
  Pallas kernels: 36.1 us -> 31.7 us
  local copies, waits for them, and re-layouts: 3.22 us -> 0.81 us
  waiting for transfers between devices: 5.55 us -> 7.84 us
  starting transfers between devices: 30.7 us -> 28.9 us
    pallas_call x12, Pallas kernels: 36.1 us -> 31.7 us  [call(): pl.pallas_call(body, out_shape=[pltpu.HBM(a.shape, F32) if i in distant e...]
    unnamed x32 -> x14, local copies, waits for them, and re-layouts: 3.22 us -> 0.81 us
    ppermute x24, starting transfers between devices: 24.1 us -> 22.3 us  [swap(): return lax.ppermute(value, AXES, pairs)]
    all_to_all x2, waiting for transfers between devices: 1.51 us -> 3.18 us  [spread(): return lax.all_to_all(rows, AXES, 0, 0, tiled=True)]
  transfers between devices with their start and end apart: 26 -> 26, of which waited for: 4 -> 6; matrix products, arithmetic and copies ran while one was open for 0% -> 0% of each run, Pallas kernels for 19% -> 20%
where the time goes in v3:
time: 81.7 us; the launch traced here: 81.2 us
  Pallas kernels  31.7 us (39%)
  starting transfers between devices  28.9 us (35%)
  blocking collectives  11.1 us (14%)
  waiting for transfers between devices  7.84 us (10%)
  between operations  0.89 us (1%)
    pallas_call x12, Pallas kernels, call(): pl.pallas_call(body, out_shape=[pltpu.HBM(a.shape, F32) if i in distant e...  31.7 us
    ppermute x24, starting transfers between devices, swap(): return lax.ppermute(value, AXES, pairs)  22.3 us
    all_to_all x1, blocking collectives, spread(): return lax.all_to_all(rows, AXES, 0, 0, tiled=True)  11.1 us
    all_to_all x2, starting transfers between devices, spread(): return lax.all_to_all(rows, AXES, 0, 0, tiled=True)  6.6 us
    ppermute x24, waiting for transfers between devices, swap(): return lax.ppermute(value, AXES, pairs)  4.66 us
    all_to_all x2, waiting for transfers between devices, spread(): return lax.all_to_all(rows, AXES, 0, 0, tiled=True)  3.18 us
  transfers between devices with their start and end apart: 26, of which 6 were waited for; matrix products, arithmetic and copies ran while one was open for 0% of the time, Pallas kernels for 20%

profile of v3, /device:TPU:0, one launch (start us, length us, event | category | flops | bytes accessed | tf_op | source)
XLA Modules:
  0.0 81.2 jit_solution(4490603519179614496)
XLA Ops:
  0.6 1.7 %shard_map.77 = (f32[16,16,256]{2,1,0:T(8,128)S(1)}, f32[3,16,16,256]{3,2,1,0:T(8,128)S(1)}, f32[16,16,256]{2,1,0:T(8,128)S(1)}, f32[16,16,256]{2,1,0:T(8,128)S(1)}, f32[24,256]{1,0:T(8,128)S(1)}) custom-call(f32[3,16,16,256]{3,2,1,0:T(8,128)} %refs_5_.1, f32[16,16,256]{2,1,0:T(8,128)} %refs_6_.2, s32[16,16,256]{2,1,0:T(8,128)} %refs_7_.2, ...), custom_call_target="tpu_custom_call" | custom-call | bytes 3170304 | tf_op jit(solution)/shard_map/pallas_call | solution.py:503
  2.3 2.4 %collective-permute-start.1 = (f32[24,256]{1,0:T(8,128)S(1)}, f32[24,256]{1,0:T(8,128)S(1)}, u32[]{:S(2)}, u32[]{:S(2)}) collective-permute-start(f32[24,256]{1,0:T(8,128)S(1)} %get-tuple-element.45), channel_id=1, source_target_pairs={{0,3},{1,2},{2,1},{3,0},{4,7},{5,6},{6,5},{7,4},{8,11},{9,10},{10,... | collective-permute-start | bytes 73736 | tf_op jit(solution)/shard_map/ppermute | solution.py:52
  4.8 0.7 collective-permute-start
  5.5 3.1 %shard_map.78.refs_6_ = f32[32,128]{1,0:T(8,128)} custom-call(f32[16,16,256]{2,1,0:T(8,128)} %refs_4_.1, f32[16,16,16,256]{3,2,1,0:T(8,128)} %refs_6_.3), custom_call_target="tpu_custom_call" | custom-call | bytes 4472832 | tf_op jit(solution)/shard_map/pallas_call | solution.py:503
  8.5 0.0 collective-permute-done.1.refs_1_
  8.6 1.5 %shard_map.79 = (f32[16,16,128]{2,1,0:T(8,128)}, f32[13,16,256]{2,1,0:T(8,128)S(1)}, f32[28,256]{1,0:T(8,128)S(1)}, f32[28,256]{1,0:T(8,128)S(1)}, f32[13,16,256...) custom-call(f32[24,256]{1,0:T(8,128)S(1)} %collective-permute-done.refs_0_, f32[24,256]{1,0:T(8,128)S(1)} %collective-permute-done.1.refs_1_, ...), custom_call_target="tpu_custom_call" | custom-call | bytes 2465792 | tf_op jit(solution)/shard_map/pallas_call | solution.py:503
  10.1 1.6 %collective-permute-start.2 = (f32[13,16,256]{2,1,0:T(8,128)S(1)}, f32[13,16,256]{2,1,0:T(8,128)S(1)}, u32[]{:S(2)}, u32[]{:S(2)}) collective-permute-start(f32[13,16,256]{2,1,0:T(8,128)S(1)} %get-tuple-element.50), channel_id=1, source_target_pairs={{0,16},{1,17},{2,18},{3,19},{4,20},{5,21},{6,22},{7,23},{8,24},{9,... | collective-permute-start | bytes 638984 | tf_op jit(solution)/shard_map/ppermute | solution.py:52
  11.7 1.6 %collective-permute-start.5 = (f32[13,16,256]{2,1,0:T(8,128)S(1)}, f32[13,16,256]{2,1,0:T(8,128)S(1)}, u32[]{:S(2)}, u32[]{:S(2)}) collective-permute-start(f32[13,16,256]{2,1,0:T(8,128)S(1)} %get-tuple-element.53), channel_id=1, source_target_pairs={{0,4},{1,5},{2,6},{3,7},{4,0},{5,1},{6,2},{7,3},{8,12},{9,13},{10,... | collective-permute-start | bytes 638984 | tf_op jit(solution)/shard_map/ppermute | solution.py:52
  13.2 3.1 %collective-permute-start.3 = (f32[28,256]{1,0:T(8,128)S(1)}, f32[28,256]{1,0:T(8,128)S(1)}, u32[]{:S(2)}, u32[]{:S(2)}) collective-permute-start(f32[28,256]{1,0:T(8,128)S(1)} %get-tuple-element.51), channel_id=1, source_target_pairs={{0,20},{1,21},{2,22},{3,23},{4,16},{5,17},{6,18},{7,19},{8,28},{9,... | collective-permute-start | bytes 86024 | tf_op jit(solution)/shard_map/ppermute | solution.py:52
  16.3 2.8 %all-to-all-start = ((f32[32,1,128]{2,1,0:T(1,128)}), f32[32,1,128]{2,1,0:T(1,128)S(1)}, u32[]{:S(2)}, u32[]{:S(2)}) async-start(f32[32,1,128]{2,1,0:T(1,128)} %bitcast.1), calls=%async_computation | async-start | bytes 32768 | tf_op jit(solution)/shard_map/all_to_all | solution.py:590
  19.1 0.1 collective-permute-done.3.refs_1_
  19.2 0.0 copy-start.2
  19.2 0.0 copy-start.3
  19.2 0.5 copy-done.5
  19.8 0.0 copy-done.6
  19.8 0.1 copy-done.2
  19.9 0.1 copy-done.3
  20.0 0.1 copy-done.4
  20.0 5.7 %shard_map.80 = (f32[22,24,384]{2,1,0:T(8,128)}, f32[22,24,384]{2,1,0:T(8,128)}, f32[22,24,384]{2,1,0:T(8,128)}, f32[7,16,16,256]{3,2,1,0:T(8,128)}, f32[22,24,3...) custom-call(f32[13,16,256]{2,1,0:T(8,128)} %copy-done.2, f32[28,256]{1,0:T(8,128)} %copy-done.5, ...), custom_call_target="tpu_custom_call" | custom-call | flops 1000000000 | bytes 9576448 | tf_op jit(solution)/shard_map/pallas_call | solution.py:503
  25.7 0.5 all-to-all-done
  26.3 3.0 %shard_map.81 = (f32[1,16,256]{2,1,0:T(8,128)S(1)}, f32[1,16,256]{2,1,0:T(8,128)S(1)}, f32[1,16,256]{2,1,0:T(8,128)S(1)}, f32[16,16,256]{2,1,0:T(8,128)}, f32[8,...) custom-call(f32[16,16,256]{2,1,0:T(8,128)S(1)} %get-tuple-element.56.refs_0_, f32[32,128]{1,0:T(8,128)S(1)} %bitcast.12, ...), custom_call_target="tpu_custom_call" | custom-call | bytes 5087232 | tf_op jit(solution)/shard_map/pallas_call | solution.py:503
  29.3 1.3 %collective-permute-start.7 = (f32[1,16,256]{2,1,0:T(8,128)S(1)}, f32[1,16,256]{2,1,0:T(8,128)S(1)}, u32[]{:S(2)}, u32[]{:S(2)}) collective-permute-start(f32[1,16,256]{2,1,0:T(8,128)S(1)} %get-tuple-element.57), channel_id=1, source_target_pairs={{0,16},{1,17},{2,18},{3,19},{4,20},{5,21},{6,22},{7,23},{8,24},{9,... | collective-permute-start | bytes 49160 | tf_op jit(solution)/shard_map/ppermute | solution.py:52
  30.6 2.7 %collective-permute-start.8 = (f32[1,16,256]{2,1,0:T(8,128)S(1)}, f32[1,16,256]{2,1,0:T(8,128)S(1)}, u32[]{:S(2)}, u32[]{:S(2)}) collective-permute-start(f32[1,16,256]{2,1,0:T(8,128)S(1)} %get-tuple-element.58), channel_id=1, source_target_pairs={{0,4},{1,5},{2,6},{3,7},{4,0},{5,1},{6,2},{7,3},{8,12},{9,13},{10,... | collective-permute-start | bytes 49160 | tf_op jit(solution)/shard_map/ppermute | solution.py:52
  33.3 0.6 collective-permute-start.11
  34.0 0.0 collective-permute-start.10
  34.0 2.4 %collective-permute-done.11.refs_4_ = f32[8,256]{1,0:T(8,128)S(1)} collective-permute-done((f32[8,256]{1,0:T(8,128)S(1)}, f32[8,256]{1,0:T(8,128)S(1)}, u32[]{:S(2)}, u32[]{:S(2)}) %collective-permute-start.11) | collective-permute-done | bytes 8224 | tf_op jit(solution)/shard_map/ppermute | solution.py:52
  36.4 1.6 %shard_map.82 = (f32[16,16,256]{2,1,0:T(8,128)S(1)}, f32[16,16,256]{2,1,0:T(8,128)}, f32[1,128]{1,0:T(1,128)S(1)}, f32[8,256]{1,0:T(8,128)S(1)}) custom-call(f32[1,16,256]{2,1,0:T(8,128)S(1)} %collective-permute-done.7.refs_0_, f32[1,16,256]{2,1,0:T(8,128)S(1)} %collective-permute-done.8.refs_1_, f32[1,16,256]{2,1,0:T(8,128)S(1)} %collective-permute-done.9.refs_2_, ...), custom_call_target="tpu_custom_call" | custom-call | bytes 2957824 | tf_op jit(solution)/shard_map/pallas_call | solution.py:503
  38.0 0.7 collective-permute-start.13
  38.7 0.0 collective-permute-start.12
  38.7 3.0 %shard_map.83.refs_3_ = f32[32,128]{1,0:T(8,128)} custom-call(f32[16,16,16,256]{3,2,1,0:T(8,128)} %refs_6_.3, f32[16,16,256]{2,1,0:T(8,128)S(1)} %get-tuple-element.64.refs_1_.refs_2_, f32[1,128]{1,0:T(1,128)S(1)} %get-tuple-element.65.refs_2_), custom_call_target="tpu_custom_call" | custom-call | bytes 4473344 | tf_op jit(solution)/shard_map/pallas_call | solution.py:503
  41.7 1.5 %shard_map.84 = (f32[16,16,128]{2,1,0:T(8,128)}, f32[3,16,256]{2,1,0:T(8,128)S(1)}, f32[8,256]{1,0:T(8,128)S(1)}, f32[8,256]{1,0:T(8,128)S(1)}, f32[3,16,256]{2,1,0:T(8,128)S(1)}, /*index=5*/f32[3,16,256]{2,1,0:T(8,128)S(1)}) custom-call(f32[8,256]{1,0:T(8,128)S(1)} %collective-permute-done.12.refs_0_, f32[8,256]{1,0:T(8,128)S(1)} %collective-permute-done.13.refs_1_, ...), custom_call_target="tpu_custom_call" | custom-call | bytes 589824 | tf_op jit(solution)/shard_map/pallas_call | solution.py:503
  43.3 0.5 collective-permute-start.14
  43.8 2.8 %collective-permute-start.17 = (f32[3,16,256]{2,1,0:T(8,128)S(1)}, f32[3,16,256]{2,1,0:T(8,128)S(1)}, u32[]{:S(2)}, u32[]{:S(2)}) collective-permute-start(f32[3,16,256]{2,1,0:T(8,128)S(1)} %get-tuple-element.69), channel_id=1, source_target_pairs={{0,4},{1,5},{2,6},{3,7},{4,0},{5,1},{6,2},{7,3},{8,12},{9,13},{10,... | collective-permute-start | bytes 147464 | tf_op jit(solution)/shard_map/ppermute | solution.py:52
  46.6 2.0 %collective-permute-start.15 = (f32[8,256]{1,0:T(8,128)S(1)}, f32[8,256]{1,0:T(8,128)S(1)}, u32[]{:S(2)}, u32[]{:S(2)}) collective-permute-start(f32[8,256]{1,0:T(8,128)S(1)} %get-tuple-element.67), channel_id=1, source_target_pairs={{0,20},{1,21},{2,22},{3,23},{4,16},{5,17},{6,18},{7,19},{8,28},{9,... | collective-permute-start | bytes 24584 | tf_op jit(solution)/shard_map/ppermute | solution.py:52
  48.6 3.8 %all-to-all-start.1 = ((f32[32,1,128]{2,1,0:T(1,128)}), f32[32,1,128]{2,1,0:T(1,128)S(1)}, u32[]{:S(2)}, u32[]{:S(2)}) async-start(f32[32,1,128]{2,1,0:T(1,128)} %bitcast.4), calls=%async_computation.1 | async-start | bytes 32768 | tf_op jit(solution)/shard_map/all_to_all | solution.py:590
  52.4 4.4 %shard_map.85.refs_0_ = f32[16,16,256]{2,1,0:T(8,128)S(1)} custom-call(f32[3,16,256]{2,1,0:T(8,128)S(1)} %collective-permute-done.14.refs_0_, f32[8,256]{1,0:T(8,128)S(1)} %collective-permute-done.15.refs_1_, f32[8,256]{1,0:T(8,128)S(1)} %collective-permute-done.16.refs_2_, f32[3,16,256]{2,1,0:T(8,128)S(1)} %collective-permute-done.17.refs_3_, ...), custom_call_target="tpu_custom_call" | custom-call | flops 1000000000 | bytes 4063232 | tf_op jit(solution)/shard_map/pallas_call | solution.py:503
  56.9 2.6 %all-to-all-done.1 = f32[32,1,128]{2,1,0:T(1,128)S(1)} async-done(((f32[32,1,128]{2,1,0:T(1,128)}), f32[32,1,128]{2,1,0:T(1,128)S(1)}, u32[]{:S(2)}, u32[]{:S(2)}) %all-to-all-start.1) | async-done | bytes 16416 | tf_op jit(solution)/shard_map/all_to_all | solution.py:590
  59.5 2.9 %shard_map.86 = (f32[1,16,256]{2,1,0:T(8,128)S(1)}, f32[1,16,256]{2,1,0:T(8,128)S(1)}, f32[1,16,256]{2,1,0:T(8,128)S(1)}, f32[16,16,256]{2,1,0:T(8,128)S(1)}, f3...) custom-call(f32[16,16,256]{2,1,0:T(8,128)S(1)} %shard_map.85.refs_0_, ...), custom_call_target="tpu_custom_call" | custom-call | bytes 5881856 | tf_op jit(solution)/shard_map/pallas_call | solution.py:503
  62.4 0.0 copy-start.1
  62.4 0.7 collective-permute-start.19
  63.1 0.5 collective-permute-start.20
  63.6 1.1 %collective-permute-start.23 = (f32[8,256]{1,0:T(8,128)S(1)}, f32[8,256]{1,0:T(8,128)S(1)}, u32[]{:S(2)}, u32[]{:S(2)}) collective-permute-start(f32[8,256]{1,0:T(8,128)S(1)} %get-tuple-element.81), channel_id=1, source_target_pairs={{0,3},{1,2},{2,1},{3,0},{4,7},{5,6},{6,5},{7,4},{8,11},{9,10},{10,... | collective-permute-start | bytes 24584 | tf_op jit(solution)/shard_map/ppermute | solution.py:52
  64.7 0.0 collective-permute-start.22
  64.7 2.0 %collective-permute-done.23.refs_4_ = f32[8,256]{1,0:T(8,128)S(1)} collective-permute-done((f32[8,256]{1,0:T(8,128)S(1)}, f32[8,256]{1,0:T(8,128)S(1)}, u32[]{:S(2)}, u32[]{:S(2)}) %collective-permute-start.23) | collective-permute-done | bytes 8224 | tf_op jit(solution)/shard_map/ppermute | solution.py:52
  66.7 0.1 collective-permute-done.20.refs_1_
  66.8 2.2 %shard_map.87 = (f32[16,16,256]{2,1,0:T(8,128)S(1)}, f32[32,128]{1,0:T(8,128)S(1)}) custom-call(f32[1,16,256]{2,1,0:T(8,128)S(1)} %collective-permute-done.19.refs_0_, f32[1,16,256]{2,1,0:T(8,128)S(1)} %collective-permute-done.20.refs_1_, f32[1,16,256]{2,1,0:T(8,128)S(1)} %collective-permute-done.21.refs_2_, f32[8,256]{1,0:T(8,128)S(1)} %collective-permute-done.22.refs_3_, ...), custom_call_target="tpu_custom_call" | custom-call | bytes 2965504 | tf_op jit(solution)/shard_map/pallas_call | solution.py:503
  69.0 11.1 %all_to_all.33 = f32[32,1,128]{2,1,0:T(1,128)S(1)} all-to-all(f32[32,1,128]{2,1,0:T(1,128)S(1)} %bitcast.15), channel_id=1, replica_groups=mesh['gx'=2,'gy'=4,'gz'=4] {'gx','gy','gz'}, dimensions={0} | all-to-all | bytes 32768 | tf_op jit(solution)/shard_map/all_to_all | solution.py:590
  80.1 1.1 %shard_map.88 = (f32[16,16,256]{2,1,0:T(8,128)}, f32[16,16,256]{2,1,0:T(8,128)}) custom-call(f32[32,128]{1,0:T(8,128)S(1)} %bitcast.14, f32[16,128]{1,0:T(8,128)S(1)} %get-tuple-element.86.refs_1_, f32[16,16,256]{2,1,0:T(8,128)S(1)} %copy-done.1, f32[16,16,256]{2,1,0:T(8,128)S(1)} %copy-done, f32[16,16,256]{2,1,0:T(8,128)S(1)} %get-tuple-element.82.refs_5_.refs_4_, ...), custom_call_target="tpu_custom_call" | custom-call | bytes 1859584 | tf_op jit(solution)/shard_map/pallas_call | solution.py:503
  (31 shorter events, 0.1 us)
Async XLA Ops:
  2.3 6.2 %collective-permute-start.1 = (f32[24,256]{1,0:T(8,128)S(1)}, f32[24,256]{1,0:T(8,128)S(1)}, u32[]{:S(2)}, u32[]{:S(2)}) collective-permute-start(f32[24,256]{1,0:T(8,128)S(1)} %get-tuple-element.45), channel_id=1, source_target_pairs={{0,3},{1,2},{2,1},{3,0},{4,7},{5,6},{6,5},{7,4},{8,11},{9,10},{10,... | collective-permute-start | bytes 73736 | tf_op jit(solution)/shard_map/ppermute | solution.py:52
  4.8 3.8 %collective-permute-start = (f32[24,256]{1,0:T(8,128)S(1)}, f32[24,256]{1,0:T(8,128)S(1)}, u32[]{:S(2)}, u32[]{:S(2)}) collective-permute-start(f32[24,256]{1,0:T(8,128)S(1)} %get-tuple-element.45), channel_id=1, source_target_pairs={{0,1},{1,0},{2,3},{3,2},{4,5},{5,4},{6,7},{7,6},{8,9},{9,8},{10,11... | collective-permute-start | bytes 73736 | tf_op jit(solution)/shard_map/ppermute | solution.py:52
  10.1 9.1 %collective-permute-start.2 = (f32[13,16,256]{2,1,0:T(8,128)S(1)}, f32[13,16,256]{2,1,0:T(8,128)S(1)}, u32[]{:S(2)}, u32[]{:S(2)}) collective-permute-start(f32[13,16,256]{2,1,0:T(8,128)S(1)} %get-tuple-element.50), channel_id=1, source_target_pairs={{0,16},{1,17},{2,18},{3,19},{4,20},{5,21},{6,22},{7,23},{8,24},{9,... | collective-permute-start | bytes 638984 | tf_op jit(solution)/shard_map/ppermute | solution.py:52
  11.7 7.6 %collective-permute-start.5 = (f32[13,16,256]{2,1,0:T(8,128)S(1)}, f32[13,16,256]{2,1,0:T(8,128)S(1)}, u32[]{:S(2)}, u32[]{:S(2)}) collective-permute-start(f32[13,16,256]{2,1,0:T(8,128)S(1)} %get-tuple-element.53), channel_id=1, source_target_pairs={{0,4},{1,5},{2,6},{3,7},{4,0},{5,1},{6,2},{7,3},{8,12},{9,13},{10,... | collective-permute-start | bytes 638984 | tf_op jit(solution)/shard_map/ppermute | solution.py:52
  13.2 6.0 %collective-permute-start.6 = (f32[13,16,256]{2,1,0:T(8,128)S(1)}, f32[13,16,256]{2,1,0:T(8,128)S(1)}, u32[]{:S(2)}, u32[]{:S(2)}) collective-permute-start(f32[13,16,256]{2,1,0:T(8,128)S(1)} %get-tuple-element.54), channel_id=1, source_target_pairs={{0,1},{1,0},{2,3},{3,2},{4,8},{5,9},{6,10},{7,11},{8,4},{9,5},{10,... | collective-permute-start | bytes 638984 | tf_op jit(solution)/shard_map/ppermute | solution.py:52
  13.2 5.9 %collective-permute-start.3 = (f32[28,256]{1,0:T(8,128)S(1)}, f32[28,256]{1,0:T(8,128)S(1)}, u32[]{:S(2)}, u32[]{:S(2)}) collective-permute-start(f32[28,256]{1,0:T(8,128)S(1)} %get-tuple-element.51), channel_id=1, source_target_pairs={{0,20},{1,21},{2,22},{3,23},{4,16},{5,17},{6,18},{7,19},{8,28},{9,... | collective-permute-start | bytes 86024 | tf_op jit(solution)/shard_map/ppermute | solution.py:52
  16.3 2.9 %collective-permute-start.4 = (f32[28,256]{1,0:T(8,128)S(1)}, f32[28,256]{1,0:T(8,128)S(1)}, u32[]{:S(2)}, u32[]{:S(2)}) collective-permute-start(f32[28,256]{1,0:T(8,128)S(1)} %get-tuple-element.52), channel_id=1, source_target_pairs={{0,1},{1,0},{2,3},{3,2},{4,24},{5,25},{6,26},{7,27},{8,20},{9,21},... | collective-permute-start | bytes 86024 | tf_op jit(solution)/shard_map/ppermute | solution.py:52
  16.3 9.9 %all-to-all-start = ((f32[32,1,128]{2,1,0:T(1,128)}), f32[32,1,128]{2,1,0:T(1,128)S(1)}, u32[]{:S(2)}, u32[]{:S(2)}) async-start(f32[32,1,128]{2,1,0:T(1,128)} %bitcast.1), calls=%async_computation | async-start | bytes 32768 | tf_op jit(solution)/shard_map/all_to_all | solution.py:590
  19.2 0.6 copy-start.5
  19.2 0.6 copy-start.6
  19.2 0.7 copy-start.2
  19.2 0.7 copy-start.3
  19.2 0.8 copy-start.4
  29.3 7.1 %collective-permute-start.7 = (f32[1,16,256]{2,1,0:T(8,128)S(1)}, f32[1,16,256]{2,1,0:T(8,128)S(1)}, u32[]{:S(2)}, u32[]{:S(2)}) collective-permute-start(f32[1,16,256]{2,1,0:T(8,128)S(1)} %get-tuple-element.57), channel_id=1, source_target_pairs={{0,16},{1,17},{2,18},{3,19},{4,20},{5,21},{6,22},{7,23},{8,24},{9,... | collective-permute-start | bytes 49160 | tf_op jit(solution)/shard_map/ppermute | solution.py:52
  30.6 5.8 %collective-permute-start.8 = (f32[1,16,256]{2,1,0:T(8,128)S(1)}, f32[1,16,256]{2,1,0:T(8,128)S(1)}, u32[]{:S(2)}, u32[]{:S(2)}) collective-permute-start(f32[1,16,256]{2,1,0:T(8,128)S(1)} %get-tuple-element.58), channel_id=1, source_target_pairs={{0,4},{1,5},{2,6},{3,7},{4,0},{5,1},{6,2},{7,3},{8,12},{9,13},{10,... | collective-permute-start | bytes 49160 | tf_op jit(solution)/shard_map/ppermute | solution.py:52
  33.3 3.1 %collective-permute-start.9 = (f32[1,16,256]{2,1,0:T(8,128)S(1)}, f32[1,16,256]{2,1,0:T(8,128)S(1)}, u32[]{:S(2)}, u32[]{:S(2)}) collective-permute-start(f32[1,16,256]{2,1,0:T(8,128)S(1)} %get-tuple-element.59), channel_id=1, source_target_pairs={{0,1},{1,0},{2,3},{3,2},{4,8},{5,9},{6,10},{7,11},{8,4},{9,5},{10,... | collective-permute-start | bytes 49160 | tf_op jit(solution)/shard_map/ppermute | solution.py:52
  33.3 3.1 %collective-permute-start.11 = (f32[8,256]{1,0:T(8,128)S(1)}, f32[8,256]{1,0:T(8,128)S(1)}, u32[]{:S(2)}, u32[]{:S(2)}) collective-permute-start(f32[8,256]{1,0:T(8,128)S(1)} %get-tuple-element.60), channel_id=1, source_target_pairs={{0,3},{1,2},{2,1},{3,0},{4,7},{5,6},{6,5},{7,4},{8,11},{9,10},{10,... | collective-permute-start | bytes 24584 | tf_op jit(solution)/shard_map/ppermute | solution.py:52
  34.0 2.4 %collective-permute-start.10 = (f32[8,256]{1,0:T(8,128)S(1)}, f32[8,256]{1,0:T(8,128)S(1)}, u32[]{:S(2)}, u32[]{:S(2)}) collective-permute-start(f32[8,256]{1,0:T(8,128)S(1)} %get-tuple-element.60), channel_id=1, source_target_pairs={{0,1},{1,0},{2,3},{3,2},{4,5},{5,4},{6,7},{7,6},{8,9},{9,8},{10,11... | collective-permute-start | bytes 24584 | tf_op jit(solution)/shard_map/ppermute | solution.py:52
  38.0 3.7 %collective-permute-start.13 = (f32[8,256]{1,0:T(8,128)S(1)}, f32[8,256]{1,0:T(8,128)S(1)}, u32[]{:S(2)}, u32[]{:S(2)}) collective-permute-start(f32[8,256]{1,0:T(8,128)S(1)} %get-tuple-element.63), channel_id=1, source_target_pairs={{0,3},{1,2},{2,1},{3,0},{4,7},{5,6},{6,5},{7,4},{8,11},{9,10},{10,... | collective-permute-start | bytes 24584 | tf_op jit(solution)/shard_map/ppermute | solution.py:52
  38.7 3.0 %collective-permute-start.12 = (f32[8,256]{1,0:T(8,128)S(1)}, f32[8,256]{1,0:T(8,128)S(1)}, u32[]{:S(2)}, u32[]{:S(2)}) collective-permute-start(f32[8,256]{1,0:T(8,128)S(1)} %get-tuple-element.63), channel_id=1, source_target_pairs={{0,1},{1,0},{2,3},{3,2},{4,5},{5,4},{6,7},{7,6},{8,9},{9,8},{10,11... | collective-permute-start | bytes 24584 | tf_op jit(solution)/shard_map/ppermute | solution.py:52
  43.3 9.2 %collective-permute-start.14 = (f32[3,16,256]{2,1,0:T(8,128)S(1)}, f32[3,16,256]{2,1,0:T(8,128)S(1)}, u32[]{:S(2)}, u32[]{:S(2)}) collective-permute-start(f32[3,16,256]{2,1,0:T(8,128)S(1)} %get-tuple-element.66), channel_id=1, source_target_pairs={{0,16},{1,17},{2,18},{3,19},{4,20},{5,21},{6,22},{7,23},{8,24},{9,... | collective-permute-start | bytes 147464 | tf_op jit(solution)/shard_map/ppermute | solution.py:52
  43.8 8.6 %collective-permute-start.17 = (f32[3,16,256]{2,1,0:T(8,128)S(1)}, f32[3,16,256]{2,1,0:T(8,128)S(1)}, u32[]{:S(2)}, u32[]{:S(2)}) collective-permute-start(f32[3,16,256]{2,1,0:T(8,128)S(1)} %get-tuple-element.69), channel_id=1, source_target_pairs={{0,4},{1,5},{2,6},{3,7},{4,0},{5,1},{6,2},{7,3},{8,12},{9,13},{10,... | collective-permute-start | bytes 147464 | tf_op jit(solution)/shard_map/ppermute | solution.py:52
  46.6 5.9 %collective-permute-start.18 = (f32[3,16,256]{2,1,0:T(8,128)S(1)}, f32[3,16,256]{2,1,0:T(8,128)S(1)}, u32[]{:S(2)}, u32[]{:S(2)}) collective-permute-start(f32[3,16,256]{2,1,0:T(8,128)S(1)} %get-tuple-element.70), channel_id=1, source_target_pairs={{0,1},{1,0},{2,3},{3,2},{4,8},{5,9},{6,10},{7,11},{8,4},{9,5},{10,... | collective-permute-start | bytes 147464 | tf_op jit(solution)/shard_map/ppermute | solution.py:52
  46.6 5.8 %collective-permute-start.15 = (f32[8,256]{1,0:T(8,128)S(1)}, f32[8,256]{1,0:T(8,128)S(1)}, u32[]{:S(2)}, u32[]{:S(2)}) collective-permute-start(f32[8,256]{1,0:T(8,128)S(1)} %get-tuple-element.67), channel_id=1, source_target_pairs={{0,20},{1,21},{2,22},{3,23},{4,16},{5,17},{6,18},{7,19},{8,28},{9,... | collective-permute-start | bytes 24584 | tf_op jit(solution)/shard_map/ppermute | solution.py:52
  48.6 3.8 %collective-permute-start.16 = (f32[8,256]{1,0:T(8,128)S(1)}, f32[8,256]{1,0:T(8,128)S(1)}, u32[]{:S(2)}, u32[]{:S(2)}) collective-permute-start(f32[8,256]{1,0:T(8,128)S(1)} %get-tuple-element.68), channel_id=1, source_target_pairs={{0,1},{1,0},{2,3},{3,2},{4,24},{5,25},{6,26},{7,27},{8,20},{9,21},... | collective-permute-start | bytes 24584 | tf_op jit(solution)/shard_map/ppermute | solution.py:52
  48.6 11.0 %all-to-all-start.1 = ((f32[32,1,128]{2,1,0:T(1,128)}), f32[32,1,128]{2,1,0:T(1,128)S(1)}, u32[]{:S(2)}, u32[]{:S(2)}) async-start(f32[32,1,128]{2,1,0:T(1,128)} %bitcast.4), calls=%async_computation.1 | async-start | bytes 32768 | tf_op jit(solution)/shard_map/all_to_all | solution.py:590
  59.5 7.3 %copy-start = (f32[16,16,256]{2,1,0:T(8,128)S(1)}, f32[16,16,256]{2,1,0:T(8,128)}, u32[]{:S(2)}) copy-start(f32[16,16,256]{2,1,0:T(8,128)} %get-tuple-element.71.refs_5_.refs_3_.refs_7_) | copy-start | bytes 786436
  62.4 17.7 %copy-start.1 = (f32[16,16,256]{2,1,0:T(8,128)S(1)}, f32[16,16,256]{2,1,0:T(8,128)}, u32[]{:S(2)}) copy-start(f32[16,16,256]{2,1,0:T(8,128)} %get-tuple-element.77.refs_5_.refs_2_) | copy-start | bytes 786436
  62.4 4.2 %collective-permute-start.19 = (f32[1,16,256]{2,1,0:T(8,128)S(1)}, f32[1,16,256]{2,1,0:T(8,128)S(1)}, u32[]{:S(2)}, u32[]{:S(2)}) collective-permute-start(f32[1,16,256]{2,1,0:T(8,128)S(1)} %get-tuple-element.78), channel_id=1, source_target_pairs={{0,16},{1,17},{2,18},{3,19},{4,20},{5,21},{6,22},{7,23},{8,24},{9,... | collective-permute-start | bytes 49160 | tf_op jit(solution)/shard_map/ppermute | solution.py:52
  63.1 3.7 %collective-permute-start.20 = (f32[1,16,256]{2,1,0:T(8,128)S(1)}, f32[1,16,256]{2,1,0:T(8,128)S(1)}, u32[]{:S(2)}, u32[]{:S(2)}) collective-permute-start(f32[1,16,256]{2,1,0:T(8,128)S(1)} %get-tuple-element.79), channel_id=1, source_target_pairs={{0,4},{1,5},{2,6},{3,7},{4,0},{5,1},{6,2},{7,3},{8,12},{9,13},{10,... | collective-permute-start | bytes 49160 | tf_op jit(solution)/shard_map/ppermute | solution.py:52
  63.6 3.2 %collective-permute-start.21 = (f32[1,16,256]{2,1,0:T(8,128)S(1)}, f32[1,16,256]{2,1,0:T(8,128)S(1)}, u32[]{:S(2)}, u32[]{:S(2)}) collective-permute-start(f32[1,16,256]{2,1,0:T(8,128)S(1)} %get-tuple-element.80), channel_id=1, source_target_pairs={{0,1},{1,0},{2,3},{3,2},{4,8},{5,9},{6,10},{7,11},{8,4},{9,5},{10,... | collective-permute-start | bytes 49160 | tf_op jit(solution)/shard_map/ppermute | solution.py:52
  63.6 3.1 %collective-permute-start.23 = (f32[8,256]{1,0:T(8,128)S(1)}, f32[8,256]{1,0:T(8,128)S(1)}, u32[]{:S(2)}, u32[]{:S(2)}) collective-permute-start(f32[8,256]{1,0:T(8,128)S(1)} %get-tuple-element.81), channel_id=1, source_target_pairs={{0,3},{1,2},{2,1},{3,0},{4,7},{5,6},{6,5},{7,4},{8,11},{9,10},{10,... | collective-permute-start | bytes 24584 | tf_op jit(solution)/shard_map/ppermute | solution.py:52
  64.7 2.0 %collective-permute-start.22 = (f32[8,256]{1,0:T(8,128)S(1)}, f32[8,256]{1,0:T(8,128)S(1)}, u32[]{:S(2)}, u32[]{:S(2)}) collective-permute-start(f32[8,256]{1,0:T(8,128)S(1)} %get-tuple-element.81), channel_id=1, source_target_pairs={{0,1},{1,0},{2,3},{3,2},{4,5},{5,4},{6,7},{7,6},{8,9},{9,8},{10,11... | collective-permute-start | bytes 24584 | tf_op jit(solution)/shard_map/ppermute | solution.py:52

commit v4 on v3

--- a/solution.py
+++ b/solution.py
@@ -14,8 +14,10 @@
 LANES = 128
 VMEM_LIMIT = 24 * 1024 * 1024
 F32 = jnp.float32
-UNROLL = 4
-PARTS = 4
+UNROLL = 16
+PARTS = 8
+NEAR_FIRST = range(1)
+NEAR_SECOND = range(5)
 SMOOTH_FLOPS = 10**9
 
 
@@ -392,7 +394,7 @@
 def add_coarse(out, smooth, basis, weights):
     nx, ny, nz = out.shape
     k = 0
-    for piece in basis:
+    for piece in jax.tree.leaves(basis):
         vectors = piece.get()
         count = vectors.shape[0]
         scale = [jnp.broadcast_to(weights[k + i : k + i + 1, 0:1], (8, LANES)) for i in range(count)]
@@ -427,7 +429,7 @@
 
 
 class Far:
-    def __init__(self, value, parts=False):
+    def __init__(self, value, parts=None):
         self.value, self.parts = value, parts
 
 
@@ -463,7 +465,7 @@
     far = [i for i, a in enumerate(leaves) if isinstance(a, Far) and i not in raw]
     distant = [i for i, a in enumerate(out_leaves) if isinstance(a, Stored) and not a.near]
     stored = [i for i, a in enumerate(out_leaves) if isinstance(a, Stored)]
-    parts = [i for i in far if leaves[i].parts]
+    parts = {i: leaves[i].parts for i in far if leaves[i].parts is not None}
     leaves = [
         pltpu.with_memory_space_constraint(a.value, pltpu.HBM) if isinstance(a, Far) else a
         for a in leaves
@@ -478,7 +480,7 @@
         for n, i in enumerate(far):
             pieces = [(sources[i], rest[n])]
             if i in parts:
-                pieces = [(sources[i].at[p], rest[n].at[p]) for p in chunks(leaves[i].shape[0])]
+                pieces = [(sources[i].at[p], rest[n].at[p]) for p in chunks(leaves[i].shape[0], parts[i])]
             arrivals = []
             for source, target in pieces:
                 copy = pltpu.make_async_copy(source, target, sems.at[used])
@@ -498,7 +500,7 @@
         for i in stored:
             results[i].done()
 
-    n_sems = len(far) - len(parts) + len(stored) + len(parts) * PARTS
+    n_sems = len(far) - len(parts) + len(stored) + sum(len(p) for p in parts.values())
     size = sum(4 * math.prod(a.shape) for a in leaves + out_leaves)
     given = pl.pallas_call(
         body,
@@ -525,9 +527,9 @@
     return jax.tree.unflatten(out_tree, given)
 
 
-def chunks(count):
+def chunks(count, parts):
     each = count // PARTS
-    return [pl.ds(p * each, each) for p in range(PARTS)]
+    return [pl.ds(p * each, each) for p in parts]
 
 
 def far(tree):
@@ -624,25 +626,24 @@
         row = project(base, rhs.get()[...])
         out[...] = jnp.broadcast_to(row, out.shape)
 
-    rows = call(first_rows, row_shape, (Far(right_side), Far(basis, True)))
+    rows = call(first_rows, row_shape, (Far(right_side), Far(basis, range(PARTS))))
     rows_a = spread(rows)
 
     def pack_all(got_z, near, free, rows, outs, ends):
         cond, store, rhs = fetch(near)
         fields = [cond.at[0], cond.at[1], cond.at[2], store, free.get(), rhs]
         ends[...] = pick_z(fetch(got_z), sizes, ends_shape)
-        outs["ends"].put(ends)
-        pack_faces(outs["faces"], fields, sizes, 2, ends)
+        pack_faces(outs, fields, sizes, 2, ends)
 
     packed = call(
         pack_all,
-        {"ends": Stored(*ends_shape), "faces": face_shapes(shape, sizes, 6, 2)},
+        face_shapes(shape, sizes, 6, 2),
         (got_z, first["near"], first["free"], rows),
         [pltpu.VMEM(ends_shape, F32)],
     )
-    got = send_faces(packed["faces"], sizes)
-
-    def first_smooth(got, cond, store, fixed, rhs, ends, outs, sems, step, *boxes):
+    got = send_faces(packed, sizes)
+
+    def first_smooth(got, cond, store, fixed, rhs, got_z, base, outs, sems, step, *boxes):
         boxes = list(boxes)
         cond, store, rhs = fetch((cond, store, rhs))
         owns = [cond.at[0], cond.at[1], cond.at[2], store, None, rhs]
@@ -656,15 +657,17 @@
         for b in boxes[:6]:
             clear_round(b, shape)
         got, fixed = fetch((got, fixed))
+        ends = pick_z(fetch(got_z), sizes, ends_shape)
         boxes[4][3 : 3 + nx, 0:ny, 0:nz] = 1.0 - fixed[...].astype(F32)
-        unpack_faces(boxes[:6], [None] * 6, got["x"], got["y"], sizes, 2, ends.get()[...])
+        unpack_faces(boxes[:6], [None] * 6, got["x"], got["y"], sizes, 2, ends)
         unpack_xy(boxes[:6], shape, got["xy"], sizes)
         for copy in copies:
             copy.wait()
+        for target, piece in zip(outs["base"], chunks(vecs, NEAR_FIRST)):
+            target.put(base.get().at[piece])
         links, boxes = boxes[6:], boxes[:6]
         coefficients(boxes, links, step, outs["own"])
-        for name, value in (("step", step), ("own", outs["own"])):
-            outs["kept"][name].put(value)
+        outs["kept"]["step"].put(step)
         for kept, link in zip(outs["kept"]["links"], links):
             kept.put(link)
         jacobi(boxes[5], step, links, boxes[0], boxes[1], boxes[5], outs["smooth"])
@@ -674,25 +677,29 @@
         {
             "smooth": shaped(*shape),
             "own": shaped(7, *shape),
+            "base": [Stored(vecs // PARTS, *shape, near=True) for _ in NEAR_FIRST],
             "kept": {
                 "links": [Stored(*boxed), Stored(*boxed), Stored(*boxed)],
                 "step": Stored(*boxed),
-                "own": Stored(7, *shape),
             },
         },
         (
-            far(got),
+            got,
             Raw(conductance),
             Raw(storage),
             Far(dirichlet),
             Raw(right_side),
-            Far(packed["ends"]),
+            got_z,
+            Raw(basis),
         ),
         [pltpu.SemaphoreType.DMA((6,))] + [vbox] * 10,
         flops=SMOOTH_FLOPS,
     )
     kept = smoothed["kept"]
     own = smoothed["own"]
+
+    def base_rest(smoothed, near):
+        return smoothed["base"] + [Far(basis, range(len(near), PARTS))]
 
     def first_direction(smooth, rows, inverse, base, outs):
         smooth, rows = fetch((smooth, rows))
@@ -710,7 +717,7 @@
             "faces": face_shapes(shape, sizes, 1, 1),
             "tile": shaped(z_rows(1), nx * ny),
         },
-        (smoothed["smooth"], rows_a, Far(coarse_inverse), Far(basis, True)),
+        (smoothed["smooth"], rows_a, Far(coarse_inverse), base_rest(smoothed, NEAR_FIRST)),
     )
     direction, kept_z = directed["z"], directed["kept"]
     got = send_faces(directed["faces"], sizes)
@@ -737,6 +744,7 @@
 
     def first_image(got, got_z, field, own, rhs, outs, vb):
         image = outs["image"]
+        outs["own"].put(own.get())
         apply(field, got, got_z, own, image, vb)
         outs["kept"].put(image)
         outs["tile"][...] = pack_z([image])
@@ -749,6 +757,7 @@
         {
             "image": shaped(*shape),
             "kept": Stored(*shape),
+            "own": Stored(7, *shape),
             "tile": shaped(z_rows(1), nx * ny),
             "sums": shaped(1, LANES),
         },
@@ -761,53 +770,60 @@
         row = project(base, field.get()[...]) + sums.get()[...]
         out[...] = jnp.broadcast_to(row, out.shape)
 
-    rows = call(second_rows, row_shape, (Far(basis, True), imaged["image"], imaged["sums"]))
+    rows = call(second_rows, row_shape, (Far(basis, range(PARTS)), imaged["image"], imaged["sums"]))
     rows_c = spread(rows)
 
     def pack_image(got_z, field, rows, outs, ends):
         ends[...] = pick_z(fetch(got_z), sizes, ends_shape)
-        outs["ends"].put(ends)
-        pack_faces(outs["faces"], [field.get()], sizes, 2, ends)
+        pack_faces(outs, [field.get()], sizes, 2, ends)
 
     packed = call(
         pack_image,
-        {"ends": Stored(*ends_shape), "faces": face_shapes(shape, sizes, 1, 2)},
+        face_shapes(shape, sizes, 1, 2),
         (got_z, imaged["image"], rows),
         [pltpu.VMEM(ends_shape, F32)],
     )
-    got = send_faces(packed["faces"], sizes)
-
-    def second_smooth(got, field, ends, step, links, outs, sem, ga, gb, vb):
+    got = send_faces(packed, sizes)
+
+    def second_smooth(got, field, got_z, step, links, base, outs, sem, ga, gb, vb):
         copy = pltpu.make_async_copy(field.get(), own_cells(vb, shape), sem)
         copy.start()
         clear_round(vb, shape)
-        got, ends = fetch((got, ends))
-        unpack_faces([vb], [None], got["x"], got["y"], sizes, 2, ends[...])
+        got = fetch(got)
+        ends = pick_z(fetch(got_z), sizes, ends_shape)
+        unpack_faces([vb], [None], got["x"], got["y"], sizes, 2, ends)
         unpack_xy([vb], shape, got["xy"], sizes)
         copy.wait()
         step, links = fetch((step, links))
+        for target, piece in zip(outs["base"], chunks(vecs, NEAR_SECOND)):
+            target.put(base.get().at[piece])
         jacobi(vb, step, links, ga, gb, vb, outs["smooth"])
 
     smoothed = call(
         second_smooth,
-        {"smooth": shaped(*shape)},
+        {
+            "smooth": shaped(*shape),
+            "base": [Stored(vecs // PARTS, *shape, near=True) for _ in NEAR_SECOND],
+        },
         (
             got,
             Raw(imaged["kept"]),
-            Far(packed["ends"]),
+            got_z,
             Far(kept["step"]),
             far(kept["links"]),
+            Raw(basis),
         ),
         [pltpu.SemaphoreType.DMA] + [vbox] * 3,
         flops=SMOOTH_FLOPS,
     )
 
-    def second_direction(smooth, rows, inverse, field, rhs, before, base, outs):
+    def second_direction(smooth, rows, inverse, field, rhs, before, base, own, outs):
         smooth, rows = fetch((smooth, rows))
         norm, curve = scalar_sums(rows, vecs, 2)
         alpha = norm / curve
         weights = coarse_weights(inverse.get(), coarse_sum(rows, vecs))
         field, rhs, before = fetch((field, rhs, before))
+        outs["own"].put(own.get())
         outs["residual"][...] = rhs[...] - alpha * field[...]
         add_coarse(outs["z"], smooth, base, weights)
         outs["z"][...] = before[...] - alpha * outs["z"][...]
@@ -822,6 +838,7 @@
         {
             "z": shaped(*shape),
             "residual": shaped(*shape),
+            "own": Stored(7, *shape, near=True),
             "scalars": shaped(16, LANES),
             "faces": face_shapes(shape, sizes, 1, 1),
             "tile": shaped(z_rows(1), nx * ny),
@@ -833,7 +850,8 @@
             Far(imaged["kept"]),
             Far(right_side),
             Far(kept_z),
-            Far(basis, True),
+            base_rest(smoothed, NEAR_SECOND),
+            Raw(imaged["own"]),
         ),
     )
     precond, residual = directed["z"], directed["residual"]
@@ -859,7 +877,7 @@
             got,
             got_z,
             precond,
-            Far(kept["own"]),
+            directed["own"],
             image,
             residual,
         ),

time: 81.7 us -> 77.3 us (0.946)
  Pallas kernels: 31.7 us -> 27.6 us
  waiting for transfers between devices: 7.84 us -> 10.1 us
  starting transfers between devices: 28.9 us -> 27.3 us
    pallas_call x12, Pallas kernels: 31.7 us -> 27.6 us  [call(): pl.pallas_call(body, out_shape=[pltpu.HBM(a.shape, F32) if i in distant e...]
    all_to_all x2, waiting for transfers between devices: 3.18 us -> 5.09 us  [spread(): return lax.all_to_all(rows, AXES, 0, 0, tiled=True)]
    ppermute x24, starting transfers between devices: 22.3 us -> 20.7 us  [swap(): return lax.ppermute(value, AXES, pairs)]
  transfers between devices with their start and end apart: 26 -> 26, of which waited for: 6 -> 5; matrix products, arithmetic and copies ran while one was open for 0% -> 0% of each run, Pallas kernels for 20% -> 19%
where the time goes in v4:
time: 77.3 us; the launch traced here: 76.9 us
  Pallas kernels  27.6 us (36%)
  starting transfers between devices  27.3 us (35%)
  blocking collectives  11.1 us (14%)
  waiting for transfers between devices  10.1 us (13%)
  between operations  0.86 us (1%)
    pallas_call x12, Pallas kernels, call(): pl.pallas_call(body, out_shape=[pltpu.HBM(a.shape, F32) if i in distant e...  27.6 us
    ppermute x24, starting transfers between devices, swap(): return lax.ppermute(value, AXES, pairs)  20.7 us
    all_to_all x1, blocking collectives, spread(): return lax.all_to_all(rows, AXES, 0, 0, tiled=True)  11.1 us
    all_to_all x2, starting transfers between devices, spread(): return lax.all_to_all(rows, AXES, 0, 0, tiled=True)  6.61 us
    all_to_all x2, waiting for transfers between devices, spread(): return lax.all_to_all(rows, AXES, 0, 0, tiled=True)  5.09 us
    ppermute x24, waiting for transfers between devices, swap(): return lax.ppermute(value, AXES, pairs)  5 us
  transfers between devices with their start and end apart: 26, of which 5 were waited for; matrix products, arithmetic and copies ran while one was open for 0% of the time, Pallas kernels for 19%

profile of v4, /device:TPU:0, one launch (start us, length us, event | category | flops | bytes accessed | tf_op | source)
XLA Modules:
  0.0 76.9 jit_solution(13239683292725370547)
XLA Ops:
  0.6 1.7 %shard_map.77 = (f32[16,16,256]{2,1,0:T(8,128)S(1)}, f32[3,16,16,256]{3,2,1,0:T(8,128)S(1)}, f32[16,16,256]{2,1,0:T(8,128)S(1)}, f32[16,16,256]{2,1,0:T(8,128)S(1)}, f32[24,256]{1,0:T(8,128)S(1)}) custom-call(f32[3,16,16,256]{3,2,1,0:T(8,128)} %refs_5_.1, f32[16,16,256]{2,1,0:T(8,128)} %refs_6_.1, s32[16,16,256]{2,1,0:T(8,128)} %refs_7_.2, ...), custom_call_target="tpu_custom_call" | custom-call | bytes 3170304 | tf_op jit(solution)/shard_map/pallas_call | solution.py:505
  2.3 2.4 %collective-permute-start.1 = (f32[24,256]{1,0:T(8,128)S(1)}, f32[24,256]{1,0:T(8,128)S(1)}, u32[]{:S(2)}, u32[]{:S(2)}) collective-permute-start(f32[24,256]{1,0:T(8,128)S(1)} %get-tuple-element.51), channel_id=1, source_target_pairs={{0,3},{1,2},{2,1},{3,0},{4,7},{5,6},{6,5},{7,4},{8,11},{9,10},{10,... | collective-permute-start | bytes 73736 | tf_op jit(solution)/shard_map/ppermute | solution.py:54
  4.8 0.7 collective-permute-start
  5.5 3.0 %shard_map.78.refs_6_ = f32[32,128]{1,0:T(8,128)} custom-call(f32[16,16,256]{2,1,0:T(8,128)} %refs_4_.3, f32[16,16,16,256]{3,2,1,0:T(8,128)} %refs_11_.3), custom_call_target="tpu_custom_call" | custom-call | bytes 4472832 | tf_op jit(solution)/shard_map/pallas_call | solution.py:505
  8.5 0.0 collective-permute-done.1.refs_1_.refs_10_
  8.5 1.1 %shard_map.79 = (f32[13,16,256]{2,1,0:T(8,128)S(1)}, f32[28,256]{1,0:T(8,128)S(1)}, f32[28,256]{1,0:T(8,128)S(1)}, f32[13,16,256]{2,1,0:T(8,128)S(1)}, f32[13,16,256]{2,1,0:T(8,128)S(1)}) custom-call(f32[24,256]{1,0:T(8,128)S(1)} %collective-permute-done.refs_0_.refs_9_, f32[24,256]{1,0:T(8,128)S(1)} %collective-permute-done.1.refs_1_.refs_10_, ...), custom_call_target="tpu_custom_call" | custom-call | bytes 2334720 | tf_op jit(solution)/shard_map/pallas_call | solution.py:505
  9.7 1.6 %collective-permute-start.2 = (f32[13,16,256]{2,1,0:T(8,128)S(1)}, f32[13,16,256]{2,1,0:T(8,128)S(1)}, u32[]{:S(2)}, u32[]{:S(2)}) collective-permute-start(f32[13,16,256]{2,1,0:T(8,128)S(1)} %get-tuple-element.56), channel_id=1, source_target_pairs={{0,16},{1,17},{2,18},{3,19},{4,20},{5,21},{6,22},{7,23},{8,24},{9,... | collective-permute-start | bytes 638984 | tf_op jit(solution)/shard_map/ppermute | solution.py:54
  11.3 1.6 %collective-permute-start.5 = (f32[13,16,256]{2,1,0:T(8,128)S(1)}, f32[13,16,256]{2,1,0:T(8,128)S(1)}, u32[]{:S(2)}, u32[]{:S(2)}) collective-permute-start(f32[13,16,256]{2,1,0:T(8,128)S(1)} %get-tuple-element.59), channel_id=1, source_target_pairs={{0,4},{1,5},{2,6},{3,7},{4,0},{5,1},{6,2},{7,3},{8,12},{9,13},{10,... | collective-permute-start | bytes 638984 | tf_op jit(solution)/shard_map/ppermute | solution.py:54
  12.8 3.1 %collective-permute-start.3 = (f32[28,256]{1,0:T(8,128)S(1)}, f32[28,256]{1,0:T(8,128)S(1)}, u32[]{:S(2)}, u32[]{:S(2)}) collective-permute-start(f32[28,256]{1,0:T(8,128)S(1)} %get-tuple-element.57), channel_id=1, source_target_pairs={{0,20},{1,21},{2,22},{3,23},{4,16},{5,17},{6,18},{7,19},{8,28},{9,... | collective-permute-start | bytes 86024 | tf_op jit(solution)/shard_map/ppermute | solution.py:54
  15.9 0.0 collective-permute-start.4
  15.9 2.8 %all-to-all-start = ((f32[32,1,128]{2,1,0:T(1,128)}), f32[32,1,128]{2,1,0:T(1,128)S(1)}, u32[]{:S(2)}, u32[]{:S(2)}) async-start(f32[32,1,128]{2,1,0:T(1,128)} %bitcast.1), calls=%async_computation | async-start | bytes 32768 | tf_op jit(solution)/shard_map/all_to_all | solution.py:592
  18.7 0.0 collective-permute-done.3.refs_1_
  18.8 0.0 collective-permute-done.4.refs_2_
  18.8 0.0 collective-permute-done.2.refs_0_
  18.8 0.0 collective-permute-done.5.refs_3_
  18.8 0.0 collective-permute-done.6.refs_4_
  18.8 5.1 %shard_map.80 = (f32[2,16,16,256]{3,2,1,0:T(8,128)S(1)}, f32[22,24,384]{2,1,0:T(8,128)}, f32[22,24,384]{2,1,0:T(8,128)}, f32[22,24,384]{2,1,0:T(8,128)}, f32[22,...) custom-call(f32[13,16,256]{2,1,0:T(8,128)S(1)} %collective-permute-done.2.refs_0_, ...), custom_call_target="tpu_custom_call" | custom-call | flops 1000000000 | bytes 12378112 | tf_op jit(solution)/shard_map/pallas_call | solution.py:505
  24.0 1.8 %all-to-all-done = f32[32,1,128]{2,1,0:T(1,128)S(1)} async-done(((f32[32,1,128]{2,1,0:T(1,128)}), f32[32,1,128]{2,1,0:T(1,128)S(1)}, u32[]{:S(2)}, u32[]{:S(2)}) %all-to-all-start) | async-done | bytes 16416 | tf_op jit(solution)/shard_map/all_to_all | solution.py:592
  25.8 2.8 %shard_map.81 = (f32[1,16,256]{2,1,0:T(8,128)S(1)}, f32[1,16,256]{2,1,0:T(8,128)S(1)}, f32[1,16,256]{2,1,0:T(8,128)S(1)}, f32[16,16,256]{2,1,0:T(8,128)}, f32[8,...) custom-call(f32[16,16,256]{2,1,0:T(8,128)S(1)} %get-tuple-element.61.refs_0_, f32[32,128]{1,0:T(8,128)S(1)} %bitcast.13, ...), custom_call_target="tpu_custom_call" | custom-call | bytes 5611520 | tf_op jit(solution)/shard_map/pallas_call | solution.py:505
  28.6 0.7 collective-permute-start.7
  29.3 2.1 %collective-permute-start.8 = (f32[1,16,256]{2,1,0:T(8,128)S(1)}, f32[1,16,256]{2,1,0:T(8,128)S(1)}, u32[]{:S(2)}, u32[]{:S(2)}) collective-permute-start(f32[1,16,256]{2,1,0:T(8,128)S(1)} %get-tuple-element.64), channel_id=1, source_target_pairs={{0,4},{1,5},{2,6},{3,7},{4,0},{5,1},{6,2},{7,3},{8,12},{9,13},{10,... | collective-permute-start | bytes 49160 | tf_op jit(solution)/shard_map/ppermute | solution.py:54
  31.3 0.6 collective-permute-start.11
  32.0 0.0 collective-permute-start.10
  32.0 2.4 %collective-permute-done.11.refs_4_ = f32[8,256]{1,0:T(8,128)S(1)} collective-permute-done((f32[8,256]{1,0:T(8,128)S(1)}, f32[8,256]{1,0:T(8,128)S(1)}, u32[]{:S(2)}, u32[]{:S(2)}) %collective-permute-start.11) | collective-permute-done | bytes 8224 | tf_op jit(solution)/shard_map/ppermute | solution.py:54
  34.4 0.0 collective-permute-done.9.refs_2_
  34.4 1.3 %shard_map.82 = (f32[16,16,256]{2,1,0:T(8,128)S(1)}, f32[16,16,256]{2,1,0:T(8,128)}, f32[7,16,16,256]{3,2,1,0:T(8,128)}, f32[1,128]{1,0:T(1,128)S(1)}, f32[8,256]{1,0:T(8,128)S(1)}) custom-call(f32[1,16,256]{2,1,0:T(8,128)S(1)} %collective-permute-done.7.refs_0_, f32[1,16,256]{2,1,0:T(8,128)S(1)} %collective-permute-done.8.refs_1_, ...), custom_call_target="tpu_custom_call" | custom-call | bytes 4792832 | tf_op jit(solution)/shard_map/pallas_call | solution.py:505
  35.8 0.7 collective-permute-start.13
  36.5 0.0 collective-permute-start.12
  36.5 3.0 %shard_map.83.refs_3_ = f32[32,128]{1,0:T(8,128)} custom-call(f32[16,16,16,256]{3,2,1,0:T(8,128)} %refs_11_.3, f32[16,16,256]{2,1,0:T(8,128)S(1)} %get-tuple-element.70.refs_1_.refs_2_, f32[1,128]{1,0:T(1,128)S(1)} %get-tuple-element.71.refs_2_), custom_call_target="tpu_custom_call" | custom-call | bytes 4473344 | tf_op jit(solution)/shard_map/pallas_call | solution.py:505
  39.5 0.0 collective-permute-done.12.refs_0_.refs_6_
  39.5 1.0 %shard_map.84 = (f32[3,16,256]{2,1,0:T(8,128)S(1)}, f32[8,256]{1,0:T(8,128)S(1)}, f32[8,256]{1,0:T(8,128)S(1)}, f32[3,16,256]{2,1,0:T(8,128)S(1)}, f32[3,16,256]{2,1,0:T(8,128)S(1)}) custom-call(f32[8,256]{1,0:T(8,128)S(1)} %collective-permute-done.12.refs_0_.refs_6_, f32[8,256]{1,0:T(8,128)S(1)} %collective-permute-done.13.refs_1_.refs_7_, ...), custom_call_target="tpu_custom_call" | custom-call | bytes 458752 | tf_op jit(solution)/shard_map/pallas_call | solution.py:505
  40.5 0.5 collective-permute-start.14
  41.0 2.8 %collective-permute-start.17 = (f32[3,16,256]{2,1,0:T(8,128)S(1)}, f32[3,16,256]{2,1,0:T(8,128)S(1)}, u32[]{:S(2)}, u32[]{:S(2)}) collective-permute-start(f32[3,16,256]{2,1,0:T(8,128)S(1)} %get-tuple-element.75), channel_id=1, source_target_pairs={{0,4},{1,5},{2,6},{3,7},{4,0},{5,1},{6,2},{7,3},{8,12},{9,13},{10,... | collective-permute-start | bytes 147464 | tf_op jit(solution)/shard_map/ppermute | solution.py:54
  43.8 2.0 %collective-permute-start.15 = (f32[8,256]{1,0:T(8,128)S(1)}, f32[8,256]{1,0:T(8,128)S(1)}, u32[]{:S(2)}, u32[]{:S(2)}) collective-permute-start(f32[8,256]{1,0:T(8,128)S(1)} %get-tuple-element.73), channel_id=1, source_target_pairs={{0,20},{1,21},{2,22},{3,23},{4,16},{5,17},{6,18},{7,19},{8,28},{9,... | collective-permute-start | bytes 24584 | tf_op jit(solution)/shard_map/ppermute | solution.py:54
  45.8 3.8 %all-to-all-start.1 = ((f32[32,1,128]{2,1,0:T(1,128)}), f32[32,1,128]{2,1,0:T(1,128)S(1)}, u32[]{:S(2)}, u32[]{:S(2)}) async-start(f32[32,1,128]{2,1,0:T(1,128)} %bitcast.4), calls=%async_computation.1 | async-start | bytes 32768 | tf_op jit(solution)/shard_map/all_to_all | solution.py:592
  49.6 3.8 %shard_map.85 = (f32[2,16,16,256]{3,2,1,0:T(8,128)S(1)}, f32[2,16,16,256]{3,2,1,0:T(8,128)S(1)}, f32[2,16,16,256]{3,2,1,0:T(8,128)S(1)}, f32[2,16,16,256]{3,2,1,...) custom-call(f32[3,16,256]{2,1,0:T(8,128)S(1)} %collective-permute-done.14.refs_0_, ...), custom_call_target="tpu_custom_call" | custom-call | flops 1000000000 | bytes 10764288 | tf_op jit(solution)/shard_map/pallas_call | solution.py:505
  53.5 3.2 %all-to-all-done.1 = f32[32,1,128]{2,1,0:T(1,128)S(1)} async-done(((f32[32,1,128]{2,1,0:T(1,128)}), f32[32,1,128]{2,1,0:T(1,128)S(1)}, u32[]{:S(2)}, u32[]{:S(2)}) %all-to-all-start.1) | async-done | bytes 16416 | tf_op jit(solution)/shard_map/all_to_all | solution.py:592
  56.7 2.9 %shard_map.86 = (f32[1,16,256]{2,1,0:T(8,128)S(1)}, f32[1,16,256]{2,1,0:T(8,128)S(1)}, f32[1,16,256]{2,1,0:T(8,128)S(1)}, f32[7,16,16,256]{3,2,1,0:T(8,128)S(1)}...) custom-call(f32[16,16,256]{2,1,0:T(8,128)S(1)} %get-tuple-element.82.re, ...), custom_call_target="tpu_custom_call" | custom-call | bytes 12173312 | tf_op jit(solution)/shard_map/pallas_call | solution.py:505
  59.6 0.0 copy-start.1
  59.6 0.7 collective-permute-start.19
  60.3 0.5 collective-permute-start.20
  60.8 0.7 collective-permute-start.23
  61.5 0.0 collective-permute-start.22
  61.5 2.3 %collective-permute-done.23.refs_4_ = f32[8,256]{1,0:T(8,128)S(1)} collective-permute-done((f32[8,256]{1,0:T(8,128)S(1)}, f32[8,256]{1,0:T(8,128)S(1)}, u32[]{:S(2)}, u32[]{:S(2)}) %collective-permute-start.23) | collective-permute-done | bytes 8224 | tf_op jit(solution)/shard_map/ppermute | solution.py:54
  63.9 0.1 collective-permute-done.20.refs_1_
  64.0 0.7 shard_map.87
  64.7 11.1 %all_to_all.33 = f32[32,1,128]{2,1,0:T(1,128)S(1)} all-to-all(f32[32,1,128]{2,1,0:T(1,128)S(1)} %bitcast.15), channel_id=1, replica_groups=mesh['gx'=2,'gy'=4,'gz'=4] {'gx','gy','gz'}, dimensions={0} | all-to-all | bytes 32768 | tf_op jit(solution)/shard_map/all_to_all | solution.py:592
  75.8 1.1 %shard_map.88 = (f32[16,16,256]{2,1,0:T(8,128)}, f32[16,16,256]{2,1,0:T(8,128)}) custom-call(f32[32,128]{1,0:T(8,128)S(1)} %bitcast.14, f32[16,128]{1,0:T(8,128)S(1)} %get-tuple-element.98.refs_1_, f32[16,16,256]{2,1,0:T(8,128)S(1)} %copy-done.1, f32[16,16,256]{2,1,0:T(8,128)S(1)} %copy-done, f32[16,16,256]{2,1,0:T(8,128)S(1)} %get-tuple-element.94.refs_5_.refs_4_, ...), custom_call_target="tpu_custom_call" | custom-call | bytes 1859584 | tf_op jit(solution)/shard_map/pallas_call | solution.py:505
  (21 shorter events, 0.1 us)
Async XLA Ops:
  2.3 6.2 %collective-permute-start.1 = (f32[24,256]{1,0:T(8,128)S(1)}, f32[24,256]{1,0:T(8,128)S(1)}, u32[]{:S(2)}, u32[]{:S(2)}) collective-permute-start(f32[24,256]{1,0:T(8,128)S(1)} %get-tuple-element.51), channel_id=1, source_target_pairs={{0,3},{1,2},{2,1},{3,0},{4,7},{5,6},{6,5},{7,4},{8,11},{9,10},{10,... | collective-permute-start | bytes 73736 | tf_op jit(solution)/shard_map/ppermute | solution.py:54
  4.8 3.7 %collective-permute-start = (f32[24,256]{1,0:T(8,128)S(1)}, f32[24,256]{1,0:T(8,128)S(1)}, u32[]{:S(2)}, u32[]{:S(2)}) collective-permute-start(f32[24,256]{1,0:T(8,128)S(1)} %get-tuple-element.51), channel_id=1, source_target_pairs={{0,1},{1,0},{2,3},{3,2},{4,5},{5,4},{6,7},{7,6},{8,9},{9,8},{10,11... | collective-permute-start | bytes 73736 | tf_op jit(solution)/shard_map/ppermute | solution.py:54
  9.7 9.1 %collective-permute-start.2 = (f32[13,16,256]{2,1,0:T(8,128)S(1)}, f32[13,16,256]{2,1,0:T(8,128)S(1)}, u32[]{:S(2)}, u32[]{:S(2)}) collective-permute-start(f32[13,16,256]{2,1,0:T(8,128)S(1)} %get-tuple-element.56), channel_id=1, source_target_pairs={{0,16},{1,17},{2,18},{3,19},{4,20},{5,21},{6,22},{7,23},{8,24},{9,... | collective-permute-start | bytes 638984 | tf_op jit(solution)/shard_map/ppermute | solution.py:54
  11.3 7.5 %collective-permute-start.5 = (f32[13,16,256]{2,1,0:T(8,128)S(1)}, f32[13,16,256]{2,1,0:T(8,128)S(1)}, u32[]{:S(2)}, u32[]{:S(2)}) collective-permute-start(f32[13,16,256]{2,1,0:T(8,128)S(1)} %get-tuple-element.59), channel_id=1, source_target_pairs={{0,4},{1,5},{2,6},{3,7},{4,0},{5,1},{6,2},{7,3},{8,12},{9,13},{10,... | collective-permute-start | bytes 638984 | tf_op jit(solution)/shard_map/ppermute | solution.py:54
  12.8 6.0 %collective-permute-start.6 = (f32[13,16,256]{2,1,0:T(8,128)S(1)}, f32[13,16,256]{2,1,0:T(8,128)S(1)}, u32[]{:S(2)}, u32[]{:S(2)}) collective-permute-start(f32[13,16,256]{2,1,0:T(8,128)S(1)} %get-tuple-element.60), channel_id=1, source_target_pairs={{0,1},{1,0},{2,3},{3,2},{4,8},{5,9},{6,10},{7,11},{8,4},{9,5},{10,... | collective-permute-start | bytes 638984 | tf_op jit(solution)/shard_map/ppermute | solution.py:54
  12.8 5.9 %collective-permute-start.3 = (f32[28,256]{1,0:T(8,128)S(1)}, f32[28,256]{1,0:T(8,128)S(1)}, u32[]{:S(2)}, u32[]{:S(2)}) collective-permute-start(f32[28,256]{1,0:T(8,128)S(1)} %get-tuple-element.57), channel_id=1, source_target_pairs={{0,20},{1,21},{2,22},{3,23},{4,16},{5,17},{6,18},{7,19},{8,28},{9,... | collective-permute-start | bytes 86024 | tf_op jit(solution)/shard_map/ppermute | solution.py:54
  15.9 2.9 %collective-permute-start.4 = (f32[28,256]{1,0:T(8,128)S(1)}, f32[28,256]{1,0:T(8,128)S(1)}, u32[]{:S(2)}, u32[]{:S(2)}) collective-permute-start(f32[28,256]{1,0:T(8,128)S(1)} %get-tuple-element.58), channel_id=1, source_target_pairs={{0,1},{1,0},{2,3},{3,2},{4,24},{5,25},{6,26},{7,27},{8,20},{9,21},... | collective-permute-start | bytes 86024 | tf_op jit(solution)/shard_map/ppermute | solution.py:54
  15.9 9.9 %all-to-all-start = ((f32[32,1,128]{2,1,0:T(1,128)}), f32[32,1,128]{2,1,0:T(1,128)S(1)}, u32[]{:S(2)}, u32[]{:S(2)}) async-start(f32[32,1,128]{2,1,0:T(1,128)} %bitcast.1), calls=%async_computation | async-start | bytes 32768 | tf_op jit(solution)/shard_map/all_to_all | solution.py:592
  28.6 5.8 %collective-permute-start.7 = (f32[1,16,256]{2,1,0:T(8,128)S(1)}, f32[1,16,256]{2,1,0:T(8,128)S(1)}, u32[]{:S(2)}, u32[]{:S(2)}) collective-permute-start(f32[1,16,256]{2,1,0:T(8,128)S(1)} %get-tuple-element.63), channel_id=1, source_target_pairs={{0,16},{1,17},{2,18},{3,19},{4,20},{5,21},{6,22},{7,23},{8,24},{9,... | collective-permute-start | bytes 49160 | tf_op jit(solution)/shard_map/ppermute | solution.py:54
  29.3 5.1 %collective-permute-start.8 = (f32[1,16,256]{2,1,0:T(8,128)S(1)}, f32[1,16,256]{2,1,0:T(8,128)S(1)}, u32[]{:S(2)}, u32[]{:S(2)}) collective-permute-start(f32[1,16,256]{2,1,0:T(8,128)S(1)} %get-tuple-element.64), channel_id=1, source_target_pairs={{0,4},{1,5},{2,6},{3,7},{4,0},{5,1},{6,2},{7,3},{8,12},{9,13},{10,... | collective-permute-start | bytes 49160 | tf_op jit(solution)/shard_map/ppermute | solution.py:54
  31.3 3.1 %collective-permute-start.9 = (f32[1,16,256]{2,1,0:T(8,128)S(1)}, f32[1,16,256]{2,1,0:T(8,128)S(1)}, u32[]{:S(2)}, u32[]{:S(2)}) collective-permute-start(f32[1,16,256]{2,1,0:T(8,128)S(1)} %get-tuple-element.65), channel_id=1, source_target_pairs={{0,1},{1,0},{2,3},{3,2},{4,8},{5,9},{6,10},{7,11},{8,4},{9,5},{10,... | collective-permute-start | bytes 49160 | tf_op jit(solution)/shard_map/ppermute | solution.py:54
  31.3 3.1 %collective-permute-start.11 = (f32[8,256]{1,0:T(8,128)S(1)}, f32[8,256]{1,0:T(8,128)S(1)}, u32[]{:S(2)}, u32[]{:S(2)}) collective-permute-start(f32[8,256]{1,0:T(8,128)S(1)} %get-tuple-element.66), channel_id=1, source_target_pairs={{0,3},{1,2},{2,1},{3,0},{4,7},{5,6},{6,5},{7,4},{8,11},{9,10},{10,... | collective-permute-start | bytes 24584 | tf_op jit(solution)/shard_map/ppermute | solution.py:54
  32.0 2.4 %collective-permute-start.10 = (f32[8,256]{1,0:T(8,128)S(1)}, f32[8,256]{1,0:T(8,128)S(1)}, u32[]{:S(2)}, u32[]{:S(2)}) collective-permute-start(f32[8,256]{1,0:T(8,128)S(1)} %get-tuple-element.66), channel_id=1, source_target_pairs={{0,1},{1,0},{2,3},{3,2},{4,5},{5,4},{6,7},{7,6},{8,9},{9,8},{10,11... | collective-permute-start | bytes 24584 | tf_op jit(solution)/shard_map/ppermute | solution.py:54
  35.8 3.7 %collective-permute-start.13 = (f32[8,256]{1,0:T(8,128)S(1)}, f32[8,256]{1,0:T(8,128)S(1)}, u32[]{:S(2)}, u32[]{:S(2)}) collective-permute-start(f32[8,256]{1,0:T(8,128)S(1)} %get-tuple-element.69), channel_id=1, source_target_pairs={{0,3},{1,2},{2,1},{3,0},{4,7},{5,6},{6,5},{7,4},{8,11},{9,10},{10,... | collective-permute-start | bytes 24584 | tf_op jit(solution)/shard_map/ppermute | solution.py:54
  36.5 3.0 %collective-permute-start.12 = (f32[8,256]{1,0:T(8,128)S(1)}, f32[8,256]{1,0:T(8,128)S(1)}, u32[]{:S(2)}, u32[]{:S(2)}) collective-permute-start(f32[8,256]{1,0:T(8,128)S(1)} %get-tuple-element.69), channel_id=1, source_target_pairs={{0,1},{1,0},{2,3},{3,2},{4,5},{5,4},{6,7},{7,6},{8,9},{9,8},{10,11... | collective-permute-start | bytes 24584 | tf_op jit(solution)/shard_map/ppermute | solution.py:54
  40.5 9.1 %collective-permute-start.14 = (f32[3,16,256]{2,1,0:T(8,128)S(1)}, f32[3,16,256]{2,1,0:T(8,128)S(1)}, u32[]{:S(2)}, u32[]{:S(2)}) collective-permute-start(f32[3,16,256]{2,1,0:T(8,128)S(1)} %get-tuple-element.72), channel_id=1, source_target_pairs={{0,16},{1,17},{2,18},{3,19},{4,20},{5,21},{6,22},{7,23},{8,24},{9,... | collective-permute-start | bytes 147464 | tf_op jit(solution)/shard_map/ppermute | solution.py:54
  41.0 8.6 %collective-permute-start.17 = (f32[3,16,256]{2,1,0:T(8,128)S(1)}, f32[3,16,256]{2,1,0:T(8,128)S(1)}, u32[]{:S(2)}, u32[]{:S(2)}) collective-permute-start(f32[3,16,256]{2,1,0:T(8,128)S(1)} %get-tuple-element.75), channel_id=1, source_target_pairs={{0,4},{1,5},{2,6},{3,7},{4,0},{5,1},{6,2},{7,3},{8,12},{9,13},{10,... | collective-permute-start | bytes 147464 | tf_op jit(solution)/shard_map/ppermute | solution.py:54
  43.8 5.9 %collective-permute-start.18 = (f32[3,16,256]{2,1,0:T(8,128)S(1)}, f32[3,16,256]{2,1,0:T(8,128)S(1)}, u32[]{:S(2)}, u32[]{:S(2)}) collective-permute-start(f32[3,16,256]{2,1,0:T(8,128)S(1)} %get-tuple-element.76), channel_id=1, source_target_pairs={{0,1},{1,0},{2,3},{3,2},{4,8},{5,9},{6,10},{7,11},{8,4},{9,5},{10,... | collective-permute-start | bytes 147464 | tf_op jit(solution)/shard_map/ppermute | solution.py:54
  43.8 5.8 %collective-permute-start.15 = (f32[8,256]{1,0:T(8,128)S(1)}, f32[8,256]{1,0:T(8,128)S(1)}, u32[]{:S(2)}, u32[]{:S(2)}) collective-permute-start(f32[8,256]{1,0:T(8,128)S(1)} %get-tuple-element.73), channel_id=1, source_target_pairs={{0,20},{1,21},{2,22},{3,23},{4,16},{5,17},{6,18},{7,19},{8,28},{9,... | collective-permute-start | bytes 24584 | tf_op jit(solution)/shard_map/ppermute | solution.py:54
  45.8 3.8 %collective-permute-start.16 = (f32[8,256]{1,0:T(8,128)S(1)}, f32[8,256]{1,0:T(8,128)S(1)}, u32[]{:S(2)}, u32[]{:S(2)}) collective-permute-start(f32[8,256]{1,0:T(8,128)S(1)} %get-tuple-element.74), channel_id=1, source_target_pairs={{0,1},{1,0},{2,3},{3,2},{4,24},{5,25},{6,26},{7,27},{8,20},{9,21},... | collective-permute-start | bytes 24584 | tf_op jit(solution)/shard_map/ppermute | solution.py:54
  45.8 11.0 %all-to-all-start.1 = ((f32[32,1,128]{2,1,0:T(1,128)}), f32[32,1,128]{2,1,0:T(1,128)S(1)}, u32[]{:S(2)}, u32[]{:S(2)}) async-start(f32[32,1,128]{2,1,0:T(1,128)} %bitcast.4), calls=%async_computation.1 | async-start | bytes 32768 | tf_op jit(solution)/shard_map/all_to_all | solution.py:592
  56.7 7.3 %copy-start = (f32[16,16,256]{2,1,0:T(8,128)S(1)}, f32[16,16,256]{2,1,0:T(8,128)}, u32[]{:S(2)}) copy-start(f32[16,16,256]{2,1,0:T(8,128)} %get-tuple-element.77.refs_5_.refs_3_.refs_7_) | copy-start | bytes 786436
  59.6 16.2 %copy-start.1 = (f32[16,16,256]{2,1,0:T(8,128)S(1)}, f32[16,16,256]{2,1,0:T(8,128)}, u32[]{:S(2)}) copy-start(f32[16,16,256]{2,1,0:T(8,128)} %get-tuple-element.83.refs_5_.refs_2_) | copy-start | bytes 786436
  59.6 4.2 %collective-permute-start.19 = (f32[1,16,256]{2,1,0:T(8,128)S(1)}, f32[1,16,256]{2,1,0:T(8,128)S(1)}, u32[]{:S(2)}, u32[]{:S(2)}) collective-permute-start(f32[1,16,256]{2,1,0:T(8,128)S(1)} %get-tuple-element.90), channel_id=1, source_target_pairs={{0,16},{1,17},{2,18},{3,19},{4,20},{5,21},{6,22},{7,23},{8,24},{9,... | collective-permute-start | bytes 49160 | tf_op jit(solution)/shard_map/ppermute | solution.py:54
  60.3 3.7 %collective-permute-start.20 = (f32[1,16,256]{2,1,0:T(8,128)S(1)}, f32[1,16,256]{2,1,0:T(8,128)S(1)}, u32[]{:S(2)}, u32[]{:S(2)}) collective-permute-start(f32[1,16,256]{2,1,0:T(8,128)S(1)} %get-tuple-element.91), channel_id=1, source_target_pairs={{0,4},{1,5},{2,6},{3,7},{4,0},{5,1},{6,2},{7,3},{8,12},{9,13},{10,... | collective-permute-start | bytes 49160 | tf_op jit(solution)/shard_map/ppermute | solution.py:54
  60.8 3.2 %collective-permute-start.21 = (f32[1,16,256]{2,1,0:T(8,128)S(1)}, f32[1,16,256]{2,1,0:T(8,128)S(1)}, u32[]{:S(2)}, u32[]{:S(2)}) collective-permute-start(f32[1,16,256]{2,1,0:T(8,128)S(1)} %get-tuple-element.92), channel_id=1, source_target_pairs={{0,1},{1,0},{2,3},{3,2},{4,8},{5,9},{6,10},{7,11},{8,4},{9,5},{10,... | collective-permute-start | bytes 49160 | tf_op jit(solution)/shard_map/ppermute | solution.py:54
  60.8 3.1 %collective-permute-start.23 = (f32[8,256]{1,0:T(8,128)S(1)}, f32[8,256]{1,0:T(8,128)S(1)}, u32[]{:S(2)}, u32[]{:S(2)}) collective-permute-start(f32[8,256]{1,0:T(8,128)S(1)} %get-tuple-element.93), channel_id=1, source_target_pairs={{0,3},{1,2},{2,1},{3,0},{4,7},{5,6},{6,5},{7,4},{8,11},{9,10},{10,... | collective-permute-start | bytes 24584 | tf_op jit(solution)/shard_map/ppermute | solution.py:54
  61.5 2.3 %collective-permute-start.22 = (f32[8,256]{1,0:T(8,128)S(1)}, f32[8,256]{1,0:T(8,128)S(1)}, u32[]{:S(2)}, u32[]{:S(2)}) collective-permute-start(f32[8,256]{1,0:T(8,128)S(1)} %get-tuple-element.93), channel_id=1, source_target_pairs={{0,1},{1,0},{2,3},{3,2},{4,5},{5,4},{6,7},{7,6},{8,9},{9,8},{10,11... | collective-permute-start | bytes 24584 | tf_op jit(solution)/shard_map/ppermute | solution.py:54

commit v5 on v4

--- a/solution.py
+++ b/solution.py
@@ -15,6 +15,7 @@
 VMEM_LIMIT = 24 * 1024 * 1024
 F32 = jnp.float32
 UNROLL = 16
+SWEEP_UNROLL = True
 PARTS = 8
 NEAR_FIRST = range(1)
 NEAR_SECOND = range(5)
@@ -281,16 +282,6 @@
 
 def behind(plane, axis):
     return pltpu.roll(plane, 1, axis)
-
-
-def neighbours(g, links, x):
-    lx, ly, lz = links
-    mid = g[x]
-    y = ly[x]
-    z = lz[x]
-    total = lx[x] * g[x + 1] + lx[x - 1] * g[x - 1]
-    total = total + y * ahead(mid, 0) + behind(y * mid, 0)
-    return total + z * ahead(mid, 1) + behind(z * mid, 1)
 
 
 def coefficients(fields, links, step, own):
@@ -344,25 +335,40 @@
 
     loop(1, planes - 1, first)
 
-    def swept(now, x):
-        return (1.0 - RELAX) * now[x] + source[x] + step[x] * neighbours(now, links, x)
+    lx, ly, lz = fetch(links)
+
+    def swept(now, x, carry):
+        before, mid, x_before = carry
+        after, x_here, y, z = now[x + 1], lx[x], ly[x], lz[x]
+        total = x_here * after + x_before * before
+        total = total + y * ahead(mid, 0) + behind(y * mid, 0)
+        total = total + z * ahead(mid, 1) + behind(z * mid, 1)
+        value = (1.0 - RELAX) * mid + source[x] + step[x] * total
+        return value, (mid, after, x_here)
+
+    def sweep_planes(now, first, last, put):
+        def body(x, carry):
+            value, carry = swept(now, x, carry)
+            put(x, value)
+            return carry
+
+        start = (now[first - 1], now[first], lx[first - 1])
+        lax.fori_loop(first, last, body, start, unroll=SWEEP_UNROLL)
 
     now, then, spare = source, ga, gb
     for sweep in range(1, SWEEPS - 1):
         edge = max(1, 3 - (SWEEPS - 1 - sweep))
 
-        def body(x, carry, now=now, then=then):
-            then[x] = swept(now, x)
-            return carry
-
-        loop(edge, planes - edge, body)
+        def put(x, value, then=then):
+            then[x] = value
+
+        sweep_planes(now, edge, planes - edge, put)
         now, then, spare = then, spare, then
 
-    def final(x, carry):
-        out[x] = swept(now, x + 3)[0:ny, 0:nz]
-        return carry
-
-    loop(0, nx, final)
+    def put_own(x, value):
+        out[x - 3] = value[0:ny, 0:nz]
+
+    sweep_planes(now, 3, 3 + nx, put_own)
 
 
 def coarse_sum(rows_ref, vecs):
@@ -537,7 +543,11 @@
 
 
 def fetch(tree):
-    return jax.tree.map(lambda one: one.get(), tree, is_leaf=lambda one: isinstance(one, Arriving))
+    return jax.tree.map(
+        lambda one: one.get() if isinstance(one, Arriving) else one,
+        tree,
+        is_leaf=lambda one: isinstance(one, Arriving),
+    )
 
 
 def loop(first, last, body):
@@ -770,7 +780,7 @@
         row = project(base, field.get()[...]) + sums.get()[...]
         out[...] = jnp.broadcast_to(row, out.shape)
 
-    rows = call(second_rows, row_shape, (Far(basis, range(PARTS)), imaged["image"], imaged["sums"]))
+    rows = call(second_rows, row_shape, ([basis], imaged["image"], imaged["sums"]))
     rows_c = spread(rows)
 
     def pack_image(got_z, field, rows, outs, ends):
@@ -794,10 +804,9 @@
         unpack_faces([vb], [None], got["x"], got["y"], sizes, 2, ends)
         unpack_xy([vb], shape, got["xy"], sizes)
         copy.wait()
-        step, links = fetch((step, links))
         for target, piece in zip(outs["base"], chunks(vecs, NEAR_SECOND)):
             target.put(base.get().at[piece])
-        jacobi(vb, step, links, ga, gb, vb, outs["smooth"])
+        jacobi(vb, step.get(), links, ga, gb, vb, outs["smooth"])
 
     smoothed = call(
         second_smooth,
@@ -817,13 +826,12 @@
         flops=SMOOTH_FLOPS,
     )
 
-    def second_direction(smooth, rows, inverse, field, rhs, before, base, own, outs):
+    def second_direction(smooth, rows, inverse, field, rhs, before, base, outs):
         smooth, rows = fetch((smooth, rows))
         norm, curve = scalar_sums(rows, vecs, 2)
         alpha = norm / curve
         weights = coarse_weights(inverse.get(), coarse_sum(rows, vecs))
         field, rhs, before = fetch((field, rhs, before))
-        outs["own"].put(own.get())
         outs["residual"][...] = rhs[...] - alpha * field[...]
         add_coarse(outs["z"], smooth, base, weights)
         outs["z"][...] = before[...] - alpha * outs["z"][...]
@@ -838,7 +846,6 @@
         {
             "z": shaped(*shape),
             "residual": shaped(*shape),
-            "own": Stored(7, *shape, near=True),
             "scalars": shaped(16, LANES),
             "faces": face_shapes(shape, sizes, 1, 1),
             "tile": shaped(z_rows(1), nx * ny),
@@ -851,7 +858,6 @@
             Far(right_side),
             Far(kept_z),
             base_rest(smoothed, NEAR_SECOND),
-            Raw(imaged["own"]),
         ),
     )
     precond, residual = directed["z"], directed["residual"]
@@ -877,7 +883,7 @@
             got,
             got_z,
             precond,
-            directed["own"],
+            imaged["own"],
             image,
             residual,
         ),

time: 77.3 us -> 75.9 us (0.982)
  Pallas kernels: 27.6 us -> 24.9 us
  waiting for transfers between devices: 10.1 us -> 11.6 us
    pallas_call x12, Pallas kernels: 27.6 us -> 24.9 us  [call(): pl.pallas_call(body, out_shape=[pltpu.HBM(a.shape, F32) if i in distant e...]
    ppermute x24, waiting for transfers between devices: 5 us -> 6.26 us  [swap(): return lax.ppermute(value, AXES, pairs)]
  transfers between devices with their start and end apart: 26 -> 26, of which waited for: 5 -> 6; matrix products, arithmetic and copies ran while one was open for 0% -> 0% of each run, Pallas kernels for 19% -> 17%
where the time goes in v5:
time: 75.9 us; the launch traced here: 75.5 us
  starting transfers between devices  27 us (36%)
  Pallas kernels  24.9 us (33%)
  waiting for transfers between devices  11.6 us (15%)
  blocking collectives  11.1 us (15%)
  between operations  0.85 us (1%)
    pallas_call x12, Pallas kernels, call(): pl.pallas_call(body, out_shape=[pltpu.HBM(a.shape, F32) if i in distant e...  24.9 us
    ppermute x24, starting transfers between devices, swap(): return lax.ppermute(value, AXES, pairs)  20.5 us
    all_to_all x1, blocking collectives, spread(): return lax.all_to_all(rows, AXES, 0, 0, tiled=True)  11.1 us
    all_to_all x2, starting transfers between devices, spread(): return lax.all_to_all(rows, AXES, 0, 0, tiled=True)  6.48 us
    ppermute x24, waiting for transfers between devices, swap(): return lax.ppermute(value, AXES, pairs)  6.26 us
    all_to_all x2, waiting for transfers between devices, spread(): return lax.all_to_all(rows, AXES, 0, 0, tiled=True)  5.36 us
  transfers between devices with their start and end apart: 26, of which 6 were waited for; matrix products, arithmetic and copies ran while one was open for 0% of the time, Pallas kernels for 17%

profile of v5, /device:TPU:0, one launch (start us, length us, event | category | flops | bytes accessed | tf_op | source)
XLA Modules:
  0.0 75.5 jit_solution(13449754712459752067)
XLA Ops:
  0.6 1.7 %shard_map.77 = (f32[16,16,256]{2,1,0:T(8,128)S(1)}, f32[3,16,16,256]{3,2,1,0:T(8,128)S(1)}, f32[16,16,256]{2,1,0:T(8,128)S(1)}, f32[16,16,256]{2,1,0:T(8,128)S(1)}, f32[24,256]{1,0:T(8,128)S(1)}) custom-call(f32[3,16,16,256]{3,2,1,0:T(8,128)} %refs_5_.1, f32[16,16,256]{2,1,0:T(8,128)} %refs_6_.1, s32[16,16,256]{2,1,0:T(8,128)} %refs_7_.2, ...), custom_call_target="tpu_custom_call" | custom-call | bytes 3170304 | tf_op jit(solution)/shard_map/pallas_call | solution.py:511
  2.3 2.4 %collective-permute-start.1 = (f32[24,256]{1,0:T(8,128)S(1)}, f32[24,256]{1,0:T(8,128)S(1)}, u32[]{:S(2)}, u32[]{:S(2)}) collective-permute-start(f32[24,256]{1,0:T(8,128)S(1)} %get-tuple-element.50), channel_id=1, source_target_pairs={{0,3},{1,2},{2,1},{3,0},{4,7},{5,6},{6,5},{7,4},{8,11},{9,10},{10,... | collective-permute-start | bytes 73736 | tf_op jit(solution)/shard_map/ppermute | solution.py:55
  4.8 0.7 collective-permute-start
  5.5 3.0 %shard_map.78.refs_6_ = f32[32,128]{1,0:T(8,128)} custom-call(f32[16,16,256]{2,1,0:T(8,128)} %refs_4_.3, f32[16,16,16,256]{3,2,1,0:T(8,128)} %refs_11_.3), custom_call_target="tpu_custom_call" | custom-call | bytes 4472832 | tf_op jit(solution)/shard_map/pallas_call | solution.py:511
  8.5 0.0 collective-permute-done.1.refs_1_.refs_10_
  8.5 1.1 %shard_map.79 = (f32[13,16,256]{2,1,0:T(8,128)S(1)}, f32[28,256]{1,0:T(8,128)S(1)}, f32[28,256]{1,0:T(8,128)S(1)}, f32[13,16,256]{2,1,0:T(8,128)S(1)}, f32[13,16,256]{2,1,0:T(8,128)S(1)}) custom-call(f32[24,256]{1,0:T(8,128)S(1)} %collective-permute-done.refs_0_.refs_9_, f32[24,256]{1,0:T(8,128)S(1)} %collective-permute-done.1.refs_1_.refs_10_, ...), custom_call_target="tpu_custom_call" | custom-call | bytes 2334720 | tf_op jit(solution)/shard_map/pallas_call | solution.py:511
  9.7 1.6 %collective-permute-start.2 = (f32[13,16,256]{2,1,0:T(8,128)S(1)}, f32[13,16,256]{2,1,0:T(8,128)S(1)}, u32[]{:S(2)}, u32[]{:S(2)}) collective-permute-start(f32[13,16,256]{2,1,0:T(8,128)S(1)} %get-tuple-element.55), channel_id=1, source_target_pairs={{0,16},{1,17},{2,18},{3,19},{4,20},{5,21},{6,22},{7,23},{8,24},{9,... | collective-permute-start | bytes 638984 | tf_op jit(solution)/shard_map/ppermute | solution.py:55
  11.3 1.6 %collective-permute-start.5 = (f32[13,16,256]{2,1,0:T(8,128)S(1)}, f32[13,16,256]{2,1,0:T(8,128)S(1)}, u32[]{:S(2)}, u32[]{:S(2)}) collective-permute-start(f32[13,16,256]{2,1,0:T(8,128)S(1)} %get-tuple-element.58), channel_id=1, source_target_pairs={{0,4},{1,5},{2,6},{3,7},{4,0},{5,1},{6,2},{7,3},{8,12},{9,13},{10,... | collective-permute-start | bytes 638984 | tf_op jit(solution)/shard_map/ppermute | solution.py:55
  12.8 3.1 %collective-permute-start.3 = (f32[28,256]{1,0:T(8,128)S(1)}, f32[28,256]{1,0:T(8,128)S(1)}, u32[]{:S(2)}, u32[]{:S(2)}) collective-permute-start(f32[28,256]{1,0:T(8,128)S(1)} %get-tuple-element.56), channel_id=1, source_target_pairs={{0,20},{1,21},{2,22},{3,23},{4,16},{5,17},{6,18},{7,19},{8,28},{9,... | collective-permute-start | bytes 86024 | tf_op jit(solution)/shard_map/ppermute | solution.py:55
  15.9 0.0 collective-permute-start.4
  15.9 2.8 %all-to-all-start = ((f32[32,1,128]{2,1,0:T(1,128)}), f32[32,1,128]{2,1,0:T(1,128)S(1)}, u32[]{:S(2)}, u32[]{:S(2)}) async-start(f32[32,1,128]{2,1,0:T(1,128)} %bitcast.1), calls=%async_computation | async-start | bytes 32768 | tf_op jit(solution)/shard_map/all_to_all | solution.py:602
  18.7 0.0 collective-permute-done.3.refs_1_
  18.8 0.0 collective-permute-done.4.refs_2_
  18.8 0.0 collective-permute-done.2.refs_0_
  18.8 0.0 collective-permute-done.5.refs_3_
  18.8 0.0 collective-permute-done.6.refs_4_
  18.8 5.0 %shard_map.80 = (f32[2,16,16,256]{3,2,1,0:T(8,128)S(1)}, f32[22,24,384]{2,1,0:T(8,128)}, f32[22,24,384]{2,1,0:T(8,128)}, f32[22,24,384]{2,1,0:T(8,128)}, f32[22,...) custom-call(f32[13,16,256]{2,1,0:T(8,128)S(1)} %collective-permute-done.2.refs_0_, ...), custom_call_target="tpu_custom_call" | custom-call | flops 1000000000 | bytes 12378112 | tf_op jit(solution)/shard_map/pallas_call | solution.py:511
  23.8 2.0 %all-to-all-done = f32[32,1,128]{2,1,0:T(1,128)S(1)} async-done(((f32[32,1,128]{2,1,0:T(1,128)}), f32[32,1,128]{2,1,0:T(1,128)S(1)}, u32[]{:S(2)}, u32[]{:S(2)}) %all-to-all-start) | async-done | bytes 16416 | tf_op jit(solution)/shard_map/all_to_all | solution.py:602
  25.8 3.0 %shard_map.81 = (f32[1,16,256]{2,1,0:T(8,128)S(1)}, f32[1,16,256]{2,1,0:T(8,128)S(1)}, f32[1,16,256]{2,1,0:T(8,128)S(1)}, f32[16,16,256]{2,1,0:T(8,128)}, f32[8,...) custom-call(f32[16,16,256]{2,1,0:T(8,128)S(1)} %get-tuple-element.60.refs_0_, f32[32,128]{1,0:T(8,128)S(1)} %bitcast.13, ...), custom_call_target="tpu_custom_call" | custom-call | bytes 5611520 | tf_op jit(solution)/shard_map/pallas_call | solution.py:511
  28.8 0.7 collective-permute-start.7
  29.4 1.9 %collective-permute-start.8 = (f32[1,16,256]{2,1,0:T(8,128)S(1)}, f32[1,16,256]{2,1,0:T(8,128)S(1)}, u32[]{:S(2)}, u32[]{:S(2)}) collective-permute-start(f32[1,16,256]{2,1,0:T(8,128)S(1)} %get-tuple-element.63), channel_id=1, source_target_pairs={{0,4},{1,5},{2,6},{3,7},{4,0},{5,1},{6,2},{7,3},{8,12},{9,13},{10,... | collective-permute-start | bytes 49160 | tf_op jit(solution)/shard_map/ppermute | solution.py:55
  31.4 0.0 collective-permute-start.9
  31.4 0.6 collective-permute-start.11
  32.0 0.0 collective-permute-start.10
  32.0 2.4 %collective-permute-done.11.refs_4_ = f32[8,256]{1,0:T(8,128)S(1)} collective-permute-done((f32[8,256]{1,0:T(8,128)S(1)}, f32[8,256]{1,0:T(8,128)S(1)}, u32[]{:S(2)}, u32[]{:S(2)}) %collective-permute-start.11) | collective-permute-done | bytes 8224 | tf_op jit(solution)/shard_map/ppermute | solution.py:55
  34.5 1.3 %shard_map.82 = (f32[16,16,256]{2,1,0:T(8,128)S(1)}, f32[16,16,256]{2,1,0:T(8,128)}, f32[7,16,16,256]{3,2,1,0:T(8,128)}, f32[1,128]{1,0:T(1,128)S(1)}, f32[8,256]{1,0:T(8,128)S(1)}) custom-call(f32[1,16,256]{2,1,0:T(8,128)S(1)} %collective-permute-done.7.refs_0_, f32[1,16,256]{2,1,0:T(8,128)S(1)} %collective-permute-done.8.refs_1_, ...), custom_call_target="tpu_custom_call" | custom-call | bytes 4792832 | tf_op jit(solution)/shard_map/pallas_call | solution.py:511
  35.8 0.7 collective-permute-start.13
  36.5 0.0 collective-permute-start.12
  36.5 1.2 %shard_map.83.refs_3_ = f32[32,128]{1,0:T(8,128)} custom-call(f32[16,16,16,256]{3,2,1,0:T(8,128)S(1)} %copy-done, f32[16,16,256]{2,1,0:T(8,128)S(1)} %get-tuple-element.69.refs_1_.refs_2_, f32[1,128]{1,0:T(1,128)S(1)} %get-tuple-element.70.refs_2_), custom_call_target="tpu_custom_call" | custom-call | bytes 4473344 | tf_op jit(solution)/shard_map/pallas_call | solution.py:511
  37.7 1.2 %collective-permute-done.13.refs_1_.refs_7_ = f32[8,256]{1,0:T(8,128)S(1)} collective-permute-done((f32[8,256]{1,0:T(8,128)S(1)}, f32[8,256]{1,0:T(8,128)S(1)}, u32[]{:S(2)}, u32[]{:S(2)}) %collective-permute-start.13) | collective-permute-done | bytes 8224 | tf_op jit(solution)/shard_map/ppermute | solution.py:55
  39.0 1.0 %shard_map.84 = (f32[3,16,256]{2,1,0:T(8,128)S(1)}, f32[8,256]{1,0:T(8,128)S(1)}, f32[8,256]{1,0:T(8,128)S(1)}, f32[3,16,256]{2,1,0:T(8,128)S(1)}, f32[3,16,256]{2,1,0:T(8,128)S(1)}) custom-call(f32[8,256]{1,0:T(8,128)S(1)} %collective-permute-done.12.refs_0_.refs_6_, f32[8,256]{1,0:T(8,128)S(1)} %collective-permute-done.13.refs_1_.refs_7_, ...), custom_call_target="tpu_custom_call" | custom-call | bytes 458752 | tf_op jit(solution)/shard_map/pallas_call | solution.py:511
  40.0 0.5 collective-permute-start.14
  40.5 1.9 %collective-permute-start.17 = (f32[3,16,256]{2,1,0:T(8,128)S(1)}, f32[3,16,256]{2,1,0:T(8,128)S(1)}, u32[]{:S(2)}, u32[]{:S(2)}) collective-permute-start(f32[3,16,256]{2,1,0:T(8,128)S(1)} %get-tuple-element.74), channel_id=1, source_target_pairs={{0,4},{1,5},{2,6},{3,7},{4,0},{5,1},{6,2},{7,3},{8,12},{9,13},{10,... | collective-permute-start | bytes 147464 | tf_op jit(solution)/shard_map/ppermute | solution.py:55
  42.3 2.9 %collective-permute-start.15 = (f32[8,256]{1,0:T(8,128)S(1)}, f32[8,256]{1,0:T(8,128)S(1)}, u32[]{:S(2)}, u32[]{:S(2)}) collective-permute-start(f32[8,256]{1,0:T(8,128)S(1)} %get-tuple-element.72), channel_id=1, source_target_pairs={{0,20},{1,21},{2,22},{3,23},{4,16},{5,17},{6,18},{7,19},{8,28},{9,... | collective-permute-start | bytes 24584 | tf_op jit(solution)/shard_map/ppermute | solution.py:55
  45.2 3.7 %all-to-all-start.1 = ((f32[32,1,128]{2,1,0:T(1,128)}), f32[32,1,128]{2,1,0:T(1,128)S(1)}, u32[]{:S(2)}, u32[]{:S(2)}) async-start(f32[32,1,128]{2,1,0:T(1,128)} %bitcast.4), calls=%async_computation.1 | async-start | bytes 32768 | tf_op jit(solution)/shard_map/all_to_all | solution.py:602
  49.0 3.7 %shard_map.85 = (f32[2,16,16,256]{3,2,1,0:T(8,128)S(1)}, f32[2,16,16,256]{3,2,1,0:T(8,128)S(1)}, f32[2,16,16,256]{3,2,1,0:T(8,128)S(1)}, f32[2,16,16,256]{3,2,1,...) custom-call(f32[3,16,256]{2,1,0:T(8,128)S(1)} %collective-permute-done.14.refs_0_, ...), custom_call_target="tpu_custom_call" | custom-call | flops 1000000000 | bytes 10764288 | tf_op jit(solution)/shard_map/pallas_call | solution.py:511
  52.7 3.4 %all-to-all-done.1 = f32[32,1,128]{2,1,0:T(1,128)S(1)} async-done(((f32[32,1,128]{2,1,0:T(1,128)}), f32[32,1,128]{2,1,0:T(1,128)S(1)}, u32[]{:S(2)}, u32[]{:S(2)}) %all-to-all-start.1) | async-done | bytes 16416 | tf_op jit(solution)/shard_map/all_to_all | solution.py:602
  56.1 2.1 %shard_map.86 = (f32[1,16,256]{2,1,0:T(8,128)S(1)}, f32[1,16,256]{2,1,0:T(8,128)S(1)}, f32[1,16,256]{2,1,0:T(8,128)S(1)}, f32[16,16,256]{2,1,0:T(8,128)S(1)}, f3...) custom-call(f32[16,16,256]{2,1,0:T(8,128)S(1)} %get-tuple-element.81.refs_0_, ...), custom_call_target="tpu_custom_call" | custom-call | bytes 8503296 | tf_op jit(solution)/shard_map/pallas_call | solution.py:511
  58.2 0.0 copy-start.3
  58.2 0.7 collective-permute-start.19
  58.8 0.5 collective-permute-start.20
  59.4 0.7 collective-permute-start.23
  60.1 0.0 collective-permute-start.22
  60.1 2.3 %collective-permute-done.23.refs_4_ = f32[8,256]{1,0:T(8,128)S(1)} collective-permute-done((f32[8,256]{1,0:T(8,128)S(1)}, f32[8,256]{1,0:T(8,128)S(1)}, u32[]{:S(2)}, u32[]{:S(2)}) %collective-permute-start.23) | collective-permute-done | bytes 8224 | tf_op jit(solution)/shard_map/ppermute | solution.py:55
  62.4 0.1 collective-permute-done.20.refs_1_
  62.6 0.7 shard_map.87
  63.3 11.1 %all_to_all.33 = f32[32,1,128]{2,1,0:T(1,128)S(1)} all-to-all(f32[32,1,128]{2,1,0:T(1,128)S(1)} %bitcast.15), channel_id=1, replica_groups=mesh['gx'=2,'gy'=4,'gz'=4] {'gx','gy','gz'}, dimensions={0} | all-to-all | bytes 32768 | tf_op jit(solution)/shard_map/all_to_all | solution.py:602
  74.4 1.1 %shard_map.88 = (f32[16,16,256]{2,1,0:T(8,128)}, f32[16,16,256]{2,1,0:T(8,128)}) custom-call(f32[32,128]{1,0:T(8,128)S(1)} %bitcast.14, f32[16,128]{1,0:T(8,128)S(1)} %get-tuple-element.96.refs_1_, f32[16,16,256]{2,1,0:T(8,128)S(1)} %copy-done.3, f32[16,16,256]{2,1,0:T(8,128)S(1)} %copy-done.1, f32[16,16,256]{2,1,0:T(8,128)S(1)} %get-tuple-element.92.refs_5_.refs_4_, ...), custom_call_target="tpu_custom_call" | custom-call | bytes 1859584 | tf_op jit(solution)/shard_map/pallas_call | solution.py:511
  (25 shorter events, 0.1 us)
Async XLA Ops:
  2.3 6.2 %collective-permute-start.1 = (f32[24,256]{1,0:T(8,128)S(1)}, f32[24,256]{1,0:T(8,128)S(1)}, u32[]{:S(2)}, u32[]{:S(2)}) collective-permute-start(f32[24,256]{1,0:T(8,128)S(1)} %get-tuple-element.50), channel_id=1, source_target_pairs={{0,3},{1,2},{2,1},{3,0},{4,7},{5,6},{6,5},{7,4},{8,11},{9,10},{10,... | collective-permute-start | bytes 73736 | tf_op jit(solution)/shard_map/ppermute | solution.py:55
  4.8 3.7 %collective-permute-start = (f32[24,256]{1,0:T(8,128)S(1)}, f32[24,256]{1,0:T(8,128)S(1)}, u32[]{:S(2)}, u32[]{:S(2)}) collective-permute-start(f32[24,256]{1,0:T(8,128)S(1)} %get-tuple-element.50), channel_id=1, source_target_pairs={{0,1},{1,0},{2,3},{3,2},{4,5},{5,4},{6,7},{7,6},{8,9},{9,8},{10,11... | collective-permute-start | bytes 73736 | tf_op jit(solution)/shard_map/ppermute | solution.py:55
  9.7 9.1 %collective-permute-start.2 = (f32[13,16,256]{2,1,0:T(8,128)S(1)}, f32[13,16,256]{2,1,0:T(8,128)S(1)}, u32[]{:S(2)}, u32[]{:S(2)}) collective-permute-start(f32[13,16,256]{2,1,0:T(8,128)S(1)} %get-tuple-element.55), channel_id=1, source_target_pairs={{0,16},{1,17},{2,18},{3,19},{4,20},{5,21},{6,22},{7,23},{8,24},{9,... | collective-permute-start | bytes 638984 | tf_op jit(solution)/shard_map/ppermute | solution.py:55
  11.3 7.5 %collective-permute-start.5 = (f32[13,16,256]{2,1,0:T(8,128)S(1)}, f32[13,16,256]{2,1,0:T(8,128)S(1)}, u32[]{:S(2)}, u32[]{:S(2)}) collective-permute-start(f32[13,16,256]{2,1,0:T(8,128)S(1)} %get-tuple-element.58), channel_id=1, source_target_pairs={{0,4},{1,5},{2,6},{3,7},{4,0},{5,1},{6,2},{7,3},{8,12},{9,13},{10,... | collective-permute-start | bytes 638984 | tf_op jit(solution)/shard_map/ppermute | solution.py:55
  12.8 6.0 %collective-permute-start.6 = (f32[13,16,256]{2,1,0:T(8,128)S(1)}, f32[13,16,256]{2,1,0:T(8,128)S(1)}, u32[]{:S(2)}, u32[]{:S(2)}) collective-permute-start(f32[13,16,256]{2,1,0:T(8,128)S(1)} %get-tuple-element.59), channel_id=1, source_target_pairs={{0,1},{1,0},{2,3},{3,2},{4,8},{5,9},{6,10},{7,11},{8,4},{9,5},{10,... | collective-permute-start | bytes 638984 | tf_op jit(solution)/shard_map/ppermute | solution.py:55
  12.8 5.9 %collective-permute-start.3 = (f32[28,256]{1,0:T(8,128)S(1)}, f32[28,256]{1,0:T(8,128)S(1)}, u32[]{:S(2)}, u32[]{:S(2)}) collective-permute-start(f32[28,256]{1,0:T(8,128)S(1)} %get-tuple-element.56), channel_id=1, source_target_pairs={{0,20},{1,21},{2,22},{3,23},{4,16},{5,17},{6,18},{7,19},{8,28},{9,... | collective-permute-start | bytes 86024 | tf_op jit(solution)/shard_map/ppermute | solution.py:55
  15.9 2.9 %collective-permute-start.4 = (f32[28,256]{1,0:T(8,128)S(1)}, f32[28,256]{1,0:T(8,128)S(1)}, u32[]{:S(2)}, u32[]{:S(2)}) collective-permute-start(f32[28,256]{1,0:T(8,128)S(1)} %get-tuple-element.57), channel_id=1, source_target_pairs={{0,1},{1,0},{2,3},{3,2},{4,24},{5,25},{6,26},{7,27},{8,20},{9,21},... | collective-permute-start | bytes 86024 | tf_op jit(solution)/shard_map/ppermute | solution.py:55
  15.9 9.9 %all-to-all-start = ((f32[32,1,128]{2,1,0:T(1,128)}), f32[32,1,128]{2,1,0:T(1,128)S(1)}, u32[]{:S(2)}, u32[]{:S(2)}) async-start(f32[32,1,128]{2,1,0:T(1,128)} %bitcast.1), calls=%async_computation | async-start | bytes 32768 | tf_op jit(solution)/shard_map/all_to_all | solution.py:602
  25.8 10.8 %copy-start = (f32[16,16,16,256]{3,2,1,0:T(8,128)S(1)}, f32[16,16,16,256]{3,2,1,0:T(8,128)}, u32[]{:S(2)}) copy-start(f32[16,16,16,256]{3,2,1,0:T(8,128)} %refs_11_.3) | copy-start | bytes 12582916
  28.8 5.7 %collective-permute-start.7 = (f32[1,16,256]{2,1,0:T(8,128)S(1)}, f32[1,16,256]{2,1,0:T(8,128)S(1)}, u32[]{:S(2)}, u32[]{:S(2)}) collective-permute-start(f32[1,16,256]{2,1,0:T(8,128)S(1)} %get-tuple-element.62), channel_id=1, source_target_pairs={{0,16},{1,17},{2,18},{3,19},{4,20},{5,21},{6,22},{7,23},{8,24},{9,... | collective-permute-start | bytes 49160 | tf_op jit(solution)/shard_map/ppermute | solution.py:55
  29.4 5.0 %collective-permute-start.8 = (f32[1,16,256]{2,1,0:T(8,128)S(1)}, f32[1,16,256]{2,1,0:T(8,128)S(1)}, u32[]{:S(2)}, u32[]{:S(2)}) collective-permute-start(f32[1,16,256]{2,1,0:T(8,128)S(1)} %get-tuple-element.63), channel_id=1, source_target_pairs={{0,4},{1,5},{2,6},{3,7},{4,0},{5,1},{6,2},{7,3},{8,12},{9,13},{10,... | collective-permute-start | bytes 49160 | tf_op jit(solution)/shard_map/ppermute | solution.py:55
  31.4 3.1 %collective-permute-start.9 = (f32[1,16,256]{2,1,0:T(8,128)S(1)}, f32[1,16,256]{2,1,0:T(8,128)S(1)}, u32[]{:S(2)}, u32[]{:S(2)}) collective-permute-start(f32[1,16,256]{2,1,0:T(8,128)S(1)} %get-tuple-element.64), channel_id=1, source_target_pairs={{0,1},{1,0},{2,3},{3,2},{4,8},{5,9},{6,10},{7,11},{8,4},{9,5},{10,... | collective-permute-start | bytes 49160 | tf_op jit(solution)/shard_map/ppermute | solution.py:55
  31.4 3.1 %collective-permute-start.11 = (f32[8,256]{1,0:T(8,128)S(1)}, f32[8,256]{1,0:T(8,128)S(1)}, u32[]{:S(2)}, u32[]{:S(2)}) collective-permute-start(f32[8,256]{1,0:T(8,128)S(1)} %get-tuple-element.65), channel_id=1, source_target_pairs={{0,3},{1,2},{2,1},{3,0},{4,7},{5,6},{6,5},{7,4},{8,11},{9,10},{10,... | collective-permute-start | bytes 24584 | tf_op jit(solution)/shard_map/ppermute | solution.py:55
  32.0 2.4 %collective-permute-start.10 = (f32[8,256]{1,0:T(8,128)S(1)}, f32[8,256]{1,0:T(8,128)S(1)}, u32[]{:S(2)}, u32[]{:S(2)}) collective-permute-start(f32[8,256]{1,0:T(8,128)S(1)} %get-tuple-element.65), channel_id=1, source_target_pairs={{0,1},{1,0},{2,3},{3,2},{4,5},{5,4},{6,7},{7,6},{8,9},{9,8},{10,11... | collective-permute-start | bytes 24584 | tf_op jit(solution)/shard_map/ppermute | solution.py:55
  35.8 3.1 %collective-permute-start.13 = (f32[8,256]{1,0:T(8,128)S(1)}, f32[8,256]{1,0:T(8,128)S(1)}, u32[]{:S(2)}, u32[]{:S(2)}) collective-permute-start(f32[8,256]{1,0:T(8,128)S(1)} %get-tuple-element.68), channel_id=1, source_target_pairs={{0,3},{1,2},{2,1},{3,0},{4,7},{5,6},{6,5},{7,4},{8,11},{9,10},{10,... | collective-permute-start | bytes 24584 | tf_op jit(solution)/shard_map/ppermute | solution.py:55
  36.5 2.4 %collective-permute-start.12 = (f32[8,256]{1,0:T(8,128)S(1)}, f32[8,256]{1,0:T(8,128)S(1)}, u32[]{:S(2)}, u32[]{:S(2)}) collective-permute-start(f32[8,256]{1,0:T(8,128)S(1)} %get-tuple-element.68), channel_id=1, source_target_pairs={{0,1},{1,0},{2,3},{3,2},{4,5},{5,4},{6,7},{7,6},{8,9},{9,8},{10,11... | collective-permute-start | bytes 24584 | tf_op jit(solution)/shard_map/ppermute | solution.py:55
  40.0 9.0 %collective-permute-start.14 = (f32[3,16,256]{2,1,0:T(8,128)S(1)}, f32[3,16,256]{2,1,0:T(8,128)S(1)}, u32[]{:S(2)}, u32[]{:S(2)}) collective-permute-start(f32[3,16,256]{2,1,0:T(8,128)S(1)} %get-tuple-element.71), channel_id=1, source_target_pairs={{0,16},{1,17},{2,18},{3,19},{4,20},{5,21},{6,22},{7,23},{8,24},{9,... | collective-permute-start | bytes 147464 | tf_op jit(solution)/shard_map/ppermute | solution.py:55
  40.5 8.5 %collective-permute-start.17 = (f32[3,16,256]{2,1,0:T(8,128)S(1)}, f32[3,16,256]{2,1,0:T(8,128)S(1)}, u32[]{:S(2)}, u32[]{:S(2)}) collective-permute-start(f32[3,16,256]{2,1,0:T(8,128)S(1)} %get-tuple-element.74), channel_id=1, source_target_pairs={{0,4},{1,5},{2,6},{3,7},{4,0},{5,1},{6,2},{7,3},{8,12},{9,13},{10,... | collective-permute-start | bytes 147464 | tf_op jit(solution)/shard_map/ppermute | solution.py:55
  42.3 6.6 %collective-permute-start.18 = (f32[3,16,256]{2,1,0:T(8,128)S(1)}, f32[3,16,256]{2,1,0:T(8,128)S(1)}, u32[]{:S(2)}, u32[]{:S(2)}) collective-permute-start(f32[3,16,256]{2,1,0:T(8,128)S(1)} %get-tuple-element.75), channel_id=1, source_target_pairs={{0,1},{1,0},{2,3},{3,2},{4,8},{5,9},{6,10},{7,11},{8,4},{9,5},{10,... | collective-permute-start | bytes 147464 | tf_op jit(solution)/shard_map/ppermute | solution.py:55
  42.3 6.6 %collective-permute-start.15 = (f32[8,256]{1,0:T(8,128)S(1)}, f32[8,256]{1,0:T(8,128)S(1)}, u32[]{:S(2)}, u32[]{:S(2)}) collective-permute-start(f32[8,256]{1,0:T(8,128)S(1)} %get-tuple-element.72), channel_id=1, source_target_pairs={{0,20},{1,21},{2,22},{3,23},{4,16},{5,17},{6,18},{7,19},{8,28},{9,... | collective-permute-start | bytes 24584 | tf_op jit(solution)/shard_map/ppermute | solution.py:55
  45.2 3.7 %collective-permute-start.16 = (f32[8,256]{1,0:T(8,128)S(1)}, f32[8,256]{1,0:T(8,128)S(1)}, u32[]{:S(2)}, u32[]{:S(2)}) collective-permute-start(f32[8,256]{1,0:T(8,128)S(1)} %get-tuple-element.73), channel_id=1, source_target_pairs={{0,1},{1,0},{2,3},{3,2},{4,24},{5,25},{6,26},{7,27},{8,20},{9,21},... | collective-permute-start | bytes 24584 | tf_op jit(solution)/shard_map/ppermute | solution.py:55
  45.2 10.8 %all-to-all-start.1 = ((f32[32,1,128]{2,1,0:T(1,128)}), f32[32,1,128]{2,1,0:T(1,128)S(1)}, u32[]{:S(2)}, u32[]{:S(2)}) async-start(f32[32,1,128]{2,1,0:T(1,128)} %bitcast.4), calls=%async_computation.1 | async-start | bytes 32768 | tf_op jit(solution)/shard_map/all_to_all | solution.py:602
  56.1 6.5 %copy-start.1 = (f32[16,16,256]{2,1,0:T(8,128)S(1)}, f32[16,16,256]{2,1,0:T(8,128)}, u32[]{:S(2)}) copy-start(f32[16,16,256]{2,1,0:T(8,128)} %get-tuple-element.76.refs_5_.refs_3_.refs_7_) | copy-start | bytes 786436
  56.1 6.5 %copy-start.2 = (f32[7,16,16,256]{3,2,1,0:T(8,128)S(1)}, f32[7,16,16,256]{3,2,1,0:T(8,128)}, u32[]{:S(2)}) copy-start(f32[7,16,16,256]{3,2,1,0:T(8,128)} %get-tuple-element.93.refs_6_) | copy-start | bytes 5505028
  58.2 16.2 %copy-start.3 = (f32[16,16,256]{2,1,0:T(8,128)S(1)}, f32[16,16,256]{2,1,0:T(8,128)}, u32[]{:S(2)}) copy-start(f32[16,16,256]{2,1,0:T(8,128)} %get-tuple-element.82.refs_5_.refs_2_) | copy-start | bytes 786436
  58.2 4.2 %collective-permute-start.19 = (f32[1,16,256]{2,1,0:T(8,128)S(1)}, f32[1,16,256]{2,1,0:T(8,128)S(1)}, u32[]{:S(2)}, u32[]{:S(2)}) collective-permute-start(f32[1,16,256]{2,1,0:T(8,128)S(1)} %get-tuple-element.88), channel_id=1, source_target_pairs={{0,16},{1,17},{2,18},{3,19},{4,20},{5,21},{6,22},{7,23},{8,24},{9,... | collective-permute-start | bytes 49160 | tf_op jit(solution)/shard_map/ppermute | solution.py:55
  58.8 3.7 %collective-permute-start.20 = (f32[1,16,256]{2,1,0:T(8,128)S(1)}, f32[1,16,256]{2,1,0:T(8,128)S(1)}, u32[]{:S(2)}, u32[]{:S(2)}) collective-permute-start(f32[1,16,256]{2,1,0:T(8,128)S(1)} %get-tuple-element.89), channel_id=1, source_target_pairs={{0,4},{1,5},{2,6},{3,7},{4,0},{5,1},{6,2},{7,3},{8,12},{9,13},{10,... | collective-permute-start | bytes 49160 | tf_op jit(solution)/shard_map/ppermute | solution.py:55
  59.3 3.2 %collective-permute-start.21 = (f32[1,16,256]{2,1,0:T(8,128)S(1)}, f32[1,16,256]{2,1,0:T(8,128)S(1)}, u32[]{:S(2)}, u32[]{:S(2)}) collective-permute-start(f32[1,16,256]{2,1,0:T(8,128)S(1)} %get-tuple-element.90), channel_id=1, source_target_pairs={{0,1},{1,0},{2,3},{3,2},{4,8},{5,9},{6,10},{7,11},{8,4},{9,5},{10,... | collective-permute-start | bytes 49160 | tf_op jit(solution)/shard_map/ppermute | solution.py:55
  59.4 3.1 %collective-permute-start.23 = (f32[8,256]{1,0:T(8,128)S(1)}, f32[8,256]{1,0:T(8,128)S(1)}, u32[]{:S(2)}, u32[]{:S(2)}) collective-permute-start(f32[8,256]{1,0:T(8,128)S(1)} %get-tuple-element.91), channel_id=1, source_target_pairs={{0,3},{1,2},{2,1},{3,0},{4,7},{5,6},{6,5},{7,4},{8,11},{9,10},{10,... | collective-permute-start | bytes 24584 | tf_op jit(solution)/shard_map/ppermute | solution.py:55
  60.1 2.4 %collective-permute-start.22 = (f32[8,256]{1,0:T(8,128)S(1)}, f32[8,256]{1,0:T(8,128)S(1)}, u32[]{:S(2)}, u32[]{:S(2)}) collective-permute-start(f32[8,256]{1,0:T(8,128)S(1)} %get-tuple-element.91), channel_id=1, source_target_pairs={{0,1},{1,0},{2,3},{3,2},{4,5},{5,4},{6,7},{7,6},{8,9},{9,8},{10,11... | collective-permute-start | bytes 24584 | tf_op jit(solution)/shard_map/ppermute | solution.py:55

commit v6 on v5

--- a/solution.py
+++ b/solution.py
@@ -666,11 +666,11 @@
                 copies[-1].start()
         for b in boxes[:6]:
             clear_round(b, shape)
-        got, fixed = fetch((got, fixed))
+        got = fetch(got)
         ends = pick_z(fetch(got_z), sizes, ends_shape)
-        boxes[4][3 : 3 + nx, 0:ny, 0:nz] = 1.0 - fixed[...].astype(F32)
         unpack_faces(boxes[:6], [None] * 6, got["x"], got["y"], sizes, 2, ends)
         unpack_xy(boxes[:6], shape, got["xy"], sizes)
+        boxes[4][3 : 3 + nx, 0:ny, 0:nz] = 1.0 - fixed.get()[...].astype(F32)
         for copy in copies:
             copy.wait()
         for target, piece in zip(outs["base"], chunks(vecs, NEAR_FIRST)):
@@ -715,7 +715,6 @@
         smooth, rows = fetch((smooth, rows))
         weights = coarse_weights(inverse.get(), coarse_sum(rows, vecs))
         add_coarse(outs["z"], smooth, base, weights)
-        outs["kept"].put(outs["z"])
         pack_faces(outs["faces"], [outs["z"]], sizes, 1)
         outs["tile"][...] = pack_z([outs["z"]])
 
@@ -723,13 +722,12 @@
         first_direction,
         {
             "z": shaped(*shape),
-            "kept": Stored(*shape),
             "faces": face_shapes(shape, sizes, 1, 1),
             "tile": shaped(z_rows(1), nx * ny),
         },
         (smoothed["smooth"], rows_a, Far(coarse_inverse), base_rest(smoothed, NEAR_FIRST)),
     )
-    direction, kept_z = directed["z"], directed["kept"]
+    direction = directed["z"]
     got = send_faces(directed["faces"], sizes)
     got_z = send_z(directed["tile"], sizes)
 
@@ -755,6 +753,7 @@
     def first_image(got, got_z, field, own, rhs, outs, vb):
         image = outs["image"]
         outs["own"].put(own.get())
+        outs["z"].put(field.get())
         apply(field, got, got_z, own, image, vb)
         outs["kept"].put(image)
         outs["tile"][...] = pack_z([image])
@@ -768,6 +767,7 @@
             "image": shaped(*shape),
             "kept": Stored(*shape),
             "own": Stored(7, *shape),
+            "z": Stored(*shape),
             "tile": shaped(z_rows(1), nx * ny),
             "sums": shaped(1, LANES),
         },
@@ -775,6 +775,7 @@
         [vbox],
     )
     got_z = send_z(imaged["tile"], sizes)
+    kept_z = imaged["z"]
 
     def second_rows(base, field, sums, out):
         row = project(base, field.get()[...]) + sums.get()[...]

time: 75.9 us -> 75.2 us (level)
  no operation moved by 1% of the time
where the time goes in v6:
time: 75.2 us; the launch traced here: 74.7 us
  starting transfers between devices  26.7 us (36%)
  Pallas kernels  24.2 us (32%)
  waiting for transfers between devices  11.9 us (16%)
  blocking collectives  11.1 us (15%)
  between operations  0.85 us (1%)
    pallas_call x12, Pallas kernels, call(): pl.pallas_call(body, out_shape=[pltpu.HBM(a.shape, F32) if i in distant e...  24.2 us
    ppermute x24, starting transfers between devices, swap(): return lax.ppermute(value, AXES, pairs)  20 us
    all_to_all x1, blocking collectives, spread(): return lax.all_to_all(rows, AXES, 0, 0, tiled=True)  11.1 us
    all_to_all x2, starting transfers between devices, spread(): return lax.all_to_all(rows, AXES, 0, 0, tiled=True)  6.69 us
    ppermute x24, waiting for transfers between devices, swap(): return lax.ppermute(value, AXES, pairs)  6.26 us
    all_to_all x2, waiting for transfers between devices, spread(): return lax.all_to_all(rows, AXES, 0, 0, tiled=True)  5.64 us
  transfers between devices with their start and end apart: 26, of which 6 were waited for; matrix products, arithmetic and copies ran while one was open for 0% of the time, Pallas kernels for 17%

profile of v6, /device:TPU:0, one launch (start us, length us, event | category | flops | bytes accessed | tf_op | source)
XLA Modules:
  0.0 74.7 jit_solution(1862764139015234922)
XLA Ops:
  0.6 1.7 %shard_map.77 = (f32[16,16,256]{2,1,0:T(8,128)S(1)}, f32[3,16,16,256]{3,2,1,0:T(8,128)S(1)}, f32[16,16,256]{2,1,0:T(8,128)S(1)}, f32[16,16,256]{2,1,0:T(8,128)S(1)}, f32[24,256]{1,0:T(8,128)S(1)}) custom-call(f32[3,16,16,256]{3,2,1,0:T(8,128)} %refs_5_.1, f32[16,16,256]{2,1,0:T(8,128)} %refs_6_.1, s32[16,16,256]{2,1,0:T(8,128)} %refs_7_.2, ...), custom_call_target="tpu_custom_call" | custom-call | bytes 3170304 | tf_op jit(solution)/shard_map/pallas_call | solution.py:511
  2.3 2.4 %collective-permute-start.1 = (f32[24,256]{1,0:T(8,128)S(1)}, f32[24,256]{1,0:T(8,128)S(1)}, u32[]{:S(2)}, u32[]{:S(2)}) collective-permute-start(f32[24,256]{1,0:T(8,128)S(1)} %get-tuple-element.50), channel_id=1, source_target_pairs={{0,3},{1,2},{2,1},{3,0},{4,7},{5,6},{6,5},{7,4},{8,11},{9,10},{10,... | collective-permute-start | bytes 73736 | tf_op jit(solution)/shard_map/ppermute | solution.py:55
  4.8 0.7 collective-permute-start
  5.5 3.0 %shard_map.78.refs_6_ = f32[32,128]{1,0:T(8,128)} custom-call(f32[16,16,256]{2,1,0:T(8,128)} %refs_4_.3, f32[16,16,16,256]{3,2,1,0:T(8,128)} %refs_11_.3), custom_call_target="tpu_custom_call" | custom-call | bytes 4472832 | tf_op jit(solution)/shard_map/pallas_call | solution.py:511
  8.5 0.0 collective-permute-done.1.refs_1_.refs_10_
  8.5 1.1 %shard_map.79 = (f32[13,16,256]{2,1,0:T(8,128)S(1)}, f32[28,256]{1,0:T(8,128)S(1)}, f32[28,256]{1,0:T(8,128)S(1)}, f32[13,16,256]{2,1,0:T(8,128)S(1)}, f32[13,16,256]{2,1,0:T(8,128)S(1)}) custom-call(f32[24,256]{1,0:T(8,128)S(1)} %collective-permute-done.refs_0_.refs_9_, f32[24,256]{1,0:T(8,128)S(1)} %collective-permute-done.1.refs_1_.refs_10_, ...), custom_call_target="tpu_custom_call" | custom-call | bytes 2334720 | tf_op jit(solution)/shard_map/pallas_call | solution.py:511
  9.7 1.6 %collective-permute-start.2 = (f32[13,16,256]{2,1,0:T(8,128)S(1)}, f32[13,16,256]{2,1,0:T(8,128)S(1)}, u32[]{:S(2)}, u32[]{:S(2)}) collective-permute-start(f32[13,16,256]{2,1,0:T(8,128)S(1)} %get-tuple-element.55), channel_id=1, source_target_pairs={{0,16},{1,17},{2,18},{3,19},{4,20},{5,21},{6,22},{7,23},{8,24},{9,... | collective-permute-start | bytes 638984 | tf_op jit(solution)/shard_map/ppermute | solution.py:55
  11.3 1.6 %collective-permute-start.5 = (f32[13,16,256]{2,1,0:T(8,128)S(1)}, f32[13,16,256]{2,1,0:T(8,128)S(1)}, u32[]{:S(2)}, u32[]{:S(2)}) collective-permute-start(f32[13,16,256]{2,1,0:T(8,128)S(1)} %get-tuple-element.58), channel_id=1, source_target_pairs={{0,4},{1,5},{2,6},{3,7},{4,0},{5,1},{6,2},{7,3},{8,12},{9,13},{10,... | collective-permute-start | bytes 638984 | tf_op jit(solution)/shard_map/ppermute | solution.py:55
  12.8 3.1 %collective-permute-start.3 = (f32[28,256]{1,0:T(8,128)S(1)}, f32[28,256]{1,0:T(8,128)S(1)}, u32[]{:S(2)}, u32[]{:S(2)}) collective-permute-start(f32[28,256]{1,0:T(8,128)S(1)} %get-tuple-element.56), channel_id=1, source_target_pairs={{0,20},{1,21},{2,22},{3,23},{4,16},{5,17},{6,18},{7,19},{8,28},{9,... | collective-permute-start | bytes 86024 | tf_op jit(solution)/shard_map/ppermute | solution.py:55
  15.9 0.0 collective-permute-start.4
  15.9 2.8 %all-to-all-start = ((f32[32,1,128]{2,1,0:T(1,128)}), f32[32,1,128]{2,1,0:T(1,128)S(1)}, u32[]{:S(2)}, u32[]{:S(2)}) async-start(f32[32,1,128]{2,1,0:T(1,128)} %bitcast.1), calls=%async_computation | async-start | bytes 32768 | tf_op jit(solution)/shard_map/all_to_all | solution.py:602
  18.7 0.0 collective-permute-done.3.refs_1_
  18.8 0.0 collective-permute-done.4.refs_2_
  18.8 0.0 collective-permute-done.2.refs_0_
  18.8 0.0 collective-permute-done.5.refs_3_
  18.8 0.0 collective-permute-done.6.refs_4_
  18.8 4.7 %shard_map.80 = (f32[2,16,16,256]{3,2,1,0:T(8,128)S(1)}, f32[22,24,384]{2,1,0:T(8,128)}, f32[22,24,384]{2,1,0:T(8,128)}, f32[22,24,384]{2,1,0:T(8,128)}, f32[22,...) custom-call(f32[13,16,256]{2,1,0:T(8,128)S(1)} %collective-permute-done.2.refs_0_, ...), custom_call_target="tpu_custom_call" | custom-call | flops 1000000000 | bytes 12378112 | tf_op jit(solution)/shard_map/pallas_call | solution.py:511
  23.6 2.2 %all-to-all-done = f32[32,1,128]{2,1,0:T(1,128)S(1)} async-done(((f32[32,1,128]{2,1,0:T(1,128)}), f32[32,1,128]{2,1,0:T(1,128)S(1)}, u32[]{:S(2)}, u32[]{:S(2)}) %all-to-all-start) | async-done | bytes 16416 | tf_op jit(solution)/shard_map/all_to_all | solution.py:602
  25.8 2.4 %shard_map.81 = (f32[1,16,256]{2,1,0:T(8,128)S(1)}, f32[1,16,256]{2,1,0:T(8,128)S(1)}, f32[1,16,256]{2,1,0:T(8,128)S(1)}, f32[8,256]{1,0:T(8,128)S(1)}, f32[16,16,256]{2,1,0:T(8,128)S(1)}) custom-call(f32[16,16,256]{2,1,0:T(8,128)S(1)} %get-tuple-element.60.refs_0_, f32[32,128]{1,0:T(8,128)S(1)} %bitcast.13, f32[16,512]{1,0:T(8,128)} %refs_2_.5, ...), custom_call_target="tpu_custom_call" | custom-call | bytes 5349376 | tf_op jit(solution)/shard_map/pallas_call | solution.py:511
  28.3 0.7 collective-permute-start.7
  28.9 1.4 %collective-permute-start.8 = (f32[1,16,256]{2,1,0:T(8,128)S(1)}, f32[1,16,256]{2,1,0:T(8,128)S(1)}, u32[]{:S(2)}, u32[]{:S(2)}) collective-permute-start(f32[1,16,256]{2,1,0:T(8,128)S(1)} %get-tuple-element.63), channel_id=1, source_target_pairs={{0,4},{1,5},{2,6},{3,7},{4,0},{5,1},{6,2},{7,3},{8,12},{9,13},{10,... | collective-permute-start | bytes 49160 | tf_op jit(solution)/shard_map/ppermute | solution.py:55
  30.3 0.0 collective-permute-start.9
  30.3 0.6 collective-permute-start.11
  31.0 0.0 collective-permute-start.10
  31.0 2.4 %collective-permute-done.11.refs_4_ = f32[8,256]{1,0:T(8,128)S(1)} collective-permute-done((f32[8,256]{1,0:T(8,128)S(1)}, f32[8,256]{1,0:T(8,128)S(1)}, u32[]{:S(2)}, u32[]{:S(2)}) %collective-permute-start.11) | collective-permute-done | bytes 8224 | tf_op jit(solution)/shard_map/ppermute | solution.py:55
  33.4 1.4 %shard_map.82 = (f32[16,16,256]{2,1,0:T(8,128)S(1)}, f32[16,16,256]{2,1,0:T(8,128)}, f32[7,16,16,256]{3,2,1,0:T(8,128)}, f32[1,128]{1,0:T(1,128)S(1)}, f32[8,256]{1,0:T(8,128)S(1)}, /*index=5*/f32[16,16,256]{2,1,0:T(8,128)}) custom-call(f32[1,16,256]{2,1,0:T(8,128)S(1)} %collective-permute-done.7.refs_0_, f32[1,16,256]{2,1,0:T(8,128)S(1)} %collective-permute-done.8.refs_1_, ...), custom_call_target="tpu_custom_call" | custom-call | bytes 5054976 | tf_op jit(solution)/shard_map/pallas_call | solution.py:511
  34.9 0.7 collective-permute-start.13
  35.6 0.0 collective-permute-start.12
  35.6 1.2 %shard_map.83.refs_3_ = f32[32,128]{1,0:T(8,128)} custom-call(f32[16,16,16,256]{3,2,1,0:T(8,128)S(1)} %copy-done, f32[16,16,256]{2,1,0:T(8,128)S(1)} %get-tuple-element.69.refs_1_.refs_2_, f32[1,128]{1,0:T(1,128)S(1)} %get-tuple-element.70.refs_2_), custom_call_target="tpu_custom_call" | custom-call | bytes 4473344 | tf_op jit(solution)/shard_map/pallas_call | solution.py:511
  36.8 1.2 %collective-permute-done.13.refs_1_.refs_7_ = f32[8,256]{1,0:T(8,128)S(1)} collective-permute-done((f32[8,256]{1,0:T(8,128)S(1)}, f32[8,256]{1,0:T(8,128)S(1)}, u32[]{:S(2)}, u32[]{:S(2)}) %collective-permute-start.13) | collective-permute-done | bytes 8224 | tf_op jit(solution)/shard_map/ppermute | solution.py:55
  38.0 1.0 %shard_map.84 = (f32[3,16,256]{2,1,0:T(8,128)S(1)}, f32[8,256]{1,0:T(8,128)S(1)}, f32[8,256]{1,0:T(8,128)S(1)}, f32[3,16,256]{2,1,0:T(8,128)S(1)}, f32[3,16,256]{2,1,0:T(8,128)S(1)}) custom-call(f32[8,256]{1,0:T(8,128)S(1)} %collective-permute-done.12.refs_0_.refs_6_, f32[8,256]{1,0:T(8,128)S(1)} %collective-permute-done.13.refs_1_.refs_7_, ...), custom_call_target="tpu_custom_call" | custom-call | bytes 458752 | tf_op jit(solution)/shard_map/pallas_call | solution.py:511
  39.0 0.8 %collective-permute-start.14 = (f32[3,16,256]{2,1,0:T(8,128)S(1)}, f32[3,16,256]{2,1,0:T(8,128)S(1)}, u32[]{:S(2)}, u32[]{:S(2)}) collective-permute-start(f32[3,16,256]{2,1,0:T(8,128)S(1)} %get-tuple-element.71), channel_id=1, source_target_pairs={{0,16},{1,17},{2,18},{3,19},{4,20},{5,21},{6,22},{7,23},{8,24},{9,... | collective-permute-start | bytes 147464 | tf_op jit(solution)/shard_map/ppermute | solution.py:55
  39.7 2.0 %collective-permute-start.17 = (f32[3,16,256]{2,1,0:T(8,128)S(1)}, f32[3,16,256]{2,1,0:T(8,128)S(1)}, u32[]{:S(2)}, u32[]{:S(2)}) collective-permute-start(f32[3,16,256]{2,1,0:T(8,128)S(1)} %get-tuple-element.74), channel_id=1, source_target_pairs={{0,4},{1,5},{2,6},{3,7},{4,0},{5,1},{6,2},{7,3},{8,12},{9,13},{10,... | collective-permute-start | bytes 147464 | tf_op jit(solution)/shard_map/ppermute | solution.py:55
  41.7 2.5 %collective-permute-start.15 = (f32[8,256]{1,0:T(8,128)S(1)}, f32[8,256]{1,0:T(8,128)S(1)}, u32[]{:S(2)}, u32[]{:S(2)}) collective-permute-start(f32[8,256]{1,0:T(8,128)S(1)} %get-tuple-element.72), channel_id=1, source_target_pairs={{0,20},{1,21},{2,22},{3,23},{4,16},{5,17},{6,18},{7,19},{8,28},{9,... | collective-permute-start | bytes 24584 | tf_op jit(solution)/shard_map/ppermute | solution.py:55
  44.3 3.9 %all-to-all-start.1 = ((f32[32,1,128]{2,1,0:T(1,128)}), f32[32,1,128]{2,1,0:T(1,128)S(1)}, u32[]{:S(2)}, u32[]{:S(2)}) async-start(f32[32,1,128]{2,1,0:T(1,128)} %bitcast.4), calls=%async_computation.1 | async-start | bytes 32768 | tf_op jit(solution)/shard_map/all_to_all | solution.py:602
  48.2 3.7 %shard_map.85 = (f32[2,16,16,256]{3,2,1,0:T(8,128)S(1)}, f32[2,16,16,256]{3,2,1,0:T(8,128)S(1)}, f32[2,16,16,256]{3,2,1,0:T(8,128)S(1)}, f32[2,16,16,256]{3,2,1,...) custom-call(f32[3,16,256]{2,1,0:T(8,128)S(1)} %collective-permute-done.14.refs_0_, ...), custom_call_target="tpu_custom_call" | custom-call | flops 1000000000 | bytes 10764288 | tf_op jit(solution)/shard_map/pallas_call | solution.py:511
  51.9 3.4 %all-to-all-done.1 = f32[32,1,128]{2,1,0:T(1,128)S(1)} async-done(((f32[32,1,128]{2,1,0:T(1,128)}), f32[32,1,128]{2,1,0:T(1,128)S(1)}, u32[]{:S(2)}, u32[]{:S(2)}) %all-to-all-start.1) | async-done | bytes 16416 | tf_op jit(solution)/shard_map/all_to_all | solution.py:602
  55.3 2.1 %shard_map.86 = (f32[1,16,256]{2,1,0:T(8,128)S(1)}, f32[1,16,256]{2,1,0:T(8,128)S(1)}, f32[1,16,256]{2,1,0:T(8,128)S(1)}, f32[16,16,256]{2,1,0:T(8,128)S(1)}, f3...) custom-call(f32[16,16,256]{2,1,0:T(8,128)S(1)} %get-tuple-element.81.refs_0_, ...), custom_call_target="tpu_custom_call" | custom-call | bytes 8503296 | tf_op jit(solution)/shard_map/pallas_call | solution.py:511
  57.4 0.0 copy-start.3
  57.4 0.7 collective-permute-start.19
  58.1 0.5 collective-permute-start.20
  58.6 0.7 collective-permute-start.23
  59.3 0.0 collective-permute-start.22
  59.3 2.3 %collective-permute-done.23.refs_4_ = f32[8,256]{1,0:T(8,128)S(1)} collective-permute-done((f32[8,256]{1,0:T(8,128)S(1)}, f32[8,256]{1,0:T(8,128)S(1)}, u32[]{:S(2)}, u32[]{:S(2)}) %collective-permute-start.23) | collective-permute-done | bytes 8224 | tf_op jit(solution)/shard_map/ppermute | solution.py:55
  61.7 0.1 collective-permute-done.20.refs_1_
  61.8 0.7 shard_map.87
  62.5 11.1 %all_to_all.33 = f32[32,1,128]{2,1,0:T(1,128)S(1)} all-to-all(f32[32,1,128]{2,1,0:T(1,128)S(1)} %bitcast.15), channel_id=1, replica_groups=mesh['gx'=2,'gy'=4,'gz'=4] {'gx','gy','gz'}, dimensions={0} | all-to-all | bytes 32768 | tf_op jit(solution)/shard_map/all_to_all | solution.py:602
  73.6 1.1 %shard_map.88 = (f32[16,16,256]{2,1,0:T(8,128)}, f32[16,16,256]{2,1,0:T(8,128)}) custom-call(f32[32,128]{1,0:T(8,128)S(1)} %bitcast.14, f32[16,128]{1,0:T(8,128)S(1)} %get-tuple-element.96.refs_1_, f32[16,16,256]{2,1,0:T(8,128)S(1)} %copy-done.3, f32[16,16,256]{2,1,0:T(8,128)S(1)} %copy-done.1, f32[16,16,256]{2,1,0:T(8,128)S(1)} %get-tuple-element.92.refs_5_.refs_4_, ...), custom_call_target="tpu_custom_call" | custom-call | bytes 1859584 | tf_op jit(solution)/shard_map/pallas_call | solution.py:511
  (25 shorter events, 0.1 us)
Async XLA Ops:
  2.3 6.2 %collective-permute-start.1 = (f32[24,256]{1,0:T(8,128)S(1)}, f32[24,256]{1,0:T(8,128)S(1)}, u32[]{:S(2)}, u32[]{:S(2)}) collective-permute-start(f32[24,256]{1,0:T(8,128)S(1)} %get-tuple-element.50), channel_id=1, source_target_pairs={{0,3},{1,2},{2,1},{3,0},{4,7},{5,6},{6,5},{7,4},{8,11},{9,10},{10,... | collective-permute-start | bytes 73736 | tf_op jit(solution)/shard_map/ppermute | solution.py:55
  4.8 3.7 %collective-permute-start = (f32[24,256]{1,0:T(8,128)S(1)}, f32[24,256]{1,0:T(8,128)S(1)}, u32[]{:S(2)}, u32[]{:S(2)}) collective-permute-start(f32[24,256]{1,0:T(8,128)S(1)} %get-tuple-element.50), channel_id=1, source_target_pairs={{0,1},{1,0},{2,3},{3,2},{4,5},{5,4},{6,7},{7,6},{8,9},{9,8},{10,11... | collective-permute-start | bytes 73736 | tf_op jit(solution)/shard_map/ppermute | solution.py:55
  9.7 9.1 %collective-permute-start.2 = (f32[13,16,256]{2,1,0:T(8,128)S(1)}, f32[13,16,256]{2,1,0:T(8,128)S(1)}, u32[]{:S(2)}, u32[]{:S(2)}) collective-permute-start(f32[13,16,256]{2,1,0:T(8,128)S(1)} %get-tuple-element.55), channel_id=1, source_target_pairs={{0,16},{1,17},{2,18},{3,19},{4,20},{5,21},{6,22},{7,23},{8,24},{9,... | collective-permute-start | bytes 638984 | tf_op jit(solution)/shard_map/ppermute | solution.py:55
  11.3 7.5 %collective-permute-start.5 = (f32[13,16,256]{2,1,0:T(8,128)S(1)}, f32[13,16,256]{2,1,0:T(8,128)S(1)}, u32[]{:S(2)}, u32[]{:S(2)}) collective-permute-start(f32[13,16,256]{2,1,0:T(8,128)S(1)} %get-tuple-element.58), channel_id=1, source_target_pairs={{0,4},{1,5},{2,6},{3,7},{4,0},{5,1},{6,2},{7,3},{8,12},{9,13},{10,... | collective-permute-start | bytes 638984 | tf_op jit(solution)/shard_map/ppermute | solution.py:55
  12.8 6.0 %collective-permute-start.6 = (f32[13,16,256]{2,1,0:T(8,128)S(1)}, f32[13,16,256]{2,1,0:T(8,128)S(1)}, u32[]{:S(2)}, u32[]{:S(2)}) collective-permute-start(f32[13,16,256]{2,1,0:T(8,128)S(1)} %get-tuple-element.59), channel_id=1, source_target_pairs={{0,1},{1,0},{2,3},{3,2},{4,8},{5,9},{6,10},{7,11},{8,4},{9,5},{10,... | collective-permute-start | bytes 638984 | tf_op jit(solution)/shard_map/ppermute | solution.py:55
  12.8 5.9 %collective-permute-start.3 = (f32[28,256]{1,0:T(8,128)S(1)}, f32[28,256]{1,0:T(8,128)S(1)}, u32[]{:S(2)}, u32[]{:S(2)}) collective-permute-start(f32[28,256]{1,0:T(8,128)S(1)} %get-tuple-element.56), channel_id=1, source_target_pairs={{0,20},{1,21},{2,22},{3,23},{4,16},{5,17},{6,18},{7,19},{8,28},{9,... | collective-permute-start | bytes 86024 | tf_op jit(solution)/shard_map/ppermute | solution.py:55
  15.9 2.9 %collective-permute-start.4 = (f32[28,256]{1,0:T(8,128)S(1)}, f32[28,256]{1,0:T(8,128)S(1)}, u32[]{:S(2)}, u32[]{:S(2)}) collective-permute-start(f32[28,256]{1,0:T(8,128)S(1)} %get-tuple-element.57), channel_id=1, source_target_pairs={{0,1},{1,0},{2,3},{3,2},{4,24},{5,25},{6,26},{7,27},{8,20},{9,21},... | collective-permute-start | bytes 86024 | tf_op jit(solution)/shard_map/ppermute | solution.py:55
  15.9 9.9 %all-to-all-start = ((f32[32,1,128]{2,1,0:T(1,128)}), f32[32,1,128]{2,1,0:T(1,128)S(1)}, u32[]{:S(2)}, u32[]{:S(2)}) async-start(f32[32,1,128]{2,1,0:T(1,128)} %bitcast.1), calls=%async_computation | async-start | bytes 32768 | tf_op jit(solution)/shard_map/all_to_all | solution.py:602
  25.8 9.8 %copy-start = (f32[16,16,16,256]{3,2,1,0:T(8,128)S(1)}, f32[16,16,16,256]{3,2,1,0:T(8,128)}, u32[]{:S(2)}) copy-start(f32[16,16,16,256]{3,2,1,0:T(8,128)} %refs_11_.3) | copy-start | bytes 12582916
  28.3 5.2 %collective-permute-start.7 = (f32[1,16,256]{2,1,0:T(8,128)S(1)}, f32[1,16,256]{2,1,0:T(8,128)S(1)}, u32[]{:S(2)}, u32[]{:S(2)}) collective-permute-start(f32[1,16,256]{2,1,0:T(8,128)S(1)} %get-tuple-element.62), channel_id=1, source_target_pairs={{0,16},{1,17},{2,18},{3,19},{4,20},{5,21},{6,22},{7,23},{8,24},{9,... | collective-permute-start | bytes 49160 | tf_op jit(solution)/shard_map/ppermute | solution.py:55
  28.9 4.5 %collective-permute-start.8 = (f32[1,16,256]{2,1,0:T(8,128)S(1)}, f32[1,16,256]{2,1,0:T(8,128)S(1)}, u32[]{:S(2)}, u32[]{:S(2)}) collective-permute-start(f32[1,16,256]{2,1,0:T(8,128)S(1)} %get-tuple-element.63), channel_id=1, source_target_pairs={{0,4},{1,5},{2,6},{3,7},{4,0},{5,1},{6,2},{7,3},{8,12},{9,13},{10,... | collective-permute-start | bytes 49160 | tf_op jit(solution)/shard_map/ppermute | solution.py:55
  30.3 3.1 %collective-permute-start.9 = (f32[1,16,256]{2,1,0:T(8,128)S(1)}, f32[1,16,256]{2,1,0:T(8,128)S(1)}, u32[]{:S(2)}, u32[]{:S(2)}) collective-permute-start(f32[1,16,256]{2,1,0:T(8,128)S(1)} %get-tuple-element.64), channel_id=1, source_target_pairs={{0,1},{1,0},{2,3},{3,2},{4,8},{5,9},{6,10},{7,11},{8,4},{9,5},{10,... | collective-permute-start | bytes 49160 | tf_op jit(solution)/shard_map/ppermute | solution.py:55
  30.3 3.1 %collective-permute-start.11 = (f32[8,256]{1,0:T(8,128)S(1)}, f32[8,256]{1,0:T(8,128)S(1)}, u32[]{:S(2)}, u32[]{:S(2)}) collective-permute-start(f32[8,256]{1,0:T(8,128)S(1)} %get-tuple-element.65), channel_id=1, source_target_pairs={{0,3},{1,2},{2,1},{3,0},{4,7},{5,6},{6,5},{7,4},{8,11},{9,10},{10,... | collective-permute-start | bytes 24584 | tf_op jit(solution)/shard_map/ppermute | solution.py:55
  31.0 2.4 %collective-permute-start.10 = (f32[8,256]{1,0:T(8,128)S(1)}, f32[8,256]{1,0:T(8,128)S(1)}, u32[]{:S(2)}, u32[]{:S(2)}) collective-permute-start(f32[8,256]{1,0:T(8,128)S(1)} %get-tuple-element.65), channel_id=1, source_target_pairs={{0,1},{1,0},{2,3},{3,2},{4,5},{5,4},{6,7},{7,6},{8,9},{9,8},{10,11... | collective-permute-start | bytes 24584 | tf_op jit(solution)/shard_map/ppermute | solution.py:55
  34.9 3.1 %collective-permute-start.13 = (f32[8,256]{1,0:T(8,128)S(1)}, f32[8,256]{1,0:T(8,128)S(1)}, u32[]{:S(2)}, u32[]{:S(2)}) collective-permute-start(f32[8,256]{1,0:T(8,128)S(1)} %get-tuple-element.68), channel_id=1, source_target_pairs={{0,3},{1,2},{2,1},{3,0},{4,7},{5,6},{6,5},{7,4},{8,11},{9,10},{10,... | collective-permute-start | bytes 24584 | tf_op jit(solution)/shard_map/ppermute | solution.py:55
  35.6 2.4 %collective-permute-start.12 = (f32[8,256]{1,0:T(8,128)S(1)}, f32[8,256]{1,0:T(8,128)S(1)}, u32[]{:S(2)}, u32[]{:S(2)}) collective-permute-start(f32[8,256]{1,0:T(8,128)S(1)} %get-tuple-element.68), channel_id=1, source_target_pairs={{0,1},{1,0},{2,3},{3,2},{4,5},{5,4},{6,7},{7,6},{8,9},{9,8},{10,11... | collective-permute-start | bytes 24584 | tf_op jit(solution)/shard_map/ppermute | solution.py:55
  39.0 9.2 %collective-permute-start.14 = (f32[3,16,256]{2,1,0:T(8,128)S(1)}, f32[3,16,256]{2,1,0:T(8,128)S(1)}, u32[]{:S(2)}, u32[]{:S(2)}) collective-permute-start(f32[3,16,256]{2,1,0:T(8,128)S(1)} %get-tuple-element.71), channel_id=1, source_target_pairs={{0,16},{1,17},{2,18},{3,19},{4,20},{5,21},{6,22},{7,23},{8,24},{9,... | collective-permute-start | bytes 147464 | tf_op jit(solution)/shard_map/ppermute | solution.py:55
  39.7 8.5 %collective-permute-start.17 = (f32[3,16,256]{2,1,0:T(8,128)S(1)}, f32[3,16,256]{2,1,0:T(8,128)S(1)}, u32[]{:S(2)}, u32[]{:S(2)}) collective-permute-start(f32[3,16,256]{2,1,0:T(8,128)S(1)} %get-tuple-element.74), channel_id=1, source_target_pairs={{0,4},{1,5},{2,6},{3,7},{4,0},{5,1},{6,2},{7,3},{8,12},{9,13},{10,... | collective-permute-start | bytes 147464 | tf_op jit(solution)/shard_map/ppermute | solution.py:55
  41.7 6.5 %collective-permute-start.18 = (f32[3,16,256]{2,1,0:T(8,128)S(1)}, f32[3,16,256]{2,1,0:T(8,128)S(1)}, u32[]{:S(2)}, u32[]{:S(2)}) collective-permute-start(f32[3,16,256]{2,1,0:T(8,128)S(1)} %get-tuple-element.75), channel_id=1, source_target_pairs={{0,1},{1,0},{2,3},{3,2},{4,8},{5,9},{6,10},{7,11},{8,4},{9,5},{10,... | collective-permute-start | bytes 147464 | tf_op jit(solution)/shard_map/ppermute | solution.py:55
  41.7 6.5 %collective-permute-start.15 = (f32[8,256]{1,0:T(8,128)S(1)}, f32[8,256]{1,0:T(8,128)S(1)}, u32[]{:S(2)}, u32[]{:S(2)}) collective-permute-start(f32[8,256]{1,0:T(8,128)S(1)} %get-tuple-element.72), channel_id=1, source_target_pairs={{0,20},{1,21},{2,22},{3,23},{4,16},{5,17},{6,18},{7,19},{8,28},{9,... | collective-permute-start | bytes 24584 | tf_op jit(solution)/shard_map/ppermute | solution.py:55
  44.3 3.9 %collective-permute-start.16 = (f32[8,256]{1,0:T(8,128)S(1)}, f32[8,256]{1,0:T(8,128)S(1)}, u32[]{:S(2)}, u32[]{:S(2)}) collective-permute-start(f32[8,256]{1,0:T(8,128)S(1)} %get-tuple-element.73), channel_id=1, source_target_pairs={{0,1},{1,0},{2,3},{3,2},{4,24},{5,25},{6,26},{7,27},{8,20},{9,21},... | collective-permute-start | bytes 24584 | tf_op jit(solution)/shard_map/ppermute | solution.py:55
  44.3 11.0 %all-to-all-start.1 = ((f32[32,1,128]{2,1,0:T(1,128)}), f32[32,1,128]{2,1,0:T(1,128)S(1)}, u32[]{:S(2)}, u32[]{:S(2)}) async-start(f32[32,1,128]{2,1,0:T(1,128)} %bitcast.4), calls=%async_computation.1 | async-start | bytes 32768 | tf_op jit(solution)/shard_map/all_to_all | solution.py:602
  55.3 6.5 %copy-start.1 = (f32[16,16,256]{2,1,0:T(8,128)S(1)}, f32[16,16,256]{2,1,0:T(8,128)}, u32[]{:S(2)}) copy-start(f32[16,16,256]{2,1,0:T(8,128)} %get-tuple-element.76.refs_5_.refs_3_.refs_7_) | copy-start | bytes 786436
  55.3 6.5 %copy-start.2 = (f32[7,16,16,256]{3,2,1,0:T(8,128)S(1)}, f32[7,16,16,256]{3,2,1,0:T(8,128)}, u32[]{:S(2)}) copy-start(f32[7,16,16,256]{3,2,1,0:T(8,128)} %get-tuple-element.93.refs_6_) | copy-start | bytes 5505028
  57.4 16.2 %copy-start.3 = (f32[16,16,256]{2,1,0:T(8,128)S(1)}, f32[16,16,256]{2,1,0:T(8,128)}, u32[]{:S(2)}) copy-start(f32[16,16,256]{2,1,0:T(8,128)} %get-tuple-element.82.refs_5_.refs_2_) | copy-start | bytes 786436
  57.4 4.2 %collective-permute-start.19 = (f32[1,16,256]{2,1,0:T(8,128)S(1)}, f32[1,16,256]{2,1,0:T(8,128)S(1)}, u32[]{:S(2)}, u32[]{:S(2)}) collective-permute-start(f32[1,16,256]{2,1,0:T(8,128)S(1)} %get-tuple-element.88), channel_id=1, source_target_pairs={{0,16},{1,17},{2,18},{3,19},{4,20},{5,21},{6,22},{7,23},{8,24},{9,... | collective-permute-start | bytes 49160 | tf_op jit(solution)/shard_map/ppermute | solution.py:55
  58.1 3.7 %collective-permute-start.20 = (f32[1,16,256]{2,1,0:T(8,128)S(1)}, f32[1,16,256]{2,1,0:T(8,128)S(1)}, u32[]{:S(2)}, u32[]{:S(2)}) collective-permute-start(f32[1,16,256]{2,1,0:T(8,128)S(1)} %get-tuple-element.89), channel_id=1, source_target_pairs={{0,4},{1,5},{2,6},{3,7},{4,0},{5,1},{6,2},{7,3},{8,12},{9,13},{10,... | collective-permute-start | bytes 49160 | tf_op jit(solution)/shard_map/ppermute | solution.py:55
  58.6 3.2 %collective-permute-start.21 = (f32[1,16,256]{2,1,0:T(8,128)S(1)}, f32[1,16,256]{2,1,0:T(8,128)S(1)}, u32[]{:S(2)}, u32[]{:S(2)}) collective-permute-start(f32[1,16,256]{2,1,0:T(8,128)S(1)} %get-tuple-element.90), channel_id=1, source_target_pairs={{0,1},{1,0},{2,3},{3,2},{4,8},{5,9},{6,10},{7,11},{8,4},{9,5},{10,... | collective-permute-start | bytes 49160 | tf_op jit(solution)/shard_map/ppermute | solution.py:55
  58.6 3.1 %collective-permute-start.23 = (f32[8,256]{1,0:T(8,128)S(1)}, f32[8,256]{1,0:T(8,128)S(1)}, u32[]{:S(2)}, u32[]{:S(2)}) collective-permute-start(f32[8,256]{1,0:T(8,128)S(1)} %get-tuple-element.91), channel_id=1, source_target_pairs={{0,3},{1,2},{2,1},{3,0},{4,7},{5,6},{6,5},{7,4},{8,11},{9,10},{10,... | collective-permute-start | bytes 24584 | tf_op jit(solution)/shard_map/ppermute | solution.py:55
  59.3 2.4 %collective-permute-start.22 = (f32[8,256]{1,0:T(8,128)S(1)}, f32[8,256]{1,0:T(8,128)S(1)}, u32[]{:S(2)}, u32[]{:S(2)}) collective-permute-start(f32[8,256]{1,0:T(8,128)S(1)} %get-tuple-element.91), channel_id=1, source_target_pairs={{0,1},{1,0},{2,3},{3,2},{4,5},{5,4},{6,7},{7,6},{8,9},{9,8},{10,11... | collective-permute-start | bytes 24584 | tf_op jit(solution)/shard_map/ppermute | solution.py:55

commit v7 on v6

--- a/solution.py
+++ b/solution.py
@@ -636,7 +636,7 @@
         row = project(base, rhs.get()[...])
         out[...] = jnp.broadcast_to(row, out.shape)
 
-    rows = call(first_rows, row_shape, (Far(right_side), Far(basis, range(PARTS))))
+    rows = call(first_rows, row_shape, (first["near"][2], Far(basis, range(PARTS))))
     rows_a = spread(rows)
 
     def pack_all(got_z, near, free, rows, outs, ends):
@@ -771,7 +771,7 @@
             "tile": shaped(z_rows(1), nx * ny),
             "sums": shaped(1, LANES),
         },
-        (got, got_z, direction, own, Far(right_side)),
+        (got, got_z, direction, own, right_side),
         [vbox],
     )
     got_z = send_z(imaged["tile"], sizes)

time: 75.2 us -> 75 us (level)
  no operation moved by 1% of the time
where the time goes in v7:
time: 75 us; the launch traced here: 74.6 us
  starting transfers between devices  26.7 us (36%)
  Pallas kernels  24.1 us (32%)
  waiting for transfers between devices  11.9 us (16%)
  blocking collectives  11.1 us (15%)
  between operations  0.85 us (1%)
    pallas_call x12, Pallas kernels, call(): pl.pallas_call(body, out_shape=[pltpu.HBM(a.shape, F32) if i in distant e...  24.1 us
    ppermute x24, starting transfers between devices, swap(): return lax.ppermute(value, AXES, pairs)  20 us
    all_to_all x1, blocking collectives, spread(): return lax.all_to_all(rows, AXES, 0, 0, tiled=True)  11.1 us
    all_to_all x2, starting transfers between devices, spread(): return lax.all_to_all(rows, AXES, 0, 0, tiled=True)  6.69 us
    ppermute x24, waiting for transfers between devices, swap(): return lax.ppermute(value, AXES, pairs)  6.24 us
    all_to_all x2, waiting for transfers between devices, spread(): return lax.all_to_all(rows, AXES, 0, 0, tiled=True)  5.67 us
  transfers between devices with their start and end apart: 26, of which 6 were waited for; matrix products, arithmetic and copies ran while one was open for 0% of the time, Pallas kernels for 17%

profile of v7, /device:TPU:0, one launch (start us, length us, event | category | flops | bytes accessed | tf_op | source)
XLA Modules:
  0.0 74.6 jit_solution(10876444654422881926)
XLA Ops:
  0.6 1.7 %shard_map.77 = (f32[16,16,256]{2,1,0:T(8,128)S(1)}, f32[3,16,16,256]{3,2,1,0:T(8,128)S(1)}, f32[16,16,256]{2,1,0:T(8,128)S(1)}, f32[16,16,256]{2,1,0:T(8,128)S(1)}, f32[24,256]{1,0:T(8,128)S(1)}) custom-call(f32[3,16,16,256]{3,2,1,0:T(8,128)} %refs_5_.1, f32[16,16,256]{2,1,0:T(8,128)} %refs_6_.1, s32[16,16,256]{2,1,0:T(8,128)} %refs_7_.2, ...), custom_call_target="tpu_custom_call" | custom-call | bytes 3170304 | tf_op jit(solution)/shard_map/pallas_call | solution.py:511
  2.3 2.4 %collective-permute-start.1 = (f32[24,256]{1,0:T(8,128)S(1)}, f32[24,256]{1,0:T(8,128)S(1)}, u32[]{:S(2)}, u32[]{:S(2)}) collective-permute-start(f32[24,256]{1,0:T(8,128)S(1)} %get-tuple-element.50), channel_id=1, source_target_pairs={{0,3},{1,2},{2,1},{3,0},{4,7},{5,6},{6,5},{7,4},{8,11},{9,10},{10,... | collective-permute-start | bytes 73736 | tf_op jit(solution)/shard_map/ppermute | solution.py:55
  4.8 0.7 collective-permute-start
  5.5 3.0 %shard_map.78.refs_6_ = f32[32,128]{1,0:T(8,128)} custom-call(f32[16,16,256]{2,1,0:T(8,128)S(1)} %get-tuple-element.53.refs_0_.refs_4_, f32[16,16,16,256]{3,2,1,0:T(8,128)} %refs_11_.3), custom_call_target="tpu_custom_call" | custom-call | bytes 4472832 | tf_op jit(solution)/shard_map/pallas_call | solution.py:511
  8.4 0.0 collective-permute-done.1.refs_1_.refs_10_
  8.4 1.1 %shard_map.79 = (f32[13,16,256]{2,1,0:T(8,128)S(1)}, f32[28,256]{1,0:T(8,128)S(1)}, f32[28,256]{1,0:T(8,128)S(1)}, f32[13,16,256]{2,1,0:T(8,128)S(1)}, f32[13,16,256]{2,1,0:T(8,128)S(1)}) custom-call(f32[24,256]{1,0:T(8,128)S(1)} %collective-permute-done.refs_0_.refs_9_, f32[24,256]{1,0:T(8,128)S(1)} %collective-permute-done.1.refs_1_.refs_10_, ...), custom_call_target="tpu_custom_call" | custom-call | bytes 2334720 | tf_op jit(solution)/shard_map/pallas_call | solution.py:511
  9.6 1.6 %collective-permute-start.2 = (f32[13,16,256]{2,1,0:T(8,128)S(1)}, f32[13,16,256]{2,1,0:T(8,128)S(1)}, u32[]{:S(2)}, u32[]{:S(2)}) collective-permute-start(f32[13,16,256]{2,1,0:T(8,128)S(1)} %get-tuple-element.55), channel_id=1, source_target_pairs={{0,16},{1,17},{2,18},{3,19},{4,20},{5,21},{6,22},{7,23},{8,24},{9,... | collective-permute-start | bytes 638984 | tf_op jit(solution)/shard_map/ppermute | solution.py:55
  11.2 1.6 %collective-permute-start.5 = (f32[13,16,256]{2,1,0:T(8,128)S(1)}, f32[13,16,256]{2,1,0:T(8,128)S(1)}, u32[]{:S(2)}, u32[]{:S(2)}) collective-permute-start(f32[13,16,256]{2,1,0:T(8,128)S(1)} %get-tuple-element.58), channel_id=1, source_target_pairs={{0,4},{1,5},{2,6},{3,7},{4,0},{5,1},{6,2},{7,3},{8,12},{9,13},{10,... | collective-permute-start | bytes 638984 | tf_op jit(solution)/shard_map/ppermute | solution.py:55
  12.7 3.1 %collective-permute-start.3 = (f32[28,256]{1,0:T(8,128)S(1)}, f32[28,256]{1,0:T(8,128)S(1)}, u32[]{:S(2)}, u32[]{:S(2)}) collective-permute-start(f32[28,256]{1,0:T(8,128)S(1)} %get-tuple-element.56), channel_id=1, source_target_pairs={{0,20},{1,21},{2,22},{3,23},{4,16},{5,17},{6,18},{7,19},{8,28},{9,... | collective-permute-start | bytes 86024 | tf_op jit(solution)/shard_map/ppermute | solution.py:55
  15.8 0.0 collective-permute-start.4
  15.8 2.8 %all-to-all-start = ((f32[32,1,128]{2,1,0:T(1,128)}), f32[32,1,128]{2,1,0:T(1,128)S(1)}, u32[]{:S(2)}, u32[]{:S(2)}) async-start(f32[32,1,128]{2,1,0:T(1,128)} %bitcast.1), calls=%async_computation | async-start | bytes 32768 | tf_op jit(solution)/shard_map/all_to_all | solution.py:602
  18.6 0.0 collective-permute-done.3.refs_1_
  18.7 0.0 collective-permute-done.4.refs_2_
  18.7 0.0 collective-permute-done.2.refs_0_
  18.7 0.0 collective-permute-done.5.refs_3_
  18.7 0.0 collective-permute-done.6.refs_4_
  18.7 4.7 %shard_map.80 = (f32[2,16,16,256]{3,2,1,0:T(8,128)S(1)}, f32[22,24,384]{2,1,0:T(8,128)}, f32[22,24,384]{2,1,0:T(8,128)}, f32[22,24,384]{2,1,0:T(8,128)}, f32[22,...) custom-call(f32[13,16,256]{2,1,0:T(8,128)S(1)} %collective-permute-done.2.refs_0_, ...), custom_call_target="tpu_custom_call" | custom-call | flops 1000000000 | bytes 12378112 | tf_op jit(solution)/shard_map/pallas_call | solution.py:511
  23.4 2.3 %all-to-all-done = f32[32,1,128]{2,1,0:T(1,128)S(1)} async-done(((f32[32,1,128]{2,1,0:T(1,128)}), f32[32,1,128]{2,1,0:T(1,128)S(1)}, u32[]{:S(2)}, u32[]{:S(2)}) %all-to-all-start) | async-done | bytes 16416 | tf_op jit(solution)/shard_map/all_to_all | solution.py:602
  25.7 2.4 %shard_map.81 = (f32[1,16,256]{2,1,0:T(8,128)S(1)}, f32[1,16,256]{2,1,0:T(8,128)S(1)}, f32[1,16,256]{2,1,0:T(8,128)S(1)}, f32[8,256]{1,0:T(8,128)S(1)}, f32[16,16,256]{2,1,0:T(8,128)S(1)}) custom-call(f32[16,16,256]{2,1,0:T(8,128)S(1)} %get-tuple-element.60.refs_0_, f32[32,128]{1,0:T(8,128)S(1)} %bitcast.13, f32[16,512]{1,0:T(8,128)} %refs_2_.5, ...), custom_call_target="tpu_custom_call" | custom-call | bytes 5349376 | tf_op jit(solution)/shard_map/pallas_call | solution.py:511
  28.2 0.7 collective-permute-start.7
  28.8 1.4 %collective-permute-start.8 = (f32[1,16,256]{2,1,0:T(8,128)S(1)}, f32[1,16,256]{2,1,0:T(8,128)S(1)}, u32[]{:S(2)}, u32[]{:S(2)}) collective-permute-start(f32[1,16,256]{2,1,0:T(8,128)S(1)} %get-tuple-element.63), channel_id=1, source_target_pairs={{0,4},{1,5},{2,6},{3,7},{4,0},{5,1},{6,2},{7,3},{8,12},{9,13},{10,... | collective-permute-start | bytes 49160 | tf_op jit(solution)/shard_map/ppermute | solution.py:55
  30.2 0.0 collective-permute-start.9
  30.2 0.6 collective-permute-start.11
  30.9 0.0 collective-permute-start.10
  30.9 2.4 %collective-permute-done.11.refs_4_ = f32[8,256]{1,0:T(8,128)S(1)} collective-permute-done((f32[8,256]{1,0:T(8,128)S(1)}, f32[8,256]{1,0:T(8,128)S(1)}, u32[]{:S(2)}, u32[]{:S(2)}) %collective-permute-start.11) | collective-permute-done | bytes 8224 | tf_op jit(solution)/shard_map/ppermute | solution.py:55
  33.3 1.4 %shard_map.82 = (f32[16,16,256]{2,1,0:T(8,128)S(1)}, f32[16,16,256]{2,1,0:T(8,128)}, f32[7,16,16,256]{3,2,1,0:T(8,128)}, f32[1,128]{1,0:T(1,128)S(1)}, f32[8,256]{1,0:T(8,128)S(1)}, /*index=5*/f32[16,16,256]{2,1,0:T(8,128)}) custom-call(f32[1,16,256]{2,1,0:T(8,128)S(1)} %collective-permute-done.7.refs_0_, f32[1,16,256]{2,1,0:T(8,128)S(1)} %collective-permute-done.8.refs_1_, ...), custom_call_target="tpu_custom_call" | custom-call | bytes 5054976 | tf_op jit(solution)/shard_map/pallas_call | solution.py:511
  34.8 0.7 collective-permute-start.13
  35.5 0.0 collective-permute-start.12
  35.5 1.2 %shard_map.83.refs_3_ = f32[32,128]{1,0:T(8,128)} custom-call(f32[16,16,16,256]{3,2,1,0:T(8,128)S(1)} %copy-done, f32[16,16,256]{2,1,0:T(8,128)S(1)} %get-tuple-element.69.refs_1_.refs_2_, f32[1,128]{1,0:T(1,128)S(1)} %get-tuple-element.70.refs_2_), custom_call_target="tpu_custom_call" | custom-call | bytes 4473344 | tf_op jit(solution)/shard_map/pallas_call | solution.py:511
  36.7 1.2 %collective-permute-done.13.refs_1_.refs_7_ = f32[8,256]{1,0:T(8,128)S(1)} collective-permute-done((f32[8,256]{1,0:T(8,128)S(1)}, f32[8,256]{1,0:T(8,128)S(1)}, u32[]{:S(2)}, u32[]{:S(2)}) %collective-permute-start.13) | collective-permute-done | bytes 8224 | tf_op jit(solution)/shard_map/ppermute | solution.py:55
  37.9 1.0 %shard_map.84 = (f32[3,16,256]{2,1,0:T(8,128)S(1)}, f32[8,256]{1,0:T(8,128)S(1)}, f32[8,256]{1,0:T(8,128)S(1)}, f32[3,16,256]{2,1,0:T(8,128)S(1)}, f32[3,16,256]{2,1,0:T(8,128)S(1)}) custom-call(f32[8,256]{1,0:T(8,128)S(1)} %collective-permute-done.12.refs_0_.refs_6_, f32[8,256]{1,0:T(8,128)S(1)} %collective-permute-done.13.refs_1_.refs_7_, ...), custom_call_target="tpu_custom_call" | custom-call | bytes 458752 | tf_op jit(solution)/shard_map/pallas_call | solution.py:511
  38.9 0.8 %collective-permute-start.14 = (f32[3,16,256]{2,1,0:T(8,128)S(1)}, f32[3,16,256]{2,1,0:T(8,128)S(1)}, u32[]{:S(2)}, u32[]{:S(2)}) collective-permute-start(f32[3,16,256]{2,1,0:T(8,128)S(1)} %get-tuple-element.71), channel_id=1, source_target_pairs={{0,16},{1,17},{2,18},{3,19},{4,20},{5,21},{6,22},{7,23},{8,24},{9,... | collective-permute-start | bytes 147464 | tf_op jit(solution)/shard_map/ppermute | solution.py:55
  39.7 2.0 %collective-permute-start.17 = (f32[3,16,256]{2,1,0:T(8,128)S(1)}, f32[3,16,256]{2,1,0:T(8,128)S(1)}, u32[]{:S(2)}, u32[]{:S(2)}) collective-permute-start(f32[3,16,256]{2,1,0:T(8,128)S(1)} %get-tuple-element.74), channel_id=1, source_target_pairs={{0,4},{1,5},{2,6},{3,7},{4,0},{5,1},{6,2},{7,3},{8,12},{9,13},{10,... | collective-permute-start | bytes 147464 | tf_op jit(solution)/shard_map/ppermute | solution.py:55
  41.6 2.5 %collective-permute-start.15 = (f32[8,256]{1,0:T(8,128)S(1)}, f32[8,256]{1,0:T(8,128)S(1)}, u32[]{:S(2)}, u32[]{:S(2)}) collective-permute-start(f32[8,256]{1,0:T(8,128)S(1)} %get-tuple-element.72), channel_id=1, source_target_pairs={{0,20},{1,21},{2,22},{3,23},{4,16},{5,17},{6,18},{7,19},{8,28},{9,... | collective-permute-start | bytes 24584 | tf_op jit(solution)/shard_map/ppermute | solution.py:55
  44.2 3.9 %all-to-all-start.1 = ((f32[32,1,128]{2,1,0:T(1,128)}), f32[32,1,128]{2,1,0:T(1,128)S(1)}, u32[]{:S(2)}, u32[]{:S(2)}) async-start(f32[32,1,128]{2,1,0:T(1,128)} %bitcast.4), calls=%async_computation.1 | async-start | bytes 32768 | tf_op jit(solution)/shard_map/all_to_all | solution.py:602
  48.1 3.7 %shard_map.85 = (f32[2,16,16,256]{3,2,1,0:T(8,128)S(1)}, f32[2,16,16,256]{3,2,1,0:T(8,128)S(1)}, f32[2,16,16,256]{3,2,1,0:T(8,128)S(1)}, f32[2,16,16,256]{3,2,1,...) custom-call(f32[3,16,256]{2,1,0:T(8,128)S(1)} %collective-permute-done.14.refs_0_, ...), custom_call_target="tpu_custom_call" | custom-call | flops 1000000000 | bytes 10764288 | tf_op jit(solution)/shard_map/pallas_call | solution.py:511
  51.8 3.4 %all-to-all-done.1 = f32[32,1,128]{2,1,0:T(1,128)S(1)} async-done(((f32[32,1,128]{2,1,0:T(1,128)}), f32[32,1,128]{2,1,0:T(1,128)S(1)}, u32[]{:S(2)}, u32[]{:S(2)}) %all-to-all-start.1) | async-done | bytes 16416 | tf_op jit(solution)/shard_map/all_to_all | solution.py:602
  55.2 2.1 %shard_map.86 = (f32[1,16,256]{2,1,0:T(8,128)S(1)}, f32[1,16,256]{2,1,0:T(8,128)S(1)}, f32[1,16,256]{2,1,0:T(8,128)S(1)}, f32[16,16,256]{2,1,0:T(8,128)S(1)}, f3...) custom-call(f32[16,16,256]{2,1,0:T(8,128)S(1)} %get-tuple-element.81.refs_0_, ...), custom_call_target="tpu_custom_call" | custom-call | bytes 8503296 | tf_op jit(solution)/shard_map/pallas_call | solution.py:511
  57.3 0.0 copy-start.4
  57.3 0.7 collective-permute-start.19
  58.0 0.5 collective-permute-start.20
  58.5 0.7 collective-permute-start.23
  59.2 0.0 collective-permute-start.22
  59.2 2.3 %collective-permute-done.23.refs_4_ = f32[8,256]{1,0:T(8,128)S(1)} collective-permute-done((f32[8,256]{1,0:T(8,128)S(1)}, f32[8,256]{1,0:T(8,128)S(1)}, u32[]{:S(2)}, u32[]{:S(2)}) %collective-permute-start.23) | collective-permute-done | bytes 8224 | tf_op jit(solution)/shard_map/ppermute | solution.py:55
  61.6 0.1 collective-permute-done.20.refs_1_
  61.7 0.7 shard_map.87
  62.4 11.1 %all_to_all.33 = f32[32,1,128]{2,1,0:T(1,128)S(1)} all-to-all(f32[32,1,128]{2,1,0:T(1,128)S(1)} %bitcast.15), channel_id=1, replica_groups=mesh['gx'=2,'gy'=4,'gz'=4] {'gx','gy','gz'}, dimensions={0} | all-to-all | bytes 32768 | tf_op jit(solution)/shard_map/all_to_all | solution.py:602
  73.5 1.1 %shard_map.88 = (f32[16,16,256]{2,1,0:T(8,128)}, f32[16,16,256]{2,1,0:T(8,128)}) custom-call(f32[32,128]{1,0:T(8,128)S(1)} %bitcast.14, f32[16,128]{1,0:T(8,128)S(1)} %get-tuple-element.96.refs_1_, f32[16,16,256]{2,1,0:T(8,128)S(1)} %copy-done.4, f32[16,16,256]{2,1,0:T(8,128)S(1)} %copy-done.2, f32[16,16,256]{2,1,0:T(8,128)S(1)} %get-tuple-element.92.refs_5_.refs_4_, ...), custom_call_target="tpu_custom_call" | custom-call | bytes 1859584 | tf_op jit(solution)/shard_map/pallas_call | solution.py:511
  (27 shorter events, 0.1 us)
Async XLA Ops:
  2.3 6.1 %collective-permute-start.1 = (f32[24,256]{1,0:T(8,128)S(1)}, f32[24,256]{1,0:T(8,128)S(1)}, u32[]{:S(2)}, u32[]{:S(2)}) collective-permute-start(f32[24,256]{1,0:T(8,128)S(1)} %get-tuple-element.50), channel_id=1, source_target_pairs={{0,3},{1,2},{2,1},{3,0},{4,7},{5,6},{6,5},{7,4},{8,11},{9,10},{10,... | collective-permute-start | bytes 73736 | tf_op jit(solution)/shard_map/ppermute | solution.py:55
  4.8 3.7 %collective-permute-start = (f32[24,256]{1,0:T(8,128)S(1)}, f32[24,256]{1,0:T(8,128)S(1)}, u32[]{:S(2)}, u32[]{:S(2)}) collective-permute-start(f32[24,256]{1,0:T(8,128)S(1)} %get-tuple-element.50), channel_id=1, source_target_pairs={{0,1},{1,0},{2,3},{3,2},{4,5},{5,4},{6,7},{7,6},{8,9},{9,8},{10,11... | collective-permute-start | bytes 73736 | tf_op jit(solution)/shard_map/ppermute | solution.py:55
  9.6 9.1 %collective-permute-start.2 = (f32[13,16,256]{2,1,0:T(8,128)S(1)}, f32[13,16,256]{2,1,0:T(8,128)S(1)}, u32[]{:S(2)}, u32[]{:S(2)}) collective-permute-start(f32[13,16,256]{2,1,0:T(8,128)S(1)} %get-tuple-element.55), channel_id=1, source_target_pairs={{0,16},{1,17},{2,18},{3,19},{4,20},{5,21},{6,22},{7,23},{8,24},{9,... | collective-permute-start | bytes 638984 | tf_op jit(solution)/shard_map/ppermute | solution.py:55
  11.2 7.5 %collective-permute-start.5 = (f32[13,16,256]{2,1,0:T(8,128)S(1)}, f32[13,16,256]{2,1,0:T(8,128)S(1)}, u32[]{:S(2)}, u32[]{:S(2)}) collective-permute-start(f32[13,16,256]{2,1,0:T(8,128)S(1)} %get-tuple-element.58), channel_id=1, source_target_pairs={{0,4},{1,5},{2,6},{3,7},{4,0},{5,1},{6,2},{7,3},{8,12},{9,13},{10,... | collective-permute-start | bytes 638984 | tf_op jit(solution)/shard_map/ppermute | solution.py:55
  12.7 6.0 %collective-permute-start.6 = (f32[13,16,256]{2,1,0:T(8,128)S(1)}, f32[13,16,256]{2,1,0:T(8,128)S(1)}, u32[]{:S(2)}, u32[]{:S(2)}) collective-permute-start(f32[13,16,256]{2,1,0:T(8,128)S(1)} %get-tuple-element.59), channel_id=1, source_target_pairs={{0,1},{1,0},{2,3},{3,2},{4,8},{5,9},{6,10},{7,11},{8,4},{9,5},{10,... | collective-permute-start | bytes 638984 | tf_op jit(solution)/shard_map/ppermute | solution.py:55
  12.7 5.9 %collective-permute-start.3 = (f32[28,256]{1,0:T(8,128)S(1)}, f32[28,256]{1,0:T(8,128)S(1)}, u32[]{:S(2)}, u32[]{:S(2)}) collective-permute-start(f32[28,256]{1,0:T(8,128)S(1)} %get-tuple-element.56), channel_id=1, source_target_pairs={{0,20},{1,21},{2,22},{3,23},{4,16},{5,17},{6,18},{7,19},{8,28},{9,... | collective-permute-start | bytes 86024 | tf_op jit(solution)/shard_map/ppermute | solution.py:55
  15.8 2.9 %collective-permute-start.4 = (f32[28,256]{1,0:T(8,128)S(1)}, f32[28,256]{1,0:T(8,128)S(1)}, u32[]{:S(2)}, u32[]{:S(2)}) collective-permute-start(f32[28,256]{1,0:T(8,128)S(1)} %get-tuple-element.57), channel_id=1, source_target_pairs={{0,1},{1,0},{2,3},{3,2},{4,24},{5,25},{6,26},{7,27},{8,20},{9,21},... | collective-permute-start | bytes 86024 | tf_op jit(solution)/shard_map/ppermute | solution.py:55
  15.8 9.9 %all-to-all-start = ((f32[32,1,128]{2,1,0:T(1,128)}), f32[32,1,128]{2,1,0:T(1,128)S(1)}, u32[]{:S(2)}, u32[]{:S(2)}) async-start(f32[32,1,128]{2,1,0:T(1,128)} %bitcast.1), calls=%async_computation | async-start | bytes 32768 | tf_op jit(solution)/shard_map/all_to_all | solution.py:602
  25.7 7.6 %copy-start.1 = (f32[16,16,256]{2,1,0:T(8,128)S(1)}, f32[16,16,256]{2,1,0:T(8,128)}, u32[]{:S(2)}) copy-start(f32[16,16,256]{2,1,0:T(8,128)} %refs_4_.3) | copy-start | bytes 786436
  25.7 9.8 %copy-start = (f32[16,16,16,256]{3,2,1,0:T(8,128)S(1)}, f32[16,16,16,256]{3,2,1,0:T(8,128)}, u32[]{:S(2)}) copy-start(f32[16,16,16,256]{3,2,1,0:T(8,128)} %refs_11_.3) | copy-start | bytes 12582916
  28.2 5.1 %collective-permute-start.7 = (f32[1,16,256]{2,1,0:T(8,128)S(1)}, f32[1,16,256]{2,1,0:T(8,128)S(1)}, u32[]{:S(2)}, u32[]{:S(2)}) collective-permute-start(f32[1,16,256]{2,1,0:T(8,128)S(1)} %get-tuple-element.62), channel_id=1, source_target_pairs={{0,16},{1,17},{2,18},{3,19},{4,20},{5,21},{6,22},{7,23},{8,24},{9,... | collective-permute-start | bytes 49160 | tf_op jit(solution)/shard_map/ppermute | solution.py:55
  28.8 4.5 %collective-permute-start.8 = (f32[1,16,256]{2,1,0:T(8,128)S(1)}, f32[1,16,256]{2,1,0:T(8,128)S(1)}, u32[]{:S(2)}, u32[]{:S(2)}) collective-permute-start(f32[1,16,256]{2,1,0:T(8,128)S(1)} %get-tuple-element.63), channel_id=1, source_target_pairs={{0,4},{1,5},{2,6},{3,7},{4,0},{5,1},{6,2},{7,3},{8,12},{9,13},{10,... | collective-permute-start | bytes 49160 | tf_op jit(solution)/shard_map/ppermute | solution.py:55
  30.2 3.1 %collective-permute-start.9 = (f32[1,16,256]{2,1,0:T(8,128)S(1)}, f32[1,16,256]{2,1,0:T(8,128)S(1)}, u32[]{:S(2)}, u32[]{:S(2)}) collective-permute-start(f32[1,16,256]{2,1,0:T(8,128)S(1)} %get-tuple-element.64), channel_id=1, source_target_pairs={{0,1},{1,0},{2,3},{3,2},{4,8},{5,9},{6,10},{7,11},{8,4},{9,5},{10,... | collective-permute-start | bytes 49160 | tf_op jit(solution)/shard_map/ppermute | solution.py:55
  30.2 3.1 %collective-permute-start.11 = (f32[8,256]{1,0:T(8,128)S(1)}, f32[8,256]{1,0:T(8,128)S(1)}, u32[]{:S(2)}, u32[]{:S(2)}) collective-permute-start(f32[8,256]{1,0:T(8,128)S(1)} %get-tuple-element.65), channel_id=1, source_target_pairs={{0,3},{1,2},{2,1},{3,0},{4,7},{5,6},{6,5},{7,4},{8,11},{9,10},{10,... | collective-permute-start | bytes 24584 | tf_op jit(solution)/shard_map/ppermute | solution.py:55
  30.9 2.4 %collective-permute-start.10 = (f32[8,256]{1,0:T(8,128)S(1)}, f32[8,256]{1,0:T(8,128)S(1)}, u32[]{:S(2)}, u32[]{:S(2)}) collective-permute-start(f32[8,256]{1,0:T(8,128)S(1)} %get-tuple-element.65), channel_id=1, source_target_pairs={{0,1},{1,0},{2,3},{3,2},{4,5},{5,4},{6,7},{7,6},{8,9},{9,8},{10,11... | collective-permute-start | bytes 24584 | tf_op jit(solution)/shard_map/ppermute | solution.py:55
  34.8 3.1 %collective-permute-start.13 = (f32[8,256]{1,0:T(8,128)S(1)}, f32[8,256]{1,0:T(8,128)S(1)}, u32[]{:S(2)}, u32[]{:S(2)}) collective-permute-start(f32[8,256]{1,0:T(8,128)S(1)} %get-tuple-element.68), channel_id=1, source_target_pairs={{0,3},{1,2},{2,1},{3,0},{4,7},{5,6},{6,5},{7,4},{8,11},{9,10},{10,... | collective-permute-start | bytes 24584 | tf_op jit(solution)/shard_map/ppermute | solution.py:55
  35.5 2.4 %collective-permute-start.12 = (f32[8,256]{1,0:T(8,128)S(1)}, f32[8,256]{1,0:T(8,128)S(1)}, u32[]{:S(2)}, u32[]{:S(2)}) collective-permute-start(f32[8,256]{1,0:T(8,128)S(1)} %get-tuple-element.68), channel_id=1, source_target_pairs={{0,1},{1,0},{2,3},{3,2},{4,5},{5,4},{6,7},{7,6},{8,9},{9,8},{10,11... | collective-permute-start | bytes 24584 | tf_op jit(solution)/shard_map/ppermute | solution.py:55
  38.9 9.2 %collective-permute-start.14 = (f32[3,16,256]{2,1,0:T(8,128)S(1)}, f32[3,16,256]{2,1,0:T(8,128)S(1)}, u32[]{:S(2)}, u32[]{:S(2)}) collective-permute-start(f32[3,16,256]{2,1,0:T(8,128)S(1)} %get-tuple-element.71), channel_id=1, source_target_pairs={{0,16},{1,17},{2,18},{3,19},{4,20},{5,21},{6,22},{7,23},{8,24},{9,... | collective-permute-start | bytes 147464 | tf_op jit(solution)/shard_map/ppermute | solution.py:55
  39.7 8.5 %collective-permute-start.17 = (f32[3,16,256]{2,1,0:T(8,128)S(1)}, f32[3,16,256]{2,1,0:T(8,128)S(1)}, u32[]{:S(2)}, u32[]{:S(2)}) collective-permute-start(f32[3,16,256]{2,1,0:T(8,128)S(1)} %get-tuple-element.74), channel_id=1, source_target_pairs={{0,4},{1,5},{2,6},{3,7},{4,0},{5,1},{6,2},{7,3},{8,12},{9,13},{10,... | collective-permute-start | bytes 147464 | tf_op jit(solution)/shard_map/ppermute | solution.py:55
  41.6 6.5 %collective-permute-start.18 = (f32[3,16,256]{2,1,0:T(8,128)S(1)}, f32[3,16,256]{2,1,0:T(8,128)S(1)}, u32[]{:S(2)}, u32[]{:S(2)}) collective-permute-start(f32[3,16,256]{2,1,0:T(8,128)S(1)} %get-tuple-element.75), channel_id=1, source_target_pairs={{0,1},{1,0},{2,3},{3,2},{4,8},{5,9},{6,10},{7,11},{8,4},{9,5},{10,... | collective-permute-start | bytes 147464 | tf_op jit(solution)/shard_map/ppermute | solution.py:55
  41.6 6.4 %collective-permute-start.15 = (f32[8,256]{1,0:T(8,128)S(1)}, f32[8,256]{1,0:T(8,128)S(1)}, u32[]{:S(2)}, u32[]{:S(2)}) collective-permute-start(f32[8,256]{1,0:T(8,128)S(1)} %get-tuple-element.72), channel_id=1, source_target_pairs={{0,20},{1,21},{2,22},{3,23},{4,16},{5,17},{6,18},{7,19},{8,28},{9,... | collective-permute-start | bytes 24584 | tf_op jit(solution)/shard_map/ppermute | solution.py:55
  44.2 3.9 %collective-permute-start.16 = (f32[8,256]{1,0:T(8,128)S(1)}, f32[8,256]{1,0:T(8,128)S(1)}, u32[]{:S(2)}, u32[]{:S(2)}) collective-permute-start(f32[8,256]{1,0:T(8,128)S(1)} %get-tuple-element.73), channel_id=1, source_target_pairs={{0,1},{1,0},{2,3},{3,2},{4,24},{5,25},{6,26},{7,27},{8,20},{9,21},... | collective-permute-start | bytes 24584 | tf_op jit(solution)/shard_map/ppermute | solution.py:55
  44.2 11.0 %all-to-all-start.1 = ((f32[32,1,128]{2,1,0:T(1,128)}), f32[32,1,128]{2,1,0:T(1,128)S(1)}, u32[]{:S(2)}, u32[]{:S(2)}) async-start(f32[32,1,128]{2,1,0:T(1,128)} %bitcast.4), calls=%async_computation.1 | async-start | bytes 32768 | tf_op jit(solution)/shard_map/all_to_all | solution.py:602
  55.2 6.5 %copy-start.2 = (f32[16,16,256]{2,1,0:T(8,128)S(1)}, f32[16,16,256]{2,1,0:T(8,128)}, u32[]{:S(2)}) copy-start(f32[16,16,256]{2,1,0:T(8,128)} %get-tuple-element.76.refs_5_.refs_3_.refs_7_) | copy-start | bytes 786436
  55.2 6.5 %copy-start.3 = (f32[7,16,16,256]{3,2,1,0:T(8,128)S(1)}, f32[7,16,16,256]{3,2,1,0:T(8,128)}, u32[]{:S(2)}) copy-start(f32[7,16,16,256]{3,2,1,0:T(8,128)} %get-tuple-element.93.refs_6_) | copy-start | bytes 5505028
  57.3 16.2 %copy-start.4 = (f32[16,16,256]{2,1,0:T(8,128)S(1)}, f32[16,16,256]{2,1,0:T(8,128)}, u32[]{:S(2)}) copy-start(f32[16,16,256]{2,1,0:T(8,128)} %get-tuple-element.82.refs_5_.refs_2_) | copy-start | bytes 786436
  57.3 4.2 %collective-permute-start.19 = (f32[1,16,256]{2,1,0:T(8,128)S(1)}, f32[1,16,256]{2,1,0:T(8,128)S(1)}, u32[]{:S(2)}, u32[]{:S(2)}) collective-permute-start(f32[1,16,256]{2,1,0:T(8,128)S(1)} %get-tuple-element.88), channel_id=1, source_target_pairs={{0,16},{1,17},{2,18},{3,19},{4,20},{5,21},{6,22},{7,23},{8,24},{9,... | collective-permute-start | bytes 49160 | tf_op jit(solution)/shard_map/ppermute | solution.py:55
  58.0 3.7 %collective-permute-start.20 = (f32[1,16,256]{2,1,0:T(8,128)S(1)}, f32[1,16,256]{2,1,0:T(8,128)S(1)}, u32[]{:S(2)}, u32[]{:S(2)}) collective-permute-start(f32[1,16,256]{2,1,0:T(8,128)S(1)} %get-tuple-element.89), channel_id=1, source_target_pairs={{0,4},{1,5},{2,6},{3,7},{4,0},{5,1},{6,2},{7,3},{8,12},{9,13},{10,... | collective-permute-start | bytes 49160 | tf_op jit(solution)/shard_map/ppermute | solution.py:55
  58.5 3.2 %collective-permute-start.21 = (f32[1,16,256]{2,1,0:T(8,128)S(1)}, f32[1,16,256]{2,1,0:T(8,128)S(1)}, u32[]{:S(2)}, u32[]{:S(2)}) collective-permute-start(f32[1,16,256]{2,1,0:T(8,128)S(1)} %get-tuple-element.90), channel_id=1, source_target_pairs={{0,1},{1,0},{2,3},{3,2},{4,8},{5,9},{6,10},{7,11},{8,4},{9,5},{10,... | collective-permute-start | bytes 49160 | tf_op jit(solution)/shard_map/ppermute | solution.py:55
  58.5 3.1 %collective-permute-start.23 = (f32[8,256]{1,0:T(8,128)S(1)}, f32[8,256]{1,0:T(8,128)S(1)}, u32[]{:S(2)}, u32[]{:S(2)}) collective-permute-start(f32[8,256]{1,0:T(8,128)S(1)} %get-tuple-element.91), channel_id=1, source_target_pairs={{0,3},{1,2},{2,1},{3,0},{4,7},{5,6},{6,5},{7,4},{8,11},{9,10},{10,... | collective-permute-start | bytes 24584 | tf_op jit(solution)/shard_map/ppermute | solution.py:55
  59.2 2.3 %collective-permute-start.22 = (f32[8,256]{1,0:T(8,128)S(1)}, f32[8,256]{1,0:T(8,128)S(1)}, u32[]{:S(2)}, u32[]{:S(2)}) collective-permute-start(f32[8,256]{1,0:T(8,128)S(1)} %get-tuple-element.91), channel_id=1, source_target_pairs={{0,1},{1,0},{2,3},{3,2},{4,5},{5,4},{6,7},{7,6},{8,9},{9,8},{10,11... | collective-permute-start | bytes 24584 | tf_op jit(solution)/shard_map/ppermute | solution.py:55

commit v8 on v7

--- a/solution.py
+++ b/solution.py
@@ -16,9 +16,9 @@
 F32 = jnp.float32
 UNROLL = 16
 SWEEP_UNROLL = True
-PARTS = 8
-NEAR_FIRST = range(1)
-NEAR_SECOND = range(5)
+PARTS = 16
+NEAR_FIRST = range(2)
+NEAR_SECOND = range(10)
 SMOOTH_FLOPS = 10**9
 
 

time: 75 us -> 75.1 us (level)
  no operation moved by 1% of the time
where the time goes in v8:
time: 75.1 us; the launch traced here: 74.7 us
  starting transfers between devices  26.7 us (36%)
  Pallas kernels  24.2 us (32%)
  waiting for transfers between devices  11.9 us (16%)
  blocking collectives  11.1 us (15%)
  between operations  0.85 us (1%)
    pallas_call x12, Pallas kernels, call(): pl.pallas_call(body, out_shape=[pltpu.HBM(a.shape, F32) if i in distant e...  24.2 us
    ppermute x24, starting transfers between devices, swap(): return lax.ppermute(value, AXES, pairs)  20 us
    all_to_all x1, blocking collectives, spread(): return lax.all_to_all(rows, AXES, 0, 0, tiled=True)  11.1 us
    all_to_all x2, starting transfers between devices, spread(): return lax.all_to_all(rows, AXES, 0, 0, tiled=True)  6.69 us
    ppermute x24, waiting for transfers between devices, swap(): return lax.ppermute(value, AXES, pairs)  6.24 us
    all_to_all x2, waiting for transfers between devices, spread(): return lax.all_to_all(rows, AXES, 0, 0, tiled=True)  5.62 us
  transfers between devices with their start and end apart: 26, of which 6 were waited for; matrix products, arithmetic and copies ran while one was open for 0% of the time, Pallas kernels for 17%

profile of v8, /device:TPU:0, one launch (start us, length us, event | category | flops | bytes accessed | tf_op | source)
XLA Modules:
  0.0 74.7 jit_solution(6365644595326911347)
XLA Ops:
  0.6 1.7 %shard_map.77 = (f32[16,16,256]{2,1,0:T(8,128)S(1)}, f32[3,16,16,256]{3,2,1,0:T(8,128)S(1)}, f32[16,16,256]{2,1,0:T(8,128)S(1)}, f32[16,16,256]{2,1,0:T(8,128)S(1)}, f32[24,256]{1,0:T(8,128)S(1)}) custom-call(f32[3,16,16,256]{3,2,1,0:T(8,128)} %refs_5_.2, f32[16,16,256]{2,1,0:T(8,128)} %refs_6_.1, s32[16,16,256]{2,1,0:T(8,128)} %refs_7_.2, ...), custom_call_target="tpu_custom_call" | custom-call | bytes 3170304 | tf_op jit(solution)/shard_map/pallas_call | solution.py:511
  2.3 2.4 %collective-permute-start.1 = (f32[24,256]{1,0:T(8,128)S(1)}, f32[24,256]{1,0:T(8,128)S(1)}, u32[]{:S(2)}, u32[]{:S(2)}) collective-permute-start(f32[24,256]{1,0:T(8,128)S(1)} %get-tuple-element.56), channel_id=1, source_target_pairs={{0,3},{1,2},{2,1},{3,0},{4,7},{5,6},{6,5},{7,4},{8,11},{9,10},{10,... | collective-permute-start | bytes 73736 | tf_op jit(solution)/shard_map/ppermute | solution.py:55
  4.8 0.7 collective-permute-start
  5.5 3.0 %shard_map.78.refs_6_ = f32[32,128]{1,0:T(8,128)} custom-call(f32[16,16,256]{2,1,0:T(8,128)S(1)} %get-tuple-element.59.refs_0_.refs_4_, f32[16,16,16,256]{3,2,1,0:T(8,128)} %refs_16_.1), custom_call_target="tpu_custom_call" | custom-call | bytes 4472832 | tf_op jit(solution)/shard_map/pallas_call | solution.py:511
  8.5 0.0 collective-permute-done.refs_0_.refs_9_
  8.5 1.1 %shard_map.79 = (f32[13,16,256]{2,1,0:T(8,128)S(1)}, f32[28,256]{1,0:T(8,128)S(1)}, f32[28,256]{1,0:T(8,128)S(1)}, f32[13,16,256]{2,1,0:T(8,128)S(1)}, f32[13,16,256]{2,1,0:T(8,128)S(1)}) custom-call(f32[24,256]{1,0:T(8,128)S(1)} %collective-permute-done.refs_0_.refs_9_, f32[24,256]{1,0:T(8,128)S(1)} %collective-permute-done.1.refs_1_.refs_10_, ...), custom_call_target="tpu_custom_call" | custom-call | bytes 2334720 | tf_op jit(solution)/shard_map/pallas_call | solution.py:511
  9.6 1.6 %collective-permute-start.2 = (f32[13,16,256]{2,1,0:T(8,128)S(1)}, f32[13,16,256]{2,1,0:T(8,128)S(1)}, u32[]{:S(2)}, u32[]{:S(2)}) collective-permute-start(f32[13,16,256]{2,1,0:T(8,128)S(1)} %get-tuple-element.61), channel_id=1, source_target_pairs={{0,16},{1,17},{2,18},{3,19},{4,20},{5,21},{6,22},{7,23},{8,24},{9,... | collective-permute-start | bytes 638984 | tf_op jit(solution)/shard_map/ppermute | solution.py:55
  11.2 1.6 %collective-permute-start.5 = (f32[13,16,256]{2,1,0:T(8,128)S(1)}, f32[13,16,256]{2,1,0:T(8,128)S(1)}, u32[]{:S(2)}, u32[]{:S(2)}) collective-permute-start(f32[13,16,256]{2,1,0:T(8,128)S(1)} %get-tuple-element.64), channel_id=1, source_target_pairs={{0,4},{1,5},{2,6},{3,7},{4,0},{5,1},{6,2},{7,3},{8,12},{9,13},{10,... | collective-permute-start | bytes 638984 | tf_op jit(solution)/shard_map/ppermute | solution.py:55
  12.8 0.0 collective-permute-start.6
  12.8 3.1 %collective-permute-start.3 = (f32[28,256]{1,0:T(8,128)S(1)}, f32[28,256]{1,0:T(8,128)S(1)}, u32[]{:S(2)}, u32[]{:S(2)}) collective-permute-start(f32[28,256]{1,0:T(8,128)S(1)} %get-tuple-element.62), channel_id=1, source_target_pairs={{0,20},{1,21},{2,22},{3,23},{4,16},{5,17},{6,18},{7,19},{8,28},{9,... | collective-permute-start | bytes 86024 | tf_op jit(solution)/shard_map/ppermute | solution.py:55
  15.9 2.8 %all-to-all-start = ((f32[32,1,128]{2,1,0:T(1,128)}), f32[32,1,128]{2,1,0:T(1,128)S(1)}, u32[]{:S(2)}, u32[]{:S(2)}) async-start(f32[32,1,128]{2,1,0:T(1,128)} %bitcast.1), calls=%async_computation | async-start | bytes 32768 | tf_op jit(solution)/shard_map/all_to_all | solution.py:602
  18.7 0.0 collective-permute-done.3.refs_1_
  18.7 0.0 collective-permute-done.4.refs_2_
  18.7 4.7 %shard_map.80 = (f32[1,16,16,256]{3,2,1,0:T(8,128)S(1)}, f32[1,16,16,256]{3,2,1,0:T(8,128)S(1)}, f32[22,24,384]{2,1,0:T(8,128)}, f32[22,24,384]{2,1,0:T(8,128)},...) custom-call(f32[13,16,256]{2,1,0:T(8,128)S(1)} %collective-permute-d, ...), custom_call_target="tpu_custom_call" | custom-call | flops 1000000000 | bytes 12378112 | tf_op jit(solution)/shard_map/pallas_call | solution.py:511
  23.5 2.3 %all-to-all-done = f32[32,1,128]{2,1,0:T(1,128)S(1)} async-done(((f32[32,1,128]{2,1,0:T(1,128)}), f32[32,1,128]{2,1,0:T(1,128)S(1)}, u32[]{:S(2)}, u32[]{:S(2)}) %all-to-all-start) | async-done | bytes 16416 | tf_op jit(solution)/shard_map/all_to_all | solution.py:602
  25.8 2.5 %shard_map.81 = (f32[1,16,256]{2,1,0:T(8,128)S(1)}, f32[1,16,256]{2,1,0:T(8,128)S(1)}, f32[1,16,256]{2,1,0:T(8,128)S(1)}, f32[8,256]{1,0:T(8,128)S(1)}, f32[16,16,256]{2,1,0:T(8,128)S(1)}) custom-call(f32[16,16,256]{2,1,0:T(8,128)S(1)} %get-tuple-element.66.refs_0_, f32[32,128]{1,0:T(8,128)S(1)} %bitcast.13, f32[16,512]{1,0:T(8,128)} %refs_2_.5, ...), custom_call_target="tpu_custom_call" | custom-call | bytes 5349376 | tf_op jit(solution)/shard_map/pallas_call | solution.py:511
  28.3 0.7 collective-permute-start.7
  28.9 1.4 %collective-permute-start.8 = (f32[1,16,256]{2,1,0:T(8,128)S(1)}, f32[1,16,256]{2,1,0:T(8,128)S(1)}, u32[]{:S(2)}, u32[]{:S(2)}) collective-permute-start(f32[1,16,256]{2,1,0:T(8,128)S(1)} %get-tuple-element.70), channel_id=1, source_target_pairs={{0,4},{1,5},{2,6},{3,7},{4,0},{5,1},{6,2},{7,3},{8,12},{9,13},{10,... | collective-permute-start | bytes 49160 | tf_op jit(solution)/shard_map/ppermute | solution.py:55
  30.3 0.6 collective-permute-start.11
  31.0 0.0 collective-permute-start.10
  31.0 2.4 %collective-permute-done.11.refs_4_ = f32[8,256]{1,0:T(8,128)S(1)} collective-permute-done((f32[8,256]{1,0:T(8,128)S(1)}, f32[8,256]{1,0:T(8,128)S(1)}, u32[]{:S(2)}, u32[]{:S(2)}) %collective-permute-start.11) | collective-permute-done | bytes 8224 | tf_op jit(solution)/shard_map/ppermute | solution.py:55
  33.4 0.0 collective-permute-done.8.refs_1_
  33.4 0.0 collective-permute-done.9.refs_2_
  33.4 1.4 %shard_map.82 = (f32[16,16,256]{2,1,0:T(8,128)S(1)}, f32[16,16,256]{2,1,0:T(8,128)}, f32[7,16,16,256]{3,2,1,0:T(8,128)}, f32[1,128]{1,0:T(1,128)S(1)}, f32[8,256]{1,0:T(8,128)S(1)}, /*index=5*/f32[16,16,256]{2,1,0:T(8,128)}) custom-call(f32[1,16,256]{2,1,0:T(8,128)S(1)} %collective-permute-done.7.refs_0_, f32[1,16,256]{2,1,0:T(8,128)S(1)} %collective-permute-done.8.refs_1_, ...), custom_call_target="tpu_custom_call" | custom-call | bytes 5054976 | tf_op jit(solution)/shard_map/pallas_call | solution.py:511
  34.9 0.7 collective-permute-start.13
  35.6 0.0 collective-permute-start.12
  35.6 1.2 %shard_map.83.refs_3_ = f32[32,128]{1,0:T(8,128)} custom-call(f32[16,16,16,256]{3,2,1,0:T(8,128)S(1)} %copy-done, f32[16,16,256]{2,1,0:T(8,128)S(1)} %get-tuple-element.76.refs_1_.refs_2_, f32[1,128]{1,0:T(1,128)S(1)} %get-tuple-element.77.refs_2_), custom_call_target="tpu_custom_call" | custom-call | bytes 4473344 | tf_op jit(solution)/shard_map/pallas_call | solution.py:511
  36.8 1.2 %collective-permute-done.13.refs_1_.refs_7_ = f32[8,256]{1,0:T(8,128)S(1)} collective-permute-done((f32[8,256]{1,0:T(8,128)S(1)}, f32[8,256]{1,0:T(8,128)S(1)}, u32[]{:S(2)}, u32[]{:S(2)}) %collective-permute-start.13) | collective-permute-done | bytes 8224 | tf_op jit(solution)/shard_map/ppermute | solution.py:55
  38.0 0.0 collective-permute-done.12.refs_0_.refs_6_
  38.0 1.0 %shard_map.84 = (f32[3,16,256]{2,1,0:T(8,128)S(1)}, f32[8,256]{1,0:T(8,128)S(1)}, f32[8,256]{1,0:T(8,128)S(1)}, f32[3,16,256]{2,1,0:T(8,128)S(1)}, f32[3,16,256]{2,1,0:T(8,128)S(1)}) custom-call(f32[8,256]{1,0:T(8,128)S(1)} %collective-permute-done.12.refs_0_.refs_6_, f32[8,256]{1,0:T(8,128)S(1)} %collective-permute-done.13.refs_1_.refs_7_, ...), custom_call_target="tpu_custom_call" | custom-call | bytes 458752 | tf_op jit(solution)/shard_map/pallas_call | solution.py:511
  39.0 0.8 %collective-permute-start.14 = (f32[3,16,256]{2,1,0:T(8,128)S(1)}, f32[3,16,256]{2,1,0:T(8,128)S(1)}, u32[]{:S(2)}, u32[]{:S(2)}) collective-permute-start(f32[3,16,256]{2,1,0:T(8,128)S(1)} %get-tuple-element.78), channel_id=1, source_target_pairs={{0,16},{1,17},{2,18},{3,19},{4,20},{5,21},{6,22},{7,23},{8,24},{9,... | collective-permute-start | bytes 147464 | tf_op jit(solution)/shard_map/ppermute | solution.py:55
  39.7 2.0 %collective-permute-start.17 = (f32[3,16,256]{2,1,0:T(8,128)S(1)}, f32[3,16,256]{2,1,0:T(8,128)S(1)}, u32[]{:S(2)}, u32[]{:S(2)}) collective-permute-start(f32[3,16,256]{2,1,0:T(8,128)S(1)} %get-tuple-element.81), channel_id=1, source_target_pairs={{0,4},{1,5},{2,6},{3,7},{4,0},{5,1},{6,2},{7,3},{8,12},{9,13},{10,... | collective-permute-start | bytes 147464 | tf_op jit(solution)/shard_map/ppermute | solution.py:55
  41.7 0.0 collective-permute-start.18
  41.7 2.5 %collective-permute-start.15 = (f32[8,256]{1,0:T(8,128)S(1)}, f32[8,256]{1,0:T(8,128)S(1)}, u32[]{:S(2)}, u32[]{:S(2)}) collective-permute-start(f32[8,256]{1,0:T(8,128)S(1)} %get-tuple-element.79), channel_id=1, source_target_pairs={{0,20},{1,21},{2,22},{3,23},{4,16},{5,17},{6,18},{7,19},{8,28},{9,... | collective-permute-start | bytes 24584 | tf_op jit(solution)/shard_map/ppermute | solution.py:55
  44.3 3.9 %all-to-all-start.1 = ((f32[32,1,128]{2,1,0:T(1,128)}), f32[32,1,128]{2,1,0:T(1,128)S(1)}, u32[]{:S(2)}, u32[]{:S(2)}) async-start(f32[32,1,128]{2,1,0:T(1,128)} %bitcast.4), calls=%async_computation.1 | async-start | bytes 32768 | tf_op jit(solution)/shard_map/all_to_all | solution.py:602
  48.2 3.7 %shard_map.85 = (f32[1,16,16,256]{3,2,1,0:T(8,128)S(1)}, f32[1,16,16,256]{3,2,1,0:T(8,128)S(1)}, f32[1,16,16,256]{3,2,1,0:T(8,128)S(1)}, f32[1,16,16,256]{3,2,1,...) custom-call(f32[3,16,256]{2,1,0:T(8,128)S(1)} %collective-permute-do, ...), custom_call_target="tpu_custom_call" | custom-call | flops 1000000000 | bytes 10764288 | tf_op jit(solution)/shard_map/pallas_call | solution.py:511
  52.0 3.4 %all-to-all-done.1 = f32[32,1,128]{2,1,0:T(1,128)S(1)} async-done(((f32[32,1,128]{2,1,0:T(1,128)}), f32[32,1,128]{2,1,0:T(1,128)S(1)}, u32[]{:S(2)}, u32[]{:S(2)}) %all-to-all-start.1) | async-done | bytes 16416 | tf_op jit(solution)/shard_map/all_to_all | solution.py:602
  55.3 2.1 %shard_map.86 = (f32[1,16,256]{2,1,0:T(8,128)S(1)}, f32[1,16,256]{2,1,0:T(8,128)S(1)}, f32[1,16,256]{2,1,0:T(8,128)S(1)}, f32[16,16,256]{2,1,0:T(8,128)S(1)}, f3...) custom-call(f32[16,16,256]{2,1,0:T(8,128)S(1)} %get-tuple-element.88.refs_0_, ...), custom_call_target="tpu_custom_call" | custom-call | bytes 8503296 | tf_op jit(solution)/shard_map/pallas_call | solution.py:511
  57.4 0.0 copy-start.4
  57.4 0.7 collective-permute-start.19
  58.1 0.5 collective-permute-start.20
  58.6 0.7 collective-permute-start.23
  59.3 0.0 collective-permute-start.22
  59.3 2.3 %collective-permute-done.23.refs_4_ = f32[8,256]{1,0:T(8,128)S(1)} collective-permute-done((f32[8,256]{1,0:T(8,128)S(1)}, f32[8,256]{1,0:T(8,128)S(1)}, u32[]{:S(2)}, u32[]{:S(2)}) %collective-permute-start.23) | collective-permute-done | bytes 8224 | tf_op jit(solution)/shard_map/ppermute | solution.py:55
  61.7 0.1 collective-permute-done.20.refs_1_
  61.8 0.7 shard_map.87
  62.5 11.1 %all_to_all.33 = f32[32,1,128]{2,1,0:T(1,128)S(1)} all-to-all(f32[32,1,128]{2,1,0:T(1,128)S(1)} %bitcast.15), channel_id=1, replica_groups=mesh['gx'=2,'gy'=4,'gz'=4] {'gx','gy','gz'}, dimensions={0} | all-to-all | bytes 32768 | tf_op jit(solution)/shard_map/all_to_all | solution.py:602
  73.6 1.1 %shard_map.88 = (f32[16,16,256]{2,1,0:T(8,128)}, f32[16,16,256]{2,1,0:T(8,128)}) custom-call(f32[32,128]{1,0:T(8,128)S(1)} %bitcast.14, f32[16,128]{1,0:T(8,128)S(1)} %get-tuple-element.108.refs_1_, f32[16,16,256]{2,1,0:T(8,128)S(1)} %copy-done.4, f32[16,16,256]{2,1,0:T(8,128)S(1)} %copy-done.2, f32[16,16,256]{2,1,0:T(8,128)S(1)} %get-tuple-element.104.refs_5_.refs_4_, ...), custom_call_target="tpu_custom_call" | custom-call | bytes 1859584 | tf_op jit(solution)/shard_map/pallas_call | solution.py:511
  (27 shorter events, 0.1 us)
Async XLA Ops:
  2.3 6.1 %collective-permute-start.1 = (f32[24,256]{1,0:T(8,128)S(1)}, f32[24,256]{1,0:T(8,128)S(1)}, u32[]{:S(2)}, u32[]{:S(2)}) collective-permute-start(f32[24,256]{1,0:T(8,128)S(1)} %get-tuple-element.56), channel_id=1, source_target_pairs={{0,3},{1,2},{2,1},{3,0},{4,7},{5,6},{6,5},{7,4},{8,11},{9,10},{10,... | collective-permute-start | bytes 73736 | tf_op jit(solution)/shard_map/ppermute | solution.py:55
  4.8 3.7 %collective-permute-start = (f32[24,256]{1,0:T(8,128)S(1)}, f32[24,256]{1,0:T(8,128)S(1)}, u32[]{:S(2)}, u32[]{:S(2)}) collective-permute-start(f32[24,256]{1,0:T(8,128)S(1)} %get-tuple-element.56), channel_id=1, source_target_pairs={{0,1},{1,0},{2,3},{3,2},{4,5},{5,4},{6,7},{7,6},{8,9},{9,8},{10,11... | collective-permute-start | bytes 73736 | tf_op jit(solution)/shard_map/ppermute | solution.py:55
  9.6 9.1 %collective-permute-start.2 = (f32[13,16,256]{2,1,0:T(8,128)S(1)}, f32[13,16,256]{2,1,0:T(8,128)S(1)}, u32[]{:S(2)}, u32[]{:S(2)}) collective-permute-start(f32[13,16,256]{2,1,0:T(8,128)S(1)} %get-tuple-element.61), channel_id=1, source_target_pairs={{0,16},{1,17},{2,18},{3,19},{4,20},{5,21},{6,22},{7,23},{8,24},{9,... | collective-permute-start | bytes 638984 | tf_op jit(solution)/shard_map/ppermute | solution.py:55
  11.2 7.5 %collective-permute-start.5 = (f32[13,16,256]{2,1,0:T(8,128)S(1)}, f32[13,16,256]{2,1,0:T(8,128)S(1)}, u32[]{:S(2)}, u32[]{:S(2)}) collective-permute-start(f32[13,16,256]{2,1,0:T(8,128)S(1)} %get-tuple-element.64), channel_id=1, source_target_pairs={{0,4},{1,5},{2,6},{3,7},{4,0},{5,1},{6,2},{7,3},{8,12},{9,13},{10,... | collective-permute-start | bytes 638984 | tf_op jit(solution)/shard_map/ppermute | solution.py:55
  12.8 6.0 %collective-permute-start.6 = (f32[13,16,256]{2,1,0:T(8,128)S(1)}, f32[13,16,256]{2,1,0:T(8,128)S(1)}, u32[]{:S(2)}, u32[]{:S(2)}) collective-permute-start(f32[13,16,256]{2,1,0:T(8,128)S(1)} %get-tuple-element.65), channel_id=1, source_target_pairs={{0,1},{1,0},{2,3},{3,2},{4,8},{5,9},{6,10},{7,11},{8,4},{9,5},{10,... | collective-permute-start | bytes 638984 | tf_op jit(solution)/shard_map/ppermute | solution.py:55
  12.8 5.9 %collective-permute-start.3 = (f32[28,256]{1,0:T(8,128)S(1)}, f32[28,256]{1,0:T(8,128)S(1)}, u32[]{:S(2)}, u32[]{:S(2)}) collective-permute-start(f32[28,256]{1,0:T(8,128)S(1)} %get-tuple-element.62), channel_id=1, source_target_pairs={{0,20},{1,21},{2,22},{3,23},{4,16},{5,17},{6,18},{7,19},{8,28},{9,... | collective-permute-start | bytes 86024 | tf_op jit(solution)/shard_map/ppermute | solution.py:55
  15.9 2.9 %collective-permute-start.4 = (f32[28,256]{1,0:T(8,128)S(1)}, f32[28,256]{1,0:T(8,128)S(1)}, u32[]{:S(2)}, u32[]{:S(2)}) collective-permute-start(f32[28,256]{1,0:T(8,128)S(1)} %get-tuple-element.63), channel_id=1, source_target_pairs={{0,1},{1,0},{2,3},{3,2},{4,24},{5,25},{6,26},{7,27},{8,20},{9,21},... | collective-permute-start | bytes 86024 | tf_op jit(solution)/shard_map/ppermute | solution.py:55
  15.9 9.9 %all-to-all-start = ((f32[32,1,128]{2,1,0:T(1,128)}), f32[32,1,128]{2,1,0:T(1,128)S(1)}, u32[]{:S(2)}, u32[]{:S(2)}) async-start(f32[32,1,128]{2,1,0:T(1,128)} %bitcast.1), calls=%async_computation | async-start | bytes 32768 | tf_op jit(solution)/shard_map/all_to_all | solution.py:602
  25.8 7.7 %copy-start.1 = (f32[16,16,256]{2,1,0:T(8,128)S(1)}, f32[16,16,256]{2,1,0:T(8,128)}, u32[]{:S(2)}) copy-start(f32[16,16,256]{2,1,0:T(8,128)} %refs_4_.1) | copy-start | bytes 786436
  25.8 9.8 %copy-start = (f32[16,16,16,256]{3,2,1,0:T(8,128)S(1)}, f32[16,16,16,256]{3,2,1,0:T(8,128)}, u32[]{:S(2)}) copy-start(f32[16,16,16,256]{3,2,1,0:T(8,128)} %refs_16_.1) | copy-start | bytes 12582916
  28.3 5.1 %collective-permute-start.7 = (f32[1,16,256]{2,1,0:T(8,128)S(1)}, f32[1,16,256]{2,1,0:T(8,128)S(1)}, u32[]{:S(2)}, u32[]{:S(2)}) collective-permute-start(f32[1,16,256]{2,1,0:T(8,128)S(1)} %get-tuple-element.69), channel_id=1, source_target_pairs={{0,16},{1,17},{2,18},{3,19},{4,20},{5,21},{6,22},{7,23},{8,24},{9,... | collective-permute-start | bytes 49160 | tf_op jit(solution)/shard_map/ppermute | solution.py:55
  28.9 4.5 %collective-permute-start.8 = (f32[1,16,256]{2,1,0:T(8,128)S(1)}, f32[1,16,256]{2,1,0:T(8,128)S(1)}, u32[]{:S(2)}, u32[]{:S(2)}) collective-permute-start(f32[1,16,256]{2,1,0:T(8,128)S(1)} %get-tuple-element.70), channel_id=1, source_target_pairs={{0,4},{1,5},{2,6},{3,7},{4,0},{5,1},{6,2},{7,3},{8,12},{9,13},{10,... | collective-permute-start | bytes 49160 | tf_op jit(solution)/shard_map/ppermute | solution.py:55
  30.3 3.1 %collective-permute-start.9 = (f32[1,16,256]{2,1,0:T(8,128)S(1)}, f32[1,16,256]{2,1,0:T(8,128)S(1)}, u32[]{:S(2)}, u32[]{:S(2)}) collective-permute-start(f32[1,16,256]{2,1,0:T(8,128)S(1)} %get-tuple-element.71), channel_id=1, source_target_pairs={{0,1},{1,0},{2,3},{3,2},{4,8},{5,9},{6,10},{7,11},{8,4},{9,5},{10,... | collective-permute-start | bytes 49160 | tf_op jit(solution)/shard_map/ppermute | solution.py:55
  30.3 3.1 %collective-permute-start.11 = (f32[8,256]{1,0:T(8,128)S(1)}, f32[8,256]{1,0:T(8,128)S(1)}, u32[]{:S(2)}, u32[]{:S(2)}) collective-permute-start(f32[8,256]{1,0:T(8,128)S(1)} %get-tuple-element.72), channel_id=1, source_target_pairs={{0,3},{1,2},{2,1},{3,0},{4,7},{5,6},{6,5},{7,4},{8,11},{9,10},{10,... | collective-permute-start | bytes 24584 | tf_op jit(solution)/shard_map/ppermute | solution.py:55
  31.0 2.4 %collective-permute-start.10 = (f32[8,256]{1,0:T(8,128)S(1)}, f32[8,256]{1,0:T(8,128)S(1)}, u32[]{:S(2)}, u32[]{:S(2)}) collective-permute-start(f32[8,256]{1,0:T(8,128)S(1)} %get-tuple-element.72), channel_id=1, source_target_pairs={{0,1},{1,0},{2,3},{3,2},{4,5},{5,4},{6,7},{7,6},{8,9},{9,8},{10,11... | collective-permute-start | bytes 24584 | tf_op jit(solution)/shard_map/ppermute | solution.py:55
  34.9 3.1 %collective-permute-start.13 = (f32[8,256]{1,0:T(8,128)S(1)}, f32[8,256]{1,0:T(8,128)S(1)}, u32[]{:S(2)}, u32[]{:S(2)}) collective-permute-start(f32[8,256]{1,0:T(8,128)S(1)} %get-tuple-element.75), channel_id=1, source_target_pairs={{0,3},{1,2},{2,1},{3,0},{4,7},{5,6},{6,5},{7,4},{8,11},{9,10},{10,... | collective-permute-start | bytes 24584 | tf_op jit(solution)/shard_map/ppermute | solution.py:55
  35.6 2.4 %collective-permute-start.12 = (f32[8,256]{1,0:T(8,128)S(1)}, f32[8,256]{1,0:T(8,128)S(1)}, u32[]{:S(2)}, u32[]{:S(2)}) collective-permute-start(f32[8,256]{1,0:T(8,128)S(1)} %get-tuple-element.75), channel_id=1, source_target_pairs={{0,1},{1,0},{2,3},{3,2},{4,5},{5,4},{6,7},{7,6},{8,9},{9,8},{10,11... | collective-permute-start | bytes 24584 | tf_op jit(solution)/shard_map/ppermute | solution.py:55
  39.0 9.2 %collective-permute-start.14 = (f32[3,16,256]{2,1,0:T(8,128)S(1)}, f32[3,16,256]{2,1,0:T(8,128)S(1)}, u32[]{:S(2)}, u32[]{:S(2)}) collective-permute-start(f32[3,16,256]{2,1,0:T(8,128)S(1)} %get-tuple-element.78), channel_id=1, source_target_pairs={{0,16},{1,17},{2,18},{3,19},{4,20},{5,21},{6,22},{7,23},{8,24},{9,... | collective-permute-start | bytes 147464 | tf_op jit(solution)/shard_map/ppermute | solution.py:55
  39.7 8.5 %collective-permute-start.17 = (f32[3,16,256]{2,1,0:T(8,128)S(1)}, f32[3,16,256]{2,1,0:T(8,128)S(1)}, u32[]{:S(2)}, u32[]{:S(2)}) collective-permute-start(f32[3,16,256]{2,1,0:T(8,128)S(1)} %get-tuple-element.81), channel_id=1, source_target_pairs={{0,4},{1,5},{2,6},{3,7},{4,0},{5,1},{6,2},{7,3},{8,12},{9,13},{10,... | collective-permute-start | bytes 147464 | tf_op jit(solution)/shard_map/ppermute | solution.py:55
  41.7 6.5 %collective-permute-start.18 = (f32[3,16,256]{2,1,0:T(8,128)S(1)}, f32[3,16,256]{2,1,0:T(8,128)S(1)}, u32[]{:S(2)}, u32[]{:S(2)}) collective-permute-start(f32[3,16,256]{2,1,0:T(8,128)S(1)} %get-tuple-element.82), channel_id=1, source_target_pairs={{0,1},{1,0},{2,3},{3,2},{4,8},{5,9},{6,10},{7,11},{8,4},{9,5},{10,... | collective-permute-start | bytes 147464 | tf_op jit(solution)/shard_map/ppermute | solution.py:55
  41.7 6.4 %collective-permute-start.15 = (f32[8,256]{1,0:T(8,128)S(1)}, f32[8,256]{1,0:T(8,128)S(1)}, u32[]{:S(2)}, u32[]{:S(2)}) collective-permute-start(f32[8,256]{1,0:T(8,128)S(1)} %get-tuple-element.79), channel_id=1, source_target_pairs={{0,20},{1,21},{2,22},{3,23},{4,16},{5,17},{6,18},{7,19},{8,28},{9,... | collective-permute-start | bytes 24584 | tf_op jit(solution)/shard_map/ppermute | solution.py:55
  44.3 3.9 %collective-permute-start.16 = (f32[8,256]{1,0:T(8,128)S(1)}, f32[8,256]{1,0:T(8,128)S(1)}, u32[]{:S(2)}, u32[]{:S(2)}) collective-permute-start(f32[8,256]{1,0:T(8,128)S(1)} %get-tuple-element.80), channel_id=1, source_target_pairs={{0,1},{1,0},{2,3},{3,2},{4,24},{5,25},{6,26},{7,27},{8,20},{9,21},... | collective-permute-start | bytes 24584 | tf_op jit(solution)/shard_map/ppermute | solution.py:55
  44.3 11.0 %all-to-all-start.1 = ((f32[32,1,128]{2,1,0:T(1,128)}), f32[32,1,128]{2,1,0:T(1,128)S(1)}, u32[]{:S(2)}, u32[]{:S(2)}) async-start(f32[32,1,128]{2,1,0:T(1,128)} %bitcast.4), calls=%async_computation.1 | async-start | bytes 32768 | tf_op jit(solution)/shard_map/all_to_all | solution.py:602
  55.3 6.5 %copy-start.2 = (f32[16,16,256]{2,1,0:T(8,128)S(1)}, f32[16,16,256]{2,1,0:T(8,128)}, u32[]{:S(2)}) copy-start(f32[16,16,256]{2,1,0:T(8,128)} %get-tuple-element.83.refs_5_.refs_3_.refs_7_) | copy-start | bytes 786436
  55.3 6.5 %copy-start.3 = (f32[7,16,16,256]{3,2,1,0:T(8,128)S(1)}, f32[7,16,16,256]{3,2,1,0:T(8,128)}, u32[]{:S(2)}) copy-start(f32[7,16,16,256]{3,2,1,0:T(8,128)} %get-tuple-element.105.refs_6_) | copy-start | bytes 5505028
  57.4 16.2 %copy-start.4 = (f32[16,16,256]{2,1,0:T(8,128)S(1)}, f32[16,16,256]{2,1,0:T(8,128)}, u32[]{:S(2)}) copy-start(f32[16,16,256]{2,1,0:T(8,128)} %get-tuple-element.89.refs_5_.refs_2_) | copy-start | bytes 786436
  57.4 4.2 %collective-permute-start.19 = (f32[1,16,256]{2,1,0:T(8,128)S(1)}, f32[1,16,256]{2,1,0:T(8,128)S(1)}, u32[]{:S(2)}, u32[]{:S(2)}) collective-permute-start(f32[1,16,256]{2,1,0:T(8,128)S(1)} %get-tuple-element.100), channel_id=1, source_target_pairs={{0,16},{1,17},{2,18},{3,19},{4,20},{5,21},{6,22},{7,23},{8,24},{9,... | collective-permute-start | bytes 49160 | tf_op jit(solution)/shard_map/ppermute | solution.py:55
  58.1 3.7 %collective-permute-start.20 = (f32[1,16,256]{2,1,0:T(8,128)S(1)}, f32[1,16,256]{2,1,0:T(8,128)S(1)}, u32[]{:S(2)}, u32[]{:S(2)}) collective-permute-start(f32[1,16,256]{2,1,0:T(8,128)S(1)} %get-tuple-element.101), channel_id=1, source_target_pairs={{0,4},{1,5},{2,6},{3,7},{4,0},{5,1},{6,2},{7,3},{8,12},{9,13},{10,... | collective-permute-start | bytes 49160 | tf_op jit(solution)/shard_map/ppermute | solution.py:55
  58.6 3.2 %collective-permute-start.21 = (f32[1,16,256]{2,1,0:T(8,128)S(1)}, f32[1,16,256]{2,1,0:T(8,128)S(1)}, u32[]{:S(2)}, u32[]{:S(2)}) collective-permute-start(f32[1,16,256]{2,1,0:T(8,128)S(1)} %get-tuple-element.102), channel_id=1, source_target_pairs={{0,1},{1,0},{2,3},{3,2},{4,8},{5,9},{6,10},{7,11},{8,4},{9,5},{10,... | collective-permute-start | bytes 49160 | tf_op jit(solution)/shard_map/ppermute | solution.py:55
  58.6 3.1 %collective-permute-start.23 = (f32[8,256]{1,0:T(8,128)S(1)}, f32[8,256]{1,0:T(8,128)S(1)}, u32[]{:S(2)}, u32[]{:S(2)}) collective-permute-start(f32[8,256]{1,0:T(8,128)S(1)} %get-tuple-element.103), channel_id=1, source_target_pairs={{0,3},{1,2},{2,1},{3,0},{4,7},{5,6},{6,5},{7,4},{8,11},{9,10},{10,... | collective-permute-start | bytes 24584 | tf_op jit(solution)/shard_map/ppermute | solution.py:55
  59.3 2.3 %collective-permute-start.22 = (f32[8,256]{1,0:T(8,128)S(1)}, f32[8,256]{1,0:T(8,128)S(1)}, u32[]{:S(2)}, u32[]{:S(2)}) collective-permute-start(f32[8,256]{1,0:T(8,128)S(1)} %get-tuple-element.103), channel_id=1, source_target_pairs={{0,1},{1,0},{2,3},{3,2},{4,5},{5,4},{6,7},{7,6},{8,9},{9,8},{10,11... | collective-permute-start | bytes 24584 | tf_op jit(solution)/shard_map/ppermute | solution.py:55
